TPU v7x, 32 devices: a whole 2x2x4 slice. The times are simulated.
32 devices in a mesh: seq: 8 (over z, x), kvh: 4 (over y, core).
Axes of the slice: x: 2, y: 2, z: 4, core: 2. Of those that a mesh axis runs over, the one named last changes fastest.
Arguments:
- queries: bfloat16 [1024, 64, 128], P('seq', 'kvh'), may hold values from -160 to 160
- keys: bfloat16 [1024, 8, 128], P('seq', 'kvh'), may hold values from -4 to 4
- values: bfloat16 [1024, 8, 128], P('seq', 'kvh'), may hold values from -6 to 6
- output_gradient: bfloat16 [1024, 64, 128], P(('seq', 'kvh')), may hold values from -6 to 6
- doc_lengths: int32 [8], replicated, may hold values from 1 to 256, 1024 in all
- prefix_lengths: int32 [8], replicated, may hold values from 0 to 127
Outputs:
- grad_queries: bfloat16 [1024, 64, 128], P(('seq', 'kvh'))
- grad_keys: bfloat16 [1024, 8, 128], P('seq', 'kvh')
- grad_values: bfloat16 [1024, 8, 128], P('seq', 'kvh')
Inputs may be any that keep to these rules, and one draw needn't show every extreme that they name: `doc_lengths`: lengths sum to 1024; the longest document has exactly 256 tokens.
All inputs are finite; a program needn't handle non-finite values.
Results may differ from a plain program's by a relative error of at most 0.015.
Values may be sent and summed in bfloat16 or wider, within the bound.
No kernel may reach another device: no remote copies, remote signals or barrier semaphores. Data moves between devices by JAX's collectives and lax.ppermute only.
A program may use at most 64 MiB of HBM per device.

v0:
```python
import jax
import jax.numpy as jnp
from jax import lax
from jax.sharding import PartitionSpec as P

BACK = 2


def shifted(block, axis, distance):
    devices = range(lax.axis_size(axis))
    route = [(i - distance, i) for i in devices if i - distance in devices]
    return lax.ppermute(block, axis, route)


def locate(positions, doc_end):
    return jnp.sum((positions[:, None] >= doc_end[None, :]).astype(jnp.int32), axis=1)


def scores_of(query_split, key_block, visible, score_scale):
    raw_scores = (
        jnp.einsum("tgqd,sgd->gqts", query_split, key_block, preferred_element_type=jnp.float32)
        * score_scale
    )
    return jnp.where(visible[None, None], raw_scores, -1e30)


def dprobs_of(cot_split, value_block):
    return jnp.einsum("tgqd,sgd->gqts", cot_split, value_block, preferred_element_type=jnp.float32)


def grads_of(probs, dprobs, row_delta, key_block, query_split, cot_split, score_scale):
    dscores = (probs * (dprobs - row_delta[..., None])).astype(jnp.bfloat16)
    probs_half = probs.astype(jnp.bfloat16)
    query_term = jnp.einsum(
        "gqts,sgd->tgqd", dscores, key_block, preferred_element_type=jnp.float32
    )
    key_term = (
        jnp.einsum("gqts,tgqd->sgd", dscores, query_split, preferred_element_type=jnp.float32)
        * score_scale
    )
    value_term = jnp.einsum(
        "gqts,tgqd->sgd", probs_half, cot_split, preferred_element_type=jnp.float32
    )
    return (query_term, key_term, value_term)


def local(queries, keys, values, output_gradient, doc_lengths, prefix_lengths):
    rows_dev, heads_dev, head_size = queries.shape
    kv_heads = keys.shape[1]
    group_size = heads_dev // kv_heads
    score_scale = head_size ** (-0.5)
    seq_count = lax.axis_size("seq")
    seq_index = lax.axis_index("seq")
    cotangent = lax.all_to_all(output_gradient, "kvh", split_axis=1, concat_axis=0, tiled=True)
    query_split = queries.reshape(rows_dev, kv_heads, group_size, head_size)
    cot_split = cotangent.reshape(rows_dev, kv_heads, group_size, head_size)
    doc_end = jnp.cumsum(doc_lengths)
    prefix_end = doc_end - doc_lengths + prefix_lengths
    doc_slots = jnp.arange(doc_lengths.shape[0], dtype=jnp.int32)
    local_rows = jnp.arange(rows_dev, dtype=jnp.int32)
    query_pos = seq_index * rows_dev + local_rows
    query_doc = locate(query_pos, doc_end)
    offsets = [0] + [back_by for back_by in range(1, BACK + 1)] + [-1]
    tiles = []
    for shift_by in offsets:
        if shift_by == 0:
            key_block, value_block = (keys, values)
        else:
            key_block, value_block = shifted((keys, values), "seq", shift_by)
        source_shard = seq_index - shift_by
        key_pos = source_shard * rows_dev + local_rows
        key_doc = locate(key_pos, doc_end)
        key_prefix = jnp.sum(
            jnp.where(key_doc[:, None] == doc_slots[None, :], prefix_end[None, :], 0), axis=1
        )
        inside = (source_shard >= 0) & (source_shard < seq_count)
        same_doc = query_doc[:, None] == key_doc[None, :]
        allowed = (key_pos[None, :] <= query_pos[:, None]) | (
            key_pos[None, :] < key_prefix[None, :]
        )
        visible = same_doc & allowed & inside
        tiles.append((key_block, value_block, visible, jnp.any(visible)))
    score_tiles = []
    row_max = None
    for key_block, value_block, visible, needed in tiles:
        tile_scores = scores_of(query_split, key_block, visible, score_scale)
        score_tiles.append(tile_scores)
        tile_max = jnp.max(tile_scores, axis=-1)
        row_max = tile_max if row_max is None else jnp.maximum(row_max, tile_max)
    expo_tiles = []
    row_sum = jnp.zeros(row_max.shape, jnp.float32)
    for number, tile_scores in enumerate(score_tiles):
        expo = jnp.where(
            tiles[number][2][None, None], jnp.exp(tile_scores - row_max[..., None]), 0.0
        )
        expo_tiles.append(expo)
        row_sum = row_sum + jnp.sum(expo, axis=-1)
    prob_tiles = []
    dprob_tiles = []
    row_delta = jnp.zeros(row_max.shape, jnp.float32)
    for number, expo in enumerate(expo_tiles):
        probs = expo / row_sum[..., None]
        value_block = tiles[number][1]
        dprobs = dprobs_of(cot_split, value_block)
        prob_tiles.append(probs)
        dprob_tiles.append(dprobs)
        row_delta = row_delta + jnp.sum(probs * dprobs, axis=-1)
    query_acc = jnp.zeros((rows_dev, kv_heads, group_size, head_size), jnp.float32)
    partial_list = []
    for number, probs in enumerate(prob_tiles):
        key_block = tiles[number][0]
        query_term, key_term, value_term = grads_of(
            probs, dprob_tiles[number], row_delta, key_block, query_split, cot_split, score_scale
        )
        query_acc = query_acc + query_term
        partial_list.append((key_term, value_term))
    keys_total, values_total = partial_list[0]
    for number, shift_by in enumerate(offsets):
        if shift_by != 0:
            got_keys, got_values = shifted(partial_list[number], "seq", -shift_by)
            keys_total = keys_total + got_keys
            values_total = values_total + got_values
    query_final = (
        (query_acc * score_scale).astype(jnp.bfloat16).reshape(rows_dev, heads_dev, head_size)
    )
    grad_queries = lax.all_to_all(query_final, "kvh", split_axis=0, concat_axis=1, tiled=True)
    return (grad_queries, keys_total.astype(jnp.bfloat16), values_total.astype(jnp.bfloat16))


def solution(mesh):
    in_specs = (
        P("seq", "kvh", None),
        P("seq", "kvh", None),
        P("seq", "kvh", None),
        P(("seq", "kvh"), None, None),
        P(),
        P(),
    )
    out_specs = (P(("seq", "kvh"), None, None), P("seq", "kvh", None), P("seq", "kvh", None))
    return jax.shard_map(local, mesh=mesh, in_specs=in_specs, out_specs=out_specs, check_vma=False)
```

profile of v0, /device:TPU:0, one launch (start us, length us, event | category | flops | bytes accessed | tf_op | source)
XLA Modules:
  0.0 81.2 jit_solution(14897418450453733318)
XLA Ops:
  0.6 0.0 copy-start
  0.7 1.6 %copy.72 = bf16[128,2,128]{2,0,1:T(8,128)(2,1)} copy(bf16[128,2,128]{2,1,0:T(2,128)(2,1)} %param.8) | data formatting | bytes 131072 | tf_op args[2]
  2.2 1.3 %collective-permute-start.5 = (bf16[128,2,128]{2,0,1:T(8,128)(2,1)}, bf16[128,2,128]{2,0,1:T(8,128)(2,1)}, u32[]{:S(2)}, u32[]{:S(2)}) collective-permute-start(bf16[128,2,128]{2,0,1:T(8,128)(2,1)} %copy.72), channel_id=1, source_target_pairs={{4,0},{8,4},{12,8},{16,12},{20,16},{24,20},{28,24},{5,1},{9,5},{13... | collective-permute-start | bytes 196616 | tf_op jit(solution)/shard_map/ppermute | solution.py:12
  3.5 6.9 %collective-permute-start.4 = (bf16[128,2,128]{2,0,1:T(8,128)(2,1)}, bf16[128,2,128]{2,0,1:T(8,128)(2,1)S(1)}, u32[]{:S(2)}, u32[]{:S(2)}) collective-permute-start(bf16[128,2,128]{2,0,1:T(8,128)(2,1)} %copy.72), channel_id=1, source_target_pairs={{0,8},{4,12},{8,16},{12,20},{16,24},{20,28},{1,9},{5,13},{9,17},{1... | collective-permute-start | bytes 196616 | tf_op jit(solution)/shard_map/ppermute | solution.py:12
  10.4 3.2 %collective-permute-start.3 = (bf16[128,2,128]{2,0,1:T(8,128)(2,1)}, bf16[128,2,128]{2,0,1:T(8,128)(2,1)}, u32[]{:S(2)}, u32[]{:S(2)}) collective-permute-start(bf16[128,2,128]{2,0,1:T(8,128)(2,1)} %copy.72), channel_id=1, source_target_pairs={{0,4},{4,8},{8,12},{12,16},{16,20},{20,24},{24,28},{1,5},{5,9},{9,... | collective-permute-start | bytes 196616 | tf_op jit(solution)/shard_map/ppermute | solution.py:12
  13.6 0.6 copy.63
  14.2 1.3 %collective-permute-start.2 = (bf16[128,2,128]{2,0,1:T(8,128)(2,1)}, bf16[128,2,128]{2,0,1:T(8,128)(2,1)S(1)}, u32[]{:S(2)}, u32[]{:S(2)}) collective-permute-start(bf16[128,2,128]{2,0,1:T(8,128)(2,1)} %copy.63), channel_id=1, source_target_pairs={{4,0},{8,4},{12,8},{16,12},{20,16},{24,20},{28,24},{5,1},{9,5},{13... | collective-permute-start | bytes 196616 | tf_op jit(solution)/shard_map/ppermute | solution.py:12
  15.5 4.5 %collective-permute-start = (bf16[128,2,128]{2,0,1:T(8,128)(2,1)}, bf16[128,2,128]{2,0,1:T(8,128)(2,1)S(1)}, u32[]{:S(2)}, u32[]{:S(2)}) collective-permute-start(bf16[128,2,128]{2,0,1:T(8,128)(2,1)} %copy.63), channel_id=1, source_target_pairs={{0,4},{4,8},{8,12},{12,16},{16,20},{20,24},{24,28},{1,5},{5,9},{9,... | collective-permute-start | bytes 196616 | tf_op jit(solution)/shard_map/ppermute | solution.py:12
  20.1 2.2 %copy.69 = bf16[32,64,128]{2,0,1:T(8,128)(2,1)} copy(bf16[32,64,128]{2,1,0:T(8,128)(2,1)} %param.9) | data formatting | bytes 1048576 | tf_op args[3]
  22.3 3.5 %all-to-all-start = ((bf16[32,64,128]{2,0,1:T(8,128)(2,1)}), bf16[32,64,128]{2,0,1:T(8,128)(2,1)S(1)}, u32[]{:S(2)}, u32[]{:S(2)}) async-start(bf16[32,64,128]{2,0,1:T(8,128)(2,1)} %copy.69), calls=%async_computation | async-start | bytes 1048576 | tf_op jit(solution)/shard_map/all_to_all | solution.py:54
  25.8 0.0 copy-start.12
  25.8 0.6 copy-done.12
  26.4 0.2 reduce-window.8
  26.6 0.5 copy-done.13
  27.1 0.1 convert_reduce_fusion.2
  27.2 0.1 select_reduce_fusion.2
  27.3 0.3 and_and_fusion.3
  27.6 0.3 fusion.71
  28.0 0.0 collective-permute-done
  28.0 3.3 %collective-permute-start.1 = (bf16[128,2,128]{2,0,1:T(8,128)(2,1)}, bf16[128,2,128]{2,0,1:T(8,128)(2,1)S(1)}, u32[]{:S(2)}, u32[]{:S(2)}) collective-permute-start(bf16[128,2,128]{2,0,1:T(8,128)(2,1)} %copy.63), channel_id=1, source_target_pairs={{0,8},{4,12},{8,16},{12,20},{16,24},{20,28},{1,9},{5,13},{9,17},{1... | collective-permute-start | bytes 196616 | tf_op jit(solution)/shard_map/ppermute | solution.py:12
  31.2 0.3 fusion.72
  31.6 1.9 %collective-permute-done.1 = bf16[128,2,128]{2,0,1:T(8,128)(2,1)S(1)} collective-permute-done((bf16[128,2,128]{2,0,1:T(8,128)(2,1)}, bf16[128,2,128]{2,0,1:T(8,128)(2,1)S(1)}, u32[]{:S(2)}, u32[]{:S(2)}) %collective-permute-start.1) | collective-permute-done | bytes 65568 | tf_op jit(solution)/shard_map/ppermute | solution.py:12
  33.5 0.3 fusion.70
  33.8 0.0 collective-permute-done.2
  33.8 0.3 fusion.69
  34.2 0.9 %fusion.30 = (f32[2,8,128]{2,1,0:T(8,128)S(1)}, f32[2,8,128]{2,1,0:T(8,128)S(1)}, f32[2,8,128]{2,1,0:T(8,128)S(1)}, f32[2,8,128]{2,1,0:T(8,128)S(1)}) fusion(f32[2,8,128,128]{2,3,1,0:T(8,128)S(1)} %get-tuple-element.43, f32[2,8,128]{2,1,0:T(8,128)S(1)} %maximum_maximum_fusion, pred[128,128]{0,1:T(8,128)(4,1)S(1)} %get-tuple-element.35, ...), kind=kLoop, calls=%fused_computation.60 | loop fusion | flops 3137536 | bytes 4300800 | tf_op jit(solution)/shard_map/reduce_sum | solution.py:97
  35.1 0.1 copy-done.3
  35.2 0.8 copy-done.9
  36.0 1.2 %copy.70 = bf16[32,4,16,128]{3,0,1,2:T(8,128)(2,1)S(1)} copy(bf16[32,4,16,128]{3,0,2,1:T(8,128)(2,1)} %bitcast.199) | data formatting | bytes 1048576 | tf_op jit(solution)/shard_map/all_to_all | solution.py:54
  37.2 0.2 copy-done.4
  37.4 1.0 %convolution_bitcast_fusion.4 = f32[128,2,128]{2,0,1:T(8,128)} fusion(bf16[128,2,8,128]{3,0,2,1:T(8,128)(2,1)S(1)} %bitcast.190, f32[2,8,128,128]{2,3,1,0:T(8,128)S(1)} %copy-done.4, f32[2,8,128]{2,1,0:T(8,128)S(1)} %add_add_fusion.1, f32[2,8,128]{2,1,0:T(8,128)S(1)} %maximum_maximum_fusion, pred[128,128]{0,1:T(8,128)(4,1)S(1)} %get-tuple-element.33), kind=kOutput, calls=%fused_computation.21 | convolution fusion | flops 68157440 | bytes 1736704 | tf_op jit(solution)/shard_map/gqts,tgqd->sgd/dot_general | solution.py:41
  38.4 0.2 copy-done.2
  38.6 1.0 %convolution_bitcast_fusion.5 = f32[128,2,128]{2,0,1:T(8,128)} fusion(bf16[128,2,8,128]{3,0,2,1:T(8,128)(2,1)S(1)} %bitcast.191, f32[2,8,128,128]{2,3,1,0:T(8,128)S(1)} %copy-done.2, f32[2,8,128]{2,1,0:T(8,128)S(1)} %add_add_fusion.1, f32[2,8,128]{2,1,0:T(8,128)S(1)} %maximum_maximum_fusion, pred[128,128]{0,1:T(8,128)(4,1)S(1)} %get-tuple-element.34), kind=kOutput, calls=%fused_computation.22 | convolution fusion | flops 68157440 | bytes 1736704 | tf_op jit(solution)/shard_map/gqts,tgqd->sgd/dot_general | solution.py:41
  39.6 1.0 %convolution_bitcast_fusion.6 = f32[128,2,128]{2,0,1:T(8,128)} fusion(bf16[128,2,8,128]{3,0,2,1:T(8,128)(2,1)S(1)} %bitcast.192, f32[2,8,128,128]{2,3,1,0:T(8,128)S(1)} %get-tuple-element.43, f32[2,8,128]{2,1,0:T(8,128)S(1)} %add_add_fusion.1, f32[2,8,128]{2,1,0:T(8,128)S(1)} %maximum_maximum_fusion, pred[128,128]{0,1:T(8,128)(4,1)S(1)} %get-tuple-element.35), kind=kOutput, calls=%fused_computation.23 | convolution fusion | flops 68157440 | bytes 1736704 | tf_op jit(solution)/shard_map/gqts,tgqd->sgd/dot_general | solution.py:41
  40.6 0.3 convolution_bitcast_fusion.3
  40.9 1.3 %collective-permute-start.9 = (f32[128,2,128]{2,0,1:T(8,128)}, f32[128,2,128]{2,0,1:T(8,128)}, u32[]{:S(2)}, u32[]{:S(2)}) collective-permute-start(f32[128,2,128]{2,0,1:T(8,128)} %convolution_bitcast_fusion.6), channel_id=1, source_target_pairs={{4,0},{8,4},{12,8},{16,12},{20,16},{24,20},{28,24},{5,1},{9,5},{13... | collective-permute-start | bytes 393224 | tf_op jit(solution)/shard_map/ppermute | solution.py:12
  42.2 1.3 %collective-permute-start.10 = (f32[128,2,128]{2,0,1:T(8,128)}, f32[128,2,128]{2,0,1:T(8,128)}, u32[]{:S(2)}, u32[]{:S(2)}) collective-permute-start(f32[128,2,128]{2,0,1:T(8,128)} %convolution_bitcast_fusion.5), channel_id=1, source_target_pairs={{8,0},{12,4},{16,8},{20,12},{24,16},{28,20},{9,1},{13,5},{17,9},{2... | collective-permute-start | bytes 393224 | tf_op jit(solution)/shard_map/ppermute | solution.py:12
  43.5 0.0 collective-permute-done.5
  43.5 6.1 %collective-permute-start.11 = (f32[128,2,128]{2,0,1:T(8,128)}, f32[128,2,128]{2,0,1:T(8,128)}, u32[]{:S(2)}, u32[]{:S(2)}) collective-permute-start(f32[128,2,128]{2,0,1:T(8,128)} %convolution_bitcast_fusion.4), channel_id=1, source_target_pairs={{0,4},{4,8},{8,12},{12,16},{16,20},{20,24},{24,28},{1,5},{5,9},{9,... | collective-permute-start | bytes 393224 | tf_op jit(solution)/shard_map/ppermute | solution.py:12
  49.6 1.1 %convolution_bitcast_fusion = f32[2,8,128,128]{2,3,1,0:T(8,128)S(1)} fusion(bf16[128,2,8,128]{3,0,2,1:T(8,128)(2,1)S(1)} %bitcast.194, bf16[128,2,128]{2,0,1:T(8,128)(2,1)} %collective-permute-done.5), kind=kOutput, calls=%fused_computation | convolution fusion | flops 67108864 | bytes 1638400 | tf_op jit(solution)/shard_map/tgqd,sgd->gqts/dot_general | solution.py:28
  50.8 0.0 collective-permute-done.4
  50.8 0.3 convolution_bitcast_fusion.1
  51.1 0.0 collective-permute-done.3
  51.1 2.1 %multiply_reduce_fusion.2 = (f32[2,8,128]{2,1,0:T(8,128)S(1)}, f32[2,8,128]{2,1,0:T(8,128)S(1)}, f32[2,8,128]{2,1,0:T(8,128)S(1)}, f32[2,8,128]{2,1,0:T(8,128)S(1)}, f32[2,8,128,128]{2,3,1,0:T(8,128)S(1)}) fusion(f32[2,8,128]{2,1,0:T(8,128)S(1)} %add_add_fusion.1, f32[2,8,128,128]{2,3,1,0:T(8,128)S(1)} %get-tuple-element.43, ...), kind=kOutput, calls=%fused_computation.51 | convolution fusion | flops 72343552 | bytes 9093120 | tf_op jit(solution)/shard_map/tgqd,sgd->gqts/dot_general | solution.py:28
  53.3 1.2 %multiply_convert_fusion.1 = (bf16[2,8,128,128]{2,3,1,0:T(8,128)(2,1)S(1)}, bf16[2,8,128,128]{2,3,1,0:T(8,128)(2,1)S(1)}, bf16[2,8,128,128]{2,3,1,0:T(8,128)(2,1)S(1)}, bf16[2,8,128,128]{2,3,1,0:T(8,128)(2,1)S(1)}) fusion(f32[2,8,128,128]{2,3,1,0:T(8,128)S(1)} %convolution_bitcast_fusion.1, f32[2,8,128]{2,1,0:T(8,128)S(1)} %add_add_fusion, ...), kind=kLoop, calls=%fused_computation.46 | loop fusion | flops 6291456 | bytes 10575872 | tf_op jit(solution)/shard_map/convert_element_type | solution.py:32
  54.5 1.0 %fusion.17 = f32[128,2,128]{2,0,1:T(8,128)} fusion(bf16[2,8,128,128]{2,3,1,0:T(8,128)(2,1)S(1)} %get-tuple-element.29, bf16[128,2,8,128]{3,2,1,0:T(8,128)(2,1)S(1)} %bitcast.185), kind=kOutput, calls=%fused_computation.35 | convolution fusion | flops 67141632 | bytes 1179648 | tf_op jit(solution)/shard_map/gqts,tgqd->sgd/dot_general | solution.py:38
  55.5 0.9 %fusion.21 = f32[128,2,128]{2,0,1:T(8,128)} fusion(bf16[2,8,128,128]{2,3,1,0:T(8,128)(2,1)S(1)} %get-tuple-element.30, bf16[128,2,8,128]{3,2,1,0:T(8,128)(2,1)S(1)} %bitcast.183), kind=kOutput, calls=%fused_computation.39 | convolution fusion | flops 67141632 | bytes 1179648 | tf_op jit(solution)/shard_map/gqts,tgqd->sgd/dot_general | solution.py:38
  56.5 5.4 %collective-permute-start.8 = (f32[128,2,128]{2,0,1:T(8,128)}, f32[128,2,128]{2,0,1:T(8,128)}, u32[]{:S(2)}, u32[]{:S(2)}) collective-permute-start(f32[128,2,128]{2,0,1:T(8,128)} %fusion.21), channel_id=1, source_target_pairs={{0,4},{4,8},{8,12},{12,16},{16,20},{20,24},{24,28},{1,5},{5,9},{9,... | collective-permute-start | bytes 393224 | tf_op jit(solution)/shard_map/ppermute | solution.py:12
  61.9 1.3 %collective-permute-start.6 = (f32[128,2,128]{2,0,1:T(8,128)}, f32[128,2,128]{2,0,1:T(8,128)}, u32[]{:S(2)}, u32[]{:S(2)}) collective-permute-start(f32[128,2,128]{2,0,1:T(8,128)} %fusion.17), channel_id=1, source_target_pairs={{4,0},{8,4},{12,8},{16,12},{20,16},{24,20},{28,24},{5,1},{9,5},{13... | collective-permute-start | bytes 393224 | tf_op jit(solution)/shard_map/ppermute | solution.py:12
  63.2 0.3 fusion.58
  63.6 0.4 fusion.50
  63.9 0.4 convolution_add_fusion.1
  64.3 0.4 fusion.10
  64.7 1.1 %copy.80 = bf16[128,16,128]{2,1,0:T(8,128)(2,1)} copy(bf16[128,16,128]{2,0,1:T(8,128)(2,1)S(1)} %bitcast.198) | data formatting | bytes 1048576 | tf_op jit(solution)/shard_map/reshape | solution.py:124
  65.8 3.6 %all-to-all-start.1 = ((bf16[128,16,128]{2,1,0:T(8,128)(2,1)}), bf16[128,16,128]{2,1,0:T(8,128)(2,1)S(1)}, u32[]{:S(2)}, u32[]{:S(2)}) async-start(bf16[128,16,128]{2,1,0:T(8,128)(2,1)} %copy.80), calls=%async_computation.1 | async-start | bytes 1048576 | tf_op jit(solution)/shard_map/all_to_all | solution.py:126
  69.5 0.3 fusion.19
  69.8 0.0 collective-permute-done.9
  69.8 1.4 %collective-permute-start.7 = (f32[128,2,128]{2,0,1:T(8,128)S(1)}, f32[128,2,128]{2,0,1:T(8,128)S(1)}, u32[]{:S(2)}, u32[]{:S(2)}) collective-permute-start(f32[128,2,128]{2,0,1:T(8,128)S(1)} %fusion.19), channel_id=1, source_target_pairs={{8,0},{12,4},{16,8},{20,12},{24,16},{28,20},{9,1},{13,5},{17,9},{2... | collective-permute-start | bytes 393224 | tf_op jit(solution)/shard_map/ppermute | solution.py:12
  71.2 1.4 %fusion.25 = bf16[128,2,128]{2,0,1:T(8,128)(2,1)S(1)} fusion(f32[128,2,128]{2,0,1:T(8,128)} %collective-permute-done.11, f32[128,2,128]{2,0,1:T(8,128)} %collective-permute-done.10, f32[128,2,128]{2,0,1:T(8,128)} %collective-permute-done.9, bf16[128,2,8,128]{3,0,2,1:T(8,128)(2,1)S(1)} %bitcast.197, f32[2,8,128,128]{2,3,1,0:T(8,128)S(1)} %get-tuple-element.41, ...), kind=kOutput, calls=%fused_computation.43 | convolution fusion | flops 68288512 | bytes 2064384 | tf_op jit(solution)/shard_map/gqts,tgqd->sgd/dot_general | solution.py:41
  72.6 0.7 copy.87
  73.3 5.0 %collective-permute-done.7 = f32[128,2,128]{2,0,1:T(8,128)S(1)} collective-permute-done((f32[128,2,128]{2,0,1:T(8,128)S(1)}, f32[128,2,128]{2,0,1:T(8,128)S(1)}, u32[]{:S(2)}, u32[]{:S(2)}) %collective-permute-start.7) | collective-permute-done | bytes 131104 | tf_op jit(solution)/shard_map/ppermute | solution.py:12
  78.3 1.3 %fusion.26 = bf16[128,2,128]{2,0,1:T(8,128)(2,1)S(1)} fusion(f32[128,2,128]{2,0,1:T(8,128)} %collective-permute-done.8, f32[128,2,128]{2,0,1:T(8,128)S(1)} %collective-permute-done.7, f32[128,2,128]{2,0,1:T(8,128)} %collective-permute-done.6, bf16[2,8,128,128]{2,3,1,0:T(8,128)(2,1)S(1)} %copy-done.6, bf16[128,2,8,128]{3,2,1,0:T(8,128)(2,1)S(1)} %bitcast.186), kind=kOutput, calls=%fused_computation.44 | convolution fusion | flops 67272704 | bytes 1507328 | tf_op jit(solution)/shard_map/gqts,tgqd->sgd/dot_general | solution.py:38
  79.6 0.7 copy.86
  80.3 0.9 %copy.81 = bf16[32,4,16,128]{3,2,1,0:T(8,128)(2,1)} copy(bf16[32,4,16,128]{3,2,0,1:T(8,128)(2,1)S(1)} %bitcast.200) | data formatting | bytes 1048576 | tf_op jit(solution)/shard_map/all_to_all | solution.py:126
  (36 shorter events, 0.1 us)
Async XLA Ops:
  0.6 27.0 %copy-start = (bf16[128,16,128]{2,1,0:T(8,128)(2,1)S(1)}, bf16[128,16,128]{2,1,0:T(8,128)(2,1)}, u32[]{:S(2)}) copy-start(bf16[128,16,128]{2,1,0:T(8,128)(2,1)} %param.6) | copy-start | bytes 1572868
  0.6 13.0 %copy-start.10 = (bf16[128,2,128]{2,1,0:T(2,128)(2,1)S(1)}, bf16[128,2,128]{2,1,0:T(2,128)(2,1)}, u32[]{:S(2)}) copy-start(bf16[128,2,128]{2,1,0:T(2,128)(2,1)} %param.7) | copy-start | bytes 196612
  2.2 41.3 %collective-permute-start.5 = (bf16[128,2,128]{2,0,1:T(8,128)(2,1)}, bf16[128,2,128]{2,0,1:T(8,128)(2,1)}, u32[]{:S(2)}, u32[]{:S(2)}) collective-permute-start(bf16[128,2,128]{2,0,1:T(8,128)(2,1)} %copy.72), channel_id=1, source_target_pairs={{4,0},{8,4},{12,8},{16,12},{20,16},{24,20},{28,24},{5,1},{9,5},{13... | collective-permute-start | bytes 196616 | tf_op jit(solution)/shard_map/ppermute | solution.py:12
  3.5 47.3 %collective-permute-start.4 = (bf16[128,2,128]{2,0,1:T(8,128)(2,1)}, bf16[128,2,128]{2,0,1:T(8,128)(2,1)S(1)}, u32[]{:S(2)}, u32[]{:S(2)}) collective-permute-start(bf16[128,2,128]{2,0,1:T(8,128)(2,1)} %copy.72), channel_id=1, source_target_pairs={{0,8},{4,12},{8,16},{12,20},{16,24},{20,28},{1,9},{5,13},{9,17},{1... | collective-permute-start | bytes 196616 | tf_op jit(solution)/shard_map/ppermute | solution.py:12
  10.4 40.7 %collective-permute-start.3 = (bf16[128,2,128]{2,0,1:T(8,128)(2,1)}, bf16[128,2,128]{2,0,1:T(8,128)(2,1)}, u32[]{:S(2)}, u32[]{:S(2)}) collective-permute-start(bf16[128,2,128]{2,0,1:T(8,128)(2,1)} %copy.72), channel_id=1, source_target_pairs={{0,4},{4,8},{8,12},{12,16},{16,20},{20,24},{24,28},{1,5},{5,9},{9,... | collective-permute-start | bytes 196616 | tf_op jit(solution)/shard_map/ppermute | solution.py:12
  14.2 19.6 %collective-permute-start.2 = (bf16[128,2,128]{2,0,1:T(8,128)(2,1)}, bf16[128,2,128]{2,0,1:T(8,128)(2,1)S(1)}, u32[]{:S(2)}, u32[]{:S(2)}) collective-permute-start(bf16[128,2,128]{2,0,1:T(8,128)(2,1)} %copy.63), channel_id=1, source_target_pairs={{4,0},{8,4},{12,8},{16,12},{20,16},{24,20},{28,24},{5,1},{9,5},{13... | collective-permute-start | bytes 196616 | tf_op jit(solution)/shard_map/ppermute | solution.py:12
  15.5 12.4 %collective-permute-start = (bf16[128,2,128]{2,0,1:T(8,128)(2,1)}, bf16[128,2,128]{2,0,1:T(8,128)(2,1)S(1)}, u32[]{:S(2)}, u32[]{:S(2)}) collective-permute-start(bf16[128,2,128]{2,0,1:T(8,128)(2,1)} %copy.63), channel_id=1, source_target_pairs={{0,4},{4,8},{8,12},{12,16},{16,20},{20,24},{24,28},{1,5},{5,9},{9,... | collective-permute-start | bytes 196616 | tf_op jit(solution)/shard_map/ppermute | solution.py:12
  22.3 12.9 %all-to-all-start = ((bf16[32,64,128]{2,0,1:T(8,128)(2,1)}), bf16[32,64,128]{2,0,1:T(8,128)(2,1)S(1)}, u32[]{:S(2)}, u32[]{:S(2)}) async-start(bf16[32,64,128]{2,0,1:T(8,128)(2,1)} %copy.69), calls=%async_computation | async-start | bytes 1048576 | tf_op jit(solution)/shard_map/all_to_all | solution.py:54
  25.8 0.7 copy-start.12
  26.4 0.7 copy-start.13
  28.0 5.5 %collective-permute-start.1 = (bf16[128,2,128]{2,0,1:T(8,128)(2,1)}, bf16[128,2,128]{2,0,1:T(8,128)(2,1)S(1)}, u32[]{:S(2)}, u32[]{:S(2)}) collective-permute-start(bf16[128,2,128]{2,0,1:T(8,128)(2,1)} %copy.63), channel_id=1, source_target_pairs={{0,8},{4,12},{8,16},{12,20},{16,24},{20,28},{1,9},{5,13},{9,17},{1... | collective-permute-start | bytes 196616 | tf_op jit(solution)/shard_map/ppermute | solution.py:12
  33.8 1.3 %copy-start.1 = (f32[2,8,128,128]{2,3,1,0:T(8,128)}, f32[2,8,128,128]{2,3,1,0:T(8,128)S(1)}, u32[]{:S(2)}) copy-start(f32[2,8,128,128]{2,3,1,0:T(8,128)S(1)} %get-tuple-element.39) | copy-start | bytes 3145732
  34.2 1.0 %copy-start.3 = (f32[2,8,128,128]{2,3,1,0:T(8,128)}, f32[2,8,128,128]{2,3,1,0:T(8,128)S(1)}, u32[]{:S(2)}) copy-start(f32[2,8,128,128]{2,3,1,0:T(8,128)S(1)} %get-tuple-element.37) | copy-start | bytes 3145732
  35.2 0.8 copy-start.9
  36.0 1.4 %copy-start.4 = (f32[2,8,128,128]{2,3,1,0:T(8,128)S(1)}, f32[2,8,128,128]{2,3,1,0:T(8,128)}, u32[]{:S(2)}) copy-start(f32[2,8,128,128]{2,3,1,0:T(8,128)} %copy-done.3) | copy-start | bytes 3145732
  37.4 1.2 %copy-start.2 = (f32[2,8,128,128]{2,3,1,0:T(8,128)S(1)}, f32[2,8,128,128]{2,3,1,0:T(8,128)}, u32[]{:S(2)}) copy-start(f32[2,8,128,128]{2,3,1,0:T(8,128)} %copy-done.1) | copy-start | bytes 3145732
  39.6 1.0 %copy-start.11 = (bf16[128,2,128]{2,1,0:T(2,128)(2,1)S(1)}, bf16[128,2,128]{2,1,0:T(2,128)(2,1)}, u32[]{:S(2)}) copy-start(bf16[128,2,128]{2,1,0:T(2,128)(2,1)} %param.8) | copy-start | bytes 196612
  40.9 28.9 %collective-permute-start.9 = (f32[128,2,128]{2,0,1:T(8,128)}, f32[128,2,128]{2,0,1:T(8,128)}, u32[]{:S(2)}, u32[]{:S(2)}) collective-permute-start(f32[128,2,128]{2,0,1:T(8,128)} %convolution_bitcast_fusion.6), channel_id=1, source_target_pairs={{4,0},{8,4},{12,8},{16,12},{20,16},{24,20},{28,24},{5,1},{9,5},{13... | collective-permute-start | bytes 393224 | tf_op jit(solution)/shard_map/ppermute | solution.py:12
  42.2 29.0 %collective-permute-start.10 = (f32[128,2,128]{2,0,1:T(8,128)}, f32[128,2,128]{2,0,1:T(8,128)}, u32[]{:S(2)}, u32[]{:S(2)}) collective-permute-start(f32[128,2,128]{2,0,1:T(8,128)} %convolution_bitcast_fusion.5), channel_id=1, source_target_pairs={{8,0},{12,4},{16,8},{20,12},{24,16},{28,20},{9,1},{13,5},{17,9},{2... | collective-permute-start | bytes 393224 | tf_op jit(solution)/shard_map/ppermute | solution.py:12
  43.5 27.7 %collective-permute-start.11 = (f32[128,2,128]{2,0,1:T(8,128)}, f32[128,2,128]{2,0,1:T(8,128)}, u32[]{:S(2)}, u32[]{:S(2)}) collective-permute-start(f32[128,2,128]{2,0,1:T(8,128)} %convolution_bitcast_fusion.4), channel_id=1, source_target_pairs={{0,4},{4,8},{8,12},{12,16},{16,20},{20,24},{24,28},{1,5},{5,9},{9,... | collective-permute-start | bytes 393224 | tf_op jit(solution)/shard_map/ppermute | solution.py:12
  54.5 8.7 %copy-start.5 = (bf16[2,8,128,128]{2,3,1,0:T(8,128)(2,1)}, bf16[2,8,128,128]{2,3,1,0:T(8,128)(2,1)S(1)}, u32[]{:S(2)}) copy-start(bf16[2,8,128,128]{2,3,1,0:T(8,128)(2,1)S(1)} %get-tuple-element.31) | copy-start | bytes 1572868
  54.5 9.8 %copy-start.7 = (bf16[2,8,128,128]{2,3,1,0:T(8,128)(2,1)}, bf16[2,8,128,128]{2,3,1,0:T(8,128)(2,1)S(1)}, u32[]{:S(2)}) copy-start(bf16[2,8,128,128]{2,3,1,0:T(8,128)(2,1)S(1)} %get-tuple-element.28) | copy-start | bytes 1572868
  56.5 16.9 %collective-permute-start.8 = (f32[128,2,128]{2,0,1:T(8,128)}, f32[128,2,128]{2,0,1:T(8,128)}, u32[]{:S(2)}, u32[]{:S(2)}) collective-permute-start(f32[128,2,128]{2,0,1:T(8,128)} %fusion.21), channel_id=1, source_target_pairs={{0,4},{4,8},{8,12},{12,16},{16,20},{20,24},{24,28},{1,5},{5,9},{9,... | collective-permute-start | bytes 393224 | tf_op jit(solution)/shard_map/ppermute | solution.py:12
  61.9 11.4 %collective-permute-start.6 = (f32[128,2,128]{2,0,1:T(8,128)}, f32[128,2,128]{2,0,1:T(8,128)}, u32[]{:S(2)}, u32[]{:S(2)}) collective-permute-start(f32[128,2,128]{2,0,1:T(8,128)} %fusion.17), channel_id=1, source_target_pairs={{4,0},{8,4},{12,8},{16,12},{20,16},{24,20},{28,24},{5,1},{9,5},{13... | collective-permute-start | bytes 393224 | tf_op jit(solution)/shard_map/ppermute | solution.py:12
  65.8 3.6 %copy-start.8 = (bf16[2,8,128,128]{2,3,1,0:T(8,128)(2,1)S(1)}, bf16[2,8,128,128]{2,3,1,0:T(8,128)(2,1)}, u32[]{:S(2)}) copy-start(bf16[2,8,128,128]{2,3,1,0:T(8,128)(2,1)} %copy-done.7) | copy-start | bytes 1572868
  65.8 14.5 %all-to-all-start.1 = ((bf16[128,16,128]{2,1,0:T(8,128)(2,1)}), bf16[128,16,128]{2,1,0:T(8,128)(2,1)S(1)}, u32[]{:S(2)}, u32[]{:S(2)}) async-start(bf16[128,16,128]{2,1,0:T(8,128)(2,1)} %copy.80), calls=%async_computation.1 | async-start | bytes 1048576 | tf_op jit(solution)/shard_map/all_to_all | solution.py:126
  69.8 8.6 %copy-start.6 = (bf16[2,8,128,128]{2,3,1,0:T(8,128)(2,1)S(1)}, bf16[2,8,128,128]{2,3,1,0:T(8,128)(2,1)}, u32[]{:S(2)}) copy-start(bf16[2,8,128,128]{2,3,1,0:T(8,128)(2,1)} %copy-done.5) | copy-start | bytes 1572868
  69.8 8.5 %collective-permute-start.7 = (f32[128,2,128]{2,0,1:T(8,128)S(1)}, f32[128,2,128]{2,0,1:T(8,128)S(1)}, u32[]{:S(2)}, u32[]{:S(2)}) collective-permute-start(f32[128,2,128]{2,0,1:T(8,128)S(1)} %fusion.19), channel_id=1, source_target_pairs={{8,0},{12,4},{16,8},{20,12},{24,16},{28,20},{9,1},{13,5},{17,9},{2... | collective-permute-start | bytes 393224 | tf_op jit(solution)/shard_map/ppermute | solution.py:12
where the time goes:
time: 82.4 us; the launch traced here: 81.2 us
  starting transfers between devices  44.4 us (54%)
  matrix products  14.5 us (18%)
  local copies, waits for them, and re-layouts  11.4 us (14%)
  waiting for transfers between devices  6.94 us (8%)
  other arithmetic  2.81 us (3%)
  between operations  1.09 us (1%)
    ppermute x12, starting transfers between devices, shifted(): return lax.ppermute(block, axis, route)  37.3 us
    unnamed x33, local copies, waits for them, and re-layouts  8.25 us
    ppermute x12, waiting for transfers between devices, shifted(): return lax.ppermute(block, axis, route)  6.94 us
    dot_general x4, matrix products, grads_of(): jnp.einsum('gqts,tgqd->sgd', probs_half, cot_split, preferred_element_typ...  4.38 us
    dot_general x4, matrix products, dprobs_of(): jnp.einsum('tgqd,sgd->gqts', cot_split, value_block, preferred_element_ty...  3.87 us
    all_to_all x1, starting transfers between devices, local(): lax.all_to_all(query_final, 'kvh', split_axis=0, concat_axis=1, tiled=True)  3.6 us
    dot_general x4, matrix products, grads_of(): jnp.einsum('gqts,tgqd->sgd', dscores, query_split, preferred_element_type...  3.53 us
    all_to_all x1, starting transfers between devices, local(): lax.all_to_all(output_gradient, 'kvh', split_axis=1, concat_axis=0, tiled...  3.47 us
  transfers between devices with their start and end apart: 14, of which 2 were waited for; matrix products, arithmetic and copies ran while one was open for 29% of the time, Pallas kernels for 0%

commit v1 on v0

v1 whole, which is shorter than its diff:
```python
import functools

import jax
import jax.numpy as jnp
from jax import lax
from jax.experimental import pallas as pl
from jax.experimental.pallas import tpu as pltpu
from jax.sharding import PartitionSpec as P

BACK = 2
AHEAD = 1
LOG2E = 1.4426950408889634
VMEM_BYTES = 40 * 1024 * 1024
NEG = -1e30

_VMEM = pl.BlockSpec(memory_space=pltpu.VMEM)
_SMEM = pl.BlockSpec(memory_space=pltpu.SMEM)
_ANY = pl.BlockSpec(memory_space=pl.ANY)


def prep_kernel(parts, cot_ref, key_ref, value_ref, cot_out, kv_out, sems):
    rows = cot_ref.shape[0]
    heads = cot_ref.shape[1] // parts
    copies = []
    for part in range(parts):
        copy = pltpu.make_async_copy(
            cot_ref.at[:, pl.ds(part * heads, heads), :],
            cot_out.at[pl.ds(part * rows, rows)],
            sems.at[part],
        )
        copy.start()
        copies.append(copy)
    for number, ref in enumerate((key_ref, value_ref)):
        wide = ref[...].astype(jnp.float32)
        for group in range(ref.shape[1]):
            kv_out[number, group] = wide[:, group, :].astype(jnp.bfloat16)
    for copy in copies:
        copy.wait()


def prepare(cotangent, keys, values, parts):
    rows, heads, size = cotangent.shape
    kv_rows, kv_heads, _ = keys.shape
    return pl.pallas_call(
        functools.partial(prep_kernel, parts),
        out_shape=(
            jax.ShapeDtypeStruct((parts * rows, heads // parts, size), jnp.bfloat16),
            jax.ShapeDtypeStruct((2, kv_heads, kv_rows, size), jnp.bfloat16),
        ),
        in_specs=[_ANY, _VMEM, _VMEM],
        out_specs=(_ANY, _VMEM),
        scratch_shapes=[pltpu.SemaphoreType.DMA((parts,))],
        compiler_params=pltpu.CompilerParams(vmem_limit_bytes=VMEM_BYTES),
        name="prepare",
    )(cotangent, keys, values)


def bounds(position, lengths, prefixes):
    docs = lengths.shape[0]

    def step(doc, carry):
        start, low, high = carry
        end = start + lengths[doc]
        inside = (position >= start) & (position < end)
        reach = jnp.minimum(end, jnp.maximum(position + 1, start + prefixes[doc]))
        return end, jnp.where(inside, start, low), jnp.where(inside, reach, high)

    zero = jnp.zeros_like(position)
    carry = (jnp.int32(0), zero, zero)
    if docs <= 16:
        for doc in range(docs):
            carry = step(doc, carry)
    else:
        carry = lax.fori_loop(0, docs, step, carry)
    return carry[1], carry[2]


def grad_kernel(
    tokens, lengths, prefixes, q_ref, cot_ref, kv_own, kv_back1, kv_back2, kv_ahead,
    dq_ref, own_out, back1_out, back2_out, ahead_out, window, acc,
):
    rows, heads, size = q_ref.shape
    kv_heads = kv_own.shape[1]
    group_size = heads // kv_heads
    span = (BACK + 1 + AHEAD) * rows
    reach = span - rows + tokens
    lanes = tokens * group_size
    scale = size ** (-0.5)
    shard = lax.axis_index("seq")

    for slot, ref in enumerate((kv_back2, kv_back1, kv_own, kv_ahead)):
        for number in range(2):
            for group in range(kv_heads):
                window[number, group, pl.ds(slot * rows, rows)] = ref[number, group]
    acc[...] = jnp.zeros_like(acc)

    contract_last = (((1,), (1,)), ((), ()))
    contract_first = (((0,), (0,)), ((), ()))
    lane_token = lax.broadcasted_iota(jnp.int32, (1, lanes), 1) // group_size
    key_iota = lax.broadcasted_iota(jnp.int32, (reach, lanes), 0)
    for chunk in range(rows // tokens):
        first = chunk * tokens
        low, high = bounds(shard * rows + first + lane_token, lengths, prefixes)
        origin = (shard - BACK) * rows + first
        low = low - origin
        high = high - origin
        visible = (key_iota >= low) & (key_iota < high)
        for group in range(kv_heads):
            pick = (pl.ds(first, tokens), pl.ds(group * group_size, group_size))
            q = q_ref[pick].astype(jnp.float32).reshape(lanes, size).astype(jnp.bfloat16)
            cot = cot_ref[pick].astype(jnp.float32).reshape(lanes, size).astype(jnp.bfloat16)
            here = pl.ds(first, reach)
            k = window[0, group, here]
            v = window[1, group, here]
            scores = lax.dot_general(k, q, contract_last, preferred_element_type=jnp.float32)
            scores = jnp.where(visible, scores * (scale * LOG2E), NEG)
            top = jnp.max(scores, axis=0, keepdims=True)
            expo = jnp.exp2(scores - top)
            total = jnp.sum(expo, axis=0, keepdims=True)
            probs = expo * (1.0 / total)
            dprobs = lax.dot_general(v, cot, contract_last, preferred_element_type=jnp.float32)
            delta = jnp.sum(probs * dprobs, axis=0, keepdims=True)
            dscores = (probs * (dprobs - delta)).astype(jnp.bfloat16)
            acc[1, group, here] += jnp.dot(
                probs.astype(jnp.bfloat16), cot, preferred_element_type=jnp.float32
            )
            acc[0, group, here] += jnp.dot(dscores, q, preferred_element_type=jnp.float32)
            dq = lax.dot_general(k, dscores, contract_first, preferred_element_type=jnp.float32)
            dq = jnp.transpose(dq * scale)
            dq_ref[pick] = dq.reshape(tokens, group_size, size).astype(jnp.bfloat16)
    for slot, ref in enumerate((back2_out, back1_out, own_out, ahead_out)):
        for group in range(kv_heads):
            part = pl.ds(slot * rows, rows)
            ref[0, group] = (acc[0, group, part] * scale).astype(ref.dtype)
            ref[1, group] = acc[1, group, part].astype(ref.dtype)


def gradients(lengths, prefixes, queries, cotangent, blocks):
    rows, heads, size = queries.shape
    kv_shape = blocks[0].shape
    kv_heads = kv_shape[1]
    span = (BACK + 1 + AHEAD) * rows
    half = jax.ShapeDtypeStruct(kv_shape, jnp.bfloat16)
    work = heads * rows * span
    return pl.pallas_call(
        functools.partial(grad_kernel, 32),
        out_shape=(
            jax.ShapeDtypeStruct(queries.shape, jnp.bfloat16),
            jax.ShapeDtypeStruct(kv_shape, jnp.float32),
            half,
            half,
            half,
        ),
        in_specs=[_SMEM, _SMEM] + [_VMEM] * 6,
        out_specs=(_VMEM,) * 5,
        scratch_shapes=[
            pltpu.VMEM((2, kv_heads, span, size), jnp.bfloat16),
            pltpu.VMEM((2, kv_heads, span, size), jnp.float32),
        ],
        compiler_params=pltpu.CompilerParams(vmem_limit_bytes=VMEM_BYTES),
        cost_estimate=pl.CostEstimate(
            flops=10 * work * size, bytes_accessed=4 * queries.size * 2, transcendentals=work
        ),
        name="gradients",
    )(lengths, prefixes, queries, cotangent, *blocks)


def finish_kernel(dq_ref, own, from_ahead1, from_ahead2, from_back, dq_out, dk_out, dv_out):
    parts, rows, heads, _ = dq_ref.shape
    for part in range(parts):
        dq_out[:, pl.ds(part * heads, heads), :] = dq_ref[part]
    for number, ref in enumerate((dk_out, dv_out)):
        sums = []
        for group in range(ref.shape[1]):
            total = own[number, group]
            for other in (from_ahead1, from_ahead2, from_back):
                total = total + other[number, group].astype(jnp.float32)
            sums.append(total)
        ref[...] = jnp.stack(sums, axis=1).astype(jnp.bfloat16)


def finish(dq, own, received, parts):
    total_rows, heads, size = dq.shape
    rows = total_rows // parts
    _, kv_heads, kv_rows, _ = own.shape
    kv_out = jax.ShapeDtypeStruct((kv_rows, kv_heads, size), jnp.bfloat16)
    return pl.pallas_call(
        finish_kernel,
        out_shape=(
            jax.ShapeDtypeStruct((rows, heads * parts, size), jnp.bfloat16),
            kv_out,
            kv_out,
        ),
        in_specs=[_VMEM] * 5,
        out_specs=(_VMEM,) * 3,
        compiler_params=pltpu.CompilerParams(vmem_limit_bytes=VMEM_BYTES),
        name="finish",
    )(dq.reshape(parts, rows, heads, size), own, *received)


def shifted(block, distance):
    devices = range(lax.axis_size("seq"))
    route = [(i - distance, i) for i in devices if i - distance in devices]
    return lax.ppermute(block, "seq", route)


def local(queries, keys, values, output_gradient, doc_lengths, prefix_lengths):
    parts = lax.axis_size("kvh")
    cot, kv = prepare(output_gradient, keys, values, parts)
    cot = lax.all_to_all(cot, "kvh", split_axis=0, concat_axis=0, tiled=True)
    blocks = (kv, shifted(kv, 1), shifted(kv, 2), shifted(kv, -1))
    dq, own, back1, back2, ahead = gradients(
        doc_lengths, prefix_lengths, queries, cot, blocks
    )
    received = (shifted(back1, -1), shifted(back2, -2), shifted(ahead, 1))
    dq = lax.all_to_all(dq, "kvh", split_axis=0, concat_axis=0, tiled=True)
    return finish(dq, own, received, parts)


def solution(mesh):
    in_specs = (
        P("seq", "kvh", None),
        P("seq", "kvh", None),
        P("seq", "kvh", None),
        P(("seq", "kvh"), None, None),
        P(),
        P(),
    )
    out_specs = (P(("seq", "kvh"), None, None), P("seq", "kvh", None), P("seq", "kvh", None))
    return jax.shard_map(local, mesh=mesh, in_specs=in_specs, out_specs=out_specs, check_vma=False)
```

time: 82.4 us -> 46.8 us (0.57)
  the two profiles are of different devices: /device:TPU:0 before, /device:TPU:28 now
where the time goes in v1:
time: 46.8 us; the launch traced here: 46.3 us
  starting transfers between devices  24.6 us (53%)
  waiting for transfers between devices  10.3 us (22%)
  Pallas kernels  7.94 us (17%)
  local copies, waits for them, and re-layouts  2.73 us (6%)
  between operations  0.74 us (2%)
    ppermute x6, starting transfers between devices, shifted(): return lax.ppermute(block, 'seq', route)  16.7 us
    ppermute x6, waiting for transfers between devices, shifted(): return lax.ppermute(block, 'seq', route)  10.3 us
    pallas_call x1, Pallas kernels, gradients(): pl.pallas_call(functools.partial(grad_kernel, 32), out_shape=(jax.ShapeDt...  6.12 us
    all_to_all x1, starting transfers between devices, local(): cot = lax.all_to_all(cot, 'kvh', split_axis=0, concat_axis=0, tiled=True)  4.09 us
    all_to_all x1, starting transfers between devices, local(): dq = lax.all_to_all(dq, 'kvh', split_axis=0, concat_axis=0, tiled=True)  3.81 us
    unnamed x12, local copies, waits for them, and re-layouts  2.73 us
    pallas_call x1, Pallas kernels, finish(): pl.pallas_call(finish_kernel, out_shape=(jax.ShapeDtypeStruct((rows, head...  1 us
  transfers between devices with their start and end apart: 8, of which 4 were waited for; matrix products, arithmetic and copies ran while one was open for 0% of the time, Pallas kernels for 0%

profile of v1, /device:TPU:28, one launch (start us, length us, event | category | flops | bytes accessed | tf_op | source)
XLA Modules:
  0.0 46.3 jit_solution(3135791067596514628)
XLA Ops:
  0.6 0.0 copy-start
  0.6 1.0 %copy-done = bf16[32,64,128]{2,1,0:T(8,128)(2,1)S(1)} copy-done((bf16[32,64,128]{2,1,0:T(8,128)(2,1)S(1)}, bf16[32,64,128]{2,1,0:T(8,128)(2,1)}, u32[]{:S(2)}) %copy-start) | copy-done | bytes 524312
  1.7 0.0 copy-start.1
  1.7 0.8 %copy-done.1 = bf16[128,2,128]{2,1,0:T(2,128)(2,1)S(1)} copy-done((bf16[128,2,128]{2,1,0:T(2,128)(2,1)S(1)}, bf16[128,2,128]{2,1,0:T(2,128)(2,1)}, u32[]{:S(2)}) %copy-start.1) | copy-done | bytes 65560
  2.5 0.0 copy-start.2
  2.5 0.8 %copy-done.2 = bf16[128,2,128]{2,1,0:T(2,128)(2,1)S(1)} copy-done((bf16[128,2,128]{2,1,0:T(2,128)(2,1)S(1)}, bf16[128,2,128]{2,1,0:T(2,128)(2,1)}, u32[]{:S(2)}) %copy-start.2) | copy-done | bytes 65560
  3.4 0.8 %prepare.1 = (bf16[128,16,128]{2,1,0:T(8,128)(2,1)}, bf16[2,2,128,128]{3,2,1,0:T(8,128)(2,1)S(1)}) custom-call(bf16[32,64,128]{2,1,0:T(8,128)(2,1)S(1)} %copy-done, bf16[128,2,128]{2,1,0:T(2,128)(2,1)S(1)} %copy-done.1, bf16[128,2,128]{2,1,0:T(2,128)(2,1)S(1)} %copy-done.2), custom_call_target="tpu_custom_call" | custom-call | tf_op jit(solution)/shard_map/prepare/pallas_call | solution.py:44
  4.2 0.0 copy-start.3
  4.2 4.1 %all-to-all-start = ((bf16[128,16,128]{2,1,0:T(8,128)(2,1)}), bf16[128,16,128]{2,1,0:T(8,128)(2,1)S(1)}, u32[]{:S(2)}, u32[]{:S(2)}) async-start(bf16[128,16,128]{2,1,0:T(8,128)(2,1)} %get-tuple-element.10), calls=%async_computation | async-start | bytes 1048576 | tf_op jit(solution)/shard_map/all_to_all | solution.py:210
  8.3 0.0 copy-start.4
  8.3 0.0 copy-start.5
  8.3 3.4 %collective-permute-start.2 = (bf16[2,2,128,128]{3,2,1,0:T(8,128)(2,1)S(1)}, bf16[2,2,128,128]{3,2,1,0:T(8,128)(2,1)S(1)}, u32[]{:S(2)}, u32[]{:S(2)}) collective-permute-start(bf16[2,2,128,128]{3,2,1,0:T(8,128)(2,1)S(1)} %get-tuple-element.11.kv_own), channel_id=1, source_target_pairs={{4,0},{8,4},{12,8},{16,12},{20,16},{24,20},{28,24},{5,1},{9,5},{13... | collective-permute-start | bytes 393224 | tf_op jit(solution)/shard_map/ppermute | solution.py:204
  11.7 1.3 %collective-permute-start.1 = (bf16[2,2,128,128]{3,2,1,0:T(8,128)(2,1)S(1)}, bf16[2,2,128,128]{3,2,1,0:T(8,128)(2,1)S(1)}, u32[]{:S(2)}, u32[]{:S(2)}) collective-permute-start(bf16[2,2,128,128]{3,2,1,0:T(8,128)(2,1)S(1)} %get-tuple-element.11.kv_own), channel_id=1, source_target_pairs={{0,8},{4,12},{8,16},{12,20},{16,24},{20,28},{1,9},{5,13},{9,17},{1... | collective-permute-start | bytes 393224 | tf_op jit(solution)/shard_map/ppermute | solution.py:204
  13.0 2.6 %collective-permute-start = (bf16[2,2,128,128]{3,2,1,0:T(8,128)(2,1)S(1)}, bf16[2,2,128,128]{3,2,1,0:T(8,128)(2,1)S(1)}, u32[]{:S(2)}, u32[]{:S(2)}) collective-permute-start(bf16[2,2,128,128]{3,2,1,0:T(8,128)(2,1)S(1)} %get-tuple-element.11.kv_own), channel_id=1, source_target_pairs={{0,4},{4,8},{8,12},{12,16},{16,20},{20,24},{24,28},{1,5},{5,9},{9,... | collective-permute-start | bytes 393224 | tf_op jit(solution)/shard_map/ppermute | solution.py:204
  15.6 0.3 collective-permute-done.2.kv_ahead
  15.9 3.0 %collective-permute-done.1.kv_back2 = bf16[2,2,128,128]{3,2,1,0:T(8,128)(2,1)S(1)} collective-permute-done((bf16[2,2,128,128]{3,2,1,0:T(8,128)(2,1)S(1)}, bf16[2,2,128,128]{3,2,1,0:T(8,128)(2,1)S(1)}, u32[]{:S(2)}, u32[]{:S(2)}) %collective-permute-start.1) | collective-permute-done | bytes 131104 | tf_op jit(solution)/shard_map/ppermute | solution.py:204
  18.9 2.9 %collective-permute-done.kv_back1 = bf16[2,2,128,128]{3,2,1,0:T(8,128)(2,1)S(1)} collective-permute-done((bf16[2,2,128,128]{3,2,1,0:T(8,128)(2,1)S(1)}, bf16[2,2,128,128]{3,2,1,0:T(8,128)(2,1)S(1)}, u32[]{:S(2)}, u32[]{:S(2)}) %collective-permute-start) | collective-permute-done | bytes 131104 | tf_op jit(solution)/shard_map/ppermute | solution.py:204
  21.8 0.0 all-to-all-done.cot_ref
  21.8 0.0 copy-done.3
  21.8 0.0 copy-done.4
  21.8 0.0 copy-done.5
  21.8 6.1 %gradients.1 = (bf16[128,16,128]{2,1,0:T(8,128)(2,1)}, f32[2,2,128,128]{3,2,1,0:T(8,128)S(1)}, bf16[2,2,128,128]{3,2,1,0:T(8,128)(2,1)S(1)}, bf16[2,2,128,128]{3...) custom-call(s32[8]{0:T(128)S(1)} %copy-done.4, s32[8]{0:T(128)S(1)} %copy-done.5, bf16[128,16,128]{2,1,0:T(8,128)(2,1)S(1)} %copy-done.3, ...), custom_call_target="tpu_custom_call" | custom-call | flops 1342177280 | bytes 2097152 | tf_op jit(solution)/shard_map/gradients/pallas_call | solution.py:145
  27.9 3.8 %all-to-all-start.1 = ((bf16[128,16,128]{2,1,0:T(8,128)(2,1)}), bf16[128,16,128]{2,1,0:T(8,128)(2,1)S(1)}, u32[]{:S(2)}, u32[]{:S(2)}) async-start(bf16[128,16,128]{2,1,0:T(8,128)(2,1)} %get-tuple-element.12), calls=%async_computation.1 | async-start | bytes 1048576 | tf_op jit(solution)/shard_map/all_to_all | solution.py:216
  31.7 2.7 %collective-permute-start.3 = (bf16[2,2,128,128]{3,2,1,0:T(8,128)(2,1)S(1)}, bf16[2,2,128,128]{3,2,1,0:T(8,128)(2,1)S(1)}, u32[]{:S(2)}, u32[]{:S(2)}) collective-permute-start(bf16[2,2,128,128]{3,2,1,0:T(8,128)(2,1)S(1)} %get-tuple-element.14), channel_id=1, source_target_pairs={{4,0},{8,4},{12,8},{16,12},{20,16},{24,20},{28,24},{5,1},{9,5},{13... | collective-permute-start | bytes 393224 | tf_op jit(solution)/shard_map/ppermute | solution.py:204
  34.5 2.7 %collective-permute-start.4 = (bf16[2,2,128,128]{3,2,1,0:T(8,128)(2,1)S(1)}, bf16[2,2,128,128]{3,2,1,0:T(8,128)(2,1)S(1)}, u32[]{:S(2)}, u32[]{:S(2)}) collective-permute-start(bf16[2,2,128,128]{3,2,1,0:T(8,128)(2,1)S(1)} %get-tuple-element.15), channel_id=1, source_target_pairs={{8,0},{12,4},{16,8},{20,12},{24,16},{28,20},{9,1},{13,5},{17,9},{2... | collective-permute-start | bytes 393224 | tf_op jit(solution)/shard_map/ppermute | solution.py:204
  37.2 3.9 %collective-permute-start.5 = (bf16[2,2,128,128]{3,2,1,0:T(8,128)(2,1)S(1)}, bf16[2,2,128,128]{3,2,1,0:T(8,128)(2,1)S(1)}, u32[]{:S(2)}, u32[]{:S(2)}) collective-permute-start(bf16[2,2,128,128]{3,2,1,0:T(8,128)(2,1)S(1)} %get-tuple-element.16), channel_id=1, source_target_pairs={{0,4},{4,8},{8,12},{12,16},{16,20},{20,24},{24,28},{1,5},{5,9},{9,... | collective-permute-start | bytes 393224 | tf_op jit(solution)/shard_map/ppermute | solution.py:204
  41.1 0.0 collective-permute-done.3.from_ahead1
  41.2 0.0 collective-permute-done.4.from_ahead2
  41.2 4.1 %collective-permute-done.5.from_back = bf16[2,2,128,128]{3,2,1,0:T(8,128)(2,1)S(1)} collective-permute-done((bf16[2,2,128,128]{3,2,1,0:T(8,128)(2,1)S(1)}, bf16[2,2,128,128]{3,2,1,0:T(8,128)(2,1)S(1)}, u32[]{:S(2)}, u32[]{:S(2)}) %collective-permute-start.5) | collective-permute-done | bytes 131104 | tf_op jit(solution)/shard_map/ppermute | solution.py:204
  45.3 0.0 all-to-all-done.1
  45.3 1.0 %finish.1 = (bf16[32,64,128]{2,1,0:T(8,128)(2,1)}, bf16[128,2,128]{2,1,0:T(2,128)(2,1)}, bf16[128,2,128]{2,1,0:T(2,128)(2,1)}) custom-call(bf16[4,32,16,128]{3,2,1,0:T(8,128)(2,1)S(1)} %bitcast.1, f32[2,2,128,128]{3,2,1,0:T(8,128)S(1)} %get-tuple-element.13.own, bf16[2,2,128,128]{3,2,1,0:T(8,128)(2,1)S(1)} %collective-permute-done.3.from_ahead1, ...), custom_call_target="tpu_custom_call" | custom-call | tf_op jit(solution)/shard_map/finish/pallas_call | solution.py:187
Async XLA Ops:
  0.6 1.0 %copy-start = (bf16[32,64,128]{2,1,0:T(8,128)(2,1)S(1)}, bf16[32,64,128]{2,1,0:T(8,128)(2,1)}, u32[]{:S(2)}) copy-start(bf16[32,64,128]{2,1,0:T(8,128)(2,1)} %cot_ref.1) | copy-start | bytes 1572868
  1.7 0.8 %copy-start.1 = (bf16[128,2,128]{2,1,0:T(2,128)(2,1)S(1)}, bf16[128,2,128]{2,1,0:T(2,128)(2,1)}, u32[]{:S(2)}) copy-start(bf16[128,2,128]{2,1,0:T(2,128)(2,1)} %key_ref.1) | copy-start | bytes 196612
  2.5 0.8 %copy-start.2 = (bf16[128,2,128]{2,1,0:T(2,128)(2,1)S(1)}, bf16[128,2,128]{2,1,0:T(2,128)(2,1)}, u32[]{:S(2)}) copy-start(bf16[128,2,128]{2,1,0:T(2,128)(2,1)} %value_ref.1) | copy-start | bytes 196612
  4.2 17.6 %copy-start.3 = (bf16[128,16,128]{2,1,0:T(8,128)(2,1)S(1)}, bf16[128,16,128]{2,1,0:T(8,128)(2,1)}, u32[]{:S(2)}) copy-start(bf16[128,16,128]{2,1,0:T(8,128)(2,1)} %q_ref.1) | copy-start | bytes 1572868
  4.2 17.6 %all-to-all-start = ((bf16[128,16,128]{2,1,0:T(8,128)(2,1)}), bf16[128,16,128]{2,1,0:T(8,128)(2,1)S(1)}, u32[]{:S(2)}, u32[]{:S(2)}) async-start(bf16[128,16,128]{2,1,0:T(8,128)(2,1)} %get-tuple-element.10), calls=%async_computation | async-start | bytes 1048576 | tf_op jit(solution)/shard_map/all_to_all | solution.py:210
  8.3 13.5 %copy-start.4 = (s32[8]{0:T(128)S(1)}, s32[8]{0:T(128)}, u32[]{:S(2)}) copy-start(s32[8]{0:T(128)} %lengths.1) | copy-start | bytes 100
  8.3 13.5 %copy-start.5 = (s32[8]{0:T(128)S(1)}, s32[8]{0:T(128)}, u32[]{:S(2)}) copy-start(s32[8]{0:T(128)} %prefixes.1) | copy-start | bytes 100
  8.3 7.6 %collective-permute-start.2 = (bf16[2,2,128,128]{3,2,1,0:T(8,128)(2,1)S(1)}, bf16[2,2,128,128]{3,2,1,0:T(8,128)(2,1)S(1)}, u32[]{:S(2)}, u32[]{:S(2)}) collective-permute-start(bf16[2,2,128,128]{3,2,1,0:T(8,128)(2,1)S(1)} %get-tuple-element.11.kv_own), channel_id=1, source_target_pairs={{4,0},{8,4},{12,8},{16,12},{20,16},{24,20},{28,24},{5,1},{9,5},{13... | collective-permute-start | bytes 393224 | tf_op jit(solution)/shard_map/ppermute | solution.py:204
  11.7 7.2 %collective-permute-start.1 = (bf16[2,2,128,128]{3,2,1,0:T(8,128)(2,1)S(1)}, bf16[2,2,128,128]{3,2,1,0:T(8,128)(2,1)S(1)}, u32[]{:S(2)}, u32[]{:S(2)}) collective-permute-start(bf16[2,2,128,128]{3,2,1,0:T(8,128)(2,1)S(1)} %get-tuple-element.11.kv_own), channel_id=1, source_target_pairs={{0,8},{4,12},{8,16},{12,20},{16,24},{20,28},{1,9},{5,13},{9,17},{1... | collective-permute-start | bytes 393224 | tf_op jit(solution)/shard_map/ppermute | solution.py:204
  13.0 8.8 %collective-permute-start = (bf16[2,2,128,128]{3,2,1,0:T(8,128)(2,1)S(1)}, bf16[2,2,128,128]{3,2,1,0:T(8,128)(2,1)S(1)}, u32[]{:S(2)}, u32[]{:S(2)}) collective-permute-start(bf16[2,2,128,128]{3,2,1,0:T(8,128)(2,1)S(1)} %get-tuple-element.11.kv_own), channel_id=1, source_target_pairs={{0,4},{4,8},{8,12},{12,16},{16,20},{20,24},{24,28},{1,5},{5,9},{9,... | collective-permute-start | bytes 393224 | tf_op jit(solution)/shard_map/ppermute | solution.py:204
  27.9 17.4 %all-to-all-start.1 = ((bf16[128,16,128]{2,1,0:T(8,128)(2,1)}), bf16[128,16,128]{2,1,0:T(8,128)(2,1)S(1)}, u32[]{:S(2)}, u32[]{:S(2)}) async-start(bf16[128,16,128]{2,1,0:T(8,128)(2,1)} %get-tuple-element.12), calls=%async_computation.1 | async-start | bytes 1048576 | tf_op jit(solution)/shard_map/all_to_all | solution.py:216
  31.7 9.4 %collective-permute-start.3 = (bf16[2,2,128,128]{3,2,1,0:T(8,128)(2,1)S(1)}, bf16[2,2,128,128]{3,2,1,0:T(8,128)(2,1)S(1)}, u32[]{:S(2)}, u32[]{:S(2)}) collective-permute-start(bf16[2,2,128,128]{3,2,1,0:T(8,128)(2,1)S(1)} %get-tuple-element.14), channel_id=1, source_target_pairs={{4,0},{8,4},{12,8},{16,12},{20,16},{24,20},{28,24},{5,1},{9,5},{13... | collective-permute-start | bytes 393224 | tf_op jit(solution)/shard_map/ppermute | solution.py:204
  34.5 6.7 %collective-permute-start.4 = (bf16[2,2,128,128]{3,2,1,0:T(8,128)(2,1)S(1)}, bf16[2,2,128,128]{3,2,1,0:T(8,128)(2,1)S(1)}, u32[]{:S(2)}, u32[]{:S(2)}) collective-permute-start(bf16[2,2,128,128]{3,2,1,0:T(8,128)(2,1)S(1)} %get-tuple-element.15), channel_id=1, source_target_pairs={{8,0},{12,4},{16,8},{20,12},{24,16},{28,20},{9,1},{13,5},{17,9},{2... | collective-permute-start | bytes 393224 | tf_op jit(solution)/shard_map/ppermute | solution.py:204
  37.2 8.1 %collective-permute-start.5 = (bf16[2,2,128,128]{3,2,1,0:T(8,128)(2,1)S(1)}, bf16[2,2,128,128]{3,2,1,0:T(8,128)(2,1)S(1)}, u32[]{:S(2)}, u32[]{:S(2)}) collective-permute-start(bf16[2,2,128,128]{3,2,1,0:T(8,128)(2,1)S(1)} %get-tuple-element.16), channel_id=1, source_target_pairs={{0,4},{4,8},{8,12},{12,16},{16,20},{20,24},{24,28},{1,5},{5,9},{9,... | collective-permute-start | bytes 393224 | tf_op jit(solution)/shard_map/ppermute | solution.py:204

commit v2 on v1

v2 whole, which is shorter than its diff:
```python
import functools

import jax
import jax.numpy as jnp
from jax import lax
from jax.experimental import pallas as pl
from jax.experimental.pallas import tpu as pltpu
from jax.sharding import PartitionSpec as P

BACK = 2
AHEAD = 1
LOG2E = 1.4426950408889634
VMEM_BYTES = 40 * 1024 * 1024
PREPARE_VMEM_BYTES = 60 * 1024 * 1024
NEG = -1e30

_VMEM = pl.BlockSpec(memory_space=pltpu.VMEM)
_SMEM = pl.BlockSpec(memory_space=pltpu.SMEM)
_HBM = pl.BlockSpec(memory_space=pltpu.HBM)


def sequence(parts, shifts):
    masks, shifts = list(range(parts - 1, 0, -1)), list(shifts)
    order = [("mask", 0)]
    while masks or shifts:
        if shifts:
            order.append(("shift", shifts.pop(0)))
        if masks:
            order.append(("mask", masks.pop(0)))
    return order


def arrange(pieces, blocks, shifts):
    return [
        pieces[which] if kind == "mask" else blocks[which]
        for kind, which in sequence(len(pieces), shifts)
    ]


def arranged(parts, shifts, refs):
    order = sequence(parts, shifts)
    found = dict(zip(order, refs))
    return (
        [found["mask", mask] for mask in range(parts)],
        {shift: found["shift", shift] for shift in shifts},
        refs[len(order):],
    )


def prep_kernel(parts, cot_ref, key_ref, value_ref, *rest):
    kv_outs, cot_outs, (key_buf, value_buf, sems) = rest[:3], rest[3 : parts + 3], rest[parts + 3 :]
    heads = cot_ref.shape[1] // parts
    me = lax.axis_index("kvh")
    loads = []
    for number, (ref, buf) in enumerate(((key_ref, key_buf), (value_ref, value_buf))):
        loads.append(pltpu.make_async_copy(ref, buf, sems.at[parts + number]))
        loads[-1].start()
    copies = []
    for mask in range(parts):
        first = pl.multiple_of((me ^ mask) * heads, heads)
        copies.append(
            pltpu.make_async_copy(
                cot_ref.at[:, pl.ds(first, heads), :], cot_outs[mask], sems.at[mask]
            )
        )
        copies[-1].start()
    for number, buf in enumerate((key_buf, value_buf)):
        loads[number].wait()
        wide = buf[...].astype(jnp.float32)
        for group in range(buf.shape[1]):
            packed = wide[:, group, :].astype(jnp.bfloat16)
            for kv_out in kv_outs:
                kv_out[number, group] = packed
    for copy in copies:
        copy.wait()


def prepare(cotangent, keys, values, parts):
    rows, heads, size = cotangent.shape
    kv_rows, kv_heads, _ = keys.shape
    piece = jax.ShapeDtypeStruct((rows, heads // parts, size), jnp.bfloat16)
    outs = pl.pallas_call(
        functools.partial(prep_kernel, parts),
        out_shape=(jax.ShapeDtypeStruct((2, kv_heads, kv_rows, size), jnp.bfloat16),) * 3
        + (piece,) * parts,
        in_specs=[_HBM] * 3,
        out_specs=(_VMEM,) * (parts + 3),
        scratch_shapes=[
            pltpu.VMEM(keys.shape, jnp.bfloat16),
            pltpu.VMEM(values.shape, jnp.bfloat16),
            pltpu.SemaphoreType.DMA((parts + 2,)),
        ],
        compiler_params=pltpu.CompilerParams(vmem_limit_bytes=PREPARE_VMEM_BYTES),
        name="prepare",
    )(cotangent, keys, values)
    return outs[:3], outs[3:]


def bounds(position, lengths, prefixes):
    docs = lengths.shape[0]

    def step(doc, carry):
        start, low, high = carry
        end = start + lengths[doc]
        inside = (position >= start) & (position < end)
        reach = jnp.minimum(end, jnp.maximum(position + 1, start + prefixes[doc]))
        return end, jnp.where(inside, start, low), jnp.where(inside, reach, high)

    zero = jnp.zeros_like(position)
    carry = (jnp.int32(0), zero, zero)
    if docs <= 16:
        for doc in range(docs):
            carry = step(doc, carry)
    else:
        carry = lax.fori_loop(0, docs, step, carry)
    return carry[1], carry[2]


def grad_kernel(parts, lengths, prefixes, q_ref, *rest):
    cot_refs, got, rest = arranged(parts, (-1, 2, 1), rest)
    kv_own, rest = rest[0], rest[1:]
    kv_back1, kv_back2, kv_ahead = got[1], got[2], got[-1]
    dq_refs, rest = rest[:parts], rest[parts:]
    own_out, back1_out, back2_out, ahead_out, window, acc, cot_own, sems = rest
    rows, heads, size = q_ref.shape
    tokens = rows // parts
    kv_heads = kv_own.shape[1]
    group_size = heads // kv_heads
    span = (BACK + 1 + AHEAD) * rows
    reach = span - rows + tokens
    lanes = tokens * group_size
    scale = size ** (-0.5)
    shard = lax.axis_index("seq")
    me = lax.axis_index("kvh")

    loads = [
        pltpu.make_async_copy(
            kv_own, window.at[:, :, pl.ds(BACK * rows, rows)], sems.at[0]
        ),
        pltpu.make_async_copy(cot_refs[0], cot_own, sems.at[1]),
    ]
    cot_refs[0] = cot_own
    for load in loads:
        load.start()
    for slot, ref in ((0, kv_back2), (1, kv_back1), (BACK + 1, kv_ahead)):
        for number in range(2):
            for group in range(kv_heads):
                window[number, group, pl.ds(slot * rows, rows)] = ref[number, group]
    acc[...] = jnp.zeros_like(acc)

    contract_last = (((1,), (1,)), ((), ()))
    contract_first = (((0,), (0,)), ((), ()))
    for load in loads:
        load.wait()
    lane_token = lax.broadcasted_iota(jnp.int32, (1, lanes), 1) // group_size
    key_iota = lax.broadcasted_iota(jnp.int32, (reach, lanes), 0)
    for mask in range(parts):
        first = pl.multiple_of((me ^ mask) * tokens, tokens)
        low, high = bounds(shard * rows + first + lane_token, lengths, prefixes)
        origin = (shard - BACK) * rows + first
        low = low - origin
        high = high - origin
        visible = (key_iota >= low) & (key_iota < high)
        here = pl.ds(first, reach)
        for group in range(kv_heads):
            of_group = pl.ds(group * group_size, group_size)
            q = q_ref[pl.ds(first, tokens), of_group].astype(jnp.float32)
            q = q.reshape(lanes, size).astype(jnp.bfloat16)
            cot = cot_refs[mask][:, of_group].astype(jnp.float32)
            cot = cot.reshape(lanes, size).astype(jnp.bfloat16)
            k = window[0, group, here]
            v = window[1, group, here]
            scores = lax.dot_general(k, q, contract_last, preferred_element_type=jnp.float32)
            scores = jnp.where(visible, scores * (scale * LOG2E), NEG)
            top = jnp.max(scores, axis=0, keepdims=True)
            expo = jnp.exp2(scores - top)
            total = jnp.sum(expo, axis=0, keepdims=True)
            probs = expo * (1.0 / total)
            dprobs = lax.dot_general(v, cot, contract_last, preferred_element_type=jnp.float32)
            delta = jnp.sum(probs * dprobs, axis=0, keepdims=True)
            dscores = (probs * (dprobs - delta)).astype(jnp.bfloat16)
            acc[1, group, here] += jnp.dot(
                probs.astype(jnp.bfloat16), cot, preferred_element_type=jnp.float32
            )
            acc[0, group, here] += jnp.dot(dscores, q, preferred_element_type=jnp.float32)
            dq = lax.dot_general(k, dscores, contract_first, preferred_element_type=jnp.float32)
            dq = jnp.transpose(dq * scale)
            dq_refs[mask][:, of_group] = dq.reshape(tokens, group_size, size).astype(jnp.bfloat16)
    for slot, ref in enumerate((back2_out, back1_out, own_out, ahead_out)):
        for group in range(kv_heads):
            part = pl.ds(slot * rows, rows)
            ref[0, group] = (acc[0, group, part] * scale).astype(ref.dtype)
            ref[1, group] = acc[1, group, part].astype(ref.dtype)


def gradients(lengths, prefixes, queries, cots, got, kv):
    rows, heads, size = queries.shape
    parts = len(cots)
    kv_shape = kv.shape
    kv_heads = kv_shape[1]
    span = (BACK + 1 + AHEAD) * rows
    half = jax.ShapeDtypeStruct(kv_shape, jnp.bfloat16)
    work = heads * rows * span
    outs = pl.pallas_call(
        functools.partial(grad_kernel, parts),
        out_shape=(jax.ShapeDtypeStruct(cots[0].shape, jnp.bfloat16),) * parts
        + (jax.ShapeDtypeStruct(kv_shape, jnp.float32), half, half, half),
        in_specs=[_SMEM, _SMEM, _VMEM, _HBM] + [_VMEM] * (parts + 2) + [_HBM],
        out_specs=(_VMEM,) * (parts + 4),
        scratch_shapes=[
            pltpu.VMEM((2, kv_heads, span, size), jnp.bfloat16),
            pltpu.VMEM((2, kv_heads, span, size), jnp.float32),
            pltpu.VMEM(cots[0].shape, jnp.bfloat16),
            pltpu.SemaphoreType.DMA((2,)),
        ],
        compiler_params=pltpu.CompilerParams(vmem_limit_bytes=VMEM_BYTES),
        cost_estimate=pl.CostEstimate(
            flops=10 * work * size, bytes_accessed=4 * queries.size * 2, transcendentals=work
        ),
        name="gradients",
    )(lengths, prefixes, queries, *arrange(cots, got, (-1, 2, 1)), kv)
    return outs[:parts], outs[parts:]


def finish_kernel(parts, *refs):
    dq_refs, got, (own, dq_out, dk_out, dv_out) = arranged(parts, (1, -2, -1), refs)
    heads = dq_refs[0].shape[1]
    me = lax.axis_index("kvh")
    for mask in range(parts):
        first = pl.multiple_of((me ^ mask) * heads, heads)
        dq_out[:, pl.ds(first, heads), :] = dq_refs[mask][...]
    for number, ref in enumerate((dk_out, dv_out)):
        sums = []
        for group in range(ref.shape[1]):
            total = own[number, group]
            for other in (got[-1], got[-2], got[1]):
                total = total + other[number, group].astype(jnp.float32)
            sums.append(total)
        ref[...] = jnp.stack(sums, axis=1).astype(jnp.bfloat16)


def finish(dqs, own, got):
    parts = len(dqs)
    rows, heads, size = dqs[0].shape
    _, kv_heads, kv_rows, _ = own.shape
    kv_out = jax.ShapeDtypeStruct((kv_rows, kv_heads, size), jnp.bfloat16)
    return pl.pallas_call(
        functools.partial(finish_kernel, parts),
        out_shape=(
            jax.ShapeDtypeStruct((rows, heads * parts, size), jnp.bfloat16),
            kv_out,
            kv_out,
        ),
        in_specs=[_VMEM] * (parts + 4),
        out_specs=(_VMEM,) * 3,
        compiler_params=pltpu.CompilerParams(vmem_limit_bytes=VMEM_BYTES),
        name="finish",
    )(*arrange(dqs, got, (1, -2, -1)), own)


def shifted(block, distance):
    devices = range(lax.axis_size("seq"))
    route = [(i - distance, i) for i in devices if i - distance in devices]
    return lax.ppermute(block, "seq", route)


def swapped(block, mask):
    return lax.ppermute(block, "kvh", [(i, i ^ mask) for i in range(lax.axis_size("kvh"))])


def exchange(pieces, blocks):
    pieces = [pieces[0]] + [swapped(pieces[mask], mask) for mask in range(1, len(pieces))]
    return pieces, {shift: shifted(block, shift) for shift, block in blocks.items()}


def local(queries, keys, values, output_gradient, doc_lengths, prefix_lengths):
    parts = lax.axis_size("kvh")
    kv, cots = prepare(output_gradient, keys, values, parts)
    cots, got = exchange(cots, {1: kv[0], 2: kv[1], -1: kv[2]})
    dqs, (own, back1, back2, ahead) = gradients(
        doc_lengths, prefix_lengths, queries, cots, got, kv[0]
    )
    dqs, got = exchange(dqs, {-1: back1, -2: back2, 1: ahead})
    return finish(dqs, own, got)


def solution(mesh):
    in_specs = (
        P("seq", "kvh", None),
        P("seq", "kvh", None),
        P("seq", "kvh", None),
        P(("seq", "kvh"), None, None),
        P(),
        P(),
    )
    out_specs = (P(("seq", "kvh"), None, None), P("seq", "kvh", None), P("seq", "kvh", None))
    return jax.shard_map(local, mesh=mesh, in_specs=in_specs, out_specs=out_specs, check_vma=False)
```

time: 46.8 us -> 44.9 us (0.959)
  the two profiles are of different devices: /device:TPU:28 before, /device:TPU:0 now
where the time goes in v2:
time: 44.9 us; the launch traced here: 44.1 us
  starting transfers between devices  22.1 us (49%)
  waiting for transfers between devices  10.5 us (23%)
  Pallas kernels  8.9 us (20%)
  local copies, waits for them, and re-layouts  1.82 us (4%)
  between operations  0.75 us (2%)
    ppermute x6, starting transfers between devices, shifted(): return lax.ppermute(block, 'seq', route)  16.6 us
    ppermute x6, waiting for transfers between devices, shifted(): return lax.ppermute(block, 'seq', route)  7.14 us
    pallas_call x1, Pallas kernels, gradients(): pl.pallas_call(functools.partial(grad_kernel, parts), out_shape=(jax.Shap...  5.69 us
    ppermute x6, starting transfers between devices, swapped(): lax.ppermute(block, 'kvh', [(i, i ^ mask) for i in range(lax.axis_size('k...  5.48 us
    ppermute x6, waiting for transfers between devices, swapped(): lax.ppermute(block, 'kvh', [(i, i ^ mask) for i in range(lax.axis_size('k...  3.4 us
    pallas_call x1, Pallas kernels, prepare(): pl.pallas_call(functools.partial(prep_kernel, parts), out_shape=(jax.Shap...  2.2 us
    unnamed x10, local copies, waits for them, and re-layouts  1.82 us
    pallas_call x1, Pallas kernels, finish(): pl.pallas_call(functools.partial(finish_kernel, parts), out_shape=(jax.Sh...  1.02 us
  transfers between devices with their start and end apart: 12, of which 6 were waited for; matrix products, arithmetic and copies ran while one was open for 0% of the time, Pallas kernels for 0%

profile of v2, /device:TPU:0, one launch (start us, length us, event | category | flops | bytes accessed | tf_op | source)
XLA Modules:
  0.0 44.1 jit_solution(13764594250825133001)
XLA Ops:
  0.6 0.0 copy-start
  0.6 2.2 %prepare.1 = (bf16[2,2,128,128]{3,2,1,0:T(8,128)(2,1)}, bf16[2,2,128,128]{3,2,1,0:T(8,128)(2,1)}, bf16[2,2,128,128]{3,2,1,0:T(8,128)(2,1)}, bf16[32,16,128]{2,1,...) custom-call(bf16[32,64,128]{2,1,0:T(8,128)(2,1)} %cot_ref.1, ...), custom_call_target="tpu_custom_call" | custom-call | tf_op jit(solution)/shard_map/prepare/pallas_call | solution.py:82
  2.8 1.3 %collective-permute-start = (bf16[2,2,128,128]{3,2,1,0:T(8,128)(2,1)}, bf16[2,2,128,128]{3,2,1,0:T(8,128)(2,1)S(1)}, u32[]{:S(2)}, u32[]{:S(2)}) collective-permute-start(bf16[2,2,128,128]{3,2,1,0:T(8,128)(2,1)} %get-tuple-element.19), channel_id=1, source_target_pairs={{4,0},{8,4},{12,8},{16,12},{20,16},{24,20},{28,24},{5,1},{9,5},{13... | collective-permute-start | bytes 393224 | tf_op jit(solution)/shard_map/ppermute | solution.py:264
  4.1 2.5 %collective-permute-start.1 = (bf16[32,16,128]{2,1,0:T(8,128)(2,1)}, bf16[32,16,128]{2,1,0:T(8,128)(2,1)S(1)}, u32[]{:S(2)}, u32[]{:S(2)}) collective-permute-start(bf16[32,16,128]{2,1,0:T(8,128)(2,1)} %get-tuple-element.20), channel_id=1, source_target_pairs={{0,3},{1,2},{2,1},{3,0},{4,7},{5,6},{6,5},{7,4},{8,11},{9,10},{10,... | collective-permute-start | bytes 393224 | tf_op jit(solution)/shard_map/ppermute | solution.py:268
  6.6 5.2 %collective-permute-start.2 = (bf16[2,2,128,128]{3,2,1,0:T(8,128)(2,1)}, bf16[2,2,128,128]{3,2,1,0:T(8,128)(2,1)S(1)}, u32[]{:S(2)}, u32[]{:S(2)}) collective-permute-start(bf16[2,2,128,128]{3,2,1,0:T(8,128)(2,1)} %get-tuple-element.21), channel_id=1, source_target_pairs={{0,8},{4,12},{8,16},{12,20},{16,24},{20,28},{1,9},{5,13},{9,17},{1... | collective-permute-start | bytes 393224 | tf_op jit(solution)/shard_map/ppermute | solution.py:264
  11.8 0.9 %collective-permute-start.3 = (bf16[32,16,128]{2,1,0:T(8,128)(2,1)}, bf16[32,16,128]{2,1,0:T(8,128)(2,1)S(1)}, u32[]{:S(2)}, u32[]{:S(2)}) collective-permute-start(bf16[32,16,128]{2,1,0:T(8,128)(2,1)} %get-tuple-element.22), channel_id=1, source_target_pairs={{0,2},{1,3},{2,0},{3,1},{4,6},{5,7},{6,4},{7,5},{8,10},{9,11},{10,... | collective-permute-start | bytes 393224 | tf_op jit(solution)/shard_map/ppermute | solution.py:268
  12.7 0.0 collective-permute-start.5
  12.8 0.0 collective-permute-done.rest_1_
  12.8 0.0 copy-start.3
  12.8 0.0 copy-start.4
  12.8 3.3 %collective-permute-start.4 = (bf16[2,2,128,128]{3,2,1,0:T(8,128)(2,1)}, bf16[2,2,128,128]{3,2,1,0:T(8,128)(2,1)S(1)}, u32[]{:S(2)}, u32[]{:S(2)}) collective-permute-start(bf16[2,2,128,128]{3,2,1,0:T(8,128)(2,1)} %get-tuple-element.23.rest_7_), channel_id=1, source_target_pairs={{0,4},{4,8},{8,12},{12,16},{16,20},{20,24},{24,28},{1,5},{5,9},{9,... | collective-permute-start | bytes 393224 | tf_op jit(solution)/shard_map/ppermute | solution.py:264
  16.1 0.0 collective-permute-done.1.rest_2_
  16.1 0.0 collective-permute-done.2.rest_3_
  16.1 2.1 %collective-permute-done.3.rest_4_ = bf16[32,16,128]{2,1,0:T(8,128)(2,1)S(1)} collective-permute-done((bf16[32,16,128]{2,1,0:T(8,128)(2,1)}, bf16[32,16,128]{2,1,0:T(8,128)(2,1)S(1)}, u32[]{:S(2)}, u32[]{:S(2)}) %collective-permute-start.3) | collective-permute-done | bytes 131104 | tf_op jit(solution)/shard_map/ppermute | solution.py:268
  18.2 0.0 collective-permute-done.5.rest_6_
  18.2 1.0 %collective-permute-done.4.rest_5_ = bf16[2,2,128,128]{3,2,1,0:T(8,128)(2,1)S(1)} collective-permute-done((bf16[2,2,128,128]{3,2,1,0:T(8,128)(2,1)}, bf16[2,2,128,128]{3,2,1,0:T(8,128)(2,1)S(1)}, u32[]{:S(2)}, u32[]{:S(2)}) %collective-permute-start.4) | collective-permute-done | bytes 131104 | tf_op jit(solution)/shard_map/ppermute | solution.py:264
  19.2 0.0 copy-done
  19.2 0.0 copy-done.3
  19.2 0.0 copy-done.4
  19.2 0.0 copy-start.1
  19.2 0.9 %copy-done.1 = bf16[2,2,128,128]{3,2,1,0:T(8,128)(2,1)S(1)} copy-done((bf16[2,2,128,128]{3,2,1,0:T(8,128)(2,1)S(1)}, bf16[2,2,128,128]{3,2,1,0:T(8,128)(2,1)}, u32[]{:S(2)}) %copy-start.1) | copy-done | bytes 131096
  20.1 0.0 copy-start.2
  20.1 0.9 %copy-done.2 = bf16[32,16,128]{2,1,0:T(8,128)(2,1)S(1)} copy-done((bf16[32,16,128]{2,1,0:T(8,128)(2,1)S(1)}, bf16[32,16,128]{2,1,0:T(8,128)(2,1)}, u32[]{:S(2)}) %copy-start.2) | copy-done | bytes 131096
  21.0 5.7 %gradients.1 = (bf16[32,16,128]{2,1,0:T(8,128)(2,1)S(1)}, bf16[32,16,128]{2,1,0:T(8,128)(2,1)S(1)}, bf16[32,16,128]{2,1,0:T(8,128)(2,1)S(1)}, bf16[32,16,128]{2,...) custom-call(s32[8]{0:T(128)S(1)} %copy-done.3, ...), custom_call_target="tpu_custom_call" | custom-call | flops 1342177280 | bytes 2097152 | tf_op jit(solution)/shard_map/gradients/pallas_call | solution.py:204
  26.7 4.3 %collective-permute-start.6 = (bf16[2,2,128,128]{3,2,1,0:T(8,128)(2,1)S(1)}, bf16[2,2,128,128]{3,2,1,0:T(8,128)(2,1)S(1)}, u32[]{:S(2)}, u32[]{:S(2)}) collective-permute-start(bf16[2,2,128,128]{3,2,1,0:T(8,128)(2,1)S(1)} %get-tuple-element.26), channel_id=1, source_target_pairs={{0,4},{4,8},{8,12},{12,16},{16,20},{20,24},{24,28},{1,5},{5,9},{9,... | collective-permute-start | bytes 393224 | tf_op jit(solution)/shard_map/ppermute | solution.py:264
  31.0 0.1 collective-permute-start.7
  31.1 1.3 %collective-permute-start.8 = (bf16[2,2,128,128]{3,2,1,0:T(8,128)(2,1)S(1)}, bf16[2,2,128,128]{3,2,1,0:T(8,128)(2,1)S(1)}, u32[]{:S(2)}, u32[]{:S(2)}) collective-permute-start(bf16[2,2,128,128]{3,2,1,0:T(8,128)(2,1)S(1)} %get-tuple-element.28), channel_id=1, source_target_pairs={{8,0},{12,4},{16,8},{20,12},{24,16},{28,20},{9,1},{13,5},{17,9},{2... | collective-permute-start | bytes 393224 | tf_op jit(solution)/shard_map/ppermute | solution.py:264
  32.4 1.3 %collective-permute-start.9 = (bf16[32,16,128]{2,1,0:T(8,128)(2,1)S(1)}, bf16[32,16,128]{2,1,0:T(8,128)(2,1)S(1)}, u32[]{:S(2)}, u32[]{:S(2)}) collective-permute-start(bf16[32,16,128]{2,1,0:T(8,128)(2,1)S(1)} %get-tuple-element.29), channel_id=1, source_target_pairs={{0,2},{1,3},{2,0},{3,1},{4,6},{5,7},{6,4},{7,5},{8,10},{9,11},{10,... | collective-permute-start | bytes 393224 | tf_op jit(solution)/shard_map/ppermute | solution.py:268
  33.6 1.3 %collective-permute-start.10 = (bf16[2,2,128,128]{3,2,1,0:T(8,128)(2,1)S(1)}, bf16[2,2,128,128]{3,2,1,0:T(8,128)(2,1)S(1)}, u32[]{:S(2)}, u32[]{:S(2)}) collective-permute-start(bf16[2,2,128,128]{3,2,1,0:T(8,128)(2,1)S(1)} %get-tuple-element.30), channel_id=1, source_target_pairs={{4,0},{8,4},{12,8},{16,12},{20,16},{24,20},{28,24},{5,1},{9,5},{13... | collective-permute-start | bytes 393224 | tf_op jit(solution)/shard_map/ppermute | solution.py:264
  34.9 0.0 collective-permute-done.6.refs_1_
  34.9 0.7 %collective-permute-start.11 = (bf16[32,16,128]{2,1,0:T(8,128)(2,1)S(1)}, bf16[32,16,128]{2,1,0:T(8,128)(2,1)S(1)}, u32[]{:S(2)}, u32[]{:S(2)}) collective-permute-start(bf16[32,16,128]{2,1,0:T(8,128)(2,1)S(1)} %get-tuple-element.31), channel_id=1, source_target_pairs={{0,1},{1,0},{2,3},{3,2},{4,5},{5,4},{6,7},{7,6},{8,9},{9,8},{10,11... | collective-permute-start | bytes 393224 | tf_op jit(solution)/shard_map/ppermute | solution.py:268
  35.6 1.2 %collective-permute-done.7.refs_2_ = bf16[32,16,128]{2,1,0:T(8,128)(2,1)S(1)} collective-permute-done((bf16[32,16,128]{2,1,0:T(8,128)(2,1)S(1)}, bf16[32,16,128]{2,1,0:T(8,128)(2,1)S(1)}, u32[]{:S(2)}, u32[]{:S(2)}) %collective-permute-start.7) | collective-permute-done | bytes 131104 | tf_op jit(solution)/shard_map/ppermute | solution.py:268
  36.8 2.2 %collective-permute-done.8.refs_3_ = bf16[2,2,128,128]{3,2,1,0:T(8,128)(2,1)S(1)} collective-permute-done((bf16[2,2,128,128]{3,2,1,0:T(8,128)(2,1)S(1)}, bf16[2,2,128,128]{3,2,1,0:T(8,128)(2,1)S(1)}, u32[]{:S(2)}, u32[]{:S(2)}) %collective-permute-start.8) | collective-permute-done | bytes 131104 | tf_op jit(solution)/shard_map/ppermute | solution.py:264
  39.0 0.1 collective-permute-done.9.refs_4_
  39.1 3.9 %collective-permute-done.10.refs_5_ = bf16[2,2,128,128]{3,2,1,0:T(8,128)(2,1)S(1)} collective-permute-done((bf16[2,2,128,128]{3,2,1,0:T(8,128)(2,1)S(1)}, bf16[2,2,128,128]{3,2,1,0:T(8,128)(2,1)S(1)}, u32[]{:S(2)}, u32[]{:S(2)}) %collective-permute-start.10) | collective-permute-done | bytes 131104 | tf_op jit(solution)/shard_map/ppermute | solution.py:264
  43.1 0.0 collective-permute-done.11.refs_6_
  43.1 1.0 %finish.1 = (bf16[32,64,128]{2,1,0:T(8,128)(2,1)}, bf16[128,2,128]{2,1,0:T(2,128)(2,1)}, bf16[128,2,128]{2,1,0:T(2,128)(2,1)}) custom-call(bf16[32,16,128]{2,1,0:T(8,128)(2,1)S(1)} %get-tuple-element.25.refs_0_, bf16[2,2,128,128]{3,2,1,0:T(8,128)(2,1)S(1)} %collective-permute-done.6.refs_1_, bf16[32,16,128]{2,1,0:T(8,128)(2,1)S(1)} %collective-permute-done.7.refs_2_, ...), custom_call_target="tpu_custom_call" | custom-call | tf_op jit(solution)/shard_map/finish/pallas_call | solution.py:247
Async XLA Ops:
  0.6 18.5 %copy-start = (bf16[128,16,128]{2,1,0:T(8,128)(2,1)S(1)}, bf16[128,16,128]{2,1,0:T(8,128)(2,1)}, u32[]{:S(2)}) copy-start(bf16[128,16,128]{2,1,0:T(8,128)(2,1)} %q_ref.1) | copy-start | bytes 1572868
  2.8 9.9 %collective-permute-start = (bf16[2,2,128,128]{3,2,1,0:T(8,128)(2,1)}, bf16[2,2,128,128]{3,2,1,0:T(8,128)(2,1)S(1)}, u32[]{:S(2)}, u32[]{:S(2)}) collective-permute-start(bf16[2,2,128,128]{3,2,1,0:T(8,128)(2,1)} %get-tuple-element.19), channel_id=1, source_target_pairs={{4,0},{8,4},{12,8},{16,12},{20,16},{24,20},{28,24},{5,1},{9,5},{13... | collective-permute-start | bytes 393224 | tf_op jit(solution)/shard_map/ppermute | solution.py:264
  4.1 11.9 %collective-permute-start.1 = (bf16[32,16,128]{2,1,0:T(8,128)(2,1)}, bf16[32,16,128]{2,1,0:T(8,128)(2,1)S(1)}, u32[]{:S(2)}, u32[]{:S(2)}) collective-permute-start(bf16[32,16,128]{2,1,0:T(8,128)(2,1)} %get-tuple-element.20), channel_id=1, source_target_pairs={{0,3},{1,2},{2,1},{3,0},{4,7},{5,6},{6,5},{7,4},{8,11},{9,10},{10,... | collective-permute-start | bytes 393224 | tf_op jit(solution)/shard_map/ppermute | solution.py:268
  6.6 9.5 %collective-permute-start.2 = (bf16[2,2,128,128]{3,2,1,0:T(8,128)(2,1)}, bf16[2,2,128,128]{3,2,1,0:T(8,128)(2,1)S(1)}, u32[]{:S(2)}, u32[]{:S(2)}) collective-permute-start(bf16[2,2,128,128]{3,2,1,0:T(8,128)(2,1)} %get-tuple-element.21), channel_id=1, source_target_pairs={{0,8},{4,12},{8,16},{12,20},{16,24},{20,28},{1,9},{5,13},{9,17},{1... | collective-permute-start | bytes 393224 | tf_op jit(solution)/shard_map/ppermute | solution.py:264
  11.8 6.4 %collective-permute-start.3 = (bf16[32,16,128]{2,1,0:T(8,128)(2,1)}, bf16[32,16,128]{2,1,0:T(8,128)(2,1)S(1)}, u32[]{:S(2)}, u32[]{:S(2)}) collective-permute-start(bf16[32,16,128]{2,1,0:T(8,128)(2,1)} %get-tuple-element.22), channel_id=1, source_target_pairs={{0,2},{1,3},{2,0},{3,1},{4,6},{5,7},{6,4},{7,5},{8,10},{9,11},{10,... | collective-permute-start | bytes 393224 | tf_op jit(solution)/shard_map/ppermute | solution.py:268
  12.7 5.4 %collective-permute-start.5 = (bf16[32,16,128]{2,1,0:T(8,128)(2,1)}, bf16[32,16,128]{2,1,0:T(8,128)(2,1)S(1)}, u32[]{:S(2)}, u32[]{:S(2)}) collective-permute-start(bf16[32,16,128]{2,1,0:T(8,128)(2,1)} %get-tuple-element.24), channel_id=1, source_target_pairs={{0,1},{1,0},{2,3},{3,2},{4,5},{5,4},{6,7},{7,6},{8,9},{9,8},{10,11... | collective-permute-start | bytes 393224 | tf_op jit(solution)/shard_map/ppermute | solution.py:268
  12.8 6.4 %copy-start.3 = (s32[8]{0:T(128)S(1)}, s32[8]{0:T(128)}, u32[]{:S(2)}) copy-start(s32[8]{0:T(128)} %lengths.1) | copy-start | bytes 100
  12.8 6.4 %copy-start.4 = (s32[8]{0:T(128)S(1)}, s32[8]{0:T(128)}, u32[]{:S(2)}) copy-start(s32[8]{0:T(128)} %prefixes.1) | copy-start | bytes 100
  12.8 6.4 %collective-permute-start.4 = (bf16[2,2,128,128]{3,2,1,0:T(8,128)(2,1)}, bf16[2,2,128,128]{3,2,1,0:T(8,128)(2,1)S(1)}, u32[]{:S(2)}, u32[]{:S(2)}) collective-permute-start(bf16[2,2,128,128]{3,2,1,0:T(8,128)(2,1)} %get-tuple-element.23.rest_7_), channel_id=1, source_target_pairs={{0,4},{4,8},{8,12},{12,16},{16,20},{20,24},{24,28},{1,5},{5,9},{9,... | collective-permute-start | bytes 393224 | tf_op jit(solution)/shard_map/ppermute | solution.py:264
  19.2 0.9 %copy-start.1 = (bf16[2,2,128,128]{3,2,1,0:T(8,128)(2,1)S(1)}, bf16[2,2,128,128]{3,2,1,0:T(8,128)(2,1)}, u32[]{:S(2)}) copy-start(bf16[2,2,128,128]{3,2,1,0:T(8,128)(2,1)} %get-tuple-element.23.rest_7_) | copy-start | bytes 393220
  20.1 0.9 %copy-start.2 = (bf16[32,16,128]{2,1,0:T(8,128)(2,1)S(1)}, bf16[32,16,128]{2,1,0:T(8,128)(2,1)}, u32[]{:S(2)}) copy-start(bf16[32,16,128]{2,1,0:T(8,128)(2,1)} %get-tuple-element.18.rest_0_) | copy-start | bytes 393220
  26.7 8.2 %collective-permute-start.6 = (bf16[2,2,128,128]{3,2,1,0:T(8,128)(2,1)S(1)}, bf16[2,2,128,128]{3,2,1,0:T(8,128)(2,1)S(1)}, u32[]{:S(2)}, u32[]{:S(2)}) collective-permute-start(bf16[2,2,128,128]{3,2,1,0:T(8,128)(2,1)S(1)} %get-tuple-element.26), channel_id=1, source_target_pairs={{0,4},{4,8},{8,12},{12,16},{16,20},{20,24},{24,28},{1,5},{5,9},{9,... | collective-permute-start | bytes 393224 | tf_op jit(solution)/shard_map/ppermute | solution.py:264
  31.0 5.9 %collective-permute-start.7 = (bf16[32,16,128]{2,1,0:T(8,128)(2,1)S(1)}, bf16[32,16,128]{2,1,0:T(8,128)(2,1)S(1)}, u32[]{:S(2)}, u32[]{:S(2)}) collective-permute-start(bf16[32,16,128]{2,1,0:T(8,128)(2,1)S(1)} %get-tuple-element.27), channel_id=1, source_target_pairs={{0,3},{1,2},{2,1},{3,0},{4,7},{5,6},{6,5},{7,4},{8,11},{9,10},{10,... | collective-permute-start | bytes 393224 | tf_op jit(solution)/shard_map/ppermute | solution.py:268
  31.1 8.0 %collective-permute-start.8 = (bf16[2,2,128,128]{3,2,1,0:T(8,128)(2,1)S(1)}, bf16[2,2,128,128]{3,2,1,0:T(8,128)(2,1)S(1)}, u32[]{:S(2)}, u32[]{:S(2)}) collective-permute-start(bf16[2,2,128,128]{3,2,1,0:T(8,128)(2,1)S(1)} %get-tuple-element.28), channel_id=1, source_target_pairs={{8,0},{12,4},{16,8},{20,12},{24,16},{28,20},{9,1},{13,5},{17,9},{2... | collective-permute-start | bytes 393224 | tf_op jit(solution)/shard_map/ppermute | solution.py:264
  32.4 6.8 %collective-permute-start.9 = (bf16[32,16,128]{2,1,0:T(8,128)(2,1)S(1)}, bf16[32,16,128]{2,1,0:T(8,128)(2,1)S(1)}, u32[]{:S(2)}, u32[]{:S(2)}) collective-permute-start(bf16[32,16,128]{2,1,0:T(8,128)(2,1)S(1)} %get-tuple-element.29), channel_id=1, source_target_pairs={{0,2},{1,3},{2,0},{3,1},{4,6},{5,7},{6,4},{7,5},{8,10},{9,11},{10,... | collective-permute-start | bytes 393224 | tf_op jit(solution)/shard_map/ppermute | solution.py:268
  33.6 9.5 %collective-permute-start.10 = (bf16[2,2,128,128]{3,2,1,0:T(8,128)(2,1)S(1)}, bf16[2,2,128,128]{3,2,1,0:T(8,128)(2,1)S(1)}, u32[]{:S(2)}, u32[]{:S(2)}) collective-permute-start(bf16[2,2,128,128]{3,2,1,0:T(8,128)(2,1)S(1)} %get-tuple-element.30), channel_id=1, source_target_pairs={{4,0},{8,4},{12,8},{16,12},{20,16},{24,20},{28,24},{5,1},{9,5},{13... | collective-permute-start | bytes 393224 | tf_op jit(solution)/shard_map/ppermute | solution.py:264
  34.9 8.2 %collective-permute-start.11 = (bf16[32,16,128]{2,1,0:T(8,128)(2,1)S(1)}, bf16[32,16,128]{2,1,0:T(8,128)(2,1)S(1)}, u32[]{:S(2)}, u32[]{:S(2)}) collective-permute-start(bf16[32,16,128]{2,1,0:T(8,128)(2,1)S(1)} %get-tuple-element.31), channel_id=1, source_target_pairs={{0,1},{1,0},{2,3},{3,2},{4,5},{5,4},{6,7},{7,6},{8,9},{9,8},{10,11... | collective-permute-start | bytes 393224 | tf_op jit(solution)/shard_map/ppermute | solution.py:268

commit v3 on v2

--- a/solution.py
+++ b/solution.py
@@ -21,7 +21,7 @@
 
 def sequence(parts, shifts):
     masks, shifts = list(range(parts - 1, 0, -1)), list(shifts)
-    order = [("mask", 0)]
+    order = []
     while masks or shifts:
         if shifts:
             order.append(("shift", shifts.pop(0)))
@@ -32,8 +32,8 @@
 
 def arrange(pieces, blocks, shifts):
     return [
-        pieces[which] if kind == "mask" else blocks[which]
-        for kind, which in sequence(len(pieces), shifts)
+        pieces[which - 1] if kind == "mask" else blocks[which]
+        for kind, which in sequence(len(pieces) + 1, shifts)
     ]
 
 
@@ -41,36 +41,42 @@
     order = sequence(parts, shifts)
     found = dict(zip(order, refs))
     return (
-        [found["mask", mask] for mask in range(parts)],
+        [found["mask", mask] for mask in range(1, parts)],
         {shift: found["shift", shift] for shift in shifts},
         refs[len(order):],
     )
 
 
+def regroup(buf):
+    wide = buf[...].astype(jnp.float32)
+    return [wide[:, group, :].astype(jnp.bfloat16) for group in range(buf.shape[1])]
+
+
 def prep_kernel(parts, cot_ref, key_ref, value_ref, *rest):
-    kv_outs, cot_outs, (key_buf, value_buf, sems) = rest[:3], rest[3 : parts + 3], rest[parts + 3 :]
+    kv_outs, cot_outs, rest = rest[:3], rest[3 : parts + 2], rest[parts + 2 :]
+    key_buf, value_buf, packed, sems, kv_sems = rest
     heads = cot_ref.shape[1] // parts
     me = lax.axis_index("kvh")
     loads = []
     for number, (ref, buf) in enumerate(((key_ref, key_buf), (value_ref, value_buf))):
-        loads.append(pltpu.make_async_copy(ref, buf, sems.at[parts + number]))
+        loads.append(pltpu.make_async_copy(ref, buf, sems.at[number]))
         loads[-1].start()
     copies = []
-    for mask in range(parts):
+    for mask in range(1, parts):
         first = pl.multiple_of((me ^ mask) * heads, heads)
         copies.append(
             pltpu.make_async_copy(
-                cot_ref.at[:, pl.ds(first, heads), :], cot_outs[mask], sems.at[mask]
+                cot_ref.at[:, pl.ds(first, heads), :], cot_outs[mask - 1], sems.at[mask + 1]
             )
         )
         copies[-1].start()
     for number, buf in enumerate((key_buf, value_buf)):
         loads[number].wait()
-        wide = buf[...].astype(jnp.float32)
-        for group in range(buf.shape[1]):
-            packed = wide[:, group, :].astype(jnp.bfloat16)
-            for kv_out in kv_outs:
-                kv_out[number, group] = packed
+        for group, block in enumerate(regroup(buf)):
+            packed[number, group] = block
+    for number, kv_out in enumerate(kv_outs):
+        copies.append(pltpu.make_async_copy(packed, kv_out, kv_sems.at[number]))
+        copies[-1].start()
     for copy in copies:
         copy.wait()
 
@@ -79,16 +85,18 @@
     rows, heads, size = cotangent.shape
     kv_rows, kv_heads, _ = keys.shape
     piece = jax.ShapeDtypeStruct((rows, heads // parts, size), jnp.bfloat16)
+    block = jax.ShapeDtypeStruct((2, kv_heads, kv_rows, size), jnp.bfloat16)
     outs = pl.pallas_call(
         functools.partial(prep_kernel, parts),
-        out_shape=(jax.ShapeDtypeStruct((2, kv_heads, kv_rows, size), jnp.bfloat16),) * 3
-        + (piece,) * parts,
+        out_shape=(block,) * 3 + (piece,) * (parts - 1),
         in_specs=[_HBM] * 3,
-        out_specs=(_VMEM,) * (parts + 3),
+        out_specs=(_HBM,) * (parts + 2),
         scratch_shapes=[
             pltpu.VMEM(keys.shape, jnp.bfloat16),
             pltpu.VMEM(values.shape, jnp.bfloat16),
-            pltpu.SemaphoreType.DMA((parts + 2,)),
+            pltpu.VMEM(block.shape, jnp.bfloat16),
+            pltpu.SemaphoreType.DMA((parts + 1,)),
+            pltpu.SemaphoreType.DMA((3,)),
         ],
         compiler_params=pltpu.CompilerParams(vmem_limit_bytes=PREPARE_VMEM_BYTES),
         name="prepare",
@@ -116,15 +124,14 @@
     return carry[1], carry[2]
 
 
-def grad_kernel(parts, lengths, prefixes, q_ref, *rest):
+def grad_kernel(parts, lengths, prefixes, q_ref, cot_ref, key_ref, value_ref, *rest):
     cot_refs, got, rest = arranged(parts, (-1, 2, 1), rest)
-    kv_own, rest = rest[0], rest[1:]
     kv_back1, kv_back2, kv_ahead = got[1], got[2], got[-1]
     dq_refs, rest = rest[:parts], rest[parts:]
-    own_out, back1_out, back2_out, ahead_out, window, acc, cot_own, sems = rest
+    own_out, back1_out, back2_out, ahead_out, window, acc = rest
     rows, heads, size = q_ref.shape
     tokens = rows // parts
-    kv_heads = kv_own.shape[1]
+    kv_heads = key_ref.shape[1]
     group_size = heads // kv_heads
     span = (BACK + 1 + AHEAD) * rows
     reach = span - rows + tokens
@@ -133,15 +140,9 @@
     shard = lax.axis_index("seq")
     me = lax.axis_index("kvh")
 
-    loads = [
-        pltpu.make_async_copy(
-            kv_own, window.at[:, :, pl.ds(BACK * rows, rows)], sems.at[0]
-        ),
-        pltpu.make_async_copy(cot_refs[0], cot_own, sems.at[1]),
-    ]
-    cot_refs[0] = cot_own
-    for load in loads:
-        load.start()
+    for number, buf in enumerate((key_ref, value_ref)):
+        for group, block in enumerate(regroup(buf)):
+            window[number, group, pl.ds(BACK * rows, rows)] = block
     for slot, ref in ((0, kv_back2), (1, kv_back1), (BACK + 1, kv_ahead)):
         for number in range(2):
             for group in range(kv_heads):
@@ -150,8 +151,6 @@
 
     contract_last = (((1,), (1,)), ((), ()))
     contract_first = (((0,), (0,)), ((), ()))
-    for load in loads:
-        load.wait()
     lane_token = lax.broadcasted_iota(jnp.int32, (1, lanes), 1) // group_size
     key_iota = lax.broadcasted_iota(jnp.int32, (reach, lanes), 0)
     for mask in range(parts):
@@ -166,7 +165,11 @@
             of_group = pl.ds(group * group_size, group_size)
             q = q_ref[pl.ds(first, tokens), of_group].astype(jnp.float32)
             q = q.reshape(lanes, size).astype(jnp.bfloat16)
-            cot = cot_refs[mask][:, of_group].astype(jnp.float32)
+            if mask == 0:
+                own_head = pl.multiple_of(me * heads + group * group_size, group_size)
+                cot = cot_ref[:, pl.ds(own_head, group_size)].astype(jnp.float32)
+            else:
+                cot = cot_refs[mask - 1][:, of_group].astype(jnp.float32)
             cot = cot.reshape(lanes, size).astype(jnp.bfloat16)
             k = window[0, group, here]
             v = window[1, group, here]
@@ -193,10 +196,10 @@
             ref[1, group] = acc[1, group, part].astype(ref.dtype)
 
 
-def gradients(lengths, prefixes, queries, cots, got, kv):
+def gradients(lengths, prefixes, queries, cotangent, keys, values, cots, got):
     rows, heads, size = queries.shape
-    parts = len(cots)
-    kv_shape = kv.shape
+    parts = len(cots) + 1
+    kv_shape = got[1].shape
     kv_heads = kv_shape[1]
     span = (BACK + 1 + AHEAD) * rows
     half = jax.ShapeDtypeStruct(kv_shape, jnp.bfloat16)
@@ -205,25 +208,25 @@
         functools.partial(grad_kernel, parts),
         out_shape=(jax.ShapeDtypeStruct(cots[0].shape, jnp.bfloat16),) * parts
         + (jax.ShapeDtypeStruct(kv_shape, jnp.float32), half, half, half),
-        in_specs=[_SMEM, _SMEM, _VMEM, _HBM] + [_VMEM] * (parts + 2) + [_HBM],
+        in_specs=[_SMEM, _SMEM] + [_VMEM] * (parts + 6),
         out_specs=(_VMEM,) * (parts + 4),
         scratch_shapes=[
             pltpu.VMEM((2, kv_heads, span, size), jnp.bfloat16),
             pltpu.VMEM((2, kv_heads, span, size), jnp.float32),
-            pltpu.VMEM(cots[0].shape, jnp.bfloat16),
-            pltpu.SemaphoreType.DMA((2,)),
         ],
         compiler_params=pltpu.CompilerParams(vmem_limit_bytes=VMEM_BYTES),
         cost_estimate=pl.CostEstimate(
             flops=10 * work * size, bytes_accessed=4 * queries.size * 2, transcendentals=work
         ),
         name="gradients",
-    )(lengths, prefixes, queries, *arrange(cots, got, (-1, 2, 1)), kv)
+    )(lengths, prefixes, queries, cotangent, keys, values, *arrange(cots, got, (-1, 2, 1)))
     return outs[:parts], outs[parts:]
 
 
 def finish_kernel(parts, *refs):
-    dq_refs, got, (own, dq_out, dk_out, dv_out) = arranged(parts, (1, -2, -1), refs)
+    dq_refs, got, rest = arranged(parts, (1, -2, -1), refs)
+    dq_own, own, dq_out, dk_out, dv_out = rest
+    dq_refs = [dq_own] + dq_refs
     heads = dq_refs[0].shape[1]
     me = lax.axis_index("kvh")
     for mask in range(parts):
@@ -239,8 +242,8 @@
         ref[...] = jnp.stack(sums, axis=1).astype(jnp.bfloat16)
 
 
-def finish(dqs, own, got):
-    parts = len(dqs)
+def finish(dq_own, dqs, own, got):
+    parts = len(dqs) + 1
     rows, heads, size = dqs[0].shape
     _, kv_heads, kv_rows, _ = own.shape
     kv_out = jax.ShapeDtypeStruct((kv_rows, kv_heads, size), jnp.bfloat16)
@@ -255,13 +258,12 @@
         out_specs=(_VMEM,) * 3,
         compiler_params=pltpu.CompilerParams(vmem_limit_bytes=VMEM_BYTES),
         name="finish",
-    )(*arrange(dqs, got, (1, -2, -1)), own)
+    )(*arrange(dqs, got, (1, -2, -1)), dq_own, own)
 
 
 def shifted(block, distance):
-    devices = range(lax.axis_size("seq"))
-    route = [(i - distance, i) for i in devices if i - distance in devices]
-    return lax.ppermute(block, "seq", route)
+    count = lax.axis_size("seq")
+    return lax.ppermute(block, "seq", [(i, (i + distance) % count) for i in range(count)])
 
 
 def swapped(block, mask):
@@ -269,7 +271,7 @@
 
 
 def exchange(pieces, blocks):
-    pieces = [pieces[0]] + [swapped(pieces[mask], mask) for mask in range(1, len(pieces))]
+    pieces = [swapped(piece, mask) for mask, piece in enumerate(pieces, 1)]
     return pieces, {shift: shifted(block, shift) for shift, block in blocks.items()}
 
 
@@ -278,10 +280,10 @@
     kv, cots = prepare(output_gradient, keys, values, parts)
     cots, got = exchange(cots, {1: kv[0], 2: kv[1], -1: kv[2]})
     dqs, (own, back1, back2, ahead) = gradients(
-        doc_lengths, prefix_lengths, queries, cots, got, kv[0]
+        doc_lengths, prefix_lengths, queries, output_gradient, keys, values, cots, got
     )
-    dqs, got = exchange(dqs, {-1: back1, -2: back2, 1: ahead})
-    return finish(dqs, own, got)
+    dqs_got, got = exchange(dqs[1:], {-1: back1, -2: back2, 1: ahead})
+    return finish(dqs[0], dqs_got, own, got)
 
 
 def solution(mesh):

time: 44.9 us -> 48.7 us (1.085); the launches traced: 44.1 us -> 48.5 us
  Pallas kernels: 8.9 us -> 19.7 us
  starting transfers between devices: 22.1 us -> 13.9 us
  waiting for transfers between devices: 10.5 us -> 13.1 us
  local copies, waits for them, and re-layouts: 1.82 us -> 1.06 us
    pallas_call x1, Pallas kernels: 2.2 us -> 13.1 us  [prepare(): pl.pallas_call(functools.partial(prep_kernel, parts), out_shape=(block,)...]
    ppermute x6, starting transfers between devices: 16.6 us -> 10.5 us  [shifted(): lax.ppermute(block, 'seq', [(i, (i + distance) % count) for i in range(co...]
    ppermute x6, waiting for transfers between devices: 7.14 us -> 10.5 us  [shifted(): lax.ppermute(block, 'seq', [(i, (i + distance) % count) for i in range(co...]
    ppermute x6, starting transfers between devices: 5.48 us -> 3.38 us  [swapped(): lax.ppermute(block, 'kvh', [(i, i ^ mask) for i in range(lax.axis_size('k...]
    ppermute x6, waiting for transfers between devices: 3.4 us -> 2.62 us  [swapped(): lax.ppermute(block, 'kvh', [(i, i ^ mask) for i in range(lax.axis_size('k...]
    unnamed x10 -> x12, local copies, waits for them, and re-layouts: 1.82 us -> 1.06 us
  transfers between devices with their start and end apart: 12 -> 12, of which waited for: 6 -> 7; matrix products, arithmetic and copies ran while one was open for 0% -> 0% of each run, Pallas kernels for 0% -> 0%
where the time goes in v3:
time: 48.7 us; the launch traced here: 48.5 us
  Pallas kernels  19.7 us (40%)
  starting transfers between devices  13.9 us (29%)
  waiting for transfers between devices  13.1 us (27%)
  local copies, waits for them, and re-layouts  1.06 us (2%)
  between operations  0.73 us (1%)
    pallas_call x1, Pallas kernels, prepare(): pl.pallas_call(functools.partial(prep_kernel, parts), out_shape=(block,)...  13.1 us
    ppermute x6, starting transfers between devices, shifted(): lax.ppermute(block, 'seq', [(i, (i + distance) % count) for i in range(co...  10.5 us
    ppermute x6, waiting for transfers between devices, shifted(): lax.ppermute(block, 'seq', [(i, (i + distance) % count) for i in range(co...  10.5 us
    pallas_call x1, Pallas kernels, gradients(): pl.pallas_call(functools.partial(grad_kernel, parts), out_shape=(jax.Shap...  5.59 us
    ppermute x6, starting transfers between devices, swapped(): lax.ppermute(block, 'kvh', [(i, i ^ mask) for i in range(lax.axis_size('k...  3.38 us
    ppermute x6, waiting for transfers between devices, swapped(): lax.ppermute(block, 'kvh', [(i, i ^ mask) for i in range(lax.axis_size('k...  2.62 us
    unnamed x12, local copies, waits for them, and re-layouts  1.06 us
    pallas_call x1, Pallas kernels, finish(): pl.pallas_call(functools.partial(finish_kernel, parts), out_shape=(jax.Sh...  1.02 us
  transfers between devices with their start and end apart: 12, of which 7 were waited for; matrix products, arithmetic and copies ran while one was open for 0% of the time, Pallas kernels for 0%

profile of v3, /device:TPU:0, one launch (start us, length us, event | category | flops | bytes accessed | tf_op | source)
XLA Modules:
  0.0 48.5 jit_solution(11616818392688050582)
XLA Ops:
  0.6 0.0 copy-start
  0.6 0.0 copy-start.2
  0.7 0.0 copy-start.1
  0.7 13.1 %prepare.1 = (bf16[2,2,128,128]{3,2,1,0:T(8,128)(2,1)}, bf16[2,2,128,128]{3,2,1,0:T(8,128)(2,1)}, bf16[2,2,128,128]{3,2,1,0:T(8,128)(2,1)}, bf16[32,16,128]{2,1,...) custom-call(bf16[32,64,128]{2,1,0:T(8,128)(2,1)} %cot_ref.3, bf16[128,2,128]{2,1,0:T(2,128)(2,1)} %key_ref.3, ...), custom_call_target="tpu_custom_call" | custom-call | tf_op jit(solution)/shard_map/prepare/pallas_call | solution.py:89
  13.8 6.0 %collective-permute-start = (bf16[2,2,128,128]{3,2,1,0:T(8,128)(2,1)}, bf16[2,2,128,128]{3,2,1,0:T(8,128)(2,1)S(1)}, u32[]{:S(2)}, u32[]{:S(2)}) collective-permute-start(bf16[2,2,128,128]{3,2,1,0:T(8,128)(2,1)} %get-tuple-element.17), channel_id=1, source_target_pairs={{0,28},{4,0},{8,4},{12,8},{16,12},{20,16},{24,20},{28,24},{1,29},{... | collective-permute-start | bytes 393224 | tf_op jit(solution)/shard_map/ppermute | solution.py:266
  19.8 0.7 %collective-permute-start.1 = (bf16[32,16,128]{2,1,0:T(8,128)(2,1)}, bf16[32,16,128]{2,1,0:T(8,128)(2,1)S(1)}, u32[]{:S(2)}, u32[]{:S(2)}) collective-permute-start(bf16[32,16,128]{2,1,0:T(8,128)(2,1)} %get-tuple-element.18), channel_id=1, source_target_pairs={{0,3},{1,2},{2,1},{3,0},{4,7},{5,6},{6,5},{7,4},{8,11},{9,10},{10,... | collective-permute-start | bytes 393224 | tf_op jit(solution)/shard_map/ppermute | solution.py:270
  20.5 0.0 collective-permute-start.2
  20.5 0.9 %collective-permute-start.3 = (bf16[32,16,128]{2,1,0:T(8,128)(2,1)}, bf16[32,16,128]{2,1,0:T(8,128)(2,1)S(1)}, u32[]{:S(2)}, u32[]{:S(2)}) collective-permute-start(bf16[32,16,128]{2,1,0:T(8,128)(2,1)} %get-tuple-element.20), channel_id=1, source_target_pairs={{0,2},{1,3},{2,0},{3,1},{4,6},{5,7},{6,4},{7,5},{8,10},{9,11},{10,... | collective-permute-start | bytes 393224 | tf_op jit(solution)/shard_map/ppermute | solution.py:270
  21.4 0.0 copy-start.4
  21.4 0.0 copy-start.5
  21.4 0.0 collective-permute-start.4
  21.4 2.3 %collective-permute-done.rest_0_ = bf16[2,2,128,128]{3,2,1,0:T(8,128)(2,1)S(1)} collective-permute-done((bf16[2,2,128,128]{3,2,1,0:T(8,128)(2,1)}, bf16[2,2,128,128]{3,2,1,0:T(8,128)(2,1)S(1)}, u32[]{:S(2)}, u32[]{:S(2)}) %collective-permute-start) | collective-permute-done | bytes 131104 | tf_op jit(solution)/shard_map/ppermute | solution.py:266
  23.7 0.0 collective-permute-start.5
  23.7 2.1 %collective-permute-done.1.rest_1_ = bf16[32,16,128]{2,1,0:T(8,128)(2,1)S(1)} collective-permute-done((bf16[32,16,128]{2,1,0:T(8,128)(2,1)}, bf16[32,16,128]{2,1,0:T(8,128)(2,1)S(1)}, u32[]{:S(2)}, u32[]{:S(2)}) %collective-permute-start.1) | collective-permute-done | bytes 131104 | tf_op jit(solution)/shard_map/ppermute | solution.py:270
  25.7 3.1 %collective-permute-done.2.rest_2_ = bf16[2,2,128,128]{3,2,1,0:T(8,128)(2,1)S(1)} collective-permute-done((bf16[2,2,128,128]{3,2,1,0:T(8,128)(2,1)}, bf16[2,2,128,128]{3,2,1,0:T(8,128)(2,1)S(1)}, u32[]{:S(2)}, u32[]{:S(2)}) %collective-permute-start.2) | collective-permute-done | bytes 131104 | tf_op jit(solution)/shard_map/ppermute | solution.py:266
  28.8 0.0 collective-permute-done.3.rest_3_
  28.8 1.1 %collective-permute-done.4.rest_4_ = bf16[2,2,128,128]{3,2,1,0:T(8,128)(2,1)S(1)} collective-permute-done((bf16[2,2,128,128]{3,2,1,0:T(8,128)(2,1)}, bf16[2,2,128,128]{3,2,1,0:T(8,128)(2,1)S(1)}, u32[]{:S(2)}, u32[]{:S(2)}) %collective-permute-start.4) | collective-permute-done | bytes 131104 | tf_op jit(solution)/shard_map/ppermute | solution.py:266
  30.0 0.0 collective-permute-done.5.rest_5_
  30.0 0.0 copy-done
  30.0 0.0 copy-done.2
  30.0 0.0 copy-done.1
  30.0 0.0 copy-done.4
  30.0 0.0 copy-done.5
  30.0 0.0 copy-start.3
  30.0 1.0 %copy-done.3 = bf16[128,16,128]{2,1,0:T(8,128)(2,1)S(1)} copy-done((bf16[128,16,128]{2,1,0:T(8,128)(2,1)S(1)}, bf16[128,16,128]{2,1,0:T(8,128)(2,1)}, u32[]{:S(2)}) %copy-start.3) | copy-done | bytes 524312
  31.1 5.6 %gradients.1 = (bf16[32,16,128]{2,1,0:T(8,128)(2,1)S(1)}, bf16[32,16,128]{2,1,0:T(8,128)(2,1)S(1)}, bf16[32,16,128]{2,1,0:T(8,128)(2,1)S(1)}, bf16[32,16,128]{2,...) custom-call(s32[8]{0:T(128)S(1)} %copy-done.4, ...), custom_call_target="tpu_custom_call" | custom-call | flops 1342177280 | bytes 2097152 | tf_op jit(solution)/shard_map/gradients/pallas_call | solution.py:207
  36.7 0.1 collective-permute-start.6
  36.7 1.0 %collective-permute-start.7 = (bf16[32,16,128]{2,1,0:T(8,128)(2,1)S(1)}, bf16[32,16,128]{2,1,0:T(8,128)(2,1)S(1)}, u32[]{:S(2)}, u32[]{:S(2)}) collective-permute-start(bf16[32,16,128]{2,1,0:T(8,128)(2,1)S(1)} %get-tuple-element.24), channel_id=1, source_target_pairs={{0,3},{1,2},{2,1},{3,0},{4,7},{5,6},{6,5},{7,4},{8,11},{9,10},{10,... | collective-permute-start | bytes 393224 | tf_op jit(solution)/shard_map/ppermute | solution.py:270
  37.8 1.6 %collective-permute-start.8 = (bf16[2,2,128,128]{3,2,1,0:T(8,128)(2,1)S(1)}, bf16[2,2,128,128]{3,2,1,0:T(8,128)(2,1)S(1)}, u32[]{:S(2)}, u32[]{:S(2)}) collective-permute-start(bf16[2,2,128,128]{3,2,1,0:T(8,128)(2,1)S(1)} %get-tuple-element.25), channel_id=1, source_target_pairs={{0,24},{4,28},{8,0},{12,4},{16,8},{20,12},{24,16},{28,20},{1,25},{... | collective-permute-start | bytes 393224 | tf_op jit(solution)/shard_map/ppermute | solution.py:266
  39.4 0.8 %collective-permute-start.9 = (bf16[32,16,128]{2,1,0:T(8,128)(2,1)S(1)}, bf16[32,16,128]{2,1,0:T(8,128)(2,1)S(1)}, u32[]{:S(2)}, u32[]{:S(2)}) collective-permute-start(bf16[32,16,128]{2,1,0:T(8,128)(2,1)S(1)} %get-tuple-element.26), channel_id=1, source_target_pairs={{0,2},{1,3},{2,0},{3,1},{4,6},{5,7},{6,4},{7,5},{8,10},{9,11},{10,... | collective-permute-start | bytes 393224 | tf_op jit(solution)/shard_map/ppermute | solution.py:270
  40.2 2.8 %collective-permute-start.10 = (bf16[2,2,128,128]{3,2,1,0:T(8,128)(2,1)S(1)}, bf16[2,2,128,128]{3,2,1,0:T(8,128)(2,1)S(1)}, u32[]{:S(2)}, u32[]{:S(2)}) collective-permute-start(bf16[2,2,128,128]{3,2,1,0:T(8,128)(2,1)S(1)} %get-tuple-element.27), channel_id=1, source_target_pairs={{0,28},{4,0},{8,4},{12,8},{16,12},{20,16},{24,20},{28,24},{1,29},{... | collective-permute-start | bytes 393224 | tf_op jit(solution)/shard_map/ppermute | solution.py:266
  43.0 1.9 %collective-permute-done.6.refs_0_ = bf16[2,2,128,128]{3,2,1,0:T(8,128)(2,1)S(1)} collective-permute-done((bf16[2,2,128,128]{3,2,1,0:T(8,128)(2,1)S(1)}, bf16[2,2,128,128]{3,2,1,0:T(8,128)(2,1)S(1)}, u32[]{:S(2)}, u32[]{:S(2)}) %collective-permute-start.6) | collective-permute-done | bytes 131104 | tf_op jit(solution)/shard_map/ppermute | solution.py:266
  44.9 0.0 collective-permute-start.11
  44.9 0.0 collective-permute-done.7.refs_1_
  44.9 0.0 collective-permute-done.8.refs_2_
  44.9 0.5 %collective-permute-done.9.refs_3_ = bf16[32,16,128]{2,1,0:T(8,128)(2,1)S(1)} collective-permute-done((bf16[32,16,128]{2,1,0:T(8,128)(2,1)S(1)}, bf16[32,16,128]{2,1,0:T(8,128)(2,1)S(1)}, u32[]{:S(2)}, u32[]{:S(2)}) %collective-permute-start.9) | collective-permute-done | bytes 131104 | tf_op jit(solution)/shard_map/ppermute | solution.py:270
  45.4 2.1 %collective-permute-done.10.refs_4_ = bf16[2,2,128,128]{3,2,1,0:T(8,128)(2,1)S(1)} collective-permute-done((bf16[2,2,128,128]{3,2,1,0:T(8,128)(2,1)S(1)}, bf16[2,2,128,128]{3,2,1,0:T(8,128)(2,1)S(1)}, u32[]{:S(2)}, u32[]{:S(2)}) %collective-permute-start.10) | collective-permute-done | bytes 131104 | tf_op jit(solution)/shard_map/ppermute | solution.py:266
  47.5 0.0 collective-permute-done.11.refs_5_
  47.5 1.0 %finish.1 = (bf16[32,64,128]{2,1,0:T(8,128)(2,1)}, bf16[128,2,128]{2,1,0:T(2,128)(2,1)}, bf16[128,2,128]{2,1,0:T(2,128)(2,1)}) custom-call(bf16[2,2,128,128]{3,2,1,0:T(8,128)(2,1)S(1)} %collective-permute-done.6.refs_0_, bf16[32,16,128]{2,1,0:T(8,128)(2,1)S(1)} %collective-permute-done.7.refs_1_, ...), custom_call_target="tpu_custom_call" | custom-call | tf_op jit(solution)/shard_map/finish/pallas_call | solution.py:250
Async XLA Ops:
  0.6 29.4 %copy-start = (bf16[32,64,128]{2,1,0:T(8,128)(2,1)S(1)}, bf16[32,64,128]{2,1,0:T(8,128)(2,1)}, u32[]{:S(2)}) copy-start(bf16[32,64,128]{2,1,0:T(8,128)(2,1)} %cot_ref.3) | copy-start | bytes 1572868
  0.6 29.3 %copy-start.2 = (bf16[128,2,128]{2,1,0:T(2,128)(2,1)S(1)}, bf16[128,2,128]{2,1,0:T(2,128)(2,1)}, u32[]{:S(2)}) copy-start(bf16[128,2,128]{2,1,0:T(2,128)(2,1)} %value_ref.3) | copy-start | bytes 196612
  0.7 29.3 %copy-start.1 = (bf16[128,2,128]{2,1,0:T(2,128)(2,1)S(1)}, bf16[128,2,128]{2,1,0:T(2,128)(2,1)}, u32[]{:S(2)}) copy-start(bf16[128,2,128]{2,1,0:T(2,128)(2,1)} %key_ref.3) | copy-start | bytes 196612
  13.8 9.9 %collective-permute-start = (bf16[2,2,128,128]{3,2,1,0:T(8,128)(2,1)}, bf16[2,2,128,128]{3,2,1,0:T(8,128)(2,1)S(1)}, u32[]{:S(2)}, u32[]{:S(2)}) collective-permute-start(bf16[2,2,128,128]{3,2,1,0:T(8,128)(2,1)} %get-tuple-element.17), channel_id=1, source_target_pairs={{0,28},{4,0},{8,4},{12,8},{16,12},{20,16},{24,20},{28,24},{1,29},{... | collective-permute-start | bytes 393224 | tf_op jit(solution)/shard_map/ppermute | solution.py:266
  19.8 5.9 %collective-permute-start.1 = (bf16[32,16,128]{2,1,0:T(8,128)(2,1)}, bf16[32,16,128]{2,1,0:T(8,128)(2,1)S(1)}, u32[]{:S(2)}, u32[]{:S(2)}) collective-permute-start(bf16[32,16,128]{2,1,0:T(8,128)(2,1)} %get-tuple-element.18), channel_id=1, source_target_pairs={{0,3},{1,2},{2,1},{3,0},{4,7},{5,6},{6,5},{7,4},{8,11},{9,10},{10,... | collective-permute-start | bytes 393224 | tf_op jit(solution)/shard_map/ppermute | solution.py:270
  20.5 8.4 %collective-permute-start.2 = (bf16[2,2,128,128]{3,2,1,0:T(8,128)(2,1)}, bf16[2,2,128,128]{3,2,1,0:T(8,128)(2,1)S(1)}, u32[]{:S(2)}, u32[]{:S(2)}) collective-permute-start(bf16[2,2,128,128]{3,2,1,0:T(8,128)(2,1)} %get-tuple-element.19), channel_id=1, source_target_pairs={{0,8},{4,12},{8,16},{12,20},{16,24},{20,28},{24,0},{28,4},{1,9},{5... | collective-permute-start | bytes 393224 | tf_op jit(solution)/shard_map/ppermute | solution.py:266
  20.5 8.4 %collective-permute-start.3 = (bf16[32,16,128]{2,1,0:T(8,128)(2,1)}, bf16[32,16,128]{2,1,0:T(8,128)(2,1)S(1)}, u32[]{:S(2)}, u32[]{:S(2)}) collective-permute-start(bf16[32,16,128]{2,1,0:T(8,128)(2,1)} %get-tuple-element.20), channel_id=1, source_target_pairs={{0,2},{1,3},{2,0},{3,1},{4,6},{5,7},{6,4},{7,5},{8,10},{9,11},{10,... | collective-permute-start | bytes 393224 | tf_op jit(solution)/shard_map/ppermute | solution.py:270
  21.4 8.6 %copy-start.4 = (s32[8]{0:T(128)S(1)}, s32[8]{0:T(128)}, u32[]{:S(2)}) copy-start(s32[8]{0:T(128)} %lengths.1) | copy-start | bytes 100
  21.4 8.7 %copy-start.5 = (s32[8]{0:T(128)S(1)}, s32[8]{0:T(128)}, u32[]{:S(2)}) copy-start(s32[8]{0:T(128)} %prefixes.1) | copy-start | bytes 100
  21.4 8.6 %collective-permute-start.4 = (bf16[2,2,128,128]{3,2,1,0:T(8,128)(2,1)}, bf16[2,2,128,128]{3,2,1,0:T(8,128)(2,1)S(1)}, u32[]{:S(2)}, u32[]{:S(2)}) collective-permute-start(bf16[2,2,128,128]{3,2,1,0:T(8,128)(2,1)} %get-tuple-element.21), channel_id=1, source_target_pairs={{0,4},{4,8},{8,12},{12,16},{16,20},{20,24},{24,28},{28,0},{1,5},{5... | collective-permute-start | bytes 393224 | tf_op jit(solution)/shard_map/ppermute | solution.py:266
  23.7 6.3 %collective-permute-start.5 = (bf16[32,16,128]{2,1,0:T(8,128)(2,1)}, bf16[32,16,128]{2,1,0:T(8,128)(2,1)S(1)}, u32[]{:S(2)}, u32[]{:S(2)}) collective-permute-start(bf16[32,16,128]{2,1,0:T(8,128)(2,1)} %get-tuple-element.22), channel_id=1, source_target_pairs={{0,1},{1,0},{2,3},{3,2},{4,5},{5,4},{6,7},{7,6},{8,9},{9,8},{10,11... | collective-permute-start | bytes 393224 | tf_op jit(solution)/shard_map/ppermute | solution.py:270
  30.0 1.0 %copy-start.3 = (bf16[128,16,128]{2,1,0:T(8,128)(2,1)S(1)}, bf16[128,16,128]{2,1,0:T(8,128)(2,1)}, u32[]{:S(2)}) copy-start(bf16[128,16,128]{2,1,0:T(8,128)(2,1)} %q_ref.1) | copy-start | bytes 1572868
  36.7 8.2 %collective-permute-start.6 = (bf16[2,2,128,128]{3,2,1,0:T(8,128)(2,1)S(1)}, bf16[2,2,128,128]{3,2,1,0:T(8,128)(2,1)S(1)}, u32[]{:S(2)}, u32[]{:S(2)}) collective-permute-start(bf16[2,2,128,128]{3,2,1,0:T(8,128)(2,1)S(1)} %get-tuple-element.23), channel_id=1, source_target_pairs={{0,4},{4,8},{8,12},{12,16},{16,20},{20,24},{24,28},{28,0},{1,5},{5... | collective-permute-start | bytes 393224 | tf_op jit(solution)/shard_map/ppermute | solution.py:266
  36.7 8.1 %collective-permute-start.7 = (bf16[32,16,128]{2,1,0:T(8,128)(2,1)S(1)}, bf16[32,16,128]{2,1,0:T(8,128)(2,1)S(1)}, u32[]{:S(2)}, u32[]{:S(2)}) collective-permute-start(bf16[32,16,128]{2,1,0:T(8,128)(2,1)S(1)} %get-tuple-element.24), channel_id=1, source_target_pairs={{0,3},{1,2},{2,1},{3,0},{4,7},{5,6},{6,5},{7,4},{8,11},{9,10},{10,... | collective-permute-start | bytes 393224 | tf_op jit(solution)/shard_map/ppermute | solution.py:270
  37.8 7.1 %collective-permute-start.8 = (bf16[2,2,128,128]{3,2,1,0:T(8,128)(2,1)S(1)}, bf16[2,2,128,128]{3,2,1,0:T(8,128)(2,1)S(1)}, u32[]{:S(2)}, u32[]{:S(2)}) collective-permute-start(bf16[2,2,128,128]{3,2,1,0:T(8,128)(2,1)S(1)} %get-tuple-element.25), channel_id=1, source_target_pairs={{0,24},{4,28},{8,0},{12,4},{16,8},{20,12},{24,16},{28,20},{1,25},{... | collective-permute-start | bytes 393224 | tf_op jit(solution)/shard_map/ppermute | solution.py:266
  39.4 6.0 %collective-permute-start.9 = (bf16[32,16,128]{2,1,0:T(8,128)(2,1)S(1)}, bf16[32,16,128]{2,1,0:T(8,128)(2,1)S(1)}, u32[]{:S(2)}, u32[]{:S(2)}) collective-permute-start(bf16[32,16,128]{2,1,0:T(8,128)(2,1)S(1)} %get-tuple-element.26), channel_id=1, source_target_pairs={{0,2},{1,3},{2,0},{3,1},{4,6},{5,7},{6,4},{7,5},{8,10},{9,11},{10,... | collective-permute-start | bytes 393224 | tf_op jit(solution)/shard_map/ppermute | solution.py:270
  40.2 7.3 %collective-permute-start.10 = (bf16[2,2,128,128]{3,2,1,0:T(8,128)(2,1)S(1)}, bf16[2,2,128,128]{3,2,1,0:T(8,128)(2,1)S(1)}, u32[]{:S(2)}, u32[]{:S(2)}) collective-permute-start(bf16[2,2,128,128]{3,2,1,0:T(8,128)(2,1)S(1)} %get-tuple-element.27), channel_id=1, source_target_pairs={{0,28},{4,0},{8,4},{12,8},{16,12},{20,16},{24,20},{28,24},{1,29},{... | collective-permute-start | bytes 393224 | tf_op jit(solution)/shard_map/ppermute | solution.py:266
  44.9 2.6 %collective-permute-start.11 = (bf16[32,16,128]{2,1,0:T(8,128)(2,1)S(1)}, bf16[32,16,128]{2,1,0:T(8,128)(2,1)S(1)}, u32[]{:S(2)}, u32[]{:S(2)}) collective-permute-start(bf16[32,16,128]{2,1,0:T(8,128)(2,1)S(1)} %get-tuple-element.28), channel_id=1, source_target_pairs={{0,1},{1,0},{2,3},{3,2},{4,5},{5,4},{6,7},{7,6},{8,9},{9,8},{10,11... | collective-permute-start | bytes 393224 | tf_op jit(solution)/shard_map/ppermute | solution.py:270

commit v4 on v2

v4 whole, which is shorter than its diff:
```python
import functools

import jax
import jax.numpy as jnp
from jax import lax
from jax.experimental import pallas as pl
from jax.experimental.pallas import tpu as pltpu
from jax.sharding import PartitionSpec as P

BACK = 2
AHEAD = 1
LOG2E = 1.4426950408889634
VMEM_BYTES = 40 * 1024 * 1024
NEG = -1e30

_VMEM = pl.BlockSpec(memory_space=pltpu.VMEM)
_SMEM = pl.BlockSpec(memory_space=pltpu.SMEM)
_HBM = pl.BlockSpec(memory_space=pltpu.HBM)


def order(parts):
    masks = ["mask", *range(parts - 1, 0, -1)][1:]
    return ["far", masks[0], "even", "odd"] + masks[1:]


def regroup(buf):
    wide = buf[...].astype(jnp.float32)
    return [wide[:, group, :].astype(jnp.bfloat16) for group in range(buf.shape[1])]


def prep_kernel(parts, cot_ref, key_ref, value_ref, *rest):
    kv_outs, cot_outs, (key_buf, value_buf, sems) = rest[:3], rest[3 : parts + 3], rest[parts + 3 :]
    heads = cot_ref.shape[1] // parts
    me = lax.axis_index("kvh")
    loads = []
    for number, (ref, buf) in enumerate(((key_ref, key_buf), (value_ref, value_buf))):
        loads.append(pltpu.make_async_copy(ref, buf, sems.at[number]))
        loads[-1].start()
    copies = []
    for mask in range(parts):
        first = pl.multiple_of((me ^ mask) * heads, heads)
        copies.append(
            pltpu.make_async_copy(
                cot_ref.at[:, pl.ds(first, heads), :], cot_outs[mask], sems.at[mask + 2]
            )
        )
        copies[-1].start()
    for number, buf in enumerate((key_buf, value_buf)):
        loads[number].wait()
        for group, block in enumerate(regroup(buf)):
            for kv_out in kv_outs:
                kv_out[number, group] = block
    for copy in copies:
        copy.wait()


def prepare(cotangent, keys, values, parts):
    rows, heads, size = cotangent.shape
    kv_rows, kv_heads, _ = keys.shape
    piece = pltpu.VMEM((rows, heads // parts, size), jnp.bfloat16)
    block = pltpu.VMEM((2, kv_heads, kv_rows, size), jnp.bfloat16)
    operands = [
        pltpu.with_memory_space_constraint(array, pltpu.HBM)
        for array in (cotangent, keys, values)
    ]
    outs = pl.pallas_call(
        functools.partial(prep_kernel, parts),
        out_shape=(block,) * 3 + (piece,) * parts,
        in_specs=[_HBM] * 3,
        out_specs=(_VMEM,) * (parts + 3),
        scratch_shapes=[
            pltpu.VMEM(keys.shape, jnp.bfloat16),
            pltpu.VMEM(values.shape, jnp.bfloat16),
            pltpu.SemaphoreType.DMA((parts + 2,)),
        ],
        compiler_params=pltpu.CompilerParams(vmem_limit_bytes=VMEM_BYTES),
        name="prepare",
    )(*operands)
    return outs[:3], outs[3:]


def bounds(position, lengths, prefixes):
    docs = lengths.shape[0]

    def step(doc, carry):
        start, low, high = carry
        end = start + lengths[doc]
        inside = (position >= start) & (position < end)
        reach = jnp.minimum(end, jnp.maximum(position + 1, start + prefixes[doc]))
        return end, jnp.where(inside, start, low), jnp.where(inside, reach, high)

    zero = jnp.zeros_like(position)
    carry = (jnp.int32(0), zero, zero)
    if docs <= 16:
        for doc in range(docs):
            carry = step(doc, carry)
    else:
        carry = lax.fori_loop(0, docs, step, carry)
    return carry[1], carry[2]


def neighbour_slots(shard):
    odd = shard % 2
    ahead, behind = BACK + 1, BACK - 1
    return jnp.where(odd == 1, behind, ahead), jnp.where(odd == 1, ahead, behind)


def grad_kernel(parts, lengths, prefixes, q_ref, cot_own, kv_own, *rest):
    names = order(parts)
    got, rest = dict(zip(names, rest)), rest[len(names) :]
    dq_refs, rest = rest[:parts], rest[parts:]
    own_out, far_out, even_out, odd_out, window, acc = rest
    rows, heads, size = q_ref.shape
    tokens = rows // parts
    kv_heads = kv_own.shape[1]
    group_size = heads // kv_heads
    span = (BACK + 1 + AHEAD) * rows
    reach = span - rows + tokens
    lanes = tokens * group_size
    scale = size ** (-0.5)
    shard = lax.axis_index("seq")
    me = lax.axis_index("kvh")

    even_slot, odd_slot = neighbour_slots(shard)
    slots = ((BACK, kv_own), (0, got["far"]), (even_slot, got["even"]), (odd_slot, got["odd"]))
    for slot, ref in slots:
        for number in range(2):
            for group in range(kv_heads):
                part = pl.ds(pl.multiple_of(slot * rows, rows), rows)
                window[number, group, part] = ref[number, group]
    acc[...] = jnp.zeros_like(acc)

    contract_last = (((1,), (1,)), ((), ()))
    contract_first = (((0,), (0,)), ((), ()))
    lane_token = lax.broadcasted_iota(jnp.int32, (1, lanes), 1) // group_size
    key_iota = lax.broadcasted_iota(jnp.int32, (reach, lanes), 0)
    for mask in range(parts):
        first = pl.multiple_of((me ^ mask) * tokens, tokens)
        low, high = bounds(shard * rows + first + lane_token, lengths, prefixes)
        origin = (shard - BACK) * rows + first
        low = low - origin
        high = high - origin
        visible = (key_iota >= low) & (key_iota < high)
        here = pl.ds(first, reach)
        for group in range(kv_heads):
            of_group = pl.ds(group * group_size, group_size)
            q = q_ref[pl.ds(first, tokens), of_group].astype(jnp.float32)
            q = q.reshape(lanes, size).astype(jnp.bfloat16)
            cot = (got[mask] if mask else cot_own)[:, of_group].astype(jnp.float32)
            cot = cot.reshape(lanes, size).astype(jnp.bfloat16)
            k = window[0, group, here]
            v = window[1, group, here]
            scores = lax.dot_general(k, q, contract_last, preferred_element_type=jnp.float32)
            scores = jnp.where(visible, scores * (scale * LOG2E), NEG)
            top = jnp.max(scores, axis=0, keepdims=True)
            expo = jnp.exp2(scores - top)
            total = jnp.sum(expo, axis=0, keepdims=True)
            probs = expo * (1.0 / total)
            dprobs = lax.dot_general(v, cot, contract_last, preferred_element_type=jnp.float32)
            delta = jnp.sum(probs * dprobs, axis=0, keepdims=True)
            dscores = (probs * (dprobs - delta)).astype(jnp.bfloat16)
            acc[1, group, here] += jnp.dot(
                probs.astype(jnp.bfloat16), cot, preferred_element_type=jnp.float32
            )
            acc[0, group, here] += jnp.dot(dscores, q, preferred_element_type=jnp.float32)
            dq = lax.dot_general(k, dscores, contract_first, preferred_element_type=jnp.float32)
            dq = jnp.transpose(dq * scale)
            dq_refs[mask][:, of_group] = dq.reshape(tokens, group_size, size).astype(jnp.bfloat16)
    for slot, ref in ((0, far_out), (even_slot, even_out), (odd_slot, odd_out), (BACK, own_out)):
        for group in range(kv_heads):
            part = pl.ds(pl.multiple_of(slot * rows, rows), rows)
            ref[0, group] = (acc[0, group, part] * scale).astype(ref.dtype)
            ref[1, group] = acc[1, group, part].astype(ref.dtype)


def gradients(lengths, prefixes, queries, cot_own, kv_own, got, parts):
    rows, heads, size = queries.shape
    kv_shape = got["far"].shape
    kv_heads = kv_shape[1]
    span = (BACK + 1 + AHEAD) * rows
    half = jax.ShapeDtypeStruct(kv_shape, jnp.bfloat16)
    work = heads * rows * span
    outs = pl.pallas_call(
        functools.partial(grad_kernel, parts),
        out_shape=(jax.ShapeDtypeStruct(got[1].shape, jnp.bfloat16),) * parts
        + (jax.ShapeDtypeStruct(kv_shape, jnp.float32), half, half, half),
        in_specs=[_SMEM, _SMEM] + [_VMEM] * (parts + 5),
        out_specs=(_VMEM,) * (parts + 4),
        scratch_shapes=[
            pltpu.VMEM((2, kv_heads, span, size), jnp.bfloat16),
            pltpu.VMEM((2, kv_heads, span, size), jnp.float32),
        ],
        compiler_params=pltpu.CompilerParams(vmem_limit_bytes=VMEM_BYTES),
        cost_estimate=pl.CostEstimate(
            flops=10 * work * size, bytes_accessed=4 * queries.size * 2, transcendentals=work
        ),
        name="gradients",
    )(lengths, prefixes, queries, cot_own, kv_own, *[got[name] for name in order(parts)])
    return outs[:parts], outs[parts:]


def finish_kernel(parts, *refs):
    names = order(parts)
    got, (dq_own, own, dq_out, dk_out, dv_out) = dict(zip(names, refs)), refs[len(names) :]
    heads = dq_own.shape[1]
    me = lax.axis_index("kvh")
    for mask in range(parts):
        first = pl.multiple_of((me ^ mask) * heads, heads)
        dq_out[:, pl.ds(first, heads), :] = (got[mask] if mask else dq_own)[...]
    for number, ref in enumerate((dk_out, dv_out)):
        sums = []
        for group in range(ref.shape[1]):
            total = own[number, group]
            for other in (got["far"], got["even"], got["odd"]):
                total = total + other[number, group].astype(jnp.float32)
            sums.append(total)
        ref[...] = jnp.stack(sums, axis=1).astype(jnp.bfloat16)


def finish(dq_own, own, got, parts):
    rows, heads, size = dq_own.shape
    _, kv_heads, kv_rows, _ = own.shape
    kv_out = jax.ShapeDtypeStruct((kv_rows, kv_heads, size), jnp.bfloat16)
    return pl.pallas_call(
        functools.partial(finish_kernel, parts),
        out_shape=(
            jax.ShapeDtypeStruct((rows, heads * parts, size), jnp.bfloat16),
            kv_out,
            kv_out,
        ),
        in_specs=[_VMEM] * (parts + 4),
        out_specs=(_VMEM,) * 3,
        compiler_params=pltpu.CompilerParams(vmem_limit_bytes=VMEM_BYTES),
        name="finish",
    )(*[got[name] for name in order(parts)], dq_own, own)


def shifted(block, distance):
    devices = range(lax.axis_size("seq"))
    route = [(i, i + distance) for i in devices if i + distance in devices]
    return lax.ppermute(block, "seq", route)


def paired(block, first):
    count = lax.axis_size("seq")
    route = []
    for i in range(count):
        partner = i + 1 if i % 2 == first else i - 1
        route.append((i, partner if 0 <= partner < count else i))
    return lax.ppermute(block, "seq", route)


def swapped(block, mask):
    return lax.ppermute(block, "kvh", [(i, i ^ mask) for i in range(lax.axis_size("kvh"))])


def exchange(pieces, far, even, odd, distance):
    got = {mask: swapped(piece, mask) for mask, piece in enumerate(pieces, 1)}
    got["far"] = shifted(far, distance)
    got["even"] = paired(even, 0)
    got["odd"] = paired(odd, 1)
    return got


def local(queries, keys, values, output_gradient, doc_lengths, prefix_lengths):
    parts = lax.axis_size("kvh")
    kv, cots = prepare(output_gradient, keys, values, parts)
    got = exchange(cots[1:], *kv, BACK)
    dqs, (own, far, even, odd) = gradients(
        doc_lengths, prefix_lengths, queries, cots[0], kv[0], got, parts
    )
    got = exchange(dqs[1:], far, even, odd, -BACK)
    return finish(dqs[0], own, got, parts)


def solution(mesh):
    in_specs = (
        P("seq", "kvh", None),
        P("seq", "kvh", None),
        P("seq", "kvh", None),
        P(("seq", "kvh"), None, None),
        P(),
        P(),
    )
    out_specs = (P(("seq", "kvh"), None, None), P("seq", "kvh", None), P("seq", "kvh", None))
    return jax.shard_map(local, mesh=mesh, in_specs=in_specs, out_specs=out_specs, check_vma=False)
```

time: 44.9 us -> 37 us (0.82)
  the two profiles are of different devices: /device:TPU:0 before, /device:TPU:10 now
where the time goes in v4:
time: 37 us; the launch traced here: 36.8 us
  starting transfers between devices  19.2 us (52%)
  waiting for transfers between devices  9.11 us (25%)
  Pallas kernels  7.77 us (21%)
  between operations  0.74 us (2%)
    ppermute x4, starting transfers between devices, paired(): return lax.ppermute(block, 'seq', route)  10 us
    ppermute x2, starting transfers between devices, shifted(): return lax.ppermute(block, 'seq', route)  5.54 us
    pallas_call x1, Pallas kernels, gradients(): pl.pallas_call(functools.partial(grad_kernel, parts), out_shape=(jax.Shap...  5.47 us
    ppermute x6, starting transfers between devices, swapped(): lax.ppermute(block, 'kvh', [(i, i ^ mask) for i in range(lax.axis_size('k...  3.64 us
    ppermute x4, waiting for transfers between devices, paired(): return lax.ppermute(block, 'seq', route)  3.05 us
    ppermute x6, waiting for transfers between devices, swapped(): lax.ppermute(block, 'kvh', [(i, i ^ mask) for i in range(lax.axis_size('k...  3.03 us
    ppermute x2, waiting for transfers between devices, shifted(): return lax.ppermute(block, 'seq', route)  3.02 us
    pallas_call x1, Pallas kernels, prepare(): pl.pallas_call(functools.partial(prep_kernel, parts), out_shape=(block,)...  1.28 us
  transfers between devices with their start and end apart: 12, of which 4 were waited for; matrix products, arithmetic and copies ran while one was open for 0% of the time, Pallas kernels for 0%

profile of v4, /device:TPU:10, one launch (start us, length us, event | category | flops | bytes accessed | tf_op | source)
XLA Modules:
  0.0 36.8 jit_solution(4522523044100517811)
XLA Ops:
  0.6 0.0 copy-start
  0.6 1.3 %prepare.1 = (bf16[2,2,128,128]{3,2,1,0:T(8,128)(2,1)S(1)}, bf16[2,2,128,128]{3,2,1,0:T(8,128)(2,1)S(1)}, bf16[2,2,128,128]{3,2,1,0:T(8,128)(2,1)S(1)}, bf16[32,...) custom-call(bf16[32,64,128]{2,1,0:T(8,128)(2,1)} %cot_ref.1, ...), custom_call_target="tpu_custom_call" | custom-call | tf_op jit(solution)/shard_map/prepare/pallas_call | solution.py:66
  1.9 1.0 %collective-permute-start.1 = (bf16[32,16,128]{2,1,0:T(8,128)(2,1)S(1)}, bf16[32,16,128]{2,1,0:T(8,128)(2,1)S(1)}, u32[]{:S(2)}, u32[]{:S(2)}) collective-permute-start(bf16[32,16,128]{2,1,0:T(8,128)(2,1)S(1)} %get-tuple-element.20), channel_id=1, source_target_pairs={{0,3},{1,2},{2,1},{3,0},{4,7},{5,6},{6,5},{7,4},{8,11},{9,10},{10,... | collective-permute-start | bytes 393224 | tf_op jit(solution)/shard_map/ppermute | solution.py:254
  2.9 0.5 %collective-permute-start.2 = (bf16[2,2,128,128]{3,2,1,0:T(8,128)(2,1)S(1)}, bf16[2,2,128,128]{3,2,1,0:T(8,128)(2,1)S(1)}, u32[]{:S(2)}, u32[]{:S(2)}) collective-permute-start(bf16[2,2,128,128]{3,2,1,0:T(8,128)(2,1)S(1)} %get-tuple-element.21), channel_id=1, source_target_pairs={{0,4},{4,0},{8,12},{12,8},{16,20},{20,16},{24,28},{28,24},{1,5},{5... | collective-permute-start | bytes 393224 | tf_op jit(solution)/shard_map/ppermute | solution.py:250
  3.5 4.4 %collective-permute-start.3 = (bf16[2,2,128,128]{3,2,1,0:T(8,128)(2,1)S(1)}, bf16[2,2,128,128]{3,2,1,0:T(8,128)(2,1)S(1)}, u32[]{:S(2)}, u32[]{:S(2)}) collective-permute-start(bf16[2,2,128,128]{3,2,1,0:T(8,128)(2,1)S(1)} %get-tuple-element.22), channel_id=1, source_target_pairs={{0,0},{4,8},{8,4},{12,16},{16,12},{20,24},{24,20},{28,28},{1,1},{5... | collective-permute-start | bytes 393224 | tf_op jit(solution)/shard_map/ppermute | solution.py:250
  7.9 0.7 %collective-permute-start.4 = (bf16[32,16,128]{2,1,0:T(8,128)(2,1)S(1)}, bf16[32,16,128]{2,1,0:T(8,128)(2,1)S(1)}, u32[]{:S(2)}, u32[]{:S(2)}) collective-permute-start(bf16[32,16,128]{2,1,0:T(8,128)(2,1)S(1)} %get-tuple-element.23), channel_id=1, source_target_pairs={{0,2},{1,3},{2,0},{3,1},{4,6},{5,7},{6,4},{7,5},{8,10},{9,11},{10,... | collective-permute-start | bytes 393224 | tf_op jit(solution)/shard_map/ppermute | solution.py:254
  8.6 0.0 collective-permute-start.5
  8.6 0.0 collective-permute-done.1.rest_1_
  8.6 0.0 copy-start.1
  8.6 0.0 copy-start.2
  8.6 3.6 %collective-permute-start = (bf16[2,2,128,128]{3,2,1,0:T(8,128)(2,1)S(1)}, bf16[2,2,128,128]{3,2,1,0:T(8,128)(2,1)S(1)}, u32[]{:S(2)}, u32[]{:S(2)}) collective-permute-start(bf16[2,2,128,128]{3,2,1,0:T(8,128)(2,1)S(1)} %get-tuple-element.19.kv_own), channel_id=1, source_target_pairs={{0,8},{4,12},{8,16},{12,20},{16,24},{20,28},{1,9},{5,13},{9,17},{1... | collective-permute-start | bytes 393224 | tf_op jit(solution)/shard_map/ppermute | solution.py:241
  12.2 0.0 collective-permute-done.2.rest_2_
  12.3 0.0 collective-permute-done.3.rest_3_
  12.3 1.2 %collective-permute-done.4.rest_4_ = bf16[32,16,128]{2,1,0:T(8,128)(2,1)S(1)} collective-permute-done((bf16[32,16,128]{2,1,0:T(8,128)(2,1)S(1)}, bf16[32,16,128]{2,1,0:T(8,128)(2,1)S(1)}, u32[]{:S(2)}, u32[]{:S(2)}) %collective-permute-start.4) | collective-permute-done | bytes 131104 | tf_op jit(solution)/shard_map/ppermute | solution.py:254
  13.5 0.0 collective-permute-done.5.rest_5_
  13.5 3.0 %collective-permute-done.rest_0_ = bf16[2,2,128,128]{3,2,1,0:T(8,128)(2,1)S(1)} collective-permute-done((bf16[2,2,128,128]{3,2,1,0:T(8,128)(2,1)S(1)}, bf16[2,2,128,128]{3,2,1,0:T(8,128)(2,1)S(1)}, u32[]{:S(2)}, u32[]{:S(2)}) %collective-permute-start) | collective-permute-done | bytes 131104 | tf_op jit(solution)/shard_map/ppermute | solution.py:241
  16.5 0.0 copy-done
  16.5 0.0 copy-done.1
  16.5 0.0 copy-done.2
  16.5 5.5 %gradients.1 = (bf16[32,16,128]{2,1,0:T(8,128)(2,1)S(1)}, bf16[32,16,128]{2,1,0:T(8,128)(2,1)S(1)}, bf16[32,16,128]{2,1,0:T(8,128)(2,1)S(1)}, bf16[32,16,128]{2,...) custom-call(s32[8]{0:T(128)S(1)} %copy-done.1, ...), custom_call_target="tpu_custom_call" | custom-call | flops 1342177280 | bytes 2097152 | tf_op jit(solution)/shard_map/gradients/pallas_call | solution.py:183
  22.0 1.9 %collective-permute-start.6 = (bf16[2,2,128,128]{3,2,1,0:T(8,128)(2,1)S(1)}, bf16[2,2,128,128]{3,2,1,0:T(8,128)(2,1)S(1)}, u32[]{:S(2)}, u32[]{:S(2)}) collective-permute-start(bf16[2,2,128,128]{3,2,1,0:T(8,128)(2,1)S(1)} %get-tuple-element.25), channel_id=1, source_target_pairs={{8,0},{12,4},{16,8},{20,12},{24,16},{28,20},{9,1},{13,5},{17,9},{2... | collective-permute-start | bytes 393224 | tf_op jit(solution)/shard_map/ppermute | solution.py:241
  24.0 0.8 %collective-permute-start.7 = (bf16[32,16,128]{2,1,0:T(8,128)(2,1)S(1)}, bf16[32,16,128]{2,1,0:T(8,128)(2,1)S(1)}, u32[]{:S(2)}, u32[]{:S(2)}) collective-permute-start(bf16[32,16,128]{2,1,0:T(8,128)(2,1)S(1)} %get-tuple-element.26), channel_id=1, source_target_pairs={{0,3},{1,2},{2,1},{3,0},{4,7},{5,6},{6,5},{7,4},{8,11},{9,10},{10,... | collective-permute-start | bytes 393224 | tf_op jit(solution)/shard_map/ppermute | solution.py:254
  24.7 0.0 collective-permute-start.8
  24.7 5.1 %collective-permute-start.9 = (bf16[2,2,128,128]{3,2,1,0:T(8,128)(2,1)S(1)}, bf16[2,2,128,128]{3,2,1,0:T(8,128)(2,1)S(1)}, u32[]{:S(2)}, u32[]{:S(2)}) collective-permute-start(bf16[2,2,128,128]{3,2,1,0:T(8,128)(2,1)S(1)} %get-tuple-element.28), channel_id=1, source_target_pairs={{0,0},{4,8},{8,4},{12,16},{16,12},{20,24},{24,20},{28,28},{1,1},{5... | collective-permute-start | bytes 393224 | tf_op jit(solution)/shard_map/ppermute | solution.py:250
  29.8 1.1 %collective-permute-start.10 = (bf16[32,16,128]{2,1,0:T(8,128)(2,1)S(1)}, bf16[32,16,128]{2,1,0:T(8,128)(2,1)S(1)}, u32[]{:S(2)}, u32[]{:S(2)}) collective-permute-start(bf16[32,16,128]{2,1,0:T(8,128)(2,1)S(1)} %get-tuple-element.29), channel_id=1, source_target_pairs={{0,2},{1,3},{2,0},{3,1},{4,6},{5,7},{6,4},{7,5},{8,10},{9,11},{10,... | collective-permute-start | bytes 393224 | tf_op jit(solution)/shard_map/ppermute | solution.py:254
  31.0 0.0 collective-permute-done.6.refs_0_
  31.0 0.0 collective-permute-start.11
  31.0 0.0 collective-permute-done.7.refs_1_
  31.0 0.0 collective-permute-done.8.refs_2_
  31.0 3.0 %collective-permute-done.9.refs_3_ = bf16[2,2,128,128]{3,2,1,0:T(8,128)(2,1)S(1)} collective-permute-done((bf16[2,2,128,128]{3,2,1,0:T(8,128)(2,1)S(1)}, bf16[2,2,128,128]{3,2,1,0:T(8,128)(2,1)S(1)}, u32[]{:S(2)}, u32[]{:S(2)}) %collective-permute-start.9) | collective-permute-done | bytes 131104 | tf_op jit(solution)/shard_map/ppermute | solution.py:250
  34.0 1.8 %collective-permute-done.10.refs_4_ = bf16[32,16,128]{2,1,0:T(8,128)(2,1)S(1)} collective-permute-done((bf16[32,16,128]{2,1,0:T(8,128)(2,1)S(1)}, bf16[32,16,128]{2,1,0:T(8,128)(2,1)S(1)}, u32[]{:S(2)}, u32[]{:S(2)}) %collective-permute-start.10) | collective-permute-done | bytes 131104 | tf_op jit(solution)/shard_map/ppermute | solution.py:254
  35.8 0.0 collective-permute-done.11.refs_5_
  35.8 1.0 %finish.1 = (bf16[32,64,128]{2,1,0:T(8,128)(2,1)}, bf16[128,2,128]{2,1,0:T(2,128)(2,1)}, bf16[128,2,128]{2,1,0:T(2,128)(2,1)}) custom-call(bf16[2,2,128,128]{3,2,1,0:T(8,128)(2,1)S(1)} %collective-permute-done.6.refs_0_, bf16[32,16,128]{2,1,0:T(8,128)(2,1)S(1)} %collective-permute-done.7.refs_1_, ...), custom_call_target="tpu_custom_call" | custom-call | tf_op jit(solution)/shard_map/finish/pallas_call | solution.py:224
Async XLA Ops:
  0.6 15.9 %copy-start = (bf16[128,16,128]{2,1,0:T(8,128)(2,1)S(1)}, bf16[128,16,128]{2,1,0:T(8,128)(2,1)}, u32[]{:S(2)}) copy-start(bf16[128,16,128]{2,1,0:T(8,128)(2,1)} %q_ref.1) | copy-start | bytes 1572868
  1.9 6.7 %collective-permute-start.1 = (bf16[32,16,128]{2,1,0:T(8,128)(2,1)S(1)}, bf16[32,16,128]{2,1,0:T(8,128)(2,1)S(1)}, u32[]{:S(2)}, u32[]{:S(2)}) collective-permute-start(bf16[32,16,128]{2,1,0:T(8,128)(2,1)S(1)} %get-tuple-element.20), channel_id=1, source_target_pairs={{0,3},{1,2},{2,1},{3,0},{4,7},{5,6},{6,5},{7,4},{8,11},{9,10},{10,... | collective-permute-start | bytes 393224 | tf_op jit(solution)/shard_map/ppermute | solution.py:254
  2.9 9.3 %collective-permute-start.2 = (bf16[2,2,128,128]{3,2,1,0:T(8,128)(2,1)S(1)}, bf16[2,2,128,128]{3,2,1,0:T(8,128)(2,1)S(1)}, u32[]{:S(2)}, u32[]{:S(2)}) collective-permute-start(bf16[2,2,128,128]{3,2,1,0:T(8,128)(2,1)S(1)} %get-tuple-element.21), channel_id=1, source_target_pairs={{0,4},{4,0},{8,12},{12,8},{16,20},{20,16},{24,28},{28,24},{1,5},{5... | collective-permute-start | bytes 393224 | tf_op jit(solution)/shard_map/ppermute | solution.py:250
  3.5 8.8 %collective-permute-start.3 = (bf16[2,2,128,128]{3,2,1,0:T(8,128)(2,1)S(1)}, bf16[2,2,128,128]{3,2,1,0:T(8,128)(2,1)S(1)}, u32[]{:S(2)}, u32[]{:S(2)}) collective-permute-start(bf16[2,2,128,128]{3,2,1,0:T(8,128)(2,1)S(1)} %get-tuple-element.22), channel_id=1, source_target_pairs={{0,0},{4,8},{8,4},{12,16},{16,12},{20,24},{24,20},{28,28},{1,1},{5... | collective-permute-start | bytes 393224 | tf_op jit(solution)/shard_map/ppermute | solution.py:250
  7.9 5.6 %collective-permute-start.4 = (bf16[32,16,128]{2,1,0:T(8,128)(2,1)S(1)}, bf16[32,16,128]{2,1,0:T(8,128)(2,1)S(1)}, u32[]{:S(2)}, u32[]{:S(2)}) collective-permute-start(bf16[32,16,128]{2,1,0:T(8,128)(2,1)S(1)} %get-tuple-element.23), channel_id=1, source_target_pairs={{0,2},{1,3},{2,0},{3,1},{4,6},{5,7},{6,4},{7,5},{8,10},{9,11},{10,... | collective-permute-start | bytes 393224 | tf_op jit(solution)/shard_map/ppermute | solution.py:254
  8.6 4.9 %collective-permute-start.5 = (bf16[32,16,128]{2,1,0:T(8,128)(2,1)S(1)}, bf16[32,16,128]{2,1,0:T(8,128)(2,1)S(1)}, u32[]{:S(2)}, u32[]{:S(2)}) collective-permute-start(bf16[32,16,128]{2,1,0:T(8,128)(2,1)S(1)} %get-tuple-element.24), channel_id=1, source_target_pairs={{0,1},{1,0},{2,3},{3,2},{4,5},{5,4},{6,7},{7,6},{8,9},{9,8},{10,11... | collective-permute-start | bytes 393224 | tf_op jit(solution)/shard_map/ppermute | solution.py:254
  8.6 7.9 %copy-start.1 = (s32[8]{0:T(128)S(1)}, s32[8]{0:T(128)}, u32[]{:S(2)}) copy-start(s32[8]{0:T(128)} %lengths.1) | copy-start | bytes 100
  8.6 7.9 %copy-start.2 = (s32[8]{0:T(128)S(1)}, s32[8]{0:T(128)}, u32[]{:S(2)}) copy-start(s32[8]{0:T(128)} %prefixes.1) | copy-start | bytes 100
  8.6 7.9 %collective-permute-start = (bf16[2,2,128,128]{3,2,1,0:T(8,128)(2,1)S(1)}, bf16[2,2,128,128]{3,2,1,0:T(8,128)(2,1)S(1)}, u32[]{:S(2)}, u32[]{:S(2)}) collective-permute-start(bf16[2,2,128,128]{3,2,1,0:T(8,128)(2,1)S(1)} %get-tuple-element.19.kv_own), channel_id=1, source_target_pairs={{0,8},{4,12},{8,16},{12,20},{16,24},{20,28},{1,9},{5,13},{9,17},{1... | collective-permute-start | bytes 393224 | tf_op jit(solution)/shard_map/ppermute | solution.py:241
  22.0 8.9 %collective-permute-start.6 = (bf16[2,2,128,128]{3,2,1,0:T(8,128)(2,1)S(1)}, bf16[2,2,128,128]{3,2,1,0:T(8,128)(2,1)S(1)}, u32[]{:S(2)}, u32[]{:S(2)}) collective-permute-start(bf16[2,2,128,128]{3,2,1,0:T(8,128)(2,1)S(1)} %get-tuple-element.25), channel_id=1, source_target_pairs={{8,0},{12,4},{16,8},{20,12},{24,16},{28,20},{9,1},{13,5},{17,9},{2... | collective-permute-start | bytes 393224 | tf_op jit(solution)/shard_map/ppermute | solution.py:241
  24.0 7.0 %collective-permute-start.7 = (bf16[32,16,128]{2,1,0:T(8,128)(2,1)S(1)}, bf16[32,16,128]{2,1,0:T(8,128)(2,1)S(1)}, u32[]{:S(2)}, u32[]{:S(2)}) collective-permute-start(bf16[32,16,128]{2,1,0:T(8,128)(2,1)S(1)} %get-tuple-element.26), channel_id=1, source_target_pairs={{0,3},{1,2},{2,1},{3,0},{4,7},{5,6},{6,5},{7,4},{8,11},{9,10},{10,... | collective-permute-start | bytes 393224 | tf_op jit(solution)/shard_map/ppermute | solution.py:254
  24.7 6.3 %collective-permute-start.8 = (bf16[2,2,128,128]{3,2,1,0:T(8,128)(2,1)S(1)}, bf16[2,2,128,128]{3,2,1,0:T(8,128)(2,1)S(1)}, u32[]{:S(2)}, u32[]{:S(2)}) collective-permute-start(bf16[2,2,128,128]{3,2,1,0:T(8,128)(2,1)S(1)} %get-tuple-element.27), channel_id=1, source_target_pairs={{0,4},{4,0},{8,12},{12,8},{16,20},{20,16},{24,28},{28,24},{1,5},{5... | collective-permute-start | bytes 393224 | tf_op jit(solution)/shard_map/ppermute | solution.py:250
  24.7 9.3 %collective-permute-start.9 = (bf16[2,2,128,128]{3,2,1,0:T(8,128)(2,1)S(1)}, bf16[2,2,128,128]{3,2,1,0:T(8,128)(2,1)S(1)}, u32[]{:S(2)}, u32[]{:S(2)}) collective-permute-start(bf16[2,2,128,128]{3,2,1,0:T(8,128)(2,1)S(1)} %get-tuple-element.28), channel_id=1, source_target_pairs={{0,0},{4,8},{8,4},{12,16},{16,12},{20,24},{24,20},{28,28},{1,1},{5... | collective-permute-start | bytes 393224 | tf_op jit(solution)/shard_map/ppermute | solution.py:250
  29.8 6.0 %collective-permute-start.10 = (bf16[32,16,128]{2,1,0:T(8,128)(2,1)S(1)}, bf16[32,16,128]{2,1,0:T(8,128)(2,1)S(1)}, u32[]{:S(2)}, u32[]{:S(2)}) collective-permute-start(bf16[32,16,128]{2,1,0:T(8,128)(2,1)S(1)} %get-tuple-element.29), channel_id=1, source_target_pairs={{0,2},{1,3},{2,0},{3,1},{4,6},{5,7},{6,4},{7,5},{8,10},{9,11},{10,... | collective-permute-start | bytes 393224 | tf_op jit(solution)/shard_map/ppermute | solution.py:254
  31.0 4.8 %collective-permute-start.11 = (bf16[32,16,128]{2,1,0:T(8,128)(2,1)S(1)}, bf16[32,16,128]{2,1,0:T(8,128)(2,1)S(1)}, u32[]{:S(2)}, u32[]{:S(2)}) collective-permute-start(bf16[32,16,128]{2,1,0:T(8,128)(2,1)S(1)} %get-tuple-element.30), channel_id=1, source_target_pairs={{0,1},{1,0},{2,3},{3,2},{4,5},{5,4},{6,7},{7,6},{8,9},{9,8},{10,11... | collective-permute-start | bytes 393224 | tf_op jit(solution)/shard_map/ppermute | solution.py:254

commit v5 on v4

--- a/solution.py
+++ b/solution.py
@@ -29,7 +29,7 @@
 
 
 def prep_kernel(parts, cot_ref, key_ref, value_ref, *rest):
-    kv_outs, cot_outs, (key_buf, value_buf, sems) = rest[:3], rest[3 : parts + 3], rest[parts + 3 :]
+    kv_outs, cot_outs, (key_buf, value_buf, sems) = rest[:4], rest[4 : parts + 4], rest[parts + 4 :]
     heads = cot_ref.shape[1] // parts
     me = lax.axis_index("kvh")
     loads = []
@@ -65,9 +65,9 @@
     ]
     outs = pl.pallas_call(
         functools.partial(prep_kernel, parts),
-        out_shape=(block,) * 3 + (piece,) * parts,
+        out_shape=(block,) * 4 + (piece,) * parts,
         in_specs=[_HBM] * 3,
-        out_specs=(_VMEM,) * (parts + 3),
+        out_specs=(_VMEM,) * (parts + 4),
         scratch_shapes=[
             pltpu.VMEM(keys.shape, jnp.bfloat16),
             pltpu.VMEM(values.shape, jnp.bfloat16),
@@ -76,7 +76,7 @@
         compiler_params=pltpu.CompilerParams(vmem_limit_bytes=VMEM_BYTES),
         name="prepare",
     )(*operands)
-    return outs[:3], outs[3:]
+    return outs[:4], outs[4:]
 
 
 def bounds(position, lengths, prefixes):
@@ -265,7 +265,7 @@
 def local(queries, keys, values, output_gradient, doc_lengths, prefix_lengths):
     parts = lax.axis_size("kvh")
     kv, cots = prepare(output_gradient, keys, values, parts)
-    got = exchange(cots[1:], *kv, BACK)
+    got = exchange(cots[1:], *kv[1:], BACK)
     dqs, (own, far, even, odd) = gradients(
         doc_lengths, prefix_lengths, queries, cots[0], kv[0], got, parts
     )

time: 37 us -> 37.3 us (level)
  the two profiles are of different devices: /device:TPU:10 before, /device:TPU:6 now
where the time goes in v5:
time: 37.3 us; the launch traced here: 37.1 us
  starting transfers between devices  18.9 us (51%)
  waiting for transfers between devices  8.99 us (24%)
  Pallas kernels  7.75 us (21%)
  between operations  0.72 us (2%)
  local copies, waits for them, and re-layouts  0.67 us (2%)
    ppermute x4, starting transfers between devices, paired(): return lax.ppermute(block, 'seq', route)  10.7 us
    ppermute x4, waiting for transfers between devices, paired(): return lax.ppermute(block, 'seq', route)  5.65 us
    pallas_call x1, Pallas kernels, gradients(): pl.pallas_call(functools.partial(grad_kernel, parts), out_shape=(jax.Shap...  5.46 us
    ppermute x2, starting transfers between devices, shifted(): return lax.ppermute(block, 'seq', route)  4.78 us
    ppermute x6, starting transfers between devices, swapped(): lax.ppermute(block, 'kvh', [(i, i ^ mask) for i in range(lax.axis_size('k...  3.44 us
    ppermute x6, waiting for transfers between devices, swapped(): lax.ppermute(block, 'kvh', [(i, i ^ mask) for i in range(lax.axis_size('k...  3.34 us
    pallas_call x1, Pallas kernels, prepare(): pl.pallas_call(functools.partial(prep_kernel, parts), out_shape=(block,)...  1.28 us
    pallas_call x1, Pallas kernels, finish(): pl.pallas_call(functools.partial(finish_kernel, parts), out_shape=(jax.Sh...  1.02 us
  transfers between devices with their start and end apart: 12, of which 4 were waited for; matrix products, arithmetic and copies ran while one was open for 0% of the time, Pallas kernels for 0%

profile of v5, /device:TPU:6, one launch (start us, length us, event | category | flops | bytes accessed | tf_op | source)
XLA Modules:
  0.0 37.1 jit_solution(18342107207458324507)
XLA Ops:
  0.6 0.0 copy-start
  0.6 1.3 %prepare.1 = (bf16[2,2,128,128]{3,2,1,0:T(8,128)(2,1)S(1)}, bf16[2,2,128,128]{3,2,1,0:T(8,128)(2,1)S(1)}, bf16[2,2,128,128]{3,2,1,0:T(8,128)(2,1)S(1)}, bf16[2,2...) custom-call(bf16[32,64,128]{2,1,0:T(8,128)(2,1)} %cot_ref.1, ...), custom_call_target="tpu_custom_call" | custom-call | tf_op jit(solution)/shard_map/prepare/pallas_call | solution.py:66
  1.9 3.5 %collective-permute-start = (bf16[2,2,128,128]{3,2,1,0:T(8,128)(2,1)S(1)}, bf16[2,2,128,128]{3,2,1,0:T(8,128)(2,1)S(1)}, u32[]{:S(2)}, u32[]{:S(2)}) collective-permute-start(bf16[2,2,128,128]{3,2,1,0:T(8,128)(2,1)S(1)} %get-tuple-element.21), channel_id=1, source_target_pairs={{0,8},{4,12},{8,16},{12,20},{16,24},{20,28},{1,9},{5,13},{9,17},{1... | collective-permute-start | bytes 393224 | tf_op jit(solution)/shard_map/ppermute | solution.py:241
  5.4 0.1 collective-permute-start.1
  5.5 0.6 %collective-permute-start.2 = (bf16[2,2,128,128]{3,2,1,0:T(8,128)(2,1)S(1)}, bf16[2,2,128,128]{3,2,1,0:T(8,128)(2,1)S(1)}, u32[]{:S(2)}, u32[]{:S(2)}) collective-permute-start(bf16[2,2,128,128]{3,2,1,0:T(8,128)(2,1)S(1)} %get-tuple-element.23), channel_id=1, source_target_pairs={{0,4},{4,0},{8,12},{12,8},{16,20},{20,16},{24,28},{28,24},{1,5},{5... | collective-permute-start | bytes 393224 | tf_op jit(solution)/shard_map/ppermute | solution.py:250
  6.1 4.4 %collective-permute-start.3 = (bf16[2,2,128,128]{3,2,1,0:T(8,128)(2,1)S(1)}, bf16[2,2,128,128]{3,2,1,0:T(8,128)(2,1)S(1)}, u32[]{:S(2)}, u32[]{:S(2)}) collective-permute-start(bf16[2,2,128,128]{3,2,1,0:T(8,128)(2,1)S(1)} %get-tuple-element.24), channel_id=1, source_target_pairs={{0,0},{4,8},{8,4},{12,16},{16,12},{20,24},{24,20},{28,28},{1,1},{5... | collective-permute-start | bytes 393224 | tf_op jit(solution)/shard_map/ppermute | solution.py:250
  10.5 1.2 %collective-permute-start.4 = (bf16[32,16,128]{2,1,0:T(8,128)(2,1)S(1)}, bf16[32,16,128]{2,1,0:T(8,128)(2,1)S(1)}, u32[]{:S(2)}, u32[]{:S(2)}) collective-permute-start(bf16[32,16,128]{2,1,0:T(8,128)(2,1)S(1)} %get-tuple-element.25), channel_id=1, source_target_pairs={{0,2},{1,3},{2,0},{3,1},{4,6},{5,7},{6,4},{7,5},{8,10},{9,11},{10,... | collective-permute-start | bytes 393224 | tf_op jit(solution)/shard_map/ppermute | solution.py:254
  11.7 0.0 collective-permute-done.rest_0_
  11.7 0.1 collective-permute-start.5
  11.8 0.0 collective-permute-done.1.rest_1_
  11.8 0.0 collective-permute-done.2.rest_2_
  11.8 2.7 %collective-permute-done.3.rest_3_ = bf16[2,2,128,128]{3,2,1,0:T(8,128)(2,1)S(1)} collective-permute-done((bf16[2,2,128,128]{3,2,1,0:T(8,128)(2,1)S(1)}, bf16[2,2,128,128]{3,2,1,0:T(8,128)(2,1)S(1)}, u32[]{:S(2)}, u32[]{:S(2)}) %collective-permute-start.3) | collective-permute-done | bytes 131104 | tf_op jit(solution)/shard_map/ppermute | solution.py:250
  14.5 1.4 %collective-permute-done.4.rest_4_ = bf16[32,16,128]{2,1,0:T(8,128)(2,1)S(1)} collective-permute-done((bf16[32,16,128]{2,1,0:T(8,128)(2,1)S(1)}, bf16[32,16,128]{2,1,0:T(8,128)(2,1)S(1)}, u32[]{:S(2)}, u32[]{:S(2)}) %collective-permute-start.4) | collective-permute-done | bytes 131104 | tf_op jit(solution)/shard_map/ppermute | solution.py:254
  16.0 0.0 collective-permute-done.5.rest_5_
  16.0 0.0 copy-start.1
  16.0 0.0 copy-start.2
  16.0 0.0 copy-done
  16.0 0.6 %copy-done.1 = s32[8]{0:T(128)S(1)} copy-done((s32[8]{0:T(128)S(1)}, s32[8]{0:T(128)}, u32[]{:S(2)}) %copy-start.1) | copy-done | bytes 56
  16.6 0.0 copy-done.2
  16.6 5.5 %gradients.1 = (bf16[32,16,128]{2,1,0:T(8,128)(2,1)S(1)}, bf16[32,16,128]{2,1,0:T(8,128)(2,1)S(1)}, bf16[32,16,128]{2,1,0:T(8,128)(2,1)S(1)}, bf16[32,16,128]{2,...) custom-call(s32[8]{0:T(128)S(1)} %copy-done.1, ...), custom_call_target="tpu_custom_call" | custom-call | flops 1342177280 | bytes 2097152 | tf_op jit(solution)/shard_map/gradients/pallas_call | solution.py:183
  22.1 1.3 %collective-permute-start.6 = (bf16[2,2,128,128]{3,2,1,0:T(8,128)(2,1)S(1)}, bf16[2,2,128,128]{3,2,1,0:T(8,128)(2,1)S(1)}, u32[]{:S(2)}, u32[]{:S(2)}) collective-permute-start(bf16[2,2,128,128]{3,2,1,0:T(8,128)(2,1)S(1)} %get-tuple-element.27), channel_id=1, source_target_pairs={{8,0},{12,4},{16,8},{20,12},{24,16},{28,20},{9,1},{13,5},{17,9},{2... | collective-permute-start | bytes 393224 | tf_op jit(solution)/shard_map/ppermute | solution.py:241
  23.4 0.9 %collective-permute-start.7 = (bf16[32,16,128]{2,1,0:T(8,128)(2,1)S(1)}, bf16[32,16,128]{2,1,0:T(8,128)(2,1)S(1)}, u32[]{:S(2)}, u32[]{:S(2)}) collective-permute-start(bf16[32,16,128]{2,1,0:T(8,128)(2,1)S(1)} %get-tuple-element.28), channel_id=1, source_target_pairs={{0,3},{1,2},{2,1},{3,0},{4,7},{5,6},{6,5},{7,4},{8,11},{9,10},{10,... | collective-permute-start | bytes 393224 | tf_op jit(solution)/shard_map/ppermute | solution.py:254
  24.3 0.0 collective-permute-start.8
  24.3 5.7 %collective-permute-start.9 = (bf16[2,2,128,128]{3,2,1,0:T(8,128)(2,1)S(1)}, bf16[2,2,128,128]{3,2,1,0:T(8,128)(2,1)S(1)}, u32[]{:S(2)}, u32[]{:S(2)}) collective-permute-start(bf16[2,2,128,128]{3,2,1,0:T(8,128)(2,1)S(1)} %get-tuple-element.30), channel_id=1, source_target_pairs={{0,0},{4,8},{8,4},{12,16},{16,12},{20,24},{24,20},{28,28},{1,1},{5... | collective-permute-start | bytes 393224 | tf_op jit(solution)/shard_map/ppermute | solution.py:250
  30.0 1.2 %collective-permute-start.10 = (bf16[32,16,128]{2,1,0:T(8,128)(2,1)S(1)}, bf16[32,16,128]{2,1,0:T(8,128)(2,1)S(1)}, u32[]{:S(2)}, u32[]{:S(2)}) collective-permute-start(bf16[32,16,128]{2,1,0:T(8,128)(2,1)S(1)} %get-tuple-element.31), channel_id=1, source_target_pairs={{0,2},{1,3},{2,0},{3,1},{4,6},{5,7},{6,4},{7,5},{8,10},{9,11},{10,... | collective-permute-start | bytes 393224 | tf_op jit(solution)/shard_map/ppermute | solution.py:254
  31.2 0.0 collective-permute-done.6.refs_0_
  31.2 0.0 collective-permute-start.11
  31.2 0.0 collective-permute-done.7.refs_1_
  31.2 0.0 collective-permute-done.8.refs_2_
  31.2 2.9 %collective-permute-done.9.refs_3_ = bf16[2,2,128,128]{3,2,1,0:T(8,128)(2,1)S(1)} collective-permute-done((bf16[2,2,128,128]{3,2,1,0:T(8,128)(2,1)S(1)}, bf16[2,2,128,128]{3,2,1,0:T(8,128)(2,1)S(1)}, u32[]{:S(2)}, u32[]{:S(2)}) %collective-permute-start.9) | collective-permute-done | bytes 131104 | tf_op jit(solution)/shard_map/ppermute | solution.py:250
  34.1 1.9 %collective-permute-done.10.refs_4_ = bf16[32,16,128]{2,1,0:T(8,128)(2,1)S(1)} collective-permute-done((bf16[32,16,128]{2,1,0:T(8,128)(2,1)S(1)}, bf16[32,16,128]{2,1,0:T(8,128)(2,1)S(1)}, u32[]{:S(2)}, u32[]{:S(2)}) %collective-permute-start.10) | collective-permute-done | bytes 131104 | tf_op jit(solution)/shard_map/ppermute | solution.py:254
  36.1 0.0 collective-permute-done.11.refs_5_
  36.1 1.0 %finish.1 = (bf16[32,64,128]{2,1,0:T(8,128)(2,1)}, bf16[128,2,128]{2,1,0:T(2,128)(2,1)}, bf16[128,2,128]{2,1,0:T(2,128)(2,1)}) custom-call(bf16[2,2,128,128]{3,2,1,0:T(8,128)(2,1)S(1)} %collective-permute-done.6.refs_0_, bf16[32,16,128]{2,1,0:T(8,128)(2,1)S(1)} %collective-permute-done.7.refs_1_, ...), custom_call_target="tpu_custom_call" | custom-call | tf_op jit(solution)/shard_map/finish/pallas_call | solution.py:224
Async XLA Ops:
  0.6 15.3 %copy-start = (bf16[128,16,128]{2,1,0:T(8,128)(2,1)S(1)}, bf16[128,16,128]{2,1,0:T(8,128)(2,1)}, u32[]{:S(2)}) copy-start(bf16[128,16,128]{2,1,0:T(8,128)(2,1)} %q_ref.1) | copy-start | bytes 1572868
  1.9 9.8 %collective-permute-start = (bf16[2,2,128,128]{3,2,1,0:T(8,128)(2,1)S(1)}, bf16[2,2,128,128]{3,2,1,0:T(8,128)(2,1)S(1)}, u32[]{:S(2)}, u32[]{:S(2)}) collective-permute-start(bf16[2,2,128,128]{3,2,1,0:T(8,128)(2,1)S(1)} %get-tuple-element.21), channel_id=1, source_target_pairs={{0,8},{4,12},{8,16},{12,20},{16,24},{20,28},{1,9},{5,13},{9,17},{1... | collective-permute-start | bytes 393224 | tf_op jit(solution)/shard_map/ppermute | solution.py:241
  5.4 6.4 %collective-permute-start.1 = (bf16[32,16,128]{2,1,0:T(8,128)(2,1)S(1)}, bf16[32,16,128]{2,1,0:T(8,128)(2,1)S(1)}, u32[]{:S(2)}, u32[]{:S(2)}) collective-permute-start(bf16[32,16,128]{2,1,0:T(8,128)(2,1)S(1)} %get-tuple-element.22), channel_id=1, source_target_pairs={{0,3},{1,2},{2,1},{3,0},{4,7},{5,6},{6,5},{7,4},{8,11},{9,10},{10,... | collective-permute-start | bytes 393224 | tf_op jit(solution)/shard_map/ppermute | solution.py:254
  5.5 6.3 %collective-permute-start.2 = (bf16[2,2,128,128]{3,2,1,0:T(8,128)(2,1)S(1)}, bf16[2,2,128,128]{3,2,1,0:T(8,128)(2,1)S(1)}, u32[]{:S(2)}, u32[]{:S(2)}) collective-permute-start(bf16[2,2,128,128]{3,2,1,0:T(8,128)(2,1)S(1)} %get-tuple-element.23), channel_id=1, source_target_pairs={{0,4},{4,0},{8,12},{12,8},{16,20},{20,16},{24,28},{28,24},{1,5},{5... | collective-permute-start | bytes 393224 | tf_op jit(solution)/shard_map/ppermute | solution.py:250
  6.1 8.4 %collective-permute-start.3 = (bf16[2,2,128,128]{3,2,1,0:T(8,128)(2,1)S(1)}, bf16[2,2,128,128]{3,2,1,0:T(8,128)(2,1)S(1)}, u32[]{:S(2)}, u32[]{:S(2)}) collective-permute-start(bf16[2,2,128,128]{3,2,1,0:T(8,128)(2,1)S(1)} %get-tuple-element.24), channel_id=1, source_target_pairs={{0,0},{4,8},{8,4},{12,16},{16,12},{20,24},{24,20},{28,28},{1,1},{5... | collective-permute-start | bytes 393224 | tf_op jit(solution)/shard_map/ppermute | solution.py:250
  10.5 5.5 %collective-permute-start.4 = (bf16[32,16,128]{2,1,0:T(8,128)(2,1)S(1)}, bf16[32,16,128]{2,1,0:T(8,128)(2,1)S(1)}, u32[]{:S(2)}, u32[]{:S(2)}) collective-permute-start(bf16[32,16,128]{2,1,0:T(8,128)(2,1)S(1)} %get-tuple-element.25), channel_id=1, source_target_pairs={{0,2},{1,3},{2,0},{3,1},{4,6},{5,7},{6,4},{7,5},{8,10},{9,11},{10,... | collective-permute-start | bytes 393224 | tf_op jit(solution)/shard_map/ppermute | solution.py:254
  11.7 4.3 %collective-permute-start.5 = (bf16[32,16,128]{2,1,0:T(8,128)(2,1)S(1)}, bf16[32,16,128]{2,1,0:T(8,128)(2,1)S(1)}, u32[]{:S(2)}, u32[]{:S(2)}) collective-permute-start(bf16[32,16,128]{2,1,0:T(8,128)(2,1)S(1)} %get-tuple-element.26), channel_id=1, source_target_pairs={{0,1},{1,0},{2,3},{3,2},{4,5},{5,4},{6,7},{7,6},{8,9},{9,8},{10,11... | collective-permute-start | bytes 393224 | tf_op jit(solution)/shard_map/ppermute | solution.py:254
  16.0 0.7 %copy-start.1 = (s32[8]{0:T(128)S(1)}, s32[8]{0:T(128)}, u32[]{:S(2)}) copy-start(s32[8]{0:T(128)} %lengths.1) | copy-start | bytes 100
  16.0 0.7 %copy-start.2 = (s32[8]{0:T(128)S(1)}, s32[8]{0:T(128)}, u32[]{:S(2)}) copy-start(s32[8]{0:T(128)} %prefixes.1) | copy-start | bytes 100
  22.1 9.1 %collective-permute-start.6 = (bf16[2,2,128,128]{3,2,1,0:T(8,128)(2,1)S(1)}, bf16[2,2,128,128]{3,2,1,0:T(8,128)(2,1)S(1)}, u32[]{:S(2)}, u32[]{:S(2)}) collective-permute-start(bf16[2,2,128,128]{3,2,1,0:T(8,128)(2,1)S(1)} %get-tuple-element.27), channel_id=1, source_target_pairs={{8,0},{12,4},{16,8},{20,12},{24,16},{28,20},{9,1},{13,5},{17,9},{2... | collective-permute-start | bytes 393224 | tf_op jit(solution)/shard_map/ppermute | solution.py:241
  23.4 7.8 %collective-permute-start.7 = (bf16[32,16,128]{2,1,0:T(8,128)(2,1)S(1)}, bf16[32,16,128]{2,1,0:T(8,128)(2,1)S(1)}, u32[]{:S(2)}, u32[]{:S(2)}) collective-permute-start(bf16[32,16,128]{2,1,0:T(8,128)(2,1)S(1)} %get-tuple-element.28), channel_id=1, source_target_pairs={{0,3},{1,2},{2,1},{3,0},{4,7},{5,6},{6,5},{7,4},{8,11},{9,10},{10,... | collective-permute-start | bytes 393224 | tf_op jit(solution)/shard_map/ppermute | solution.py:254
  24.3 6.9 %collective-permute-start.8 = (bf16[2,2,128,128]{3,2,1,0:T(8,128)(2,1)S(1)}, bf16[2,2,128,128]{3,2,1,0:T(8,128)(2,1)S(1)}, u32[]{:S(2)}, u32[]{:S(2)}) collective-permute-start(bf16[2,2,128,128]{3,2,1,0:T(8,128)(2,1)S(1)} %get-tuple-element.29), channel_id=1, source_target_pairs={{0,4},{4,0},{8,12},{12,8},{16,20},{20,16},{24,28},{28,24},{1,5},{5... | collective-permute-start | bytes 393224 | tf_op jit(solution)/shard_map/ppermute | solution.py:250
  24.3 9.9 %collective-permute-start.9 = (bf16[2,2,128,128]{3,2,1,0:T(8,128)(2,1)S(1)}, bf16[2,2,128,128]{3,2,1,0:T(8,128)(2,1)S(1)}, u32[]{:S(2)}, u32[]{:S(2)}) collective-permute-start(bf16[2,2,128,128]{3,2,1,0:T(8,128)(2,1)S(1)} %get-tuple-element.30), channel_id=1, source_target_pairs={{0,0},{4,8},{8,4},{12,16},{16,12},{20,24},{24,20},{28,28},{1,1},{5... | collective-permute-start | bytes 393224 | tf_op jit(solution)/shard_map/ppermute | solution.py:250
  30.0 6.1 %collective-permute-start.10 = (bf16[32,16,128]{2,1,0:T(8,128)(2,1)S(1)}, bf16[32,16,128]{2,1,0:T(8,128)(2,1)S(1)}, u32[]{:S(2)}, u32[]{:S(2)}) collective-permute-start(bf16[32,16,128]{2,1,0:T(8,128)(2,1)S(1)} %get-tuple-element.31), channel_id=1, source_target_pairs={{0,2},{1,3},{2,0},{3,1},{4,6},{5,7},{6,4},{7,5},{8,10},{9,11},{10,... | collective-permute-start | bytes 393224 | tf_op jit(solution)/shard_map/ppermute | solution.py:254
  31.2 4.9 %collective-permute-start.11 = (bf16[32,16,128]{2,1,0:T(8,128)(2,1)S(1)}, bf16[32,16,128]{2,1,0:T(8,128)(2,1)S(1)}, u32[]{:S(2)}, u32[]{:S(2)}) collective-permute-start(bf16[32,16,128]{2,1,0:T(8,128)(2,1)S(1)} %get-tuple-element.32), channel_id=1, source_target_pairs={{0,1},{1,0},{2,3},{3,2},{4,5},{5,4},{6,7},{7,6},{8,9},{9,8},{10,11... | collective-permute-start | bytes 393224 | tf_op jit(solution)/shard_map/ppermute | solution.py:254

commit v6 on v5

--- a/solution.py
+++ b/solution.py
@@ -18,9 +18,9 @@
 _HBM = pl.BlockSpec(memory_space=pltpu.HBM)
 
 
-def order(parts):
-    masks = ["mask", *range(parts - 1, 0, -1)][1:]
-    return ["far", masks[0], "even", "odd"] + masks[1:]
+def stages(parts):
+    rest = list(range(parts - 1, 1, -1))
+    return [[0, 1], rest]
 
 
 def regroup(buf):
@@ -105,11 +105,13 @@
     return jnp.where(odd == 1, behind, ahead), jnp.where(odd == 1, ahead, behind)
 
 
-def grad_kernel(parts, lengths, prefixes, q_ref, cot_own, kv_own, *rest):
-    names = order(parts)
-    got, rest = dict(zip(names, rest)), rest[len(names) :]
-    dq_refs, rest = rest[:parts], rest[parts:]
-    own_out, far_out, even_out, odd_out, window, acc = rest
+def grad_kernel(masks, parts, is_first, is_last, lengths, prefixes, q_ref, *refs):
+    refs = list(refs)
+    kv_own, kv_even, kv_far, kv_odd = [refs.pop(0) for _ in range(4)]
+    cots = {mask: refs.pop(0) for mask in masks}
+    carried = None if is_first else refs.pop(0)
+    dqs = {mask: refs.pop(0) for mask in masks}
+    outs, (window, acc) = refs[:-2], refs[-2:]
     rows, heads, size = q_ref.shape
     tokens = rows // parts
     kv_heads = kv_own.shape[1]
@@ -122,19 +124,18 @@
     me = lax.axis_index("kvh")
 
     even_slot, odd_slot = neighbour_slots(shard)
-    slots = ((BACK, kv_own), (0, got["far"]), (even_slot, got["even"]), (odd_slot, got["odd"]))
-    for slot, ref in slots:
+    for slot, ref in ((BACK, kv_own), (0, kv_far), (even_slot, kv_even), (odd_slot, kv_odd)):
+        part = pl.ds(pl.multiple_of(slot * rows, rows), rows)
         for number in range(2):
             for group in range(kv_heads):
-                part = pl.ds(pl.multiple_of(slot * rows, rows), rows)
                 window[number, group, part] = ref[number, group]
-    acc[...] = jnp.zeros_like(acc)
+    acc[...] = jnp.zeros_like(acc) if is_first else carried[...]
 
     contract_last = (((1,), (1,)), ((), ()))
     contract_first = (((0,), (0,)), ((), ()))
     lane_token = lax.broadcasted_iota(jnp.int32, (1, lanes), 1) // group_size
     key_iota = lax.broadcasted_iota(jnp.int32, (reach, lanes), 0)
-    for mask in range(parts):
+    for mask in masks:
         first = pl.multiple_of((me ^ mask) * tokens, tokens)
         low, high = bounds(shard * rows + first + lane_token, lengths, prefixes)
         origin = (shard - BACK) * rows + first
@@ -146,7 +147,7 @@
             of_group = pl.ds(group * group_size, group_size)
             q = q_ref[pl.ds(first, tokens), of_group].astype(jnp.float32)
             q = q.reshape(lanes, size).astype(jnp.bfloat16)
-            cot = (got[mask] if mask else cot_own)[:, of_group].astype(jnp.float32)
+            cot = cots[mask][:, of_group].astype(jnp.float32)
             cot = cot.reshape(lanes, size).astype(jnp.bfloat16)
             k = window[0, group, here]
             v = window[1, group, here]
@@ -165,62 +166,79 @@
             acc[0, group, here] += jnp.dot(dscores, q, preferred_element_type=jnp.float32)
             dq = lax.dot_general(k, dscores, contract_first, preferred_element_type=jnp.float32)
             dq = jnp.transpose(dq * scale)
-            dq_refs[mask][:, of_group] = dq.reshape(tokens, group_size, size).astype(jnp.bfloat16)
-    for slot, ref in ((0, far_out), (even_slot, even_out), (odd_slot, odd_out), (BACK, own_out)):
+            dqs[mask][:, of_group] = dq.reshape(tokens, group_size, size).astype(jnp.bfloat16)
+    if not is_last:
+        outs[0][...] = acc[...]
+        return
+    for slot, ref in zip((BACK, 0, even_slot, odd_slot), outs):
+        part = pl.ds(pl.multiple_of(slot * rows, rows), rows)
         for group in range(kv_heads):
-            part = pl.ds(pl.multiple_of(slot * rows, rows), rows)
             ref[0, group] = (acc[0, group, part] * scale).astype(ref.dtype)
             ref[1, group] = acc[1, group, part].astype(ref.dtype)
 
 
-def gradients(lengths, prefixes, queries, cot_own, kv_own, got, parts):
+def gradients(masks, parts, lengths, prefixes, queries, cots, blocks, carried):
     rows, heads, size = queries.shape
-    kv_shape = got["far"].shape
+    is_last = masks == stages(parts)[-1]
+    kv_shape = blocks[0].shape
     kv_heads = kv_shape[1]
     span = (BACK + 1 + AHEAD) * rows
-    half = jax.ShapeDtypeStruct(kv_shape, jnp.bfloat16)
-    work = heads * rows * span
+    acc_shape = (2, kv_heads, span, size)
+    work = heads * rows // parts * span * len(masks)
+    outs = [pltpu.VMEM(cots[0].shape, jnp.bfloat16)] * len(masks)
+    if is_last:
+        outs += [pltpu.VMEM(kv_shape, jnp.float32)] + [pltpu.VMEM(kv_shape, jnp.bfloat16)] * 3
+    else:
+        outs += [pltpu.VMEM(acc_shape, jnp.float32)]
+    operands = [queries, blocks[0], blocks[2], blocks[1], blocks[3], *cots] + ([] if carried is None else [carried])
     outs = pl.pallas_call(
-        functools.partial(grad_kernel, parts),
-        out_shape=(jax.ShapeDtypeStruct(got[1].shape, jnp.bfloat16),) * parts
-        + (jax.ShapeDtypeStruct(kv_shape, jnp.float32), half, half, half),
-        in_specs=[_SMEM, _SMEM] + [_VMEM] * (parts + 5),
-        out_specs=(_VMEM,) * (parts + 4),
+        functools.partial(grad_kernel, masks, parts, carried is None, is_last),
+        out_shape=tuple(outs),
+        in_specs=[_SMEM, _SMEM] + [_VMEM] * len(operands),
+        out_specs=(_VMEM,) * len(outs),
         scratch_shapes=[
-            pltpu.VMEM((2, kv_heads, span, size), jnp.bfloat16),
-            pltpu.VMEM((2, kv_heads, span, size), jnp.float32),
+            pltpu.VMEM(acc_shape, jnp.bfloat16),
+            pltpu.VMEM(acc_shape, jnp.float32),
         ],
         compiler_params=pltpu.CompilerParams(vmem_limit_bytes=VMEM_BYTES),
         cost_estimate=pl.CostEstimate(
             flops=10 * work * size, bytes_accessed=4 * queries.size * 2, transcendentals=work
         ),
         name="gradients",
-    )(lengths, prefixes, queries, cot_own, kv_own, *[got[name] for name in order(parts)])
-    return outs[:parts], outs[parts:]
+    )(lengths, prefixes, *operands)
+    return outs[: len(masks)], outs[len(masks) :]
+
+
+def finish_order(parts):
+    return ["even", "far", parts - 1, "odd", *range(parts - 2, -1, -1), "own"]
 
 
 def finish_kernel(parts, *refs):
-    names = order(parts)
-    got, (dq_own, own, dq_out, dk_out, dv_out) = dict(zip(names, refs)), refs[len(names) :]
-    heads = dq_own.shape[1]
+    *refs, dq_out, dk_out, dv_out = refs
+    refs = dict(zip(finish_order(parts), refs))
+    dqs = [refs[mask] for mask in range(parts)]
+    own, far, even, odd = [refs[name] for name in ("own", "far", "even", "odd")]
+    heads = dqs[0].shape[1]
     me = lax.axis_index("kvh")
     for mask in range(parts):
         first = pl.multiple_of((me ^ mask) * heads, heads)
-        dq_out[:, pl.ds(first, heads), :] = (got[mask] if mask else dq_own)[...]
+        dq_out[:, pl.ds(first, heads), :] = dqs[mask][...]
     for number, ref in enumerate((dk_out, dv_out)):
         sums = []
         for group in range(ref.shape[1]):
             total = own[number, group]
-            for other in (got["far"], got["even"], got["odd"]):
+            for other in (far, even, odd):
                 total = total + other[number, group].astype(jnp.float32)
             sums.append(total)
         ref[...] = jnp.stack(sums, axis=1).astype(jnp.bfloat16)
 
 
-def finish(dq_own, own, got, parts):
-    rows, heads, size = dq_own.shape
-    _, kv_heads, kv_rows, _ = own.shape
+def finish(dqs, partials):
+    parts = len(dqs)
+    rows, heads, size = dqs[0].shape
+    _, kv_heads, kv_rows, _ = partials[0].shape
     kv_out = jax.ShapeDtypeStruct((kv_rows, kv_heads, size), jnp.bfloat16)
+    operands = dict(enumerate(dqs)) | dict(zip(("own", "far", "even", "odd"), partials))
     return pl.pallas_call(
         functools.partial(finish_kernel, parts),
         out_shape=(
@@ -232,13 +250,12 @@
         out_specs=(_VMEM,) * 3,
         compiler_params=pltpu.CompilerParams(vmem_limit_bytes=VMEM_BYTES),
         name="finish",
-    )(*[got[name] for name in order(parts)], dq_own, own)
+    )(*[operands[name] for name in finish_order(parts)])
 
 
 def shifted(block, distance):
-    devices = range(lax.axis_size("seq"))
-    route = [(i, i + distance) for i in devices if i + distance in devices]
-    return lax.ppermute(block, "seq", route)
+    count = lax.axis_size("seq")
+    return lax.ppermute(block, "seq", [(i, (i + distance) % count) for i in range(count)])
 
 
 def paired(block, first):
@@ -254,23 +271,25 @@
     return lax.ppermute(block, "kvh", [(i, i ^ mask) for i in range(lax.axis_size("kvh"))])
 
 
-def exchange(pieces, far, even, odd, distance):
-    got = {mask: swapped(piece, mask) for mask, piece in enumerate(pieces, 1)}
-    got["far"] = shifted(far, distance)
-    got["even"] = paired(even, 0)
-    got["odd"] = paired(odd, 1)
-    return got
+def neighbours(far, even, odd, distance):
+    return [shifted(far, distance), paired(even, 0), paired(odd, 1)]
 
 
 def local(queries, keys, values, output_gradient, doc_lengths, prefix_lengths):
     parts = lax.axis_size("kvh")
     kv, cots = prepare(output_gradient, keys, values, parts)
-    got = exchange(cots[1:], *kv[1:], BACK)
-    dqs, (own, far, even, odd) = gradients(
-        doc_lengths, prefix_lengths, queries, cots[0], kv[0], got, parts
-    )
-    got = exchange(dqs[1:], far, even, odd, -BACK)
-    return finish(dqs[0], own, got, parts)
+    blocks = [kv[0]] + neighbours(*kv[1:], BACK)
+    cots = [cots[0]] + [swapped(cots[mask], mask) for mask in range(1, parts)]
+    dqs, carried = {}, [None]
+    for masks in stages(parts):
+        found, carried = gradients(
+            masks, parts, doc_lengths, prefix_lengths, queries,
+            [cots[mask] for mask in masks], blocks, carried[0],
+        )
+        for mask, dq in zip(masks, found):
+            dqs[mask] = swapped(dq, mask) if mask else dq
+    partials = [carried[0]] + neighbours(*carried[1:], -BACK)
+    return finish([dqs[mask] for mask in range(parts)], partials)
 
 
 def solution(mesh):

time: 37.3 us -> 34.5 us (0.925)
  the two profiles are of different devices: /device:TPU:6 before, /device:TPU:0 now
where the time goes in v6:
time: 34.5 us; the launch traced here: 34.1 us
  starting transfers between devices  16.2 us (47%)
  Pallas kernels  8.59 us (25%)
  waiting for transfers between devices  7.88 us (23%)
  between operations  0.72 us (2%)
  local copies, waits for them, and re-layouts  0.66 us (2%)
    ppermute x4, starting transfers between devices, paired(): return lax.ppermute(block, 'seq', route)  8.65 us
    pallas_call x2, Pallas kernels, gradients(): pl.pallas_call(functools.partial(grad_kernel, masks, parts, carried is No...  6.29 us
    ppermute x6, starting transfers between devices, swapped(): lax.ppermute(block, 'kvh', [(i, i ^ mask) for i in range(lax.axis_size('k...  4.94 us
    ppermute x6, waiting for transfers between devices, swapped(): lax.ppermute(block, 'kvh', [(i, i ^ mask) for i in range(lax.axis_size('k...  4.9 us
    ppermute x2, waiting for transfers between devices, shifted(): lax.ppermute(block, 'seq', [(i, (i + distance) % count) for i in range(co...  2.97 us
    ppermute x2, starting transfers between devices, shifted(): lax.ppermute(block, 'seq', [(i, (i + distance) % count) for i in range(co...  2.62 us
    pallas_call x1, Pallas kernels, prepare(): pl.pallas_call(functools.partial(prep_kernel, parts), out_shape=(block,)...  1.28 us
    pallas_call x1, Pallas kernels, finish(): pl.pallas_call(functools.partial(finish_kernel, parts), out_shape=(jax.Sh...  1.02 us
  transfers between devices with their start and end apart: 12, of which 5 were waited for; matrix products, arithmetic and copies ran while one was open for 0% of the time, Pallas kernels for 9%

profile of v6, /device:TPU:0, one launch (start us, length us, event | category | flops | bytes accessed | tf_op | source)
XLA Modules:
  0.0 34.1 jit_solution(11174936470433702184)
XLA Ops:
  0.6 0.0 copy-start
  0.6 1.3 %prepare.1 = (bf16[2,2,128,128]{3,2,1,0:T(8,128)(2,1)S(1)}, bf16[2,2,128,128]{3,2,1,0:T(8,128)(2,1)S(1)}, bf16[2,2,128,128]{3,2,1,0:T(8,128)(2,1)S(1)}, bf16[2,2...) custom-call(bf16[32,64,128]{2,1,0:T(8,128)(2,1)} %cot_ref.1, ...), custom_call_target="tpu_custom_call" | custom-call | tf_op jit(solution)/shard_map/prepare/pallas_call | solution.py:66
  1.9 3.0 %collective-permute-start = (bf16[2,2,128,128]{3,2,1,0:T(8,128)(2,1)S(1)}, bf16[2,2,128,128]{3,2,1,0:T(8,128)(2,1)S(1)}, u32[]{:S(2)}, u32[]{:S(2)}) collective-permute-start(bf16[2,2,128,128]{3,2,1,0:T(8,128)(2,1)S(1)} %get-tuple-element.21), channel_id=1, source_target_pairs={{0,4},{4,0},{8,12},{12,8},{16,20},{20,16},{24,28},{28,24},{1,5},{5... | collective-permute-start | bytes 393224 | tf_op jit(solution)/shard_map/ppermute | solution.py:267
  4.9 1.6 %collective-permute-start.1 = (bf16[2,2,128,128]{3,2,1,0:T(8,128)(2,1)S(1)}, bf16[2,2,128,128]{3,2,1,0:T(8,128)(2,1)S(1)}, u32[]{:S(2)}, u32[]{:S(2)}) collective-permute-start(bf16[2,2,128,128]{3,2,1,0:T(8,128)(2,1)S(1)} %get-tuple-element.22), channel_id=1, source_target_pairs={{0,8},{4,12},{8,16},{12,20},{16,24},{20,28},{24,0},{28,4},{1,9},{5... | collective-permute-start | bytes 393224 | tf_op jit(solution)/shard_map/ppermute | solution.py:258
  6.5 0.7 %collective-permute-start.2 = (bf16[2,2,128,128]{3,2,1,0:T(8,128)(2,1)S(1)}, bf16[2,2,128,128]{3,2,1,0:T(8,128)(2,1)S(1)}, u32[]{:S(2)}, u32[]{:S(2)}) collective-permute-start(bf16[2,2,128,128]{3,2,1,0:T(8,128)(2,1)S(1)} %get-tuple-element.23), channel_id=1, source_target_pairs={{0,0},{4,8},{8,4},{12,16},{16,12},{20,24},{24,20},{28,28},{1,1},{5... | collective-permute-start | bytes 393224 | tf_op jit(solution)/shard_map/ppermute | solution.py:267
  7.2 0.1 collective-permute-start.5
  7.2 1.6 %collective-permute-start.3 = (bf16[32,16,128]{2,1,0:T(8,128)(2,1)S(1)}, bf16[32,16,128]{2,1,0:T(8,128)(2,1)S(1)}, u32[]{:S(2)}, u32[]{:S(2)}) collective-permute-start(bf16[32,16,128]{2,1,0:T(8,128)(2,1)S(1)} %get-tuple-element.24), channel_id=1, source_target_pairs={{0,3},{1,2},{2,1},{3,0},{4,7},{5,6},{6,5},{7,4},{8,11},{9,10},{10,... | collective-permute-start | bytes 393224 | tf_op jit(solution)/shard_map/ppermute | solution.py:271
  8.9 0.0 collective-permute-done.refs_1_
  8.9 1.3 %collective-permute-start.4 = (bf16[32,16,128]{2,1,0:T(8,128)(2,1)S(1)}, bf16[32,16,128]{2,1,0:T(8,128)(2,1)S(1)}, u32[]{:S(2)}, u32[]{:S(2)}) collective-permute-start(bf16[32,16,128]{2,1,0:T(8,128)(2,1)S(1)} %get-tuple-element.25), channel_id=1, source_target_pairs={{0,2},{1,3},{2,0},{3,1},{4,6},{5,7},{6,4},{7,5},{8,10},{9,11},{10,... | collective-permute-start | bytes 393224 | tf_op jit(solution)/shard_map/ppermute | solution.py:271
  10.2 1.6 %collective-permute-done.1.refs_2_ = bf16[2,2,128,128]{3,2,1,0:T(8,128)(2,1)S(1)} collective-permute-done((bf16[2,2,128,128]{3,2,1,0:T(8,128)(2,1)S(1)}, bf16[2,2,128,128]{3,2,1,0:T(8,128)(2,1)S(1)}, u32[]{:S(2)}, u32[]{:S(2)}) %collective-permute-start.1) | collective-permute-done | bytes 131104 | tf_op jit(solution)/shard_map/ppermute | solution.py:258
  11.8 0.0 collective-permute-done.2.refs_3_
  11.8 0.0 collective-permute-done.5.refs_5_
  11.8 0.0 copy-start.1
  11.9 0.0 copy-start.2
  11.9 0.0 copy-done
  11.9 0.6 %copy-done.1 = s32[8]{0:T(128)S(1)} copy-done((s32[8]{0:T(128)S(1)}, s32[8]{0:T(128)}, u32[]{:S(2)}) %copy-start.1) | copy-done | bytes 56
  12.5 0.0 copy-done.2
  12.5 3.2 %gradients.2 = (bf16[32,16,128]{2,1,0:T(8,128)(2,1)S(1)}, bf16[32,16,128]{2,1,0:T(8,128)(2,1)S(1)}, f32[2,2,512,128]{3,2,1,0:T(8,128)S(1)}) custom-call(s32[8]{0:T(128)S(1)} %copy-done.1, s32[8]{0:T(128)S(1)} %copy-done.2, bf16[128,16,128]{2,1,0:T(8,128)(2,1)S(1)} %copy-done, bf16[2,2,128,128]{3,2,1,0:T(8,128)(2,1)S(1)} %get-tuple-element.20.refs_0_, ...), custom_call_target="tpu_custom_call" | custom-call | flops 671088640 | bytes 2097152 | tf_op jit(solution)/shard_map/gradients/pallas_call | solution.py:194
  15.7 0.0 collective-permute-done.3.refs_4_
  15.7 0.2 collective-permute-done.4.refs_5_
  15.9 3.1 %gradients.3 = (bf16[32,16,128]{2,1,0:T(8,128)(2,1)S(1)}, bf16[32,16,128]{2,1,0:T(8,128)(2,1)S(1)}, f32[2,2,128,128]{3,2,1,0:T(8,128)S(1)}, bf16[2,2,128,128]{3,...) custom-call(s32[8]{0:T(128)S(1)} %copy-done.1, s32[8]{0:T(128)S(1)} %copy-done.2, ...), custom_call_target="tpu_custom_call" | custom-call | flops 671088640 | bytes 2097152 | tf_op jit(solution)/shard_map/gradients/pallas_call | solution.py:194
  19.0 4.3 %collective-permute-start.6 = (bf16[2,2,128,128]{3,2,1,0:T(8,128)(2,1)S(1)}, bf16[2,2,128,128]{3,2,1,0:T(8,128)(2,1)S(1)}, u32[]{:S(2)}, u32[]{:S(2)}) collective-permute-start(bf16[2,2,128,128]{3,2,1,0:T(8,128)(2,1)S(1)} %get-tuple-element.29), channel_id=1, source_target_pairs={{0,4},{4,0},{8,12},{12,8},{16,20},{20,16},{24,28},{28,24},{1,5},{5... | collective-permute-start | bytes 393224 | tf_op jit(solution)/shard_map/ppermute | solution.py:267
  23.4 1.0 %collective-permute-start.7 = (bf16[2,2,128,128]{3,2,1,0:T(8,128)(2,1)S(1)}, bf16[2,2,128,128]{3,2,1,0:T(8,128)(2,1)S(1)}, u32[]{:S(2)}, u32[]{:S(2)}) collective-permute-start(bf16[2,2,128,128]{3,2,1,0:T(8,128)(2,1)S(1)} %get-tuple-element.30), channel_id=1, source_target_pairs={{0,24},{4,28},{8,0},{12,4},{16,8},{20,12},{24,16},{28,20},{1,25},{... | collective-permute-start | bytes 393224 | tf_op jit(solution)/shard_map/ppermute | solution.py:258
  24.4 0.4 %collective-permute-start.8 = (bf16[32,16,128]{2,1,0:T(8,128)(2,1)S(1)}, bf16[32,16,128]{2,1,0:T(8,128)(2,1)S(1)}, u32[]{:S(2)}, u32[]{:S(2)}) collective-permute-start(bf16[32,16,128]{2,1,0:T(8,128)(2,1)S(1)} %get-tuple-element.31), channel_id=1, source_target_pairs={{0,3},{1,2},{2,1},{3,0},{4,7},{5,6},{6,5},{7,4},{8,11},{9,10},{10,... | collective-permute-start | bytes 393224 | tf_op jit(solution)/shard_map/ppermute | solution.py:271
  24.8 0.7 %collective-permute-start.9 = (bf16[2,2,128,128]{3,2,1,0:T(8,128)(2,1)S(1)}, bf16[2,2,128,128]{3,2,1,0:T(8,128)(2,1)S(1)}, u32[]{:S(2)}, u32[]{:S(2)}) collective-permute-start(bf16[2,2,128,128]{3,2,1,0:T(8,128)(2,1)S(1)} %get-tuple-element.32), channel_id=1, source_target_pairs={{0,0},{4,8},{8,4},{12,16},{16,12},{20,24},{24,20},{28,28},{1,1},{5... | collective-permute-start | bytes 393224 | tf_op jit(solution)/shard_map/ppermute | solution.py:267
  25.5 1.2 %collective-permute-start.10 = (bf16[32,16,128]{2,1,0:T(8,128)(2,1)S(1)}, bf16[32,16,128]{2,1,0:T(8,128)(2,1)S(1)}, u32[]{:S(2)}, u32[]{:S(2)}) collective-permute-start(bf16[32,16,128]{2,1,0:T(8,128)(2,1)S(1)} %get-tuple-element.33), channel_id=1, source_target_pairs={{0,2},{1,3},{2,0},{3,1},{4,6},{5,7},{6,4},{7,5},{8,10},{9,11},{10,... | collective-permute-start | bytes 393224 | tf_op jit(solution)/shard_map/ppermute | solution.py:271
  26.7 0.0 collective-permute-done.6.refs_0_
  26.7 0.3 collective-permute-start.11
  27.0 1.3 %collective-permute-done.7.refs_1_ = bf16[2,2,128,128]{3,2,1,0:T(8,128)(2,1)S(1)} collective-permute-done((bf16[2,2,128,128]{3,2,1,0:T(8,128)(2,1)S(1)}, bf16[2,2,128,128]{3,2,1,0:T(8,128)(2,1)S(1)}, u32[]{:S(2)}, u32[]{:S(2)}) %collective-permute-start.7) | collective-permute-done | bytes 131104 | tf_op jit(solution)/shard_map/ppermute | solution.py:258
  28.4 1.8 %collective-permute-done.8.refs_2_ = bf16[32,16,128]{2,1,0:T(8,128)(2,1)S(1)} collective-permute-done((bf16[32,16,128]{2,1,0:T(8,128)(2,1)S(1)}, bf16[32,16,128]{2,1,0:T(8,128)(2,1)S(1)}, u32[]{:S(2)}, u32[]{:S(2)}) %collective-permute-start.8) | collective-permute-done | bytes 131104 | tf_op jit(solution)/shard_map/ppermute | solution.py:271
  30.2 0.0 collective-permute-done.9.refs_3_
  30.2 2.9 %collective-permute-done.10.refs_4_ = bf16[32,16,128]{2,1,0:T(8,128)(2,1)S(1)} collective-permute-done((bf16[32,16,128]{2,1,0:T(8,128)(2,1)S(1)}, bf16[32,16,128]{2,1,0:T(8,128)(2,1)S(1)}, u32[]{:S(2)}, u32[]{:S(2)}) %collective-permute-start.10) | collective-permute-done | bytes 131104 | tf_op jit(solution)/shard_map/ppermute | solution.py:271
  33.0 0.0 collective-permute-done.11.refs_5_
  33.0 1.0 %finish.1 = (bf16[32,64,128]{2,1,0:T(8,128)(2,1)}, bf16[128,2,128]{2,1,0:T(2,128)(2,1)}, bf16[128,2,128]{2,1,0:T(2,128)(2,1)}) custom-call(bf16[2,2,128,128]{3,2,1,0:T(8,128)(2,1)S(1)} %collective-permute-done.6.refs_0_, bf16[2,2,128,128]{3,2,1,0:T(8,128)(2,1)S(1)} %collective-permute-done.7.refs_1_, ...), custom_call_target="tpu_custom_call" | custom-call | tf_op jit(solution)/shard_map/finish/pallas_call | solution.py:242
Async XLA Ops:
  0.6 11.2 %copy-start = (bf16[128,16,128]{2,1,0:T(8,128)(2,1)S(1)}, bf16[128,16,128]{2,1,0:T(8,128)(2,1)}, u32[]{:S(2)}) copy-start(bf16[128,16,128]{2,1,0:T(8,128)(2,1)} %q_ref.3) | copy-start | bytes 1572868
  1.9 7.0 %collective-permute-start = (bf16[2,2,128,128]{3,2,1,0:T(8,128)(2,1)S(1)}, bf16[2,2,128,128]{3,2,1,0:T(8,128)(2,1)S(1)}, u32[]{:S(2)}, u32[]{:S(2)}) collective-permute-start(bf16[2,2,128,128]{3,2,1,0:T(8,128)(2,1)S(1)} %get-tuple-element.21), channel_id=1, source_target_pairs={{0,4},{4,0},{8,12},{12,8},{16,20},{20,16},{24,28},{28,24},{1,5},{5... | collective-permute-start | bytes 393224 | tf_op jit(solution)/shard_map/ppermute | solution.py:267
  4.9 6.9 %collective-permute-start.1 = (bf16[2,2,128,128]{3,2,1,0:T(8,128)(2,1)S(1)}, bf16[2,2,128,128]{3,2,1,0:T(8,128)(2,1)S(1)}, u32[]{:S(2)}, u32[]{:S(2)}) collective-permute-start(bf16[2,2,128,128]{3,2,1,0:T(8,128)(2,1)S(1)} %get-tuple-element.22), channel_id=1, source_target_pairs={{0,8},{4,12},{8,16},{12,20},{16,24},{20,28},{24,0},{28,4},{1,9},{5... | collective-permute-start | bytes 393224 | tf_op jit(solution)/shard_map/ppermute | solution.py:258
  6.5 5.3 %collective-permute-start.2 = (bf16[2,2,128,128]{3,2,1,0:T(8,128)(2,1)S(1)}, bf16[2,2,128,128]{3,2,1,0:T(8,128)(2,1)S(1)}, u32[]{:S(2)}, u32[]{:S(2)}) collective-permute-start(bf16[2,2,128,128]{3,2,1,0:T(8,128)(2,1)S(1)} %get-tuple-element.23), channel_id=1, source_target_pairs={{0,0},{4,8},{8,4},{12,16},{16,12},{20,24},{24,20},{28,28},{1,1},{5... | collective-permute-start | bytes 393224 | tf_op jit(solution)/shard_map/ppermute | solution.py:267
  7.2 4.7 %collective-permute-start.5 = (bf16[32,16,128]{2,1,0:T(8,128)(2,1)S(1)}, bf16[32,16,128]{2,1,0:T(8,128)(2,1)S(1)}, u32[]{:S(2)}, u32[]{:S(2)}) collective-permute-start(bf16[32,16,128]{2,1,0:T(8,128)(2,1)S(1)} %get-tuple-element.27), channel_id=1, source_target_pairs={{0,1},{1,0},{2,3},{3,2},{4,5},{5,4},{6,7},{7,6},{8,9},{9,8},{10,11... | collective-permute-start | bytes 393224 | tf_op jit(solution)/shard_map/ppermute | solution.py:271
  7.2 8.5 %collective-permute-start.3 = (bf16[32,16,128]{2,1,0:T(8,128)(2,1)S(1)}, bf16[32,16,128]{2,1,0:T(8,128)(2,1)S(1)}, u32[]{:S(2)}, u32[]{:S(2)}) collective-permute-start(bf16[32,16,128]{2,1,0:T(8,128)(2,1)S(1)} %get-tuple-element.24), channel_id=1, source_target_pairs={{0,3},{1,2},{2,1},{3,0},{4,7},{5,6},{6,5},{7,4},{8,11},{9,10},{10,... | collective-permute-start | bytes 393224 | tf_op jit(solution)/shard_map/ppermute | solution.py:271
  8.9 7.0 %collective-permute-start.4 = (bf16[32,16,128]{2,1,0:T(8,128)(2,1)S(1)}, bf16[32,16,128]{2,1,0:T(8,128)(2,1)S(1)}, u32[]{:S(2)}, u32[]{:S(2)}) collective-permute-start(bf16[32,16,128]{2,1,0:T(8,128)(2,1)S(1)} %get-tuple-element.25), channel_id=1, source_target_pairs={{0,2},{1,3},{2,0},{3,1},{4,6},{5,7},{6,4},{7,5},{8,10},{9,11},{10,... | collective-permute-start | bytes 393224 | tf_op jit(solution)/shard_map/ppermute | solution.py:271
  11.8 0.7 %copy-start.1 = (s32[8]{0:T(128)S(1)}, s32[8]{0:T(128)}, u32[]{:S(2)}) copy-start(s32[8]{0:T(128)} %lengths.3) | copy-start | bytes 100
  11.9 0.7 %copy-start.2 = (s32[8]{0:T(128)S(1)}, s32[8]{0:T(128)}, u32[]{:S(2)}) copy-start(s32[8]{0:T(128)} %prefixes.3) | copy-start | bytes 100
  19.0 7.6 %collective-permute-start.6 = (bf16[2,2,128,128]{3,2,1,0:T(8,128)(2,1)S(1)}, bf16[2,2,128,128]{3,2,1,0:T(8,128)(2,1)S(1)}, u32[]{:S(2)}, u32[]{:S(2)}) collective-permute-start(bf16[2,2,128,128]{3,2,1,0:T(8,128)(2,1)S(1)} %get-tuple-element.29), channel_id=1, source_target_pairs={{0,4},{4,0},{8,12},{12,8},{16,20},{20,16},{24,28},{28,24},{1,5},{5... | collective-permute-start | bytes 393224 | tf_op jit(solution)/shard_map/ppermute | solution.py:267
  23.4 5.0 %collective-permute-start.7 = (bf16[2,2,128,128]{3,2,1,0:T(8,128)(2,1)S(1)}, bf16[2,2,128,128]{3,2,1,0:T(8,128)(2,1)S(1)}, u32[]{:S(2)}, u32[]{:S(2)}) collective-permute-start(bf16[2,2,128,128]{3,2,1,0:T(8,128)(2,1)S(1)} %get-tuple-element.30), channel_id=1, source_target_pairs={{0,24},{4,28},{8,0},{12,4},{16,8},{20,12},{24,16},{28,20},{1,25},{... | collective-permute-start | bytes 393224 | tf_op jit(solution)/shard_map/ppermute | solution.py:258
  24.4 5.7 %collective-permute-start.8 = (bf16[32,16,128]{2,1,0:T(8,128)(2,1)S(1)}, bf16[32,16,128]{2,1,0:T(8,128)(2,1)S(1)}, u32[]{:S(2)}, u32[]{:S(2)}) collective-permute-start(bf16[32,16,128]{2,1,0:T(8,128)(2,1)S(1)} %get-tuple-element.31), channel_id=1, source_target_pairs={{0,3},{1,2},{2,1},{3,0},{4,7},{5,6},{6,5},{7,4},{8,11},{9,10},{10,... | collective-permute-start | bytes 393224 | tf_op jit(solution)/shard_map/ppermute | solution.py:271
  24.8 5.3 %collective-permute-start.9 = (bf16[2,2,128,128]{3,2,1,0:T(8,128)(2,1)S(1)}, bf16[2,2,128,128]{3,2,1,0:T(8,128)(2,1)S(1)}, u32[]{:S(2)}, u32[]{:S(2)}) collective-permute-start(bf16[2,2,128,128]{3,2,1,0:T(8,128)(2,1)S(1)} %get-tuple-element.32), channel_id=1, source_target_pairs={{0,0},{4,8},{8,4},{12,16},{16,12},{20,24},{24,20},{28,28},{1,1},{5... | collective-permute-start | bytes 393224 | tf_op jit(solution)/shard_map/ppermute | solution.py:267
  25.5 7.5 %collective-permute-start.10 = (bf16[32,16,128]{2,1,0:T(8,128)(2,1)S(1)}, bf16[32,16,128]{2,1,0:T(8,128)(2,1)S(1)}, u32[]{:S(2)}, u32[]{:S(2)}) collective-permute-start(bf16[32,16,128]{2,1,0:T(8,128)(2,1)S(1)} %get-tuple-element.33), channel_id=1, source_target_pairs={{0,2},{1,3},{2,0},{3,1},{4,6},{5,7},{6,4},{7,5},{8,10},{9,11},{10,... | collective-permute-start | bytes 393224 | tf_op jit(solution)/shard_map/ppermute | solution.py:271
  26.7 6.4 %collective-permute-start.11 = (bf16[32,16,128]{2,1,0:T(8,128)(2,1)S(1)}, bf16[32,16,128]{2,1,0:T(8,128)(2,1)S(1)}, u32[]{:S(2)}, u32[]{:S(2)}) collective-permute-start(bf16[32,16,128]{2,1,0:T(8,128)(2,1)S(1)} %get-tuple-element.34), channel_id=1, source_target_pairs={{0,1},{1,0},{2,3},{3,2},{4,5},{5,4},{6,7},{7,6},{8,9},{9,8},{10,11... | collective-permute-start | bytes 393224 | tf_op jit(solution)/shard_map/ppermute | solution.py:271

commit v7 on v6

--- a/solution.py
+++ b/solution.py
@@ -28,10 +28,17 @@
     return [wide[:, group, :].astype(jnp.bfloat16) for group in range(buf.shape[1])]
 
 
-def prep_kernel(parts, cot_ref, key_ref, value_ref, *rest):
-    kv_outs, cot_outs, (key_buf, value_buf, sems) = rest[:4], rest[4 : parts + 4], rest[parts + 4 :]
+def prep_kernel(parts, lengths_ref, prefixes_ref, cot_ref, key_ref, value_ref, *rest):
+    kv_outs, cot_outs, rest = rest[:4], rest[4 : parts + 4], rest[parts + 4 :]
+    range_out, key_buf, value_buf, lengths, prefixes, sems, scalar_sems = rest
     heads = cot_ref.shape[1] // parts
     me = lax.axis_index("kvh")
+    scalars = [
+        pltpu.make_async_copy(lengths_ref, lengths, scalar_sems.at[0]),
+        pltpu.make_async_copy(prefixes_ref, prefixes, scalar_sems.at[1]),
+    ]
+    for copy in scalars:
+        copy.start()
     loads = []
     for number, (ref, buf) in enumerate(((key_ref, key_buf), (value_ref, value_buf))):
         loads.append(pltpu.make_async_copy(ref, buf, sems.at[number]))
@@ -50,33 +57,50 @@
         for group, block in enumerate(regroup(buf)):
             for kv_out in kv_outs:
                 kv_out[number, group] = block
+    for copy in scalars:
+        copy.wait()
+    rows = key_buf.shape[0]
+    tokens = rows // parts
+    lanes = range_out.shape[2]
+    lane_token = lax.broadcasted_iota(jnp.int32, (1, lanes), 1) // (lanes // tokens)
+    shard = lax.axis_index("seq")
+    for mask in range(parts):
+        first = (me ^ mask) * tokens
+        low, high = bounds(shard * rows + first + lane_token, lengths, prefixes)
+        origin = (shard - BACK) * rows + first
+        range_out[mask, 0:1, :] = low - origin
+        range_out[mask, 1:2, :] = high - origin
     for copy in copies:
         copy.wait()
 
 
-def prepare(cotangent, keys, values, parts):
+def prepare(lengths, prefixes, cotangent, keys, values, parts):
     rows, heads, size = cotangent.shape
     kv_rows, kv_heads, _ = keys.shape
+    lanes = kv_rows // parts * (heads // parts // kv_heads)
     piece = pltpu.VMEM((rows, heads // parts, size), jnp.bfloat16)
     block = pltpu.VMEM((2, kv_heads, kv_rows, size), jnp.bfloat16)
     operands = [
         pltpu.with_memory_space_constraint(array, pltpu.HBM)
-        for array in (cotangent, keys, values)
+        for array in (lengths, prefixes, cotangent, keys, values)
     ]
     outs = pl.pallas_call(
         functools.partial(prep_kernel, parts),
-        out_shape=(block,) * 4 + (piece,) * parts,
-        in_specs=[_HBM] * 3,
-        out_specs=(_VMEM,) * (parts + 4),
+        out_shape=(block,) * 4 + (piece,) * parts + (pltpu.VMEM((parts, 2, lanes), jnp.int32),),
+        in_specs=[_HBM] * 5,
+        out_specs=(_VMEM,) * (parts + 5),
         scratch_shapes=[
             pltpu.VMEM(keys.shape, jnp.bfloat16),
             pltpu.VMEM(values.shape, jnp.bfloat16),
+            pltpu.SMEM(lengths.shape, jnp.int32),
+            pltpu.SMEM(prefixes.shape, jnp.int32),
             pltpu.SemaphoreType.DMA((parts + 2,)),
+            pltpu.SemaphoreType.DMA((2,)),
         ],
         compiler_params=pltpu.CompilerParams(vmem_limit_bytes=VMEM_BYTES),
         name="prepare",
     )(*operands)
-    return outs[:4], outs[4:]
+    return outs[:4], outs[4:-1], outs[-1]
 
 
 def bounds(position, lengths, prefixes):
@@ -105,13 +129,13 @@
     return jnp.where(odd == 1, behind, ahead), jnp.where(odd == 1, ahead, behind)
 
 
-def grad_kernel(masks, parts, is_first, is_last, lengths, prefixes, q_ref, *refs):
+def grad_kernel(masks, parts, is_first, is_last, range_ref, q_ref, *refs):
     refs = list(refs)
     kv_own, kv_even, kv_far, kv_odd = [refs.pop(0) for _ in range(4)]
-    cots = {mask: refs.pop(0) for mask in masks}
+    cots = [refs.pop(0) for _ in masks]
     carried = None if is_first else refs.pop(0)
-    dqs = {mask: refs.pop(0) for mask in masks}
-    outs, (window, acc) = refs[:-2], refs[-2:]
+    dqs = [refs.pop(0) for _ in masks]
+    outs, (window, acc, q_rows, cot_rows, dq_rows) = refs[:-5], refs[-5:]
     rows, heads, size = q_ref.shape
     tokens = rows // parts
     kv_heads = kv_own.shape[1]
@@ -130,43 +154,51 @@
             for group in range(kv_heads):
                 window[number, group, part] = ref[number, group]
     acc[...] = jnp.zeros_like(acc) if is_first else carried[...]
+    for place, mask in enumerate(masks):
+        first = pl.multiple_of((me ^ mask) * tokens, tokens)
+        for group in range(kv_heads):
+            of_group = pl.ds(group * group_size, group_size)
+            item = place * kv_heads + group
+            q = q_ref[pl.ds(first, tokens), of_group].astype(jnp.float32)
+            q_rows[item] = q.reshape(lanes, size).astype(jnp.bfloat16)
+            cot = cots[place][:, of_group].astype(jnp.float32)
+            cot_rows[item] = cot.reshape(lanes, size).astype(jnp.bfloat16)
 
     contract_last = (((1,), (1,)), ((), ()))
     contract_first = (((0,), (0,)), ((), ()))
-    lane_token = lax.broadcasted_iota(jnp.int32, (1, lanes), 1) // group_size
     key_iota = lax.broadcasted_iota(jnp.int32, (reach, lanes), 0)
-    for mask in masks:
-        first = pl.multiple_of((me ^ mask) * tokens, tokens)
-        low, high = bounds(shard * rows + first + lane_token, lengths, prefixes)
-        origin = (shard - BACK) * rows + first
-        low = low - origin
-        high = high - origin
+    step = masks[1] - masks[0] if len(masks) > 1 else 0
+
+    def work(item, _):
+        group = lax.rem(item, kv_heads)
+        mask = masks[0] + step * lax.div(item, kv_heads)
+        here = pl.ds(pl.multiple_of((me ^ mask) * tokens, tokens), reach)
+        low, high = range_ref[mask, 0:1, :], range_ref[mask, 1:2, :]
         visible = (key_iota >= low) & (key_iota < high)
-        here = pl.ds(first, reach)
+        q, cot = q_rows[item], cot_rows[item]
+        k, v = window[0, group, here], window[1, group, here]
+        scores = lax.dot_general(k, q, contract_last, preferred_element_type=jnp.float32)
+        scores = jnp.where(visible, scores * (scale * LOG2E), NEG)
+        top = jnp.max(scores, axis=0, keepdims=True)
+        expo = jnp.exp2(scores - top)
+        total = jnp.sum(expo, axis=0, keepdims=True)
+        probs = expo * (1.0 / total)
+        dprobs = lax.dot_general(v, cot, contract_last, preferred_element_type=jnp.float32)
+        delta = jnp.sum(probs * dprobs, axis=0, keepdims=True)
+        dscores = (probs * (dprobs - delta)).astype(jnp.bfloat16)
+        acc[1, group, here] += jnp.dot(
+            probs.astype(jnp.bfloat16), cot, preferred_element_type=jnp.float32
+        )
+        acc[0, group, here] += jnp.dot(dscores, q, preferred_element_type=jnp.float32)
+        dq = lax.dot_general(k, dscores, contract_first, preferred_element_type=jnp.float32)
+        dq_rows[item] = jnp.transpose(dq * scale)
+        return 0
+
+    lax.fori_loop(0, len(masks) * kv_heads, work, 0)
+    for place in range(len(masks)):
         for group in range(kv_heads):
-            of_group = pl.ds(group * group_size, group_size)
-            q = q_ref[pl.ds(first, tokens), of_group].astype(jnp.float32)
-            q = q.reshape(lanes, size).astype(jnp.bfloat16)
-            cot = cots[mask][:, of_group].astype(jnp.float32)
-            cot = cot.reshape(lanes, size).astype(jnp.bfloat16)
-            k = window[0, group, here]
-            v = window[1, group, here]
-            scores = lax.dot_general(k, q, contract_last, preferred_element_type=jnp.float32)
-            scores = jnp.where(visible, scores * (scale * LOG2E), NEG)
-            top = jnp.max(scores, axis=0, keepdims=True)
-            expo = jnp.exp2(scores - top)
-            total = jnp.sum(expo, axis=0, keepdims=True)
-            probs = expo * (1.0 / total)
-            dprobs = lax.dot_general(v, cot, contract_last, preferred_element_type=jnp.float32)
-            delta = jnp.sum(probs * dprobs, axis=0, keepdims=True)
-            dscores = (probs * (dprobs - delta)).astype(jnp.bfloat16)
-            acc[1, group, here] += jnp.dot(
-                probs.astype(jnp.bfloat16), cot, preferred_element_type=jnp.float32
-            )
-            acc[0, group, here] += jnp.dot(dscores, q, preferred_element_type=jnp.float32)
-            dq = lax.dot_general(k, dscores, contract_first, preferred_element_type=jnp.float32)
-            dq = jnp.transpose(dq * scale)
-            dqs[mask][:, of_group] = dq.reshape(tokens, group_size, size).astype(jnp.bfloat16)
+            dq = dq_rows[place * kv_heads + group].reshape(tokens, group_size, size)
+            dqs[place][:, pl.ds(group * group_size, group_size)] = dq.astype(jnp.bfloat16)
     if not is_last:
         outs[0][...] = acc[...]
         return
@@ -177,35 +209,41 @@
             ref[1, group] = acc[1, group, part].astype(ref.dtype)
 
 
-def gradients(masks, parts, lengths, prefixes, queries, cots, blocks, carried):
+def gradients(masks, parts, ranges, queries, cots, blocks, carried):
     rows, heads, size = queries.shape
     is_last = masks == stages(parts)[-1]
     kv_shape = blocks[0].shape
     kv_heads = kv_shape[1]
     span = (BACK + 1 + AHEAD) * rows
     acc_shape = (2, kv_heads, span, size)
+    row_shape = (len(masks) * kv_heads, rows // parts * (heads // kv_heads), size)
     work = heads * rows // parts * span * len(masks)
     outs = [pltpu.VMEM(cots[0].shape, jnp.bfloat16)] * len(masks)
     if is_last:
         outs += [pltpu.VMEM(kv_shape, jnp.float32)] + [pltpu.VMEM(kv_shape, jnp.bfloat16)] * 3
     else:
         outs += [pltpu.VMEM(acc_shape, jnp.float32)]
-    operands = [queries, blocks[0], blocks[2], blocks[1], blocks[3], *cots] + ([] if carried is None else [carried])
+    own, far, even, odd = blocks
+    operands = [ranges, queries, own, even, far, odd, *cots]
+    operands += [] if carried is None else [carried]
     outs = pl.pallas_call(
         functools.partial(grad_kernel, masks, parts, carried is None, is_last),
         out_shape=tuple(outs),
-        in_specs=[_SMEM, _SMEM] + [_VMEM] * len(operands),
+        in_specs=[_VMEM] * len(operands),
         out_specs=(_VMEM,) * len(outs),
         scratch_shapes=[
             pltpu.VMEM(acc_shape, jnp.bfloat16),
             pltpu.VMEM(acc_shape, jnp.float32),
+            pltpu.VMEM(row_shape, jnp.bfloat16),
+            pltpu.VMEM(row_shape, jnp.bfloat16),
+            pltpu.VMEM(row_shape, jnp.float32),
         ],
         compiler_params=pltpu.CompilerParams(vmem_limit_bytes=VMEM_BYTES),
         cost_estimate=pl.CostEstimate(
             flops=10 * work * size, bytes_accessed=4 * queries.size * 2, transcendentals=work
         ),
         name="gradients",
-    )(lengths, prefixes, *operands)
+    )(*operands)
     return outs[: len(masks)], outs[len(masks) :]
 
 
@@ -277,14 +315,15 @@
 
 def local(queries, keys, values, output_gradient, doc_lengths, prefix_lengths):
     parts = lax.axis_size("kvh")
-    kv, cots = prepare(output_gradient, keys, values, parts)
+    kv, cots, ranges = prepare(
+        doc_lengths, prefix_lengths, output_gradient, keys, values, parts
+    )
     blocks = [kv[0]] + neighbours(*kv[1:], BACK)
     cots = [cots[0]] + [swapped(cots[mask], mask) for mask in range(1, parts)]
     dqs, carried = {}, [None]
     for masks in stages(parts):
         found, carried = gradients(
-            masks, parts, doc_lengths, prefix_lengths, queries,
-            [cots[mask] for mask in masks], blocks, carried[0],
+            masks, parts, ranges, queries, [cots[mask] for mask in masks], blocks, carried[0]
         )
         for mask, dq in zip(masks, found):
             dqs[mask] = swapped(dq, mask) if mask else dq

time: 34.5 us -> 34.8 us (level)
  Pallas kernels: 8.59 us -> 9.24 us
  local copies, waits for them, and re-layouts: 0.66 us -> 0.01 us
  waiting for transfers between devices: 7.88 us -> 8.27 us
    unnamed x6 -> x2, local copies, waits for them, and re-layouts: 0.66 us -> 0.01 us
    pallas_call x2, Pallas kernels: 6.29 us -> 6.92 us  [gradients(): pl.pallas_call(functools.partial(grad_kernel, masks, parts, carried is No...]
    ppermute x6, waiting for transfers between devices: 4.9 us -> 5.29 us  [swapped(): lax.ppermute(block, 'kvh', [(i, i ^ mask) for i in range(lax.axis_size('k...]
  transfers between devices with their start and end apart: 12 -> 12, of which waited for: 5 -> 5; matrix products, arithmetic and copies ran while one was open for 0% -> 0% of each run, Pallas kernels for 9% -> 10%
where the time goes in v7:
time: 34.8 us; the launch traced here: 34.4 us
  starting transfers between devices  16.2 us (47%)
  Pallas kernels  9.24 us (27%)
  waiting for transfers between devices  8.27 us (24%)
  between operations  0.71 us (2%)
    ppermute x4, starting transfers between devices, paired(): return lax.ppermute(block, 'seq', route)  8.66 us
    pallas_call x2, Pallas kernels, gradients(): pl.pallas_call(functools.partial(grad_kernel, masks, parts, carried is No...  6.92 us
    ppermute x6, waiting for transfers between devices, swapped(): lax.ppermute(block, 'kvh', [(i, i ^ mask) for i in range(lax.axis_size('k...  5.29 us
    ppermute x6, starting transfers between devices, swapped(): lax.ppermute(block, 'kvh', [(i, i ^ mask) for i in range(lax.axis_size('k...  4.94 us
    ppermute x2, waiting for transfers between devices, shifted(): lax.ppermute(block, 'seq', [(i, (i + distance) % count) for i in range(co...  2.97 us
    ppermute x2, starting transfers between devices, shifted(): lax.ppermute(block, 'seq', [(i, (i + distance) % count) for i in range(co...  2.62 us
    pallas_call x1, Pallas kernels, prepare(): pl.pallas_call(functools.partial(prep_kernel, parts), out_shape=(block,)...  1.3 us
    pallas_call x1, Pallas kernels, finish(): pl.pallas_call(functools.partial(finish_kernel, parts), out_shape=(jax.Sh...  1.02 us
  transfers between devices with their start and end apart: 12, of which 5 were waited for; matrix products, arithmetic and copies ran while one was open for 0% of the time, Pallas kernels for 10%

profile of v7, /device:TPU:0, one launch (start us, length us, event | category | flops | bytes accessed | tf_op | source)
XLA Modules:
  0.0 34.4 jit_solution(689683317993566084)
XLA Ops:
  0.6 0.0 copy-start
  0.6 1.3 %prepare.1 = (bf16[2,2,128,128]{3,2,1,0:T(8,128)(2,1)S(1)}, bf16[2,2,128,128]{3,2,1,0:T(8,128)(2,1)S(1)}, bf16[2,2,128,128]{3,2,1,0:T(8,128)(2,1)S(1)}, bf16[2,2...) custom-call(s32[8]{0:T(128)} %lengths_ref.1, ...), custom_call_target="tpu_custom_call" | custom-call | tf_op jit(solution)/shard_map/prepare/pallas_call | solution.py:87
  2.0 3.0 %collective-permute-start = (bf16[2,2,128,128]{3,2,1,0:T(8,128)(2,1)S(1)}, bf16[2,2,128,128]{3,2,1,0:T(8,128)(2,1)S(1)}, u32[]{:S(2)}, u32[]{:S(2)}) collective-permute-start(bf16[2,2,128,128]{3,2,1,0:T(8,128)(2,1)S(1)} %get-tuple-element.23), channel_id=1, source_target_pairs={{0,4},{4,0},{8,12},{12,8},{16,20},{20,16},{24,28},{28,24},{1,5},{5... | collective-permute-start | bytes 393224 | tf_op jit(solution)/shard_map/ppermute | solution.py:305
  5.0 1.6 %collective-permute-start.1 = (bf16[2,2,128,128]{3,2,1,0:T(8,128)(2,1)S(1)}, bf16[2,2,128,128]{3,2,1,0:T(8,128)(2,1)S(1)}, u32[]{:S(2)}, u32[]{:S(2)}) collective-permute-start(bf16[2,2,128,128]{3,2,1,0:T(8,128)(2,1)S(1)} %get-tuple-element.24), channel_id=1, source_target_pairs={{0,8},{4,12},{8,16},{12,20},{16,24},{20,28},{24,0},{28,4},{1,9},{5... | collective-permute-start | bytes 393224 | tf_op jit(solution)/shard_map/ppermute | solution.py:296
  6.5 0.7 %collective-permute-start.2 = (bf16[2,2,128,128]{3,2,1,0:T(8,128)(2,1)S(1)}, bf16[2,2,128,128]{3,2,1,0:T(8,128)(2,1)S(1)}, u32[]{:S(2)}, u32[]{:S(2)}) collective-permute-start(bf16[2,2,128,128]{3,2,1,0:T(8,128)(2,1)S(1)} %get-tuple-element.25), channel_id=1, source_target_pairs={{0,0},{4,8},{8,4},{12,16},{16,12},{20,24},{24,20},{28,28},{1,1},{5... | collective-permute-start | bytes 393224 | tf_op jit(solution)/shard_map/ppermute | solution.py:305
  7.2 0.1 collective-permute-start.5
  7.3 1.6 %collective-permute-start.3 = (bf16[32,16,128]{2,1,0:T(8,128)(2,1)S(1)}, bf16[32,16,128]{2,1,0:T(8,128)(2,1)S(1)}, u32[]{:S(2)}, u32[]{:S(2)}) collective-permute-start(bf16[32,16,128]{2,1,0:T(8,128)(2,1)S(1)} %get-tuple-element.26), channel_id=1, source_target_pairs={{0,3},{1,2},{2,1},{3,0},{4,7},{5,6},{6,5},{7,4},{8,11},{9,10},{10,... | collective-permute-start | bytes 393224 | tf_op jit(solution)/shard_map/ppermute | solution.py:309
  8.9 0.0 collective-permute-done.refs_1_
  8.9 1.3 %collective-permute-start.4 = (bf16[32,16,128]{2,1,0:T(8,128)(2,1)S(1)}, bf16[32,16,128]{2,1,0:T(8,128)(2,1)S(1)}, u32[]{:S(2)}, u32[]{:S(2)}) collective-permute-start(bf16[32,16,128]{2,1,0:T(8,128)(2,1)S(1)} %get-tuple-element.27), channel_id=1, source_target_pairs={{0,2},{1,3},{2,0},{3,1},{4,6},{5,7},{6,4},{7,5},{8,10},{9,11},{10,... | collective-permute-start | bytes 393224 | tf_op jit(solution)/shard_map/ppermute | solution.py:309
  10.2 1.6 %collective-permute-done.1.refs_2_ = bf16[2,2,128,128]{3,2,1,0:T(8,128)(2,1)S(1)} collective-permute-done((bf16[2,2,128,128]{3,2,1,0:T(8,128)(2,1)S(1)}, bf16[2,2,128,128]{3,2,1,0:T(8,128)(2,1)S(1)}, u32[]{:S(2)}, u32[]{:S(2)}) %collective-permute-start.1) | collective-permute-done | bytes 131104 | tf_op jit(solution)/shard_map/ppermute | solution.py:296
  11.9 0.0 collective-permute-done.2.refs_3_
  11.9 0.0 collective-permute-done.5.refs_5_
  11.9 0.0 copy-done
  11.9 3.4 %gradients.2 = (bf16[32,16,128]{2,1,0:T(8,128)(2,1)S(1)}, bf16[32,16,128]{2,1,0:T(8,128)(2,1)S(1)}, f32[2,2,512,128]{3,2,1,0:T(8,128)S(1)}) custom-call(s32[4,2,256]{2,1,0:T(2,128)S(1)} %get-tuple-element.21.range_ref, bf16[128,16,128]{2,1,0:T(8,128)(2,1)S(1)} %copy-done, bf16[2,2,128,128]{3,2,1,0:T(8,128)(2,1)S(1)} %get-tuple-element.22.refs_0_, ...), custom_call_target="tpu_custom_call" | custom-call | flops 671088640 | bytes 2097152 | tf_op jit(solution)/shard_map/gradients/pallas_call | solution.py:229
  15.3 0.0 collective-permute-done.3.refs_4_
  15.4 0.6 %collective-permute-done.4.refs_5_ = bf16[32,16,128]{2,1,0:T(8,128)(2,1)S(1)} collective-permute-done((bf16[32,16,128]{2,1,0:T(8,128)(2,1)S(1)}, bf16[32,16,128]{2,1,0:T(8,128)(2,1)S(1)}, u32[]{:S(2)}, u32[]{:S(2)}) %collective-permute-start.4) | collective-permute-done | bytes 131104 | tf_op jit(solution)/shard_map/ppermute | solution.py:309
  16.0 3.5 %gradients.3 = (bf16[32,16,128]{2,1,0:T(8,128)(2,1)S(1)}, bf16[32,16,128]{2,1,0:T(8,128)(2,1)S(1)}, f32[2,2,128,128]{3,2,1,0:T(8,128)S(1)}, bf16[2,2,128,128]{3,...) custom-call(s32[4,2,256]{2,1,0:T(2,128)S(1)} %get-tuple-element.21.range_ref, ...), custom_call_target="tpu_custom_call" | custom-call | flops 671088640 | bytes 2097152 | tf_op jit(solution)/shard_map/gradients/pallas_call | solution.py:229
  19.4 4.3 %collective-permute-start.6 = (bf16[2,2,128,128]{3,2,1,0:T(8,128)(2,1)S(1)}, bf16[2,2,128,128]{3,2,1,0:T(8,128)(2,1)S(1)}, u32[]{:S(2)}, u32[]{:S(2)}) collective-permute-start(bf16[2,2,128,128]{3,2,1,0:T(8,128)(2,1)S(1)} %get-tuple-element.31), channel_id=1, source_target_pairs={{0,4},{4,0},{8,12},{12,8},{16,20},{20,16},{24,28},{28,24},{1,5},{5... | collective-permute-start | bytes 393224 | tf_op jit(solution)/shard_map/ppermute | solution.py:305
  23.8 1.0 %collective-permute-start.7 = (bf16[2,2,128,128]{3,2,1,0:T(8,128)(2,1)S(1)}, bf16[2,2,128,128]{3,2,1,0:T(8,128)(2,1)S(1)}, u32[]{:S(2)}, u32[]{:S(2)}) collective-permute-start(bf16[2,2,128,128]{3,2,1,0:T(8,128)(2,1)S(1)} %get-tuple-element.32), channel_id=1, source_target_pairs={{0,24},{4,28},{8,0},{12,4},{16,8},{20,12},{24,16},{28,20},{1,25},{... | collective-permute-start | bytes 393224 | tf_op jit(solution)/shard_map/ppermute | solution.py:296
  24.8 0.4 %collective-permute-start.8 = (bf16[32,16,128]{2,1,0:T(8,128)(2,1)S(1)}, bf16[32,16,128]{2,1,0:T(8,128)(2,1)S(1)}, u32[]{:S(2)}, u32[]{:S(2)}) collective-permute-start(bf16[32,16,128]{2,1,0:T(8,128)(2,1)S(1)} %get-tuple-element.33), channel_id=1, source_target_pairs={{0,3},{1,2},{2,1},{3,0},{4,7},{5,6},{6,5},{7,4},{8,11},{9,10},{10,... | collective-permute-start | bytes 393224 | tf_op jit(solution)/shard_map/ppermute | solution.py:309
  25.2 0.7 %collective-permute-start.9 = (bf16[2,2,128,128]{3,2,1,0:T(8,128)(2,1)S(1)}, bf16[2,2,128,128]{3,2,1,0:T(8,128)(2,1)S(1)}, u32[]{:S(2)}, u32[]{:S(2)}) collective-permute-start(bf16[2,2,128,128]{3,2,1,0:T(8,128)(2,1)S(1)} %get-tuple-element.34), channel_id=1, source_target_pairs={{0,0},{4,8},{8,4},{12,16},{16,12},{20,24},{24,20},{28,28},{1,1},{5... | collective-permute-start | bytes 393224 | tf_op jit(solution)/shard_map/ppermute | solution.py:305
  25.9 1.2 %collective-permute-start.10 = (bf16[32,16,128]{2,1,0:T(8,128)(2,1)S(1)}, bf16[32,16,128]{2,1,0:T(8,128)(2,1)S(1)}, u32[]{:S(2)}, u32[]{:S(2)}) collective-permute-start(bf16[32,16,128]{2,1,0:T(8,128)(2,1)S(1)} %get-tuple-element.35), channel_id=1, source_target_pairs={{0,2},{1,3},{2,0},{3,1},{4,6},{5,7},{6,4},{7,5},{8,10},{9,11},{10,... | collective-permute-start | bytes 393224 | tf_op jit(solution)/shard_map/ppermute | solution.py:309
  27.1 0.0 collective-permute-done.6.refs_0_
  27.1 0.3 collective-permute-start.11
  27.4 1.3 %collective-permute-done.7.refs_1_ = bf16[2,2,128,128]{3,2,1,0:T(8,128)(2,1)S(1)} collective-permute-done((bf16[2,2,128,128]{3,2,1,0:T(8,128)(2,1)S(1)}, bf16[2,2,128,128]{3,2,1,0:T(8,128)(2,1)S(1)}, u32[]{:S(2)}, u32[]{:S(2)}) %collective-permute-start.7) | collective-permute-done | bytes 131104 | tf_op jit(solution)/shard_map/ppermute | solution.py:296
  28.7 1.8 %collective-permute-done.8.refs_2_ = bf16[32,16,128]{2,1,0:T(8,128)(2,1)S(1)} collective-permute-done((bf16[32,16,128]{2,1,0:T(8,128)(2,1)S(1)}, bf16[32,16,128]{2,1,0:T(8,128)(2,1)S(1)}, u32[]{:S(2)}, u32[]{:S(2)}) %collective-permute-start.8) | collective-permute-done | bytes 131104 | tf_op jit(solution)/shard_map/ppermute | solution.py:309
  30.5 0.0 collective-permute-done.9.refs_3_
  30.5 2.9 %collective-permute-done.10.refs_4_ = bf16[32,16,128]{2,1,0:T(8,128)(2,1)S(1)} collective-permute-done((bf16[32,16,128]{2,1,0:T(8,128)(2,1)S(1)}, bf16[32,16,128]{2,1,0:T(8,128)(2,1)S(1)}, u32[]{:S(2)}, u32[]{:S(2)}) %collective-permute-start.10) | collective-permute-done | bytes 131104 | tf_op jit(solution)/shard_map/ppermute | solution.py:309
  33.4 0.0 collective-permute-done.11.refs_5_
  33.4 1.0 %finish.1 = (bf16[32,64,128]{2,1,0:T(8,128)(2,1)}, bf16[128,2,128]{2,1,0:T(2,128)(2,1)}, bf16[128,2,128]{2,1,0:T(2,128)(2,1)}) custom-call(bf16[2,2,128,128]{3,2,1,0:T(8,128)(2,1)S(1)} %collective-permute-done.6.refs_0_, bf16[2,2,128,128]{3,2,1,0:T(8,128)(2,1)S(1)} %collective-permute-done.7.refs_1_, ...), custom_call_target="tpu_custom_call" | custom-call | tf_op jit(solution)/shard_map/finish/pallas_call | solution.py:280
Async XLA Ops:
  0.6 11.2 %copy-start = (bf16[128,16,128]{2,1,0:T(8,128)(2,1)S(1)}, bf16[128,16,128]{2,1,0:T(8,128)(2,1)}, u32[]{:S(2)}) copy-start(bf16[128,16,128]{2,1,0:T(8,128)(2,1)} %q_ref.3) | copy-start | bytes 1572868
  2.0 7.0 %collective-permute-start = (bf16[2,2,128,128]{3,2,1,0:T(8,128)(2,1)S(1)}, bf16[2,2,128,128]{3,2,1,0:T(8,128)(2,1)S(1)}, u32[]{:S(2)}, u32[]{:S(2)}) collective-permute-start(bf16[2,2,128,128]{3,2,1,0:T(8,128)(2,1)S(1)} %get-tuple-element.23), channel_id=1, source_target_pairs={{0,4},{4,0},{8,12},{12,8},{16,20},{20,16},{24,28},{28,24},{1,5},{5... | collective-permute-start | bytes 393224 | tf_op jit(solution)/shard_map/ppermute | solution.py:305
  5.0 6.9 %collective-permute-start.1 = (bf16[2,2,128,128]{3,2,1,0:T(8,128)(2,1)S(1)}, bf16[2,2,128,128]{3,2,1,0:T(8,128)(2,1)S(1)}, u32[]{:S(2)}, u32[]{:S(2)}) collective-permute-start(bf16[2,2,128,128]{3,2,1,0:T(8,128)(2,1)S(1)} %get-tuple-element.24), channel_id=1, source_target_pairs={{0,8},{4,12},{8,16},{12,20},{16,24},{20,28},{24,0},{28,4},{1,9},{5... | collective-permute-start | bytes 393224 | tf_op jit(solution)/shard_map/ppermute | solution.py:296
  6.5 5.3 %collective-permute-start.2 = (bf16[2,2,128,128]{3,2,1,0:T(8,128)(2,1)S(1)}, bf16[2,2,128,128]{3,2,1,0:T(8,128)(2,1)S(1)}, u32[]{:S(2)}, u32[]{:S(2)}) collective-permute-start(bf16[2,2,128,128]{3,2,1,0:T(8,128)(2,1)S(1)} %get-tuple-element.25), channel_id=1, source_target_pairs={{0,0},{4,8},{8,4},{12,16},{16,12},{20,24},{24,20},{28,28},{1,1},{5... | collective-permute-start | bytes 393224 | tf_op jit(solution)/shard_map/ppermute | solution.py:305
  7.2 4.7 %collective-permute-start.5 = (bf16[32,16,128]{2,1,0:T(8,128)(2,1)S(1)}, bf16[32,16,128]{2,1,0:T(8,128)(2,1)S(1)}, u32[]{:S(2)}, u32[]{:S(2)}) collective-permute-start(bf16[32,16,128]{2,1,0:T(8,128)(2,1)S(1)} %get-tuple-element.29), channel_id=1, source_target_pairs={{0,1},{1,0},{2,3},{3,2},{4,5},{5,4},{6,7},{7,6},{8,9},{9,8},{10,11... | collective-permute-start | bytes 393224 | tf_op jit(solution)/shard_map/ppermute | solution.py:309
  7.3 8.1 %collective-permute-start.3 = (bf16[32,16,128]{2,1,0:T(8,128)(2,1)S(1)}, bf16[32,16,128]{2,1,0:T(8,128)(2,1)S(1)}, u32[]{:S(2)}, u32[]{:S(2)}) collective-permute-start(bf16[32,16,128]{2,1,0:T(8,128)(2,1)S(1)} %get-tuple-element.26), channel_id=1, source_target_pairs={{0,3},{1,2},{2,1},{3,0},{4,7},{5,6},{6,5},{7,4},{8,11},{9,10},{10,... | collective-permute-start | bytes 393224 | tf_op jit(solution)/shard_map/ppermute | solution.py:309
  8.9 7.0 %collective-permute-start.4 = (bf16[32,16,128]{2,1,0:T(8,128)(2,1)S(1)}, bf16[32,16,128]{2,1,0:T(8,128)(2,1)S(1)}, u32[]{:S(2)}, u32[]{:S(2)}) collective-permute-start(bf16[32,16,128]{2,1,0:T(8,128)(2,1)S(1)} %get-tuple-element.27), channel_id=1, source_target_pairs={{0,2},{1,3},{2,0},{3,1},{4,6},{5,7},{6,4},{7,5},{8,10},{9,11},{10,... | collective-permute-start | bytes 393224 | tf_op jit(solution)/shard_map/ppermute | solution.py:309
  19.4 7.6 %collective-permute-start.6 = (bf16[2,2,128,128]{3,2,1,0:T(8,128)(2,1)S(1)}, bf16[2,2,128,128]{3,2,1,0:T(8,128)(2,1)S(1)}, u32[]{:S(2)}, u32[]{:S(2)}) collective-permute-start(bf16[2,2,128,128]{3,2,1,0:T(8,128)(2,1)S(1)} %get-tuple-element.31), channel_id=1, source_target_pairs={{0,4},{4,0},{8,12},{12,8},{16,20},{20,16},{24,28},{28,24},{1,5},{5... | collective-permute-start | bytes 393224 | tf_op jit(solution)/shard_map/ppermute | solution.py:305
  23.8 5.0 %collective-permute-start.7 = (bf16[2,2,128,128]{3,2,1,0:T(8,128)(2,1)S(1)}, bf16[2,2,128,128]{3,2,1,0:T(8,128)(2,1)S(1)}, u32[]{:S(2)}, u32[]{:S(2)}) collective-permute-start(bf16[2,2,128,128]{3,2,1,0:T(8,128)(2,1)S(1)} %get-tuple-element.32), channel_id=1, source_target_pairs={{0,24},{4,28},{8,0},{12,4},{16,8},{20,12},{24,16},{28,20},{1,25},{... | collective-permute-start | bytes 393224 | tf_op jit(solution)/shard_map/ppermute | solution.py:296
  24.8 5.7 %collective-permute-start.8 = (bf16[32,16,128]{2,1,0:T(8,128)(2,1)S(1)}, bf16[32,16,128]{2,1,0:T(8,128)(2,1)S(1)}, u32[]{:S(2)}, u32[]{:S(2)}) collective-permute-start(bf16[32,16,128]{2,1,0:T(8,128)(2,1)S(1)} %get-tuple-element.33), channel_id=1, source_target_pairs={{0,3},{1,2},{2,1},{3,0},{4,7},{5,6},{6,5},{7,4},{8,11},{9,10},{10,... | collective-permute-start | bytes 393224 | tf_op jit(solution)/shard_map/ppermute | solution.py:309
  25.2 5.3 %collective-permute-start.9 = (bf16[2,2,128,128]{3,2,1,0:T(8,128)(2,1)S(1)}, bf16[2,2,128,128]{3,2,1,0:T(8,128)(2,1)S(1)}, u32[]{:S(2)}, u32[]{:S(2)}) collective-permute-start(bf16[2,2,128,128]{3,2,1,0:T(8,128)(2,1)S(1)} %get-tuple-element.34), channel_id=1, source_target_pairs={{0,0},{4,8},{8,4},{12,16},{16,12},{20,24},{24,20},{28,28},{1,1},{5... | collective-permute-start | bytes 393224 | tf_op jit(solution)/shard_map/ppermute | solution.py:305
  25.9 7.6 %collective-permute-start.10 = (bf16[32,16,128]{2,1,0:T(8,128)(2,1)S(1)}, bf16[32,16,128]{2,1,0:T(8,128)(2,1)S(1)}, u32[]{:S(2)}, u32[]{:S(2)}) collective-permute-start(bf16[32,16,128]{2,1,0:T(8,128)(2,1)S(1)} %get-tuple-element.35), channel_id=1, source_target_pairs={{0,2},{1,3},{2,0},{3,1},{4,6},{5,7},{6,4},{7,5},{8,10},{9,11},{10,... | collective-permute-start | bytes 393224 | tf_op jit(solution)/shard_map/ppermute | solution.py:309
  27.1 6.4 %collective-permute-start.11 = (bf16[32,16,128]{2,1,0:T(8,128)(2,1)S(1)}, bf16[32,16,128]{2,1,0:T(8,128)(2,1)S(1)}, u32[]{:S(2)}, u32[]{:S(2)}) collective-permute-start(bf16[32,16,128]{2,1,0:T(8,128)(2,1)S(1)} %get-tuple-element.36), channel_id=1, source_target_pairs={{0,1},{1,0},{2,3},{3,2},{4,5},{5,4},{6,7},{7,6},{8,9},{9,8},{10,11... | collective-permute-start | bytes 393224 | tf_op jit(solution)/shard_map/ppermute | solution.py:309

commit v8 on v7

--- a/solution.py
+++ b/solution.py
@@ -12,6 +12,7 @@
 LOG2E = 1.4426950408889634
 VMEM_BYTES = 40 * 1024 * 1024
 NEG = -1e30
+TILE = 8
 
 _VMEM = pl.BlockSpec(memory_space=pltpu.VMEM)
 _SMEM = pl.BlockSpec(memory_space=pltpu.SMEM)
@@ -131,11 +132,11 @@
 
 def grad_kernel(masks, parts, is_first, is_last, range_ref, q_ref, *refs):
     refs = list(refs)
-    kv_own, kv_even, kv_far, kv_odd = [refs.pop(0) for _ in range(4)]
+    kv_own, kv_odd, kv_even, kv_far = [refs.pop(0) for _ in range(4)]
     cots = [refs.pop(0) for _ in masks]
     carried = None if is_first else refs.pop(0)
     dqs = [refs.pop(0) for _ in masks]
-    outs, (window, acc, q_rows, cot_rows, dq_rows) = refs[:-5], refs[-5:]
+    outs, (window, acc, score_buf, dprob_buf, prob_buf, dscore_buf) = refs[:-6], refs[-6:]
     rows, heads, size = q_ref.shape
     tokens = rows // parts
     kv_heads = kv_own.shape[1]
@@ -154,51 +155,83 @@
             for group in range(kv_heads):
                 window[number, group, part] = ref[number, group]
     acc[...] = jnp.zeros_like(acc) if is_first else carried[...]
-    for place, mask in enumerate(masks):
-        first = pl.multiple_of((me ^ mask) * tokens, tokens)
-        for group in range(kv_heads):
-            of_group = pl.ds(group * group_size, group_size)
-            item = place * kv_heads + group
-            q = q_ref[pl.ds(first, tokens), of_group].astype(jnp.float32)
-            q_rows[item] = q.reshape(lanes, size).astype(jnp.bfloat16)
-            cot = cots[place][:, of_group].astype(jnp.float32)
-            cot_rows[item] = cot.reshape(lanes, size).astype(jnp.bfloat16)
 
     contract_last = (((1,), (1,)), ((), ()))
     contract_first = (((0,), (0,)), ((), ()))
-    key_iota = lax.broadcasted_iota(jnp.int32, (reach, lanes), 0)
-    step = masks[1] - masks[0] if len(masks) > 1 else 0
-
-    def work(item, _):
-        group = lax.rem(item, kv_heads)
-        mask = masks[0] + step * lax.div(item, kv_heads)
-        here = pl.ds(pl.multiple_of((me ^ mask) * tokens, tokens), reach)
-        low, high = range_ref[mask, 0:1, :], range_ref[mask, 1:2, :]
-        visible = (key_iota >= low) & (key_iota < high)
-        q, cot = q_rows[item], cot_rows[item]
-        k, v = window[0, group, here], window[1, group, here]
-        scores = lax.dot_general(k, q, contract_last, preferred_element_type=jnp.float32)
-        scores = jnp.where(visible, scores * (scale * LOG2E), NEG)
-        top = jnp.max(scores, axis=0, keepdims=True)
-        expo = jnp.exp2(scores - top)
-        total = jnp.sum(expo, axis=0, keepdims=True)
-        probs = expo * (1.0 / total)
-        dprobs = lax.dot_general(v, cot, contract_last, preferred_element_type=jnp.float32)
-        delta = jnp.sum(probs * dprobs, axis=0, keepdims=True)
-        dscores = (probs * (dprobs - delta)).astype(jnp.bfloat16)
-        acc[1, group, here] += jnp.dot(
-            probs.astype(jnp.bfloat16), cot, preferred_element_type=jnp.float32
-        )
+    sublane = lax.broadcasted_iota(jnp.int32, (TILE, lanes), 0)
+    items = [(place, group) for place in range(len(masks)) for group in range(kv_heads)]
+
+    def operands(item):
+        place, group = items[item]
+        first = pl.multiple_of((me ^ masks[place]) * tokens, tokens)
+        of_group = pl.ds(group * group_size, group_size)
+        q = q_ref[pl.ds(first, tokens), of_group].astype(jnp.float32)
+        cot = cots[place][:, of_group].astype(jnp.float32)
+        return (
+            pl.ds(first, reach),
+            q.reshape(lanes, size).astype(jnp.bfloat16),
+            cot.reshape(lanes, size).astype(jnp.bfloat16),
+        )
+
+    def scores_of(item):
+        place, group = items[item]
+        slot = item % 2
+        here, q, cot = operands(item)
+        scores = lax.dot_general(
+            window[0, group, here], q, contract_last, preferred_element_type=jnp.float32
+        )
+        low = range_ref[masks[place], 0:1, :] - sublane
+        high = range_ref[masks[place], 1:2, :] - sublane
+        top = jnp.full((TILE, lanes), NEG, jnp.float32)
+        for row in range(0, reach, TILE):
+            visible = (low <= row) & (high > row)
+            tile = jnp.where(visible, scores[row : row + TILE] * (scale * LOG2E), NEG)
+            top = jnp.maximum(top, tile)
+            score_buf[slot, row : row + TILE] = tile
+        dprob_buf[slot] = lax.dot_general(
+            window[1, group, here], cot, contract_last, preferred_element_type=jnp.float32
+        )
+        return jnp.max(top, axis=0, keepdims=True)
+
+    def softmax_of(item, top):
+        slot = item % 2
+        total = jnp.zeros((TILE, lanes), jnp.float32)
+        delta = jnp.zeros((TILE, lanes), jnp.float32)
+        for row in range(0, reach, TILE):
+            tile = slice(row, row + TILE)
+            expo = jnp.exp2(score_buf[slot, tile] - top)
+            total = total + expo
+            delta = delta + expo * dprob_buf[slot, tile]
+            score_buf[slot, tile] = expo
+        inverse = 1.0 / jnp.sum(total, axis=0, keepdims=True)
+        delta = jnp.sum(delta, axis=0, keepdims=True) * inverse
+        for row in range(0, reach, 2 * TILE):
+            tile = slice(row, row + 2 * TILE)
+            probs = score_buf[slot, tile] * inverse
+            dscores = probs * (dprob_buf[slot, tile] - delta)
+            prob_buf[slot, tile] = probs.astype(jnp.bfloat16)
+            dscore_buf[slot, tile] = dscores.astype(jnp.bfloat16)
+
+    def gradients_of(item):
+        place, group = items[item]
+        slot = item % 2
+        here, q, cot = operands(item)
+        dscores = dscore_buf[slot]
+        acc[1, group, here] += jnp.dot(prob_buf[slot], cot, preferred_element_type=jnp.float32)
         acc[0, group, here] += jnp.dot(dscores, q, preferred_element_type=jnp.float32)
-        dq = lax.dot_general(k, dscores, contract_first, preferred_element_type=jnp.float32)
-        dq_rows[item] = jnp.transpose(dq * scale)
-        return 0
-
-    lax.fori_loop(0, len(masks) * kv_heads, work, 0)
-    for place in range(len(masks)):
-        for group in range(kv_heads):
-            dq = dq_rows[place * kv_heads + group].reshape(tokens, group_size, size)
-            dqs[place][:, pl.ds(group * group_size, group_size)] = dq.astype(jnp.bfloat16)
+        dq = lax.dot_general(
+            window[0, group, here], dscores, contract_first, preferred_element_type=jnp.float32
+        )
+        dq = jnp.transpose(dq * scale).reshape(tokens, group_size, size)
+        dqs[place][:, pl.ds(group * group_size, group_size)] = dq.astype(jnp.bfloat16)
+
+    top = scores_of(0)
+    for item in range(len(items)):
+        later = scores_of(item + 1) if item + 1 < len(items) else None
+        softmax_of(item, top)
+        gradients_of(item)
+        top = later
+
     if not is_last:
         outs[0][...] = acc[...]
         return
@@ -216,7 +249,8 @@
     kv_heads = kv_shape[1]
     span = (BACK + 1 + AHEAD) * rows
     acc_shape = (2, kv_heads, span, size)
-    row_shape = (len(masks) * kv_heads, rows // parts * (heads // kv_heads), size)
+    tokens = rows // parts
+    tile_shape = (2, span - rows + tokens, tokens * (heads // kv_heads))
     work = heads * rows // parts * span * len(masks)
     outs = [pltpu.VMEM(cots[0].shape, jnp.bfloat16)] * len(masks)
     if is_last:
@@ -224,7 +258,7 @@
     else:
         outs += [pltpu.VMEM(acc_shape, jnp.float32)]
     own, far, even, odd = blocks
-    operands = [ranges, queries, own, even, far, odd, *cots]
+    operands = [ranges, queries, own, odd, even, far, *cots]
     operands += [] if carried is None else [carried]
     outs = pl.pallas_call(
         functools.partial(grad_kernel, masks, parts, carried is None, is_last),
@@ -234,9 +268,10 @@
         scratch_shapes=[
             pltpu.VMEM(acc_shape, jnp.bfloat16),
             pltpu.VMEM(acc_shape, jnp.float32),
-            pltpu.VMEM(row_shape, jnp.bfloat16),
-            pltpu.VMEM(row_shape, jnp.bfloat16),
-            pltpu.VMEM(row_shape, jnp.float32),
+            pltpu.VMEM(tile_shape, jnp.float32),
+            pltpu.VMEM(tile_shape, jnp.float32),
+            pltpu.VMEM(tile_shape, jnp.bfloat16),
+            pltpu.VMEM(tile_shape, jnp.bfloat16),
         ],
         compiler_params=pltpu.CompilerParams(vmem_limit_bytes=VMEM_BYTES),
         cost_estimate=pl.CostEstimate(
@@ -248,7 +283,7 @@
 
 
 def finish_order(parts):
-    return ["even", "far", parts - 1, "odd", *range(parts - 2, -1, -1), "own"]
+    return ["odd", parts - 1, "even", "far", *range(parts - 2, -1, -1), "own"]
 
 
 def finish_kernel(parts, *refs):

time: 34.8 us -> 34 us (0.977)
  Pallas kernels: 9.24 us -> 6.3 us
  starting transfers between devices: 16.2 us -> 17.7 us
  waiting for transfers between devices: 8.27 us -> 9.06 us
    ppermute x6, waiting for transfers between devices: 5.29 us -> 0.78 us  [swapped(): lax.ppermute(block, 'kvh', [(i, i ^ mask) for i in range(lax.axis_size('k...]
    pallas_call x2, Pallas kernels: 6.92 us -> 3.98 us  [gradients(): pl.pallas_call(functools.partial(grad_kernel, masks, parts, carried is No...]
    ppermute x4, waiting for transfers between devices: 0.01 us -> 2.71 us  [paired(): return lax.ppermute(block, 'seq', route)]
    ppermute x2, waiting for transfers between devices: 2.97 us -> 5.57 us  [shifted(): lax.ppermute(block, 'seq', [(i, (i + distance) % count) for i in range(co...]
    ppermute x4, starting transfers between devices: 8.66 us -> 11.1 us  [paired(): return lax.ppermute(block, 'seq', route)]
    ppermute x6, starting transfers between devices: 4.94 us -> 4.33 us  [swapped(): lax.ppermute(block, 'kvh', [(i, i ^ mask) for i in range(lax.axis_size('k...]
    ppermute x2, starting transfers between devices: 2.62 us -> 2.26 us  [shifted(): lax.ppermute(block, 'seq', [(i, (i + distance) % count) for i in range(co...]
  transfers between devices with their start and end apart: 12 -> 12, of which waited for: 5 -> 6; matrix products, arithmetic and copies ran while one was open for 0% -> 0% of each run, Pallas kernels for 10% -> 6%
where the time goes in v8:
time: 34 us; the launch traced here: 33.8 us
  starting transfers between devices  17.7 us (52%)
  waiting for transfers between devices  9.06 us (27%)
  Pallas kernels  6.3 us (19%)
  between operations  0.69 us (2%)
    ppermute x4, starting transfers between devices, paired(): return lax.ppermute(block, 'seq', route)  11.1 us
    ppermute x2, waiting for transfers between devices, shifted(): lax.ppermute(block, 'seq', [(i, (i + distance) % count) for i in range(co...  5.57 us
    ppermute x6, starting transfers between devices, swapped(): lax.ppermute(block, 'kvh', [(i, i ^ mask) for i in range(lax.axis_size('k...  4.33 us
    pallas_call x2, Pallas kernels, gradients(): pl.pallas_call(functools.partial(grad_kernel, masks, parts, carried is No...  3.98 us
    ppermute x4, waiting for transfers between devices, paired(): return lax.ppermute(block, 'seq', route)  2.71 us
    ppermute x2, starting transfers between devices, shifted(): lax.ppermute(block, 'seq', [(i, (i + distance) % count) for i in range(co...  2.26 us
    pallas_call x1, Pallas kernels, prepare(): pl.pallas_call(functools.partial(prep_kernel, parts), out_shape=(block,)...  1.3 us
    pallas_call x1, Pallas kernels, finish(): pl.pallas_call(functools.partial(finish_kernel, parts), out_shape=(jax.Sh...  1.02 us
  transfers between devices with their start and end apart: 12, of which 6 were waited for; matrix products, arithmetic and copies ran while one was open for 0% of the time, Pallas kernels for 6%

profile of v8, /device:TPU:0, one launch (start us, length us, event | category | flops | bytes accessed | tf_op | source)
XLA Modules:
  0.0 33.8 jit_solution(6554297616406167514)
XLA Ops:
  0.6 0.0 copy-start
  0.6 1.3 %prepare.1 = (bf16[2,2,128,128]{3,2,1,0:T(8,128)(2,1)S(1)}, bf16[2,2,128,128]{3,2,1,0:T(8,128)(2,1)S(1)}, bf16[2,2,128,128]{3,2,1,0:T(8,128)(2,1)S(1)}, bf16[2,2...) custom-call(s32[8]{0:T(128)} %lengths_ref.1, ...), custom_call_target="tpu_custom_call" | custom-call | tf_op jit(solution)/shard_map/prepare/pallas_call | solution.py:88
  2.0 0.7 %collective-permute-start = (bf16[2,2,128,128]{3,2,1,0:T(8,128)(2,1)S(1)}, bf16[2,2,128,128]{3,2,1,0:T(8,128)(2,1)S(1)}, u32[]{:S(2)}, u32[]{:S(2)}) collective-permute-start(bf16[2,2,128,128]{3,2,1,0:T(8,128)(2,1)S(1)} %get-tuple-element.23), channel_id=1, source_target_pairs={{0,0},{4,8},{8,4},{12,16},{16,12},{20,24},{24,20},{28,28},{1,1},{5... | collective-permute-start | bytes 393224 | tf_op jit(solution)/shard_map/ppermute | solution.py:340
  2.6 5.8 %collective-permute-start.1 = (bf16[2,2,128,128]{3,2,1,0:T(8,128)(2,1)S(1)}, bf16[2,2,128,128]{3,2,1,0:T(8,128)(2,1)S(1)}, u32[]{:S(2)}, u32[]{:S(2)}) collective-permute-start(bf16[2,2,128,128]{3,2,1,0:T(8,128)(2,1)S(1)} %get-tuple-element.24), channel_id=1, source_target_pairs={{0,4},{4,0},{8,12},{12,8},{16,20},{20,16},{24,28},{28,24},{1,5},{5... | collective-permute-start | bytes 393224 | tf_op jit(solution)/shard_map/ppermute | solution.py:340
  8.4 1.6 %collective-permute-start.2 = (bf16[2,2,128,128]{3,2,1,0:T(8,128)(2,1)S(1)}, bf16[2,2,128,128]{3,2,1,0:T(8,128)(2,1)S(1)}, u32[]{:S(2)}, u32[]{:S(2)}) collective-permute-start(bf16[2,2,128,128]{3,2,1,0:T(8,128)(2,1)S(1)} %get-tuple-element.25), channel_id=1, source_target_pairs={{0,8},{4,12},{8,16},{12,20},{16,24},{20,28},{24,0},{28,4},{1,9},{5... | collective-permute-start | bytes 393224 | tf_op jit(solution)/shard_map/ppermute | solution.py:331
  10.0 0.0 collective-permute-start.5
  10.0 1.6 %collective-permute-start.3 = (bf16[32,16,128]{2,1,0:T(8,128)(2,1)S(1)}, bf16[32,16,128]{2,1,0:T(8,128)(2,1)S(1)}, u32[]{:S(2)}, u32[]{:S(2)}) collective-permute-start(bf16[32,16,128]{2,1,0:T(8,128)(2,1)S(1)} %get-tuple-element.26), channel_id=1, source_target_pairs={{0,3},{1,2},{2,1},{3,0},{4,7},{5,6},{6,5},{7,4},{8,11},{9,10},{10,... | collective-permute-start | bytes 393224 | tf_op jit(solution)/shard_map/ppermute | solution.py:344
  11.6 0.0 collective-permute-done.refs_1_
  11.6 0.5 %collective-permute-start.4 = (bf16[32,16,128]{2,1,0:T(8,128)(2,1)S(1)}, bf16[32,16,128]{2,1,0:T(8,128)(2,1)S(1)}, u32[]{:S(2)}, u32[]{:S(2)}) collective-permute-start(bf16[32,16,128]{2,1,0:T(8,128)(2,1)S(1)} %get-tuple-element.27), channel_id=1, source_target_pairs={{0,2},{1,3},{2,0},{3,1},{4,6},{5,7},{6,4},{7,5},{8,10},{9,11},{10,... | collective-permute-start | bytes 393224 | tf_op jit(solution)/shard_map/ppermute | solution.py:344
  12.1 1.1 %collective-permute-done.1.refs_2_ = bf16[2,2,128,128]{3,2,1,0:T(8,128)(2,1)S(1)} collective-permute-done((bf16[2,2,128,128]{3,2,1,0:T(8,128)(2,1)S(1)}, bf16[2,2,128,128]{3,2,1,0:T(8,128)(2,1)S(1)}, u32[]{:S(2)}, u32[]{:S(2)}) %collective-permute-start.1) | collective-permute-done | bytes 131104 | tf_op jit(solution)/shard_map/ppermute | solution.py:340
  13.2 3.0 %collective-permute-done.2.refs_3_ = bf16[2,2,128,128]{3,2,1,0:T(8,128)(2,1)S(1)} collective-permute-done((bf16[2,2,128,128]{3,2,1,0:T(8,128)(2,1)S(1)}, bf16[2,2,128,128]{3,2,1,0:T(8,128)(2,1)S(1)}, u32[]{:S(2)}, u32[]{:S(2)}) %collective-permute-start.2) | collective-permute-done | bytes 131104 | tf_op jit(solution)/shard_map/ppermute | solution.py:331
  16.3 0.0 collective-permute-done.5.refs_5_
  16.3 0.0 copy-done
  16.3 2.0 %gradients.2 = (bf16[32,16,128]{2,1,0:T(8,128)(2,1)S(1)}, bf16[32,16,128]{2,1,0:T(8,128)(2,1)S(1)}, f32[2,2,512,128]{3,2,1,0:T(8,128)S(1)}) custom-call(s32[4,2,256]{2,1,0:T(2,128)S(1)} %get-tuple-element.21.range_ref, bf16[128,16,128]{2,1,0:T(8,128)(2,1)S(1)} %copy-done, bf16[2,2,128,128]{3,2,1,0:T(8,128)(2,1)S(1)} %get-tuple-element.22.refs_0_, ...), custom_call_target="tpu_custom_call" | custom-call | flops 671088640 | bytes 2097152 | tf_op jit(solution)/shard_map/gradients/pallas_call | solution.py:263
  18.3 0.0 collective-permute-done.3.refs_4_
  18.3 0.3 collective-permute-done.4.refs_5_
  18.6 2.0 %gradients.3 = (bf16[32,16,128]{2,1,0:T(8,128)(2,1)S(1)}, bf16[32,16,128]{2,1,0:T(8,128)(2,1)S(1)}, f32[2,2,128,128]{3,2,1,0:T(8,128)S(1)}, bf16[2,2,128,128]{3,...) custom-call(s32[4,2,256]{2,1,0:T(2,128)S(1)} %get-tuple-element.21.range_ref, ...), custom_call_target="tpu_custom_call" | custom-call | flops 671088640 | bytes 2097152 | tf_op jit(solution)/shard_map/gradients/pallas_call | solution.py:263
  20.6 0.7 %collective-permute-start.6 = (bf16[2,2,128,128]{3,2,1,0:T(8,128)(2,1)S(1)}, bf16[2,2,128,128]{3,2,1,0:T(8,128)(2,1)S(1)}, u32[]{:S(2)}, u32[]{:S(2)}) collective-permute-start(bf16[2,2,128,128]{3,2,1,0:T(8,128)(2,1)S(1)} %get-tuple-element.31), channel_id=1, source_target_pairs={{0,0},{4,8},{8,4},{12,16},{16,12},{20,24},{24,20},{28,28},{1,1},{5... | collective-permute-start | bytes 393224 | tf_op jit(solution)/shard_map/ppermute | solution.py:340
  21.3 0.7 %collective-permute-start.7 = (bf16[32,16,128]{2,1,0:T(8,128)(2,1)S(1)}, bf16[32,16,128]{2,1,0:T(8,128)(2,1)S(1)}, u32[]{:S(2)}, u32[]{:S(2)}) collective-permute-start(bf16[32,16,128]{2,1,0:T(8,128)(2,1)S(1)} %get-tuple-element.32), channel_id=1, source_target_pairs={{0,3},{1,2},{2,1},{3,0},{4,7},{5,6},{6,5},{7,4},{8,11},{9,10},{10,... | collective-permute-start | bytes 393224 | tf_op jit(solution)/shard_map/ppermute | solution.py:344
  21.9 4.0 %collective-permute-start.8 = (bf16[2,2,128,128]{3,2,1,0:T(8,128)(2,1)S(1)}, bf16[2,2,128,128]{3,2,1,0:T(8,128)(2,1)S(1)}, u32[]{:S(2)}, u32[]{:S(2)}) collective-permute-start(bf16[2,2,128,128]{3,2,1,0:T(8,128)(2,1)S(1)} %get-tuple-element.33), channel_id=1, source_target_pairs={{0,4},{4,0},{8,12},{12,8},{16,20},{20,16},{24,28},{28,24},{1,5},{5... | collective-permute-start | bytes 393224 | tf_op jit(solution)/shard_map/ppermute | solution.py:340
  26.0 0.7 %collective-permute-start.9 = (bf16[2,2,128,128]{3,2,1,0:T(8,128)(2,1)S(1)}, bf16[2,2,128,128]{3,2,1,0:T(8,128)(2,1)S(1)}, u32[]{:S(2)}, u32[]{:S(2)}) collective-permute-start(bf16[2,2,128,128]{3,2,1,0:T(8,128)(2,1)S(1)} %get-tuple-element.34), channel_id=1, source_target_pairs={{0,24},{4,28},{8,0},{12,4},{16,8},{20,12},{24,16},{28,20},{1,25},{... | collective-permute-start | bytes 393224 | tf_op jit(solution)/shard_map/ppermute | solution.py:331
  26.6 1.5 %collective-permute-start.10 = (bf16[32,16,128]{2,1,0:T(8,128)(2,1)S(1)}, bf16[32,16,128]{2,1,0:T(8,128)(2,1)S(1)}, u32[]{:S(2)}, u32[]{:S(2)}) collective-permute-start(bf16[32,16,128]{2,1,0:T(8,128)(2,1)S(1)} %get-tuple-element.35), channel_id=1, source_target_pairs={{0,2},{1,3},{2,0},{3,1},{4,6},{5,7},{6,4},{7,5},{8,10},{9,11},{10,... | collective-permute-start | bytes 393224 | tf_op jit(solution)/shard_map/ppermute | solution.py:344
  28.1 0.0 collective-permute-done.6.refs_0_
  28.2 0.0 collective-permute-start.11
  28.2 0.0 collective-permute-done.7.refs_1_
  28.2 1.6 %collective-permute-done.8.refs_2_ = bf16[2,2,128,128]{3,2,1,0:T(8,128)(2,1)S(1)} collective-permute-done((bf16[2,2,128,128]{3,2,1,0:T(8,128)(2,1)S(1)}, bf16[2,2,128,128]{3,2,1,0:T(8,128)(2,1)S(1)}, u32[]{:S(2)}, u32[]{:S(2)}) %collective-permute-start.8) | collective-permute-done | bytes 131104 | tf_op jit(solution)/shard_map/ppermute | solution.py:340
  29.8 2.5 %collective-permute-done.9.refs_3_ = bf16[2,2,128,128]{3,2,1,0:T(8,128)(2,1)S(1)} collective-permute-done((bf16[2,2,128,128]{3,2,1,0:T(8,128)(2,1)S(1)}, bf16[2,2,128,128]{3,2,1,0:T(8,128)(2,1)S(1)}, u32[]{:S(2)}, u32[]{:S(2)}) %collective-permute-start.9) | collective-permute-done | bytes 131104 | tf_op jit(solution)/shard_map/ppermute | solution.py:331
  32.3 0.5 %collective-permute-done.10.refs_4_ = bf16[32,16,128]{2,1,0:T(8,128)(2,1)S(1)} collective-permute-done((bf16[32,16,128]{2,1,0:T(8,128)(2,1)S(1)}, bf16[32,16,128]{2,1,0:T(8,128)(2,1)S(1)}, u32[]{:S(2)}, u32[]{:S(2)}) %collective-permute-start.10) | collective-permute-done | bytes 131104 | tf_op jit(solution)/shard_map/ppermute | solution.py:344
  32.8 0.0 collective-permute-done.11.refs_5_
  32.8 1.0 %finish.1 = (bf16[32,64,128]{2,1,0:T(8,128)(2,1)}, bf16[128,2,128]{2,1,0:T(2,128)(2,1)}, bf16[128,2,128]{2,1,0:T(2,128)(2,1)}) custom-call(bf16[2,2,128,128]{3,2,1,0:T(8,128)(2,1)S(1)} %collective-permute-done.6.refs_0_, bf16[32,16,128]{2,1,0:T(8,128)(2,1)S(1)} %collective-permute-done.7.refs_1_, ...), custom_call_target="tpu_custom_call" | custom-call | tf_op jit(solution)/shard_map/finish/pallas_call | solution.py:315
Async XLA Ops:
  0.6 15.7 %copy-start = (bf16[128,16,128]{2,1,0:T(8,128)(2,1)S(1)}, bf16[128,16,128]{2,1,0:T(8,128)(2,1)}, u32[]{:S(2)}) copy-start(bf16[128,16,128]{2,1,0:T(8,128)(2,1)} %q_ref.3) | copy-start | bytes 1572868
  2.0 9.7 %collective-permute-start = (bf16[2,2,128,128]{3,2,1,0:T(8,128)(2,1)S(1)}, bf16[2,2,128,128]{3,2,1,0:T(8,128)(2,1)S(1)}, u32[]{:S(2)}, u32[]{:S(2)}) collective-permute-start(bf16[2,2,128,128]{3,2,1,0:T(8,128)(2,1)S(1)} %get-tuple-element.23), channel_id=1, source_target_pairs={{0,0},{4,8},{8,4},{12,16},{16,12},{20,24},{24,20},{28,28},{1,1},{5... | collective-permute-start | bytes 393224 | tf_op jit(solution)/shard_map/ppermute | solution.py:340
  2.6 10.6 %collective-permute-start.1 = (bf16[2,2,128,128]{3,2,1,0:T(8,128)(2,1)S(1)}, bf16[2,2,128,128]{3,2,1,0:T(8,128)(2,1)S(1)}, u32[]{:S(2)}, u32[]{:S(2)}) collective-permute-start(bf16[2,2,128,128]{3,2,1,0:T(8,128)(2,1)S(1)} %get-tuple-element.24), channel_id=1, source_target_pairs={{0,4},{4,0},{8,12},{12,8},{16,20},{20,16},{24,28},{28,24},{1,5},{5... | collective-permute-start | bytes 393224 | tf_op jit(solution)/shard_map/ppermute | solution.py:340
  8.4 7.9 %collective-permute-start.2 = (bf16[2,2,128,128]{3,2,1,0:T(8,128)(2,1)S(1)}, bf16[2,2,128,128]{3,2,1,0:T(8,128)(2,1)S(1)}, u32[]{:S(2)}, u32[]{:S(2)}) collective-permute-start(bf16[2,2,128,128]{3,2,1,0:T(8,128)(2,1)S(1)} %get-tuple-element.25), channel_id=1, source_target_pairs={{0,8},{4,12},{8,16},{12,20},{16,24},{20,28},{24,0},{28,4},{1,9},{5... | collective-permute-start | bytes 393224 | tf_op jit(solution)/shard_map/ppermute | solution.py:331
  10.0 6.3 %collective-permute-start.5 = (bf16[32,16,128]{2,1,0:T(8,128)(2,1)S(1)}, bf16[32,16,128]{2,1,0:T(8,128)(2,1)S(1)}, u32[]{:S(2)}, u32[]{:S(2)}) collective-permute-start(bf16[32,16,128]{2,1,0:T(8,128)(2,1)S(1)} %get-tuple-element.29), channel_id=1, source_target_pairs={{0,1},{1,0},{2,3},{3,2},{4,5},{5,4},{6,7},{7,6},{8,9},{9,8},{10,11... | collective-permute-start | bytes 393224 | tf_op jit(solution)/shard_map/ppermute | solution.py:344
  10.0 8.3 %collective-permute-start.3 = (bf16[32,16,128]{2,1,0:T(8,128)(2,1)S(1)}, bf16[32,16,128]{2,1,0:T(8,128)(2,1)S(1)}, u32[]{:S(2)}, u32[]{:S(2)}) collective-permute-start(bf16[32,16,128]{2,1,0:T(8,128)(2,1)S(1)} %get-tuple-element.26), channel_id=1, source_target_pairs={{0,3},{1,2},{2,1},{3,0},{4,7},{5,6},{6,5},{7,4},{8,11},{9,10},{10,... | collective-permute-start | bytes 393224 | tf_op jit(solution)/shard_map/ppermute | solution.py:344
  11.6 7.0 %collective-permute-start.4 = (bf16[32,16,128]{2,1,0:T(8,128)(2,1)S(1)}, bf16[32,16,128]{2,1,0:T(8,128)(2,1)S(1)}, u32[]{:S(2)}, u32[]{:S(2)}) collective-permute-start(bf16[32,16,128]{2,1,0:T(8,128)(2,1)S(1)} %get-tuple-element.27), channel_id=1, source_target_pairs={{0,2},{1,3},{2,0},{3,1},{4,6},{5,7},{6,4},{7,5},{8,10},{9,11},{10,... | collective-permute-start | bytes 393224 | tf_op jit(solution)/shard_map/ppermute | solution.py:344
  20.6 7.6 %collective-permute-start.6 = (bf16[2,2,128,128]{3,2,1,0:T(8,128)(2,1)S(1)}, bf16[2,2,128,128]{3,2,1,0:T(8,128)(2,1)S(1)}, u32[]{:S(2)}, u32[]{:S(2)}) collective-permute-start(bf16[2,2,128,128]{3,2,1,0:T(8,128)(2,1)S(1)} %get-tuple-element.31), channel_id=1, source_target_pairs={{0,0},{4,8},{8,4},{12,16},{16,12},{20,24},{24,20},{28,28},{1,1},{5... | collective-permute-start | bytes 393224 | tf_op jit(solution)/shard_map/ppermute | solution.py:340
  21.3 6.9 %collective-permute-start.7 = (bf16[32,16,128]{2,1,0:T(8,128)(2,1)S(1)}, bf16[32,16,128]{2,1,0:T(8,128)(2,1)S(1)}, u32[]{:S(2)}, u32[]{:S(2)}) collective-permute-start(bf16[32,16,128]{2,1,0:T(8,128)(2,1)S(1)} %get-tuple-element.32), channel_id=1, source_target_pairs={{0,3},{1,2},{2,1},{3,0},{4,7},{5,6},{6,5},{7,4},{8,11},{9,10},{10,... | collective-permute-start | bytes 393224 | tf_op jit(solution)/shard_map/ppermute | solution.py:344
  21.9 7.8 %collective-permute-start.8 = (bf16[2,2,128,128]{3,2,1,0:T(8,128)(2,1)S(1)}, bf16[2,2,128,128]{3,2,1,0:T(8,128)(2,1)S(1)}, u32[]{:S(2)}, u32[]{:S(2)}) collective-permute-start(bf16[2,2,128,128]{3,2,1,0:T(8,128)(2,1)S(1)} %get-tuple-element.33), channel_id=1, source_target_pairs={{0,4},{4,0},{8,12},{12,8},{16,20},{20,16},{24,28},{28,24},{1,5},{5... | collective-permute-start | bytes 393224 | tf_op jit(solution)/shard_map/ppermute | solution.py:340
  26.0 6.3 %collective-permute-start.9 = (bf16[2,2,128,128]{3,2,1,0:T(8,128)(2,1)S(1)}, bf16[2,2,128,128]{3,2,1,0:T(8,128)(2,1)S(1)}, u32[]{:S(2)}, u32[]{:S(2)}) collective-permute-start(bf16[2,2,128,128]{3,2,1,0:T(8,128)(2,1)S(1)} %get-tuple-element.34), channel_id=1, source_target_pairs={{0,24},{4,28},{8,0},{12,4},{16,8},{20,12},{24,16},{28,20},{1,25},{... | collective-permute-start | bytes 393224 | tf_op jit(solution)/shard_map/ppermute | solution.py:331
  26.6 6.1 %collective-permute-start.10 = (bf16[32,16,128]{2,1,0:T(8,128)(2,1)S(1)}, bf16[32,16,128]{2,1,0:T(8,128)(2,1)S(1)}, u32[]{:S(2)}, u32[]{:S(2)}) collective-permute-start(bf16[32,16,128]{2,1,0:T(8,128)(2,1)S(1)} %get-tuple-element.35), channel_id=1, source_target_pairs={{0,2},{1,3},{2,0},{3,1},{4,6},{5,7},{6,4},{7,5},{8,10},{9,11},{10,... | collective-permute-start | bytes 393224 | tf_op jit(solution)/shard_map/ppermute | solution.py:344
  28.2 4.6 %collective-permute-start.11 = (bf16[32,16,128]{2,1,0:T(8,128)(2,1)S(1)}, bf16[32,16,128]{2,1,0:T(8,128)(2,1)S(1)}, u32[]{:S(2)}, u32[]{:S(2)}) collective-permute-start(bf16[32,16,128]{2,1,0:T(8,128)(2,1)S(1)} %get-tuple-element.36), channel_id=1, source_target_pairs={{0,1},{1,0},{2,3},{3,2},{4,5},{5,4},{6,7},{7,6},{8,9},{9,8},{10,11... | collective-permute-start | bytes 393224 | tf_op jit(solution)/shard_map/ppermute | solution.py:344

commit v9 on v8

--- a/solution.py
+++ b/solution.py
@@ -21,7 +21,7 @@
 
 def stages(parts):
     rest = list(range(parts - 1, 1, -1))
-    return [[0, 1], rest]
+    return [[0, 1, *rest[:-1]], rest[-1:]]
 
 
 def regroup(buf):
@@ -30,7 +30,7 @@
 
 
 def prep_kernel(parts, lengths_ref, prefixes_ref, cot_ref, key_ref, value_ref, *rest):
-    kv_outs, cot_outs, rest = rest[:4], rest[4 : parts + 4], rest[parts + 4 :]
+    kv_outs, cot_outs, rest = rest[:3], rest[3 : parts + 3], rest[parts + 3 :]
     range_out, key_buf, value_buf, lengths, prefixes, sems, scalar_sems = rest
     heads = cot_ref.shape[1] // parts
     me = lax.axis_index("kvh")
@@ -87,9 +87,9 @@
     ]
     outs = pl.pallas_call(
         functools.partial(prep_kernel, parts),
-        out_shape=(block,) * 4 + (piece,) * parts + (pltpu.VMEM((parts, 2, lanes), jnp.int32),),
+        out_shape=(block,) * 3 + (piece,) * parts + (pltpu.VMEM((parts, 2, lanes), jnp.int32),),
         in_specs=[_HBM] * 5,
-        out_specs=(_VMEM,) * (parts + 5),
+        out_specs=(_VMEM,) * (parts + 4),
         scratch_shapes=[
             pltpu.VMEM(keys.shape, jnp.bfloat16),
             pltpu.VMEM(values.shape, jnp.bfloat16),
@@ -101,7 +101,7 @@
         compiler_params=pltpu.CompilerParams(vmem_limit_bytes=VMEM_BYTES),
         name="prepare",
     )(*operands)
-    return outs[:4], outs[4:-1], outs[-1]
+    return outs[:3], outs[3:-1], outs[-1]
 
 
 def bounds(position, lengths, prefixes):
@@ -132,7 +132,7 @@
 
 def grad_kernel(masks, parts, is_first, is_last, range_ref, q_ref, *refs):
     refs = list(refs)
-    kv_own, kv_odd, kv_even, kv_far = [refs.pop(0) for _ in range(4)]
+    kv_own, kv_even, kv_far, kv_odd = [refs.pop(0) for _ in range(4)]
     cots = [refs.pop(0) for _ in masks]
     carried = None if is_first else refs.pop(0)
     dqs = [refs.pop(0) for _ in masks]
@@ -258,7 +258,7 @@
     else:
         outs += [pltpu.VMEM(acc_shape, jnp.float32)]
     own, far, even, odd = blocks
-    operands = [ranges, queries, own, odd, even, far, *cots]
+    operands = [ranges, queries, own, even, far, odd, *cots]
     operands += [] if carried is None else [carried]
     outs = pl.pallas_call(
         functools.partial(grad_kernel, masks, parts, carried is None, is_last),
@@ -283,7 +283,7 @@
 
 
 def finish_order(parts):
-    return ["odd", parts - 1, "even", "far", *range(parts - 2, -1, -1), "own"]
+    return ["odd", "far", parts - 1, "even", *range(parts - 2, -1, -1), "own"]
 
 
 def finish_kernel(parts, *refs):
@@ -331,21 +331,21 @@
     return lax.ppermute(block, "seq", [(i, (i + distance) % count) for i in range(count)])
 
 
-def paired(block, first):
+def paired(block):
+    return lax.ppermute(block, "seq", [(i, i ^ 1) for i in range(lax.axis_size("seq"))])
+
+
+def ringed(block):
     count = lax.axis_size("seq")
     route = []
     for i in range(count):
-        partner = i + 1 if i % 2 == first else i - 1
-        route.append((i, partner if 0 <= partner < count else i))
+        target = i + 2 if i % 2 == 0 else i - 2
+        route.append((i, min(max(target, 0), count - 1)))
     return lax.ppermute(block, "seq", route)
 
 
 def swapped(block, mask):
     return lax.ppermute(block, "kvh", [(i, i ^ mask) for i in range(lax.axis_size("kvh"))])
-
-
-def neighbours(far, even, odd, distance):
-    return [shifted(far, distance), paired(even, 0), paired(odd, 1)]
 
 
 def local(queries, keys, values, output_gradient, doc_lengths, prefix_lengths):
@@ -353,7 +353,8 @@
     kv, cots, ranges = prepare(
         doc_lengths, prefix_lengths, output_gradient, keys, values, parts
     )
-    blocks = [kv[0]] + neighbours(*kv[1:], BACK)
+    even = paired(kv[2])
+    blocks = [kv[0], shifted(kv[1], BACK), even, ringed(even)]
     cots = [cots[0]] + [swapped(cots[mask], mask) for mask in range(1, parts)]
     dqs, carried = {}, [None]
     for masks in stages(parts):
@@ -362,7 +363,8 @@
         )
         for mask, dq in zip(masks, found):
             dqs[mask] = swapped(dq, mask) if mask else dq
-    partials = [carried[0]] + neighbours(*carried[1:], -BACK)
+    own, far, even, odd = carried
+    partials = [own, shifted(far, -BACK), paired(even), ringed(paired(odd))]
     return finish([dqs[mask] for mask in range(parts)], partials)
 
 

time: 34 us -> 32 us (0.941)
  waiting for transfers between devices: 9.06 us -> 7.26 us
    ppermute x2, waiting for transfers between devices: 5.57 us -> 0.01 us  [shifted(): lax.ppermute(block, 'seq', [(i, (i + distance) % count) for i in range(co...]
    ppermute x4 -> x5, starting transfers between devices: 11.1 us -> 7.27 us  [the longest x3 5.18 us: paired(): lax.ppermute(block, 'seq', [(i, i ^ 1) for i in range(lax.axis_size('seq'...]
    ppermute x2, starting transfers between devices: 2.26 us -> 5.18 us  [shifted(): lax.ppermute(block, 'seq', [(i, (i + distance) % count) for i in range(co...]
    ppermute x6, waiting for transfers between devices: 0.78 us -> 3.09 us  [swapped(): lax.ppermute(block, 'kvh', [(i, i ^ mask) for i in range(lax.axis_size('k...]
    ppermute x4 -> x5, waiting for transfers between devices: 2.71 us -> 4.17 us  [the longest x3 2.31 us: paired(): lax.ppermute(block, 'seq', [(i, i ^ 1) for i in range(lax.axis_size('seq'...]
    ppermute x6, starting transfers between devices: 4.33 us -> 5.3 us  [swapped(): lax.ppermute(block, 'kvh', [(i, i ^ mask) for i in range(lax.axis_size('k...]
  transfers between devices with their start and end apart: 12 -> 13, of which waited for: 6 -> 7; matrix products, arithmetic and copies ran while one was open for 0% -> 0% of each run, Pallas kernels for 6% -> 9%
where the time goes in v9:
time: 32 us; the launch traced here: 31.9 us
  starting transfers between devices  17.7 us (55%)
  waiting for transfers between devices  7.26 us (23%)
  Pallas kernels  6.21 us (19%)
  between operations  0.68 us (2%)
    ppermute x6, starting transfers between devices, swapped(): lax.ppermute(block, 'kvh', [(i, i ^ mask) for i in range(lax.axis_size('k...  5.3 us
    ppermute x3, starting transfers between devices, paired(): lax.ppermute(block, 'seq', [(i, i ^ 1) for i in range(lax.axis_size('seq'...  5.18 us
    ppermute x2, starting transfers between devices, shifted(): lax.ppermute(block, 'seq', [(i, (i + distance) % count) for i in range(co...  5.18 us
    pallas_call x2, Pallas kernels, gradients(): pl.pallas_call(functools.partial(grad_kernel, masks, parts, carried is No...  3.9 us
    ppermute x6, waiting for transfers between devices, swapped(): lax.ppermute(block, 'kvh', [(i, i ^ mask) for i in range(lax.axis_size('k...  3.09 us
    ppermute x3, waiting for transfers between devices, paired(): lax.ppermute(block, 'seq', [(i, i ^ 1) for i in range(lax.axis_size('seq'...  2.31 us
    ppermute x2, starting transfers between devices, ringed(): return lax.ppermute(block, 'seq', route)  2.09 us
    ppermute x2, waiting for transfers between devices, ringed(): return lax.ppermute(block, 'seq', route)  1.86 us
  transfers between devices with their start and end apart: 13, of which 7 were waited for; matrix products, arithmetic and copies ran while one was open for 0% of the time, Pallas kernels for 9%

profile of v9, /device:TPU:0, one launch (start us, length us, event | category | flops | bytes accessed | tf_op | source)
XLA Modules:
  0.0 31.9 jit_solution(5758909326795003488)
XLA Ops:
  0.6 0.0 copy-start
  0.6 1.3 %prepare.1 = (bf16[2,2,128,128]{3,2,1,0:T(8,128)(2,1)S(1)}, bf16[2,2,128,128]{3,2,1,0:T(8,128)(2,1)S(1)}, bf16[2,2,128,128]{3,2,1,0:T(8,128)(2,1)S(1)}, bf16[32,...) custom-call(s32[8]{0:T(128)} %lengths_ref.1, ...), custom_call_target="tpu_custom_call" | custom-call | tf_op jit(solution)/shard_map/prepare/pallas_call | solution.py:88
  1.9 3.0 %collective-permute-start = (bf16[2,2,128,128]{3,2,1,0:T(8,128)(2,1)S(1)}, bf16[2,2,128,128]{3,2,1,0:T(8,128)(2,1)S(1)}, u32[]{:S(2)}, u32[]{:S(2)}) collective-permute-start(bf16[2,2,128,128]{3,2,1,0:T(8,128)(2,1)S(1)} %get-tuple-element.22), channel_id=1, source_target_pairs={{0,4},{4,0},{8,12},{12,8},{16,20},{20,16},{24,28},{28,24},{1,5},{5... | collective-permute-start | bytes 393224 | tf_op jit(solution)/shard_map/ppermute | solution.py:335
  4.9 1.6 %collective-permute-start.1 = (bf16[2,2,128,128]{3,2,1,0:T(8,128)(2,1)S(1)}, bf16[2,2,128,128]{3,2,1,0:T(8,128)(2,1)S(1)}, u32[]{:S(2)}, u32[]{:S(2)}) collective-permute-start(bf16[2,2,128,128]{3,2,1,0:T(8,128)(2,1)S(1)} %get-tuple-element.23), channel_id=1, source_target_pairs={{0,8},{4,12},{8,16},{12,20},{16,24},{20,28},{24,0},{28,4},{1,9},{5... | collective-permute-start | bytes 393224 | tf_op jit(solution)/shard_map/ppermute | solution.py:331
  6.5 0.0 collective-permute-start.4
  6.5 1.6 %collective-permute-start.5 = (bf16[32,16,128]{2,1,0:T(8,128)(2,1)S(1)}, bf16[32,16,128]{2,1,0:T(8,128)(2,1)S(1)}, u32[]{:S(2)}, u32[]{:S(2)}) collective-permute-start(bf16[32,16,128]{2,1,0:T(8,128)(2,1)S(1)} %get-tuple-element.27), channel_id=1, source_target_pairs={{0,3},{1,2},{2,1},{3,0},{4,7},{5,6},{6,5},{7,4},{8,11},{9,10},{10,... | collective-permute-start | bytes 393224 | tf_op jit(solution)/shard_map/ppermute | solution.py:348
  8.2 0.3 collective-permute-done.refs_1_
  8.4 1.8 %collective-permute-start.2 = (bf16[2,2,128,128]{3,2,1,0:T(8,128)(2,1)S(1)}, bf16[2,2,128,128]{3,2,1,0:T(8,128)(2,1)S(1)}, u32[]{:S(2)}, u32[]{:S(2)}) collective-permute-start(bf16[2,2,128,128]{3,2,1,0:T(8,128)(2,1)S(1)} %collective-permute-done.refs_1_), channel_id=1, source_target_pairs={{0,8},{4,0},{8,16},{12,4},{16,24},{20,12},{24,28},{28,20},{1,9},{5... | collective-permute-start | bytes 393224 | tf_op jit(solution)/shard_map/ppermute | solution.py:344
  10.3 1.5 %collective-permute-start.3 = (bf16[32,16,128]{2,1,0:T(8,128)(2,1)S(1)}, bf16[32,16,128]{2,1,0:T(8,128)(2,1)S(1)}, u32[]{:S(2)}, u32[]{:S(2)}) collective-permute-start(bf16[32,16,128]{2,1,0:T(8,128)(2,1)S(1)} %get-tuple-element.24), channel_id=1, source_target_pairs={{0,2},{1,3},{2,0},{3,1},{4,6},{5,7},{6,4},{7,5},{8,10},{9,11},{10,... | collective-permute-start | bytes 393224 | tf_op jit(solution)/shard_map/ppermute | solution.py:348
  11.8 0.0 collective-permute-done.1.refs_2_
  11.8 0.0 collective-permute-done.4.refs_5_
  11.8 0.2 collective-permute-done.5.refs_6_
  12.0 1.6 %collective-permute-done.2.refs_3_ = bf16[2,2,128,128]{3,2,1,0:T(8,128)(2,1)S(1)} collective-permute-done((bf16[2,2,128,128]{3,2,1,0:T(8,128)(2,1)S(1)}, bf16[2,2,128,128]{3,2,1,0:T(8,128)(2,1)S(1)}, u32[]{:S(2)}, u32[]{:S(2)}) %collective-permute-start.2) | collective-permute-done | bytes 131104 | tf_op jit(solution)/shard_map/ppermute | solution.py:344
  13.6 0.0 copy-done
  13.6 2.7 %gradients.2 = (bf16[32,16,128]{2,1,0:T(8,128)(2,1)S(1)}, bf16[32,16,128]{2,1,0:T(8,128)(2,1)S(1)}, bf16[32,16,128]{2,1,0:T(8,128)(2,1)S(1)}, f32[2,2,512,128]{3,2,1,0:T(8,128)S(1)}) custom-call(s32[4,2,256]{2,1,0:T(2,128)S(1)} %get-tuple-element.20.range_ref, bf16[128,16,128]{2,1,0:T(8,128)(2,1)S(1)} %copy-done, ...), custom_call_target="tpu_custom_call" | custom-call | flops 1006632960 | bytes 2097152 | tf_op jit(solution)/shard_map/gradients/pallas_call | solution.py:263
  16.3 0.0 collective-permute-done.3.refs_4_
  16.3 1.2 %gradients.3 = (bf16[32,16,128]{2,1,0:T(8,128)(2,1)S(1)}, f32[2,2,128,128]{3,2,1,0:T(8,128)S(1)}, bf16[2,2,128,128]{3,2,1,0:T(8,128)(2,1)S(1)}, bf16[2,2,128,128...) custom-call(s32[4,2,256]{2,1,0:T(2,128)S(1)} %get-tuple-element.20.range_ref, bf16[128,16,128]{2,1,0:T(8,128)(2,1)S(1)} %copy-done, ...), custom_call_target="tpu_custom_call" | custom-call | flops 335544320 | bytes 2097152 | tf_op jit(solution)/shard_map/gradients/pallas_call | solution.py:263
  17.5 1.6 %collective-permute-start.6 = (bf16[2,2,128,128]{3,2,1,0:T(8,128)(2,1)S(1)}, bf16[2,2,128,128]{3,2,1,0:T(8,128)(2,1)S(1)}, u32[]{:S(2)}, u32[]{:S(2)}) collective-permute-start(bf16[2,2,128,128]{3,2,1,0:T(8,128)(2,1)S(1)} %get-tuple-element.29), channel_id=1, source_target_pairs={{0,4},{4,0},{8,12},{12,8},{16,20},{20,16},{24,28},{28,24},{1,5},{5... | collective-permute-start | bytes 393224 | tf_op jit(solution)/shard_map/ppermute | solution.py:335
  19.1 3.6 %collective-permute-start.8 = (bf16[2,2,128,128]{3,2,1,0:T(8,128)(2,1)S(1)}, bf16[2,2,128,128]{3,2,1,0:T(8,128)(2,1)S(1)}, u32[]{:S(2)}, u32[]{:S(2)}) collective-permute-start(bf16[2,2,128,128]{3,2,1,0:T(8,128)(2,1)S(1)} %get-tuple-element.30), channel_id=1, source_target_pairs={{0,24},{4,28},{8,0},{12,4},{16,8},{20,12},{24,16},{28,20},{1,25},{... | collective-permute-start | bytes 393224 | tf_op jit(solution)/shard_map/ppermute | solution.py:331
  22.7 0.5 %collective-permute-start.10 = (bf16[2,2,128,128]{3,2,1,0:T(8,128)(2,1)S(1)}, bf16[2,2,128,128]{3,2,1,0:T(8,128)(2,1)S(1)}, u32[]{:S(2)}, u32[]{:S(2)}) collective-permute-start(bf16[2,2,128,128]{3,2,1,0:T(8,128)(2,1)S(1)} %get-tuple-element.32), channel_id=1, source_target_pairs={{0,4},{4,0},{8,12},{12,8},{16,20},{20,16},{24,28},{28,24},{1,5},{5... | collective-permute-start | bytes 393224 | tf_op jit(solution)/shard_map/ppermute | solution.py:335
  23.3 1.5 %collective-permute-start.11 = (bf16[32,16,128]{2,1,0:T(8,128)(2,1)S(1)}, bf16[32,16,128]{2,1,0:T(8,128)(2,1)S(1)}, u32[]{:S(2)}, u32[]{:S(2)}) collective-permute-start(bf16[32,16,128]{2,1,0:T(8,128)(2,1)S(1)} %get-tuple-element.33), channel_id=1, source_target_pairs={{0,2},{1,3},{2,0},{3,1},{4,6},{5,7},{6,4},{7,5},{8,10},{9,11},{10,... | collective-permute-start | bytes 393224 | tf_op jit(solution)/shard_map/ppermute | solution.py:348
  24.8 0.0 collective-permute-start.9
  24.8 0.0 collective-permute-done.6
  24.8 0.6 %collective-permute-start.12 = (bf16[32,16,128]{2,1,0:T(8,128)(2,1)S(1)}, bf16[32,16,128]{2,1,0:T(8,128)(2,1)S(1)}, u32[]{:S(2)}, u32[]{:S(2)}) collective-permute-start(bf16[32,16,128]{2,1,0:T(8,128)(2,1)S(1)} %get-tuple-element.34), channel_id=1, source_target_pairs={{0,1},{1,0},{2,3},{3,2},{4,5},{5,4},{6,7},{7,6},{8,9},{9,8},{10,11... | collective-permute-start | bytes 393224 | tf_op jit(solution)/shard_map/ppermute | solution.py:348
  25.4 0.0 collective-permute-done.8.refs_1_
  25.4 0.3 collective-permute-start.7
  25.7 2.0 %collective-permute-done.10.refs_3_ = bf16[2,2,128,128]{3,2,1,0:T(8,128)(2,1)S(1)} collective-permute-done((bf16[2,2,128,128]{3,2,1,0:T(8,128)(2,1)S(1)}, bf16[2,2,128,128]{3,2,1,0:T(8,128)(2,1)S(1)}, u32[]{:S(2)}, u32[]{:S(2)}) %collective-permute-start.10) | collective-permute-done | bytes 131104 | tf_op jit(solution)/shard_map/ppermute | solution.py:335
  27.7 1.0 %collective-permute-done.11.refs_4_ = bf16[32,16,128]{2,1,0:T(8,128)(2,1)S(1)} collective-permute-done((bf16[32,16,128]{2,1,0:T(8,128)(2,1)S(1)}, bf16[32,16,128]{2,1,0:T(8,128)(2,1)S(1)}, u32[]{:S(2)}, u32[]{:S(2)}) %collective-permute-start.11) | collective-permute-done | bytes 131104 | tf_op jit(solution)/shard_map/ppermute | solution.py:348
  28.7 1.9 %collective-permute-done.9.refs_2_ = bf16[32,16,128]{2,1,0:T(8,128)(2,1)S(1)} collective-permute-done((bf16[32,16,128]{2,1,0:T(8,128)(2,1)S(1)}, bf16[32,16,128]{2,1,0:T(8,128)(2,1)S(1)}, u32[]{:S(2)}, u32[]{:S(2)}) %collective-permute-start.9) | collective-permute-done | bytes 131104 | tf_op jit(solution)/shard_map/ppermute | solution.py:348
  30.6 0.0 collective-permute-done.12.refs_5_
  30.6 0.3 collective-permute-done.7.refs_0_
  30.9 1.0 %finish.1 = (bf16[32,64,128]{2,1,0:T(8,128)(2,1)}, bf16[128,2,128]{2,1,0:T(2,128)(2,1)}, bf16[128,2,128]{2,1,0:T(2,128)(2,1)}) custom-call(bf16[2,2,128,128]{3,2,1,0:T(8,128)(2,1)S(1)} %collective-permute-done.7.refs_0_, bf16[2,2,128,128]{3,2,1,0:T(8,128)(2,1)S(1)} %collective-permute-done.8.refs_1_, ...), custom_call_target="tpu_custom_call" | custom-call | tf_op jit(solution)/shard_map/finish/pallas_call | solution.py:315
Async XLA Ops:
  0.6 12.9 %copy-start = (bf16[128,16,128]{2,1,0:T(8,128)(2,1)S(1)}, bf16[128,16,128]{2,1,0:T(8,128)(2,1)}, u32[]{:S(2)}) copy-start(bf16[128,16,128]{2,1,0:T(8,128)(2,1)} %q_ref.3) | copy-start | bytes 1572868
  1.9 6.5 %collective-permute-start = (bf16[2,2,128,128]{3,2,1,0:T(8,128)(2,1)S(1)}, bf16[2,2,128,128]{3,2,1,0:T(8,128)(2,1)S(1)}, u32[]{:S(2)}, u32[]{:S(2)}) collective-permute-start(bf16[2,2,128,128]{3,2,1,0:T(8,128)(2,1)S(1)} %get-tuple-element.22), channel_id=1, source_target_pairs={{0,4},{4,0},{8,12},{12,8},{16,20},{20,16},{24,28},{28,24},{1,5},{5... | collective-permute-start | bytes 393224 | tf_op jit(solution)/shard_map/ppermute | solution.py:335
  4.9 6.8 %collective-permute-start.1 = (bf16[2,2,128,128]{3,2,1,0:T(8,128)(2,1)S(1)}, bf16[2,2,128,128]{3,2,1,0:T(8,128)(2,1)S(1)}, u32[]{:S(2)}, u32[]{:S(2)}) collective-permute-start(bf16[2,2,128,128]{3,2,1,0:T(8,128)(2,1)S(1)} %get-tuple-element.23), channel_id=1, source_target_pairs={{0,8},{4,12},{8,16},{12,20},{16,24},{20,28},{24,0},{28,4},{1,9},{5... | collective-permute-start | bytes 393224 | tf_op jit(solution)/shard_map/ppermute | solution.py:331
  6.5 5.3 %collective-permute-start.4 = (bf16[32,16,128]{2,1,0:T(8,128)(2,1)S(1)}, bf16[32,16,128]{2,1,0:T(8,128)(2,1)S(1)}, u32[]{:S(2)}, u32[]{:S(2)}) collective-permute-start(bf16[32,16,128]{2,1,0:T(8,128)(2,1)S(1)} %get-tuple-element.26), channel_id=1, source_target_pairs={{0,1},{1,0},{2,3},{3,2},{4,5},{5,4},{6,7},{7,6},{8,9},{9,8},{10,11... | collective-permute-start | bytes 393224 | tf_op jit(solution)/shard_map/ppermute | solution.py:348
  6.5 5.5 %collective-permute-start.5 = (bf16[32,16,128]{2,1,0:T(8,128)(2,1)S(1)}, bf16[32,16,128]{2,1,0:T(8,128)(2,1)S(1)}, u32[]{:S(2)}, u32[]{:S(2)}) collective-permute-start(bf16[32,16,128]{2,1,0:T(8,128)(2,1)S(1)} %get-tuple-element.27), channel_id=1, source_target_pairs={{0,3},{1,2},{2,1},{3,0},{4,7},{5,6},{6,5},{7,4},{8,11},{9,10},{10,... | collective-permute-start | bytes 393224 | tf_op jit(solution)/shard_map/ppermute | solution.py:348
  8.4 5.1 %collective-permute-start.2 = (bf16[2,2,128,128]{3,2,1,0:T(8,128)(2,1)S(1)}, bf16[2,2,128,128]{3,2,1,0:T(8,128)(2,1)S(1)}, u32[]{:S(2)}, u32[]{:S(2)}) collective-permute-start(bf16[2,2,128,128]{3,2,1,0:T(8,128)(2,1)S(1)} %collective-permute-done.refs_1_), channel_id=1, source_target_pairs={{0,8},{4,0},{8,16},{12,4},{16,24},{20,12},{24,28},{28,20},{1,9},{5... | collective-permute-start | bytes 393224 | tf_op jit(solution)/shard_map/ppermute | solution.py:344
  10.3 6.0 %collective-permute-start.3 = (bf16[32,16,128]{2,1,0:T(8,128)(2,1)S(1)}, bf16[32,16,128]{2,1,0:T(8,128)(2,1)S(1)}, u32[]{:S(2)}, u32[]{:S(2)}) collective-permute-start(bf16[32,16,128]{2,1,0:T(8,128)(2,1)S(1)} %get-tuple-element.24), channel_id=1, source_target_pairs={{0,2},{1,3},{2,0},{3,1},{4,6},{5,7},{6,4},{7,5},{8,10},{9,11},{10,... | collective-permute-start | bytes 393224 | tf_op jit(solution)/shard_map/ppermute | solution.py:348
  17.5 7.3 %collective-permute-start.6 = (bf16[2,2,128,128]{3,2,1,0:T(8,128)(2,1)S(1)}, bf16[2,2,128,128]{3,2,1,0:T(8,128)(2,1)S(1)}, u32[]{:S(2)}, u32[]{:S(2)}) collective-permute-start(bf16[2,2,128,128]{3,2,1,0:T(8,128)(2,1)S(1)} %get-tuple-element.29), channel_id=1, source_target_pairs={{0,4},{4,0},{8,12},{12,8},{16,20},{20,16},{24,28},{28,24},{1,5},{5... | collective-permute-start | bytes 393224 | tf_op jit(solution)/shard_map/ppermute | solution.py:335
  19.1 6.3 %collective-permute-start.8 = (bf16[2,2,128,128]{3,2,1,0:T(8,128)(2,1)S(1)}, bf16[2,2,128,128]{3,2,1,0:T(8,128)(2,1)S(1)}, u32[]{:S(2)}, u32[]{:S(2)}) collective-permute-start(bf16[2,2,128,128]{3,2,1,0:T(8,128)(2,1)S(1)} %get-tuple-element.30), channel_id=1, source_target_pairs={{0,24},{4,28},{8,0},{12,4},{16,8},{20,12},{24,16},{28,20},{1,25},{... | collective-permute-start | bytes 393224 | tf_op jit(solution)/shard_map/ppermute | solution.py:331
  22.7 5.0 %collective-permute-start.10 = (bf16[2,2,128,128]{3,2,1,0:T(8,128)(2,1)S(1)}, bf16[2,2,128,128]{3,2,1,0:T(8,128)(2,1)S(1)}, u32[]{:S(2)}, u32[]{:S(2)}) collective-permute-start(bf16[2,2,128,128]{3,2,1,0:T(8,128)(2,1)S(1)} %get-tuple-element.32), channel_id=1, source_target_pairs={{0,4},{4,0},{8,12},{12,8},{16,20},{20,16},{24,28},{28,24},{1,5},{5... | collective-permute-start | bytes 393224 | tf_op jit(solution)/shard_map/ppermute | solution.py:335
  23.3 5.4 %collective-permute-start.11 = (bf16[32,16,128]{2,1,0:T(8,128)(2,1)S(1)}, bf16[32,16,128]{2,1,0:T(8,128)(2,1)S(1)}, u32[]{:S(2)}, u32[]{:S(2)}) collective-permute-start(bf16[32,16,128]{2,1,0:T(8,128)(2,1)S(1)} %get-tuple-element.33), channel_id=1, source_target_pairs={{0,2},{1,3},{2,0},{3,1},{4,6},{5,7},{6,4},{7,5},{8,10},{9,11},{10,... | collective-permute-start | bytes 393224 | tf_op jit(solution)/shard_map/ppermute | solution.py:348
  24.8 5.8 %collective-permute-start.9 = (bf16[32,16,128]{2,1,0:T(8,128)(2,1)S(1)}, bf16[32,16,128]{2,1,0:T(8,128)(2,1)S(1)}, u32[]{:S(2)}, u32[]{:S(2)}) collective-permute-start(bf16[32,16,128]{2,1,0:T(8,128)(2,1)S(1)} %get-tuple-element.31), channel_id=1, source_target_pairs={{0,3},{1,2},{2,1},{3,0},{4,7},{5,6},{6,5},{7,4},{8,11},{9,10},{10,... | collective-permute-start | bytes 393224 | tf_op jit(solution)/shard_map/ppermute | solution.py:348
  24.8 5.8 %collective-permute-start.12 = (bf16[32,16,128]{2,1,0:T(8,128)(2,1)S(1)}, bf16[32,16,128]{2,1,0:T(8,128)(2,1)S(1)}, u32[]{:S(2)}, u32[]{:S(2)}) collective-permute-start(bf16[32,16,128]{2,1,0:T(8,128)(2,1)S(1)} %get-tuple-element.34), channel_id=1, source_target_pairs={{0,1},{1,0},{2,3},{3,2},{4,5},{5,4},{6,7},{7,6},{8,9},{9,8},{10,11... | collective-permute-start | bytes 393224 | tf_op jit(solution)/shard_map/ppermute | solution.py:348
  25.4 5.5 %collective-permute-start.7 = (bf16[2,2,128,128]{3,2,1,0:T(8,128)(2,1)S(1)}, bf16[2,2,128,128]{3,2,1,0:T(8,128)(2,1)S(1)}, u32[]{:S(2)}, u32[]{:S(2)}) collective-permute-start(bf16[2,2,128,128]{3,2,1,0:T(8,128)(2,1)S(1)} %collective-permute-done.6), channel_id=1, source_target_pairs={{0,8},{4,0},{8,16},{12,4},{16,24},{20,12},{24,28},{28,20},{1,9},{5... | collective-permute-start | bytes 393224 | tf_op jit(solution)/shard_map/ppermute | solution.py:344

commit v10 on v9

--- a/solution.py
+++ b/solution.py
@@ -328,7 +328,10 @@
 
 def shifted(block, distance):
     count = lax.axis_size("seq")
-    return lax.ppermute(block, "seq", [(i, (i + distance) % count) for i in range(count)])
+    route = [(i, (i + distance) % count) for i in range(count)]
+    if distance < 0:
+        route = [(i, target) for i, target in route if target < i]
+    return lax.ppermute(block, "seq", route)
 
 
 def paired(block):

time: 32 us -> 32.1 us (level)
  waiting for transfers between devices: 7.26 us -> 8.88 us
  starting transfers between devices: 17.7 us -> 16.2 us
    ppermute x2, starting transfers between devices: 5.18 us -> 2.86 us  [shifted(): return lax.ppermute(block, 'seq', route)]
    ppermute x2, waiting for transfers between devices: 1.86 us -> 4.17 us  [ringed(): return lax.ppermute(block, 'seq', route)]
    ppermute x6, waiting for transfers between devices: 3.09 us -> 0.99 us  [swapped(): lax.ppermute(block, 'kvh', [(i, i ^ mask) for i in range(lax.axis_size('k...]
    ppermute x2, waiting for transfers between devices: 0.01 us -> 2.09 us  [shifted(): return lax.ppermute(block, 'seq', route)]
    ppermute x2, starting transfers between devices: 2.09 us -> 3.41 us  [ringed(): return lax.ppermute(block, 'seq', route)]
    ppermute x3, waiting for transfers between devices: 2.31 us -> 1.63 us  [paired(): lax.ppermute(block, 'seq', [(i, i ^ 1) for i in range(lax.axis_size('seq'...]
    ppermute x6, starting transfers between devices: 5.3 us -> 4.77 us  [swapped(): lax.ppermute(block, 'kvh', [(i, i ^ mask) for i in range(lax.axis_size('k...]
where the time goes in v10:
time: 32.1 us; the launch traced here: 32 us
  starting transfers between devices  16.2 us (50%)
  waiting for transfers between devices  8.88 us (28%)
  Pallas kernels  6.21 us (19%)
  between operations  0.69 us (2%)
    ppermute x3, starting transfers between devices, paired(): lax.ppermute(block, 'seq', [(i, i ^ 1) for i in range(lax.axis_size('seq'...  5.16 us
    ppermute x6, starting transfers between devices, swapped(): lax.ppermute(block, 'kvh', [(i, i ^ mask) for i in range(lax.axis_size('k...  4.77 us
    ppermute x2, waiting for transfers between devices, ringed(): return lax.ppermute(block, 'seq', route)  4.17 us
    pallas_call x2, Pallas kernels, gradients(): pl.pallas_call(functools.partial(grad_kernel, masks, parts, carried is No...  3.9 us
    ppermute x2, starting transfers between devices, ringed(): return lax.ppermute(block, 'seq', route)  3.41 us
    ppermute x2, starting transfers between devices, shifted(): return lax.ppermute(block, 'seq', route)  2.86 us
    ppermute x2, waiting for transfers between devices, shifted(): return lax.ppermute(block, 'seq', route)  2.09 us
    ppermute x3, waiting for transfers between devices, paired(): lax.ppermute(block, 'seq', [(i, i ^ 1) for i in range(lax.axis_size('seq'...  1.63 us
  transfers between devices with their start and end apart: 13, of which 7 were waited for; matrix products, arithmetic and copies ran while one was open for 0% of the time, Pallas kernels for 9%

profile of v10, /device:TPU:0, one launch (start us, length us, event | category | flops | bytes accessed | tf_op | source)
XLA Modules:
  0.0 32.0 jit_solution(18277486950548372664)
XLA Ops:
  0.6 0.0 copy-start
  0.6 1.3 %prepare.1 = (bf16[2,2,128,128]{3,2,1,0:T(8,128)(2,1)S(1)}, bf16[2,2,128,128]{3,2,1,0:T(8,128)(2,1)S(1)}, bf16[2,2,128,128]{3,2,1,0:T(8,128)(2,1)S(1)}, bf16[32,...) custom-call(s32[8]{0:T(128)} %lengths_ref.1, ...), custom_call_target="tpu_custom_call" | custom-call | tf_op jit(solution)/shard_map/prepare/pallas_call | solution.py:88
  1.9 3.0 %collective-permute-start = (bf16[2,2,128,128]{3,2,1,0:T(8,128)(2,1)S(1)}, bf16[2,2,128,128]{3,2,1,0:T(8,128)(2,1)S(1)}, u32[]{:S(2)}, u32[]{:S(2)}) collective-permute-start(bf16[2,2,128,128]{3,2,1,0:T(8,128)(2,1)S(1)} %get-tuple-element.22), channel_id=1, source_target_pairs={{0,4},{4,0},{8,12},{12,8},{16,20},{20,16},{24,28},{28,24},{1,5},{5... | collective-permute-start | bytes 393224 | tf_op jit(solution)/shard_map/ppermute | solution.py:338
  4.9 1.6 %collective-permute-start.1 = (bf16[2,2,128,128]{3,2,1,0:T(8,128)(2,1)S(1)}, bf16[2,2,128,128]{3,2,1,0:T(8,128)(2,1)S(1)}, u32[]{:S(2)}, u32[]{:S(2)}) collective-permute-start(bf16[2,2,128,128]{3,2,1,0:T(8,128)(2,1)S(1)} %get-tuple-element.23), channel_id=1, source_target_pairs={{0,8},{4,12},{8,16},{12,20},{16,24},{20,28},{24,0},{28,4},{1,9},{5... | collective-permute-start | bytes 393224 | tf_op jit(solution)/shard_map/ppermute | solution.py:334
  6.5 0.0 collective-permute-start.4
  6.5 1.6 %collective-permute-start.5 = (bf16[32,16,128]{2,1,0:T(8,128)(2,1)S(1)}, bf16[32,16,128]{2,1,0:T(8,128)(2,1)S(1)}, u32[]{:S(2)}, u32[]{:S(2)}) collective-permute-start(bf16[32,16,128]{2,1,0:T(8,128)(2,1)S(1)} %get-tuple-element.27), channel_id=1, source_target_pairs={{0,3},{1,2},{2,1},{3,0},{4,7},{5,6},{6,5},{7,4},{8,11},{9,10},{10,... | collective-permute-start | bytes 393224 | tf_op jit(solution)/shard_map/ppermute | solution.py:351
  8.2 0.3 collective-permute-done.refs_1_
  8.4 1.8 %collective-permute-start.2 = (bf16[2,2,128,128]{3,2,1,0:T(8,128)(2,1)S(1)}, bf16[2,2,128,128]{3,2,1,0:T(8,128)(2,1)S(1)}, u32[]{:S(2)}, u32[]{:S(2)}) collective-permute-start(bf16[2,2,128,128]{3,2,1,0:T(8,128)(2,1)S(1)} %collective-permute-done.refs_1_), channel_id=1, source_target_pairs={{0,8},{4,0},{8,16},{12,4},{16,24},{20,12},{24,28},{28,20},{1,9},{5... | collective-permute-start | bytes 393224 | tf_op jit(solution)/shard_map/ppermute | solution.py:347
  10.3 1.5 %collective-permute-start.3 = (bf16[32,16,128]{2,1,0:T(8,128)(2,1)S(1)}, bf16[32,16,128]{2,1,0:T(8,128)(2,1)S(1)}, u32[]{:S(2)}, u32[]{:S(2)}) collective-permute-start(bf16[32,16,128]{2,1,0:T(8,128)(2,1)S(1)} %get-tuple-element.24), channel_id=1, source_target_pairs={{0,2},{1,3},{2,0},{3,1},{4,6},{5,7},{6,4},{7,5},{8,10},{9,11},{10,... | collective-permute-start | bytes 393224 | tf_op jit(solution)/shard_map/ppermute | solution.py:351
  11.8 0.0 collective-permute-done.1.refs_2_
  11.8 0.0 collective-permute-done.4.refs_5_
  11.8 0.2 collective-permute-done.5.refs_6_
  12.0 1.6 %collective-permute-done.2.refs_3_ = bf16[2,2,128,128]{3,2,1,0:T(8,128)(2,1)S(1)} collective-permute-done((bf16[2,2,128,128]{3,2,1,0:T(8,128)(2,1)S(1)}, bf16[2,2,128,128]{3,2,1,0:T(8,128)(2,1)S(1)}, u32[]{:S(2)}, u32[]{:S(2)}) %collective-permute-start.2) | collective-permute-done | bytes 131104 | tf_op jit(solution)/shard_map/ppermute | solution.py:347
  13.6 0.0 copy-done
  13.6 2.7 %gradients.2 = (bf16[32,16,128]{2,1,0:T(8,128)(2,1)S(1)}, bf16[32,16,128]{2,1,0:T(8,128)(2,1)S(1)}, bf16[32,16,128]{2,1,0:T(8,128)(2,1)S(1)}, f32[2,2,512,128]{3,2,1,0:T(8,128)S(1)}) custom-call(s32[4,2,256]{2,1,0:T(2,128)S(1)} %get-tuple-element.20.range_ref, bf16[128,16,128]{2,1,0:T(8,128)(2,1)S(1)} %copy-done, ...), custom_call_target="tpu_custom_call" | custom-call | flops 1006632960 | bytes 2097152 | tf_op jit(solution)/shard_map/gradients/pallas_call | solution.py:263
  16.3 0.0 collective-permute-done.3.refs_4_
  16.3 1.2 %gradients.3 = (bf16[32,16,128]{2,1,0:T(8,128)(2,1)S(1)}, f32[2,2,128,128]{3,2,1,0:T(8,128)S(1)}, bf16[2,2,128,128]{3,2,1,0:T(8,128)(2,1)S(1)}, bf16[2,2,128,128...) custom-call(s32[4,2,256]{2,1,0:T(2,128)S(1)} %get-tuple-element.20.range_ref, bf16[128,16,128]{2,1,0:T(8,128)(2,1)S(1)} %copy-done, ...), custom_call_target="tpu_custom_call" | custom-call | flops 335544320 | bytes 2097152 | tf_op jit(solution)/shard_map/gradients/pallas_call | solution.py:263
  17.5 1.6 %collective-permute-start.6 = (bf16[2,2,128,128]{3,2,1,0:T(8,128)(2,1)S(1)}, bf16[2,2,128,128]{3,2,1,0:T(8,128)(2,1)S(1)}, u32[]{:S(2)}, u32[]{:S(2)}) collective-permute-start(bf16[2,2,128,128]{3,2,1,0:T(8,128)(2,1)S(1)} %get-tuple-element.29), channel_id=1, source_target_pairs={{0,4},{4,0},{8,12},{12,8},{16,20},{20,16},{24,28},{28,24},{1,5},{5... | collective-permute-start | bytes 393224 | tf_op jit(solution)/shard_map/ppermute | solution.py:338
  19.1 1.3 %collective-permute-start.8 = (bf16[2,2,128,128]{3,2,1,0:T(8,128)(2,1)S(1)}, bf16[2,2,128,128]{3,2,1,0:T(8,128)(2,1)S(1)}, u32[]{:S(2)}, u32[]{:S(2)}) collective-permute-start(bf16[2,2,128,128]{3,2,1,0:T(8,128)(2,1)S(1)} %get-tuple-element.30), channel_id=1, source_target_pairs={{8,0},{12,4},{16,8},{20,12},{24,16},{28,20},{9,1},{13,5},{17,9},{2... | collective-permute-start | bytes 393224 | tf_op jit(solution)/shard_map/ppermute | solution.py:334
  20.4 0.5 %collective-permute-start.10 = (bf16[2,2,128,128]{3,2,1,0:T(8,128)(2,1)S(1)}, bf16[2,2,128,128]{3,2,1,0:T(8,128)(2,1)S(1)}, u32[]{:S(2)}, u32[]{:S(2)}) collective-permute-start(bf16[2,2,128,128]{3,2,1,0:T(8,128)(2,1)S(1)} %get-tuple-element.32), channel_id=1, source_target_pairs={{0,4},{4,0},{8,12},{12,8},{16,20},{20,16},{24,28},{28,24},{1,5},{5... | collective-permute-start | bytes 393224 | tf_op jit(solution)/shard_map/ppermute | solution.py:338
  20.9 1.6 %collective-permute-start.11 = (bf16[32,16,128]{2,1,0:T(8,128)(2,1)S(1)}, bf16[32,16,128]{2,1,0:T(8,128)(2,1)S(1)}, u32[]{:S(2)}, u32[]{:S(2)}) collective-permute-start(bf16[32,16,128]{2,1,0:T(8,128)(2,1)S(1)} %get-tuple-element.33), channel_id=1, source_target_pairs={{0,2},{1,3},{2,0},{3,1},{4,6},{5,7},{6,4},{7,5},{8,10},{9,11},{10,... | collective-permute-start | bytes 393224 | tf_op jit(solution)/shard_map/ppermute | solution.py:351
  22.5 0.0 collective-permute-start.9
  22.5 1.3 %collective-permute-done.6 = bf16[2,2,128,128]{3,2,1,0:T(8,128)(2,1)S(1)} collective-permute-done((bf16[2,2,128,128]{3,2,1,0:T(8,128)(2,1)S(1)}, bf16[2,2,128,128]{3,2,1,0:T(8,128)(2,1)S(1)}, u32[]{:S(2)}, u32[]{:S(2)}) %collective-permute-start.6) | collective-permute-done | bytes 131104 | tf_op jit(solution)/shard_map/ppermute | solution.py:338
  23.9 0.0 collective-permute-start.12
  23.9 2.1 %collective-permute-done.8.refs_1_ = bf16[2,2,128,128]{3,2,1,0:T(8,128)(2,1)S(1)} collective-permute-done((bf16[2,2,128,128]{3,2,1,0:T(8,128)(2,1)S(1)}, bf16[2,2,128,128]{3,2,1,0:T(8,128)(2,1)S(1)}, u32[]{:S(2)}, u32[]{:S(2)}) %collective-permute-start.8) | collective-permute-done | bytes 131104 | tf_op jit(solution)/shard_map/ppermute | solution.py:334
  26.0 1.6 %collective-permute-start.7 = (bf16[2,2,128,128]{3,2,1,0:T(8,128)(2,1)S(1)}, bf16[2,2,128,128]{3,2,1,0:T(8,128)(2,1)S(1)}, u32[]{:S(2)}, u32[]{:S(2)}) collective-permute-start(bf16[2,2,128,128]{3,2,1,0:T(8,128)(2,1)S(1)} %collective-permute-done.6), channel_id=1, source_target_pairs={{0,8},{4,0},{8,16},{12,4},{16,24},{20,12},{24,28},{28,20},{1,9},{5... | collective-permute-start | bytes 393224 | tf_op jit(solution)/shard_map/ppermute | solution.py:347
  27.6 0.0 collective-permute-done.10.refs_3_
  27.6 0.0 collective-permute-done.11.refs_4_
  27.6 0.8 %collective-permute-done.9.refs_2_ = bf16[32,16,128]{2,1,0:T(8,128)(2,1)S(1)} collective-permute-done((bf16[32,16,128]{2,1,0:T(8,128)(2,1)S(1)}, bf16[32,16,128]{2,1,0:T(8,128)(2,1)S(1)}, u32[]{:S(2)}, u32[]{:S(2)}) %collective-permute-start.9) | collective-permute-done | bytes 131104 | tf_op jit(solution)/shard_map/ppermute | solution.py:351
  28.3 0.0 collective-permute-done.12.refs_5_
  28.3 2.6 %collective-permute-done.7.refs_0_ = bf16[2,2,128,128]{3,2,1,0:T(8,128)(2,1)S(1)} collective-permute-done((bf16[2,2,128,128]{3,2,1,0:T(8,128)(2,1)S(1)}, bf16[2,2,128,128]{3,2,1,0:T(8,128)(2,1)S(1)}, u32[]{:S(2)}, u32[]{:S(2)}) %collective-permute-start.7) | collective-permute-done | bytes 131104 | tf_op jit(solution)/shard_map/ppermute | solution.py:347
  31.0 1.0 %finish.1 = (bf16[32,64,128]{2,1,0:T(8,128)(2,1)}, bf16[128,2,128]{2,1,0:T(2,128)(2,1)}, bf16[128,2,128]{2,1,0:T(2,128)(2,1)}) custom-call(bf16[2,2,128,128]{3,2,1,0:T(8,128)(2,1)S(1)} %collective-permute-done.7.refs_0_, bf16[2,2,128,128]{3,2,1,0:T(8,128)(2,1)S(1)} %collective-permute-done.8.refs_1_, ...), custom_call_target="tpu_custom_call" | custom-call | tf_op jit(solution)/shard_map/finish/pallas_call | solution.py:315
Async XLA Ops:
  0.6 12.9 %copy-start = (bf16[128,16,128]{2,1,0:T(8,128)(2,1)S(1)}, bf16[128,16,128]{2,1,0:T(8,128)(2,1)}, u32[]{:S(2)}) copy-start(bf16[128,16,128]{2,1,0:T(8,128)(2,1)} %q_ref.3) | copy-start | bytes 1572868
  1.9 6.5 %collective-permute-start = (bf16[2,2,128,128]{3,2,1,0:T(8,128)(2,1)S(1)}, bf16[2,2,128,128]{3,2,1,0:T(8,128)(2,1)S(1)}, u32[]{:S(2)}, u32[]{:S(2)}) collective-permute-start(bf16[2,2,128,128]{3,2,1,0:T(8,128)(2,1)S(1)} %get-tuple-element.22), channel_id=1, source_target_pairs={{0,4},{4,0},{8,12},{12,8},{16,20},{20,16},{24,28},{28,24},{1,5},{5... | collective-permute-start | bytes 393224 | tf_op jit(solution)/shard_map/ppermute | solution.py:338
  4.9 6.8 %collective-permute-start.1 = (bf16[2,2,128,128]{3,2,1,0:T(8,128)(2,1)S(1)}, bf16[2,2,128,128]{3,2,1,0:T(8,128)(2,1)S(1)}, u32[]{:S(2)}, u32[]{:S(2)}) collective-permute-start(bf16[2,2,128,128]{3,2,1,0:T(8,128)(2,1)S(1)} %get-tuple-element.23), channel_id=1, source_target_pairs={{0,8},{4,12},{8,16},{12,20},{16,24},{20,28},{24,0},{28,4},{1,9},{5... | collective-permute-start | bytes 393224 | tf_op jit(solution)/shard_map/ppermute | solution.py:334
  6.5 5.3 %collective-permute-start.4 = (bf16[32,16,128]{2,1,0:T(8,128)(2,1)S(1)}, bf16[32,16,128]{2,1,0:T(8,128)(2,1)S(1)}, u32[]{:S(2)}, u32[]{:S(2)}) collective-permute-start(bf16[32,16,128]{2,1,0:T(8,128)(2,1)S(1)} %get-tuple-element.26), channel_id=1, source_target_pairs={{0,1},{1,0},{2,3},{3,2},{4,5},{5,4},{6,7},{7,6},{8,9},{9,8},{10,11... | collective-permute-start | bytes 393224 | tf_op jit(solution)/shard_map/ppermute | solution.py:351
  6.5 5.5 %collective-permute-start.5 = (bf16[32,16,128]{2,1,0:T(8,128)(2,1)S(1)}, bf16[32,16,128]{2,1,0:T(8,128)(2,1)S(1)}, u32[]{:S(2)}, u32[]{:S(2)}) collective-permute-start(bf16[32,16,128]{2,1,0:T(8,128)(2,1)S(1)} %get-tuple-element.27), channel_id=1, source_target_pairs={{0,3},{1,2},{2,1},{3,0},{4,7},{5,6},{6,5},{7,4},{8,11},{9,10},{10,... | collective-permute-start | bytes 393224 | tf_op jit(solution)/shard_map/ppermute | solution.py:351
  8.4 5.1 %collective-permute-start.2 = (bf16[2,2,128,128]{3,2,1,0:T(8,128)(2,1)S(1)}, bf16[2,2,128,128]{3,2,1,0:T(8,128)(2,1)S(1)}, u32[]{:S(2)}, u32[]{:S(2)}) collective-permute-start(bf16[2,2,128,128]{3,2,1,0:T(8,128)(2,1)S(1)} %collective-permute-done.refs_1_), channel_id=1, source_target_pairs={{0,8},{4,0},{8,16},{12,4},{16,24},{20,12},{24,28},{28,20},{1,9},{5... | collective-permute-start | bytes 393224 | tf_op jit(solution)/shard_map/ppermute | solution.py:347
  10.3 6.0 %collective-permute-start.3 = (bf16[32,16,128]{2,1,0:T(8,128)(2,1)S(1)}, bf16[32,16,128]{2,1,0:T(8,128)(2,1)S(1)}, u32[]{:S(2)}, u32[]{:S(2)}) collective-permute-start(bf16[32,16,128]{2,1,0:T(8,128)(2,1)S(1)} %get-tuple-element.24), channel_id=1, source_target_pairs={{0,2},{1,3},{2,0},{3,1},{4,6},{5,7},{6,4},{7,5},{8,10},{9,11},{10,... | collective-permute-start | bytes 393224 | tf_op jit(solution)/shard_map/ppermute | solution.py:351
  17.5 6.4 %collective-permute-start.6 = (bf16[2,2,128,128]{3,2,1,0:T(8,128)(2,1)S(1)}, bf16[2,2,128,128]{3,2,1,0:T(8,128)(2,1)S(1)}, u32[]{:S(2)}, u32[]{:S(2)}) collective-permute-start(bf16[2,2,128,128]{3,2,1,0:T(8,128)(2,1)S(1)} %get-tuple-element.29), channel_id=1, source_target_pairs={{0,4},{4,0},{8,12},{12,8},{16,20},{20,16},{24,28},{28,24},{1,5},{5... | collective-permute-start | bytes 393224 | tf_op jit(solution)/shard_map/ppermute | solution.py:338
  19.1 6.8 %collective-permute-start.8 = (bf16[2,2,128,128]{3,2,1,0:T(8,128)(2,1)S(1)}, bf16[2,2,128,128]{3,2,1,0:T(8,128)(2,1)S(1)}, u32[]{:S(2)}, u32[]{:S(2)}) collective-permute-start(bf16[2,2,128,128]{3,2,1,0:T(8,128)(2,1)S(1)} %get-tuple-element.30), channel_id=1, source_target_pairs={{8,0},{12,4},{16,8},{20,12},{24,16},{28,20},{9,1},{13,5},{17,9},{2... | collective-permute-start | bytes 393224 | tf_op jit(solution)/shard_map/ppermute | solution.py:334
  20.4 7.1 %collective-permute-start.10 = (bf16[2,2,128,128]{3,2,1,0:T(8,128)(2,1)S(1)}, bf16[2,2,128,128]{3,2,1,0:T(8,128)(2,1)S(1)}, u32[]{:S(2)}, u32[]{:S(2)}) collective-permute-start(bf16[2,2,128,128]{3,2,1,0:T(8,128)(2,1)S(1)} %get-tuple-element.32), channel_id=1, source_target_pairs={{0,4},{4,0},{8,12},{12,8},{16,20},{20,16},{24,28},{28,24},{1,5},{5... | collective-permute-start | bytes 393224 | tf_op jit(solution)/shard_map/ppermute | solution.py:338
  20.9 6.6 %collective-permute-start.11 = (bf16[32,16,128]{2,1,0:T(8,128)(2,1)S(1)}, bf16[32,16,128]{2,1,0:T(8,128)(2,1)S(1)}, u32[]{:S(2)}, u32[]{:S(2)}) collective-permute-start(bf16[32,16,128]{2,1,0:T(8,128)(2,1)S(1)} %get-tuple-element.33), channel_id=1, source_target_pairs={{0,2},{1,3},{2,0},{3,1},{4,6},{5,7},{6,4},{7,5},{8,10},{9,11},{10,... | collective-permute-start | bytes 393224 | tf_op jit(solution)/shard_map/ppermute | solution.py:351
  22.5 5.8 %collective-permute-start.9 = (bf16[32,16,128]{2,1,0:T(8,128)(2,1)S(1)}, bf16[32,16,128]{2,1,0:T(8,128)(2,1)S(1)}, u32[]{:S(2)}, u32[]{:S(2)}) collective-permute-start(bf16[32,16,128]{2,1,0:T(8,128)(2,1)S(1)} %get-tuple-element.31), channel_id=1, source_target_pairs={{0,3},{1,2},{2,1},{3,0},{4,7},{5,6},{6,5},{7,4},{8,11},{9,10},{10,... | collective-permute-start | bytes 393224 | tf_op jit(solution)/shard_map/ppermute | solution.py:351
  23.9 4.4 %collective-permute-start.12 = (bf16[32,16,128]{2,1,0:T(8,128)(2,1)S(1)}, bf16[32,16,128]{2,1,0:T(8,128)(2,1)S(1)}, u32[]{:S(2)}, u32[]{:S(2)}) collective-permute-start(bf16[32,16,128]{2,1,0:T(8,128)(2,1)S(1)} %get-tuple-element.34), channel_id=1, source_target_pairs={{0,1},{1,0},{2,3},{3,2},{4,5},{5,4},{6,7},{7,6},{8,9},{9,8},{10,11... | collective-permute-start | bytes 393224 | tf_op jit(solution)/shard_map/ppermute | solution.py:351
  26.0 5.0 %collective-permute-start.7 = (bf16[2,2,128,128]{3,2,1,0:T(8,128)(2,1)S(1)}, bf16[2,2,128,128]{3,2,1,0:T(8,128)(2,1)S(1)}, u32[]{:S(2)}, u32[]{:S(2)}) collective-permute-start(bf16[2,2,128,128]{3,2,1,0:T(8,128)(2,1)S(1)} %collective-permute-done.6), channel_id=1, source_target_pairs={{0,8},{4,0},{8,16},{12,4},{16,24},{20,12},{24,28},{28,20},{1,9},{5... | collective-permute-start | bytes 393224 | tf_op jit(solution)/shard_map/ppermute | solution.py:347

commit v11 on v9

--- a/solution.py
+++ b/solution.py
@@ -235,11 +235,13 @@
     if not is_last:
         outs[0][...] = acc[...]
         return
-    for slot, ref in zip((BACK, 0, even_slot, odd_slot), outs):
+    is_odd = (shard % 2).astype(jnp.float32)
+    weights = (1.0, 1.0 - is_odd, is_odd, 1.0, 1.0)
+    for slot, weight, ref in zip((BACK, 0, 0, even_slot, odd_slot), weights, outs):
         part = pl.ds(pl.multiple_of(slot * rows, rows), rows)
         for group in range(kv_heads):
-            ref[0, group] = (acc[0, group, part] * scale).astype(ref.dtype)
-            ref[1, group] = acc[1, group, part].astype(ref.dtype)
+            ref[0, group] = (acc[0, group, part] * (scale * weight)).astype(ref.dtype)
+            ref[1, group] = (acc[1, group, part] * weight).astype(ref.dtype)
 
 
 def gradients(masks, parts, ranges, queries, cots, blocks, carried):
@@ -254,7 +256,7 @@
     work = heads * rows // parts * span * len(masks)
     outs = [pltpu.VMEM(cots[0].shape, jnp.bfloat16)] * len(masks)
     if is_last:
-        outs += [pltpu.VMEM(kv_shape, jnp.float32)] + [pltpu.VMEM(kv_shape, jnp.bfloat16)] * 3
+        outs += [pltpu.VMEM(kv_shape, jnp.float32)] + [pltpu.VMEM(kv_shape, jnp.bfloat16)] * 4
     else:
         outs += [pltpu.VMEM(acc_shape, jnp.float32)]
     own, far, even, odd = blocks
@@ -282,8 +284,23 @@
     return outs[: len(masks)], outs[len(masks) :]
 
 
+def add_kernel(left, right, out):
+    out[...] = (left[...].astype(jnp.float32) + right[...].astype(jnp.float32)).astype(out.dtype)
+
+
+def add(left, right):
+    return pl.pallas_call(
+        add_kernel,
+        out_shape=pltpu.VMEM(left.shape, left.dtype),
+        in_specs=[_VMEM] * 2,
+        out_specs=_VMEM,
+        compiler_params=pltpu.CompilerParams(vmem_limit_bytes=VMEM_BYTES),
+        name="add",
+    )(left, right)
+
+
 def finish_order(parts):
-    return ["odd", "far", parts - 1, "even", *range(parts - 2, -1, -1), "own"]
+    return [1, "odd", "far", *range(2, parts - 1), "even", parts - 1, 0, "own"]
 
 
 def finish_kernel(parts, *refs):
@@ -335,12 +352,12 @@
     return lax.ppermute(block, "seq", [(i, i ^ 1) for i in range(lax.axis_size("seq"))])
 
 
-def ringed(block):
+def ringed(block, direction=1):
     count = lax.axis_size("seq")
     route = []
     for i in range(count):
         target = i + 2 if i % 2 == 0 else i - 2
-        route.append((i, min(max(target, 0), count - 1)))
+        route.append((i, min(max(target, 0), count - 1))[::direction])
     return lax.ppermute(block, "seq", route)
 
 
@@ -363,8 +380,9 @@
         )
         for mask, dq in zip(masks, found):
             dqs[mask] = swapped(dq, mask) if mask else dq
-    own, far, even, odd = carried
-    partials = [own, shifted(far, -BACK), paired(even), ringed(paired(odd))]
+    own, far_even, far_odd, even, odd = carried
+    relayed = add(paired(odd), far_odd)
+    partials = [own, ringed(far_even, -1), paired(even), ringed(relayed)]
     return finish([dqs[mask] for mask in range(parts)], partials)
 
 

time: 32 us -> 30.7 us (0.959)
  waiting for transfers between devices: 7.26 us -> 6.54 us
  starting transfers between devices: 17.7 us -> 17 us
    ppermute x2 -> x1, starting transfers between devices: 5.18 us -> 1.58 us  [shifted(): lax.ppermute(block, 'seq', [(i, (i + distance) % count) for i in range(co...]
    ppermute x2 -> x3, starting transfers between devices: 2.09 us -> 3.84 us  [ringed(): return lax.ppermute(block, 'seq', route)]
    ppermute x2 -> x3, waiting for transfers between devices: 1.86 us -> 3.36 us  [ringed(): return lax.ppermute(block, 'seq', route)]
    ppermute x6, waiting for transfers between devices: 3.09 us -> 1.78 us  [swapped(): lax.ppermute(block, 'kvh', [(i, i ^ mask) for i in range(lax.axis_size('k...]
    ppermute x3, starting transfers between devices: 5.18 us -> 6.37 us  [paired(): lax.ppermute(block, 'seq', [(i, i ^ 1) for i in range(lax.axis_size('seq'...]
    ppermute x3, waiting for transfers between devices: 2.31 us -> 1.4 us  [paired(): lax.ppermute(block, 'seq', [(i, i ^ 1) for i in range(lax.axis_size('seq'...]
  transfers between devices with their start and end apart: 13 -> 13, of which waited for: 7 -> 8; matrix products, arithmetic and copies ran while one was open for 0% -> 0% of each run, Pallas kernels for 9% -> 9%
where the time goes in v11:
time: 30.7 us; the launch traced here: 30.5 us
  starting transfers between devices  17 us (55%)
  waiting for transfers between devices  6.54 us (21%)
  Pallas kernels  6.28 us (20%)
  between operations  0.69 us (2%)
    ppermute x3, starting transfers between devices, paired(): lax.ppermute(block, 'seq', [(i, i ^ 1) for i in range(lax.axis_size('seq'...  6.37 us
    ppermute x6, starting transfers between devices, swapped(): lax.ppermute(block, 'kvh', [(i, i ^ mask) for i in range(lax.axis_size('k...  5.21 us
    pallas_call x2, Pallas kernels, gradients(): pl.pallas_call(functools.partial(grad_kernel, masks, parts, carried is No...  3.93 us
    ppermute x3, starting transfers between devices, ringed(): return lax.ppermute(block, 'seq', route)  3.84 us
    ppermute x3, waiting for transfers between devices, ringed(): return lax.ppermute(block, 'seq', route)  3.36 us
    ppermute x6, waiting for transfers between devices, swapped(): lax.ppermute(block, 'kvh', [(i, i ^ mask) for i in range(lax.axis_size('k...  1.78 us
    ppermute x1, starting transfers between devices, shifted(): lax.ppermute(block, 'seq', [(i, (i + distance) % count) for i in range(co...  1.58 us
    ppermute x3, waiting for transfers between devices, paired(): lax.ppermute(block, 'seq', [(i, i ^ 1) for i in range(lax.axis_size('seq'...  1.4 us
  transfers between devices with their start and end apart: 13, of which 8 were waited for; matrix products, arithmetic and copies ran while one was open for 0% of the time, Pallas kernels for 9%

profile of v11, /device:TPU:0, one launch (start us, length us, event | category | flops | bytes accessed | tf_op | source)
XLA Modules:
  0.0 30.5 jit_solution(2806435400167939920)
XLA Ops:
  0.6 0.0 copy-start
  0.6 1.3 %prepare.1 = (bf16[2,2,128,128]{3,2,1,0:T(8,128)(2,1)S(1)}, bf16[2,2,128,128]{3,2,1,0:T(8,128)(2,1)S(1)}, bf16[2,2,128,128]{3,2,1,0:T(8,128)(2,1)S(1)}, bf16[32,...) custom-call(s32[8]{0:T(128)} %lengths_ref.1, ...), custom_call_target="tpu_custom_call" | custom-call | tf_op jit(solution)/shard_map/prepare/pallas_call | solution.py:88
  1.9 3.0 %collective-permute-start = (bf16[2,2,128,128]{3,2,1,0:T(8,128)(2,1)S(1)}, bf16[2,2,128,128]{3,2,1,0:T(8,128)(2,1)S(1)}, u32[]{:S(2)}, u32[]{:S(2)}) collective-permute-start(bf16[2,2,128,128]{3,2,1,0:T(8,128)(2,1)S(1)} %get-tuple-element.23), channel_id=1, source_target_pairs={{0,4},{4,0},{8,12},{12,8},{16,20},{20,16},{24,28},{28,24},{1,5},{5... | collective-permute-start | bytes 393224 | tf_op jit(solution)/shard_map/ppermute | solution.py:352
  4.9 1.6 %collective-permute-start.1 = (bf16[2,2,128,128]{3,2,1,0:T(8,128)(2,1)S(1)}, bf16[2,2,128,128]{3,2,1,0:T(8,128)(2,1)S(1)}, u32[]{:S(2)}, u32[]{:S(2)}) collective-permute-start(bf16[2,2,128,128]{3,2,1,0:T(8,128)(2,1)S(1)} %get-tuple-element.24), channel_id=1, source_target_pairs={{0,8},{4,12},{8,16},{12,20},{16,24},{20,28},{24,0},{28,4},{1,9},{5... | collective-permute-start | bytes 393224 | tf_op jit(solution)/shard_map/ppermute | solution.py:348
  6.5 0.0 collective-permute-start.3
  6.5 1.6 %collective-permute-start.4 = (bf16[32,16,128]{2,1,0:T(8,128)(2,1)S(1)}, bf16[32,16,128]{2,1,0:T(8,128)(2,1)S(1)}, u32[]{:S(2)}, u32[]{:S(2)}) collective-permute-start(bf16[32,16,128]{2,1,0:T(8,128)(2,1)S(1)} %get-tuple-element.27), channel_id=1, source_target_pairs={{0,3},{1,2},{2,1},{3,0},{4,7},{5,6},{6,5},{7,4},{8,11},{9,10},{10,... | collective-permute-start | bytes 393224 | tf_op jit(solution)/shard_map/ppermute | solution.py:365
  8.2 0.3 collective-permute-done.refs_1_
  8.4 1.8 %collective-permute-start.2 = (bf16[2,2,128,128]{3,2,1,0:T(8,128)(2,1)S(1)}, bf16[2,2,128,128]{3,2,1,0:T(8,128)(2,1)S(1)}, u32[]{:S(2)}, u32[]{:S(2)}) collective-permute-start(bf16[2,2,128,128]{3,2,1,0:T(8,128)(2,1)S(1)} %collective-permute-done.refs_1_), channel_id=1, source_target_pairs={{0,8},{4,0},{8,16},{12,4},{16,24},{20,12},{24,28},{28,20},{1,9},{5... | collective-permute-start | bytes 393224 | tf_op jit(solution)/shard_map/ppermute | solution.py:361
  10.3 1.5 %collective-permute-start.6 = (bf16[32,16,128]{2,1,0:T(8,128)(2,1)S(1)}, bf16[32,16,128]{2,1,0:T(8,128)(2,1)S(1)}, u32[]{:S(2)}, u32[]{:S(2)}) collective-permute-start(bf16[32,16,128]{2,1,0:T(8,128)(2,1)S(1)} %get-tuple-element.29), channel_id=1, source_target_pairs={{0,2},{1,3},{2,0},{3,1},{4,6},{5,7},{6,4},{7,5},{8,10},{9,11},{10,... | collective-permute-start | bytes 393224 | tf_op jit(solution)/shard_map/ppermute | solution.py:365
  11.8 0.0 collective-permute-done.1.refs_2_
  11.8 0.0 collective-permute-done.3.refs_5_
  11.8 0.2 collective-permute-done.4.refs_6_
  12.0 1.6 %collective-permute-done.2.refs_3_ = bf16[2,2,128,128]{3,2,1,0:T(8,128)(2,1)S(1)} collective-permute-done((bf16[2,2,128,128]{3,2,1,0:T(8,128)(2,1)S(1)}, bf16[2,2,128,128]{3,2,1,0:T(8,128)(2,1)S(1)}, u32[]{:S(2)}, u32[]{:S(2)}) %collective-permute-start.2) | collective-permute-done | bytes 131104 | tf_op jit(solution)/shard_map/ppermute | solution.py:361
  13.6 0.0 copy-done
  13.6 2.8 %gradients.2 = (bf16[32,16,128]{2,1,0:T(8,128)(2,1)S(1)}, bf16[32,16,128]{2,1,0:T(8,128)(2,1)S(1)}, bf16[32,16,128]{2,1,0:T(8,128)(2,1)S(1)}, f32[2,2,512,128]{3,2,1,0:T(8,128)S(1)}) custom-call(s32[4,2,256]{2,1,0:T(2,128)S(1)} %get-tuple-element.21.range_ref, bf16[128,16,128]{2,1,0:T(8,128)(2,1)S(1)} %copy-done, ...), custom_call_target="tpu_custom_call" | custom-call | flops 1006632960 | bytes 2097152 | tf_op jit(solution)/shard_map/gradients/pallas_call | solution.py:265
  16.3 0.0 collective-permute-done.6.refs_4_
  16.4 1.2 %gradients.3 = (bf16[32,16,128]{2,1,0:T(8,128)(2,1)S(1)}, f32[2,2,128,128]{3,2,1,0:T(8,128)S(1)}, bf16[2,2,128,128]{3,2,1,0:T(8,128)(2,1)S(1)}, bf16[2,2,128,128...) custom-call(s32[4,2,256]{2,1,0:T(2,128)S(1)} %get-tuple-element.21.range_ref, ...), custom_call_target="tpu_custom_call" | custom-call | flops 335544320 | bytes 2097152 | tf_op jit(solution)/shard_map/gradients/pallas_call | solution.py:265
  17.5 1.6 %collective-permute-start.7 = (bf16[2,2,128,128]{3,2,1,0:T(8,128)(2,1)S(1)}, bf16[2,2,128,128]{3,2,1,0:T(8,128)(2,1)S(1)}, u32[]{:S(2)}, u32[]{:S(2)}) collective-permute-start(bf16[2,2,128,128]{3,2,1,0:T(8,128)(2,1)S(1)} %get-tuple-element.31), channel_id=1, source_target_pairs={{0,4},{4,0},{8,12},{12,8},{16,20},{20,16},{24,28},{28,24},{1,5},{5... | collective-permute-start | bytes 393224 | tf_op jit(solution)/shard_map/ppermute | solution.py:352
  19.2 0.0 collective-permute-start.5
  19.2 1.6 %collective-permute-start.12 = (bf16[32,16,128]{2,1,0:T(8,128)(2,1)S(1)}, bf16[32,16,128]{2,1,0:T(8,128)(2,1)S(1)}, u32[]{:S(2)}, u32[]{:S(2)}) collective-permute-start(bf16[32,16,128]{2,1,0:T(8,128)(2,1)S(1)} %get-tuple-element.36), channel_id=1, source_target_pairs={{0,3},{1,2},{2,1},{3,0},{4,7},{5,6},{6,5},{7,4},{8,11},{9,10},{10,... | collective-permute-start | bytes 393224 | tf_op jit(solution)/shard_map/ppermute | solution.py:365
  20.8 0.5 %collective-permute-start.9 = (bf16[2,2,128,128]{3,2,1,0:T(8,128)(2,1)S(1)}, bf16[2,2,128,128]{3,2,1,0:T(8,128)(2,1)S(1)}, u32[]{:S(2)}, u32[]{:S(2)}) collective-permute-start(bf16[2,2,128,128]{3,2,1,0:T(8,128)(2,1)S(1)} %get-tuple-element.33), channel_id=1, source_target_pairs={{8,0},{0,4},{16,8},{4,12},{24,16},{12,20},{28,24},{20,28},{9,1},{1... | collective-permute-start | bytes 393224 | tf_op jit(solution)/shard_map/ppermute | solution.py:361
  21.3 0.4 %collective-permute-start.10 = (bf16[32,16,128]{2,1,0:T(8,128)(2,1)S(1)}, bf16[32,16,128]{2,1,0:T(8,128)(2,1)S(1)}, u32[]{:S(2)}, u32[]{:S(2)}) collective-permute-start(bf16[32,16,128]{2,1,0:T(8,128)(2,1)S(1)} %get-tuple-element.34), channel_id=1, source_target_pairs={{0,2},{1,3},{2,0},{3,1},{4,6},{5,7},{6,4},{7,5},{8,10},{9,11},{10,... | collective-permute-start | bytes 393224 | tf_op jit(solution)/shard_map/ppermute | solution.py:365
  21.8 0.8 %collective-permute-done.7.left = bf16[2,2,128,128]{3,2,1,0:T(8,128)(2,1)S(1)} collective-permute-done((bf16[2,2,128,128]{3,2,1,0:T(8,128)(2,1)S(1)}, bf16[2,2,128,128]{3,2,1,0:T(8,128)(2,1)S(1)}, u32[]{:S(2)}, u32[]{:S(2)}) %collective-permute-start.7) | collective-permute-done | bytes 131104 | tf_op jit(solution)/shard_map/ppermute | solution.py:352
  22.6 1.7 %collective-permute-start.11 = (bf16[2,2,128,128]{3,2,1,0:T(8,128)(2,1)S(1)}, bf16[2,2,128,128]{3,2,1,0:T(8,128)(2,1)S(1)}, u32[]{:S(2)}, u32[]{:S(2)}) collective-permute-start(bf16[2,2,128,128]{3,2,1,0:T(8,128)(2,1)S(1)} %get-tuple-element.35), channel_id=1, source_target_pairs={{0,4},{4,0},{8,12},{12,8},{16,20},{20,16},{24,28},{28,24},{1,5},{5... | collective-permute-start | bytes 393224 | tf_op jit(solution)/shard_map/ppermute | solution.py:352
  24.3 0.0 collective-permute-done.5.refs_0_
  24.3 1.5 %collective-permute-start.8 = (bf16[2,2,128,128]{3,2,1,0:T(8,128)(2,1)S(1)}, bf16[2,2,128,128]{3,2,1,0:T(8,128)(2,1)S(1)}, u32[]{:S(2)}, u32[]{:S(2)}) collective-permute-start(bf16[2,2,128,128]{3,2,1,0:T(8,128)(2,1)S(1)} %add.1), channel_id=1, source_target_pairs={{0,8},{4,0},{8,16},{12,4},{16,24},{20,12},{24,28},{28,20},{1,9},{5... | collective-permute-start | bytes 393224 | tf_op jit(solution)/shard_map/ppermute | solution.py:361
  25.8 0.0 collective-permute-done.12.refs_5_
  25.8 0.4 %collective-permute-done.9.refs_2_ = bf16[2,2,128,128]{3,2,1,0:T(8,128)(2,1)S(1)} collective-permute-done((bf16[2,2,128,128]{3,2,1,0:T(8,128)(2,1)S(1)}, bf16[2,2,128,128]{3,2,1,0:T(8,128)(2,1)S(1)}, u32[]{:S(2)}, u32[]{:S(2)}) %collective-permute-start.9) | collective-permute-done | bytes 131104 | tf_op jit(solution)/shard_map/ppermute | solution.py:361
  26.2 1.6 %collective-permute-done.10.refs_3_ = bf16[32,16,128]{2,1,0:T(8,128)(2,1)S(1)} collective-permute-done((bf16[32,16,128]{2,1,0:T(8,128)(2,1)S(1)}, bf16[32,16,128]{2,1,0:T(8,128)(2,1)S(1)}, u32[]{:S(2)}, u32[]{:S(2)}) %collective-permute-start.10) | collective-permute-done | bytes 131104 | tf_op jit(solution)/shard_map/ppermute | solution.py:365
  27.8 0.3 %collective-permute-done.11.refs_4_ = bf16[2,2,128,128]{3,2,1,0:T(8,128)(2,1)S(1)} collective-permute-done((bf16[2,2,128,128]{3,2,1,0:T(8,128)(2,1)S(1)}, bf16[2,2,128,128]{3,2,1,0:T(8,128)(2,1)S(1)}, u32[]{:S(2)}, u32[]{:S(2)}) %collective-permute-start.11) | collective-permute-done | bytes 131104 | tf_op jit(solution)/shard_map/ppermute | solution.py:352
  28.1 1.4 %collective-permute-done.8.refs_1_ = bf16[2,2,128,128]{3,2,1,0:T(8,128)(2,1)S(1)} collective-permute-done((bf16[2,2,128,128]{3,2,1,0:T(8,128)(2,1)S(1)}, bf16[2,2,128,128]{3,2,1,0:T(8,128)(2,1)S(1)}, u32[]{:S(2)}, u32[]{:S(2)}) %collective-permute-start.8) | collective-permute-done | bytes 131104 | tf_op jit(solution)/shard_map/ppermute | solution.py:361
  29.5 1.0 %finish.1 = (bf16[32,64,128]{2,1,0:T(8,128)(2,1)}, bf16[128,2,128]{2,1,0:T(2,128)(2,1)}, bf16[128,2,128]{2,1,0:T(2,128)(2,1)}) custom-call(bf16[32,16,128]{2,1,0:T(8,128)(2,1)S(1)} %collective-permute-done.5.refs_0_, bf16[2,2,128,128]{3,2,1,0:T(8,128)(2,1)S(1)} %collective-permute-done.8.refs_1_, ...), custom_call_target="tpu_custom_call" | custom-call | tf_op jit(solution)/shard_map/finish/pallas_call | solution.py:332
  (1 shorter events, 0.0 us)
Async XLA Ops:
  0.6 12.9 %copy-start = (bf16[128,16,128]{2,1,0:T(8,128)(2,1)S(1)}, bf16[128,16,128]{2,1,0:T(8,128)(2,1)}, u32[]{:S(2)}) copy-start(bf16[128,16,128]{2,1,0:T(8,128)(2,1)} %q_ref.3) | copy-start | bytes 1572868
  1.9 6.5 %collective-permute-start = (bf16[2,2,128,128]{3,2,1,0:T(8,128)(2,1)S(1)}, bf16[2,2,128,128]{3,2,1,0:T(8,128)(2,1)S(1)}, u32[]{:S(2)}, u32[]{:S(2)}) collective-permute-start(bf16[2,2,128,128]{3,2,1,0:T(8,128)(2,1)S(1)} %get-tuple-element.23), channel_id=1, source_target_pairs={{0,4},{4,0},{8,12},{12,8},{16,20},{20,16},{24,28},{28,24},{1,5},{5... | collective-permute-start | bytes 393224 | tf_op jit(solution)/shard_map/ppermute | solution.py:352
  4.9 6.8 %collective-permute-start.1 = (bf16[2,2,128,128]{3,2,1,0:T(8,128)(2,1)S(1)}, bf16[2,2,128,128]{3,2,1,0:T(8,128)(2,1)S(1)}, u32[]{:S(2)}, u32[]{:S(2)}) collective-permute-start(bf16[2,2,128,128]{3,2,1,0:T(8,128)(2,1)S(1)} %get-tuple-element.24), channel_id=1, source_target_pairs={{0,8},{4,12},{8,16},{12,20},{16,24},{20,28},{24,0},{28,4},{1,9},{5... | collective-permute-start | bytes 393224 | tf_op jit(solution)/shard_map/ppermute | solution.py:348
  6.5 5.3 %collective-permute-start.3 = (bf16[32,16,128]{2,1,0:T(8,128)(2,1)S(1)}, bf16[32,16,128]{2,1,0:T(8,128)(2,1)S(1)}, u32[]{:S(2)}, u32[]{:S(2)}) collective-permute-start(bf16[32,16,128]{2,1,0:T(8,128)(2,1)S(1)} %get-tuple-element.26), channel_id=1, source_target_pairs={{0,1},{1,0},{2,3},{3,2},{4,5},{5,4},{6,7},{7,6},{8,9},{9,8},{10,11... | collective-permute-start | bytes 393224 | tf_op jit(solution)/shard_map/ppermute | solution.py:365
  6.5 5.5 %collective-permute-start.4 = (bf16[32,16,128]{2,1,0:T(8,128)(2,1)S(1)}, bf16[32,16,128]{2,1,0:T(8,128)(2,1)S(1)}, u32[]{:S(2)}, u32[]{:S(2)}) collective-permute-start(bf16[32,16,128]{2,1,0:T(8,128)(2,1)S(1)} %get-tuple-element.27), channel_id=1, source_target_pairs={{0,3},{1,2},{2,1},{3,0},{4,7},{5,6},{6,5},{7,4},{8,11},{9,10},{10,... | collective-permute-start | bytes 393224 | tf_op jit(solution)/shard_map/ppermute | solution.py:365
  8.4 5.1 %collective-permute-start.2 = (bf16[2,2,128,128]{3,2,1,0:T(8,128)(2,1)S(1)}, bf16[2,2,128,128]{3,2,1,0:T(8,128)(2,1)S(1)}, u32[]{:S(2)}, u32[]{:S(2)}) collective-permute-start(bf16[2,2,128,128]{3,2,1,0:T(8,128)(2,1)S(1)} %collective-permute-done.refs_1_), channel_id=1, source_target_pairs={{0,8},{4,0},{8,16},{12,4},{16,24},{20,12},{24,28},{28,20},{1,9},{5... | collective-permute-start | bytes 393224 | tf_op jit(solution)/shard_map/ppermute | solution.py:361
  10.3 6.1 %collective-permute-start.6 = (bf16[32,16,128]{2,1,0:T(8,128)(2,1)S(1)}, bf16[32,16,128]{2,1,0:T(8,128)(2,1)S(1)}, u32[]{:S(2)}, u32[]{:S(2)}) collective-permute-start(bf16[32,16,128]{2,1,0:T(8,128)(2,1)S(1)} %get-tuple-element.29), channel_id=1, source_target_pairs={{0,2},{1,3},{2,0},{3,1},{4,6},{5,7},{6,4},{7,5},{8,10},{9,11},{10,... | collective-permute-start | bytes 393224 | tf_op jit(solution)/shard_map/ppermute | solution.py:365
  17.5 5.0 %collective-permute-start.7 = (bf16[2,2,128,128]{3,2,1,0:T(8,128)(2,1)S(1)}, bf16[2,2,128,128]{3,2,1,0:T(8,128)(2,1)S(1)}, u32[]{:S(2)}, u32[]{:S(2)}) collective-permute-start(bf16[2,2,128,128]{3,2,1,0:T(8,128)(2,1)S(1)} %get-tuple-element.31), channel_id=1, source_target_pairs={{0,4},{4,0},{8,12},{12,8},{16,20},{20,16},{24,28},{28,24},{1,5},{5... | collective-permute-start | bytes 393224 | tf_op jit(solution)/shard_map/ppermute | solution.py:352
  19.2 5.2 %collective-permute-start.5 = (bf16[32,16,128]{2,1,0:T(8,128)(2,1)S(1)}, bf16[32,16,128]{2,1,0:T(8,128)(2,1)S(1)}, u32[]{:S(2)}, u32[]{:S(2)}) collective-permute-start(bf16[32,16,128]{2,1,0:T(8,128)(2,1)S(1)} %get-tuple-element.28), channel_id=1, source_target_pairs={{0,1},{1,0},{2,3},{3,2},{4,5},{5,4},{6,7},{7,6},{8,9},{9,8},{10,11... | collective-permute-start | bytes 393224 | tf_op jit(solution)/shard_map/ppermute | solution.py:365
  19.2 6.7 %collective-permute-start.12 = (bf16[32,16,128]{2,1,0:T(8,128)(2,1)S(1)}, bf16[32,16,128]{2,1,0:T(8,128)(2,1)S(1)}, u32[]{:S(2)}, u32[]{:S(2)}) collective-permute-start(bf16[32,16,128]{2,1,0:T(8,128)(2,1)S(1)} %get-tuple-element.36), channel_id=1, source_target_pairs={{0,3},{1,2},{2,1},{3,0},{4,7},{5,6},{6,5},{7,4},{8,11},{9,10},{10,... | collective-permute-start | bytes 393224 | tf_op jit(solution)/shard_map/ppermute | solution.py:365
  20.8 5.4 %collective-permute-start.9 = (bf16[2,2,128,128]{3,2,1,0:T(8,128)(2,1)S(1)}, bf16[2,2,128,128]{3,2,1,0:T(8,128)(2,1)S(1)}, u32[]{:S(2)}, u32[]{:S(2)}) collective-permute-start(bf16[2,2,128,128]{3,2,1,0:T(8,128)(2,1)S(1)} %get-tuple-element.33), channel_id=1, source_target_pairs={{8,0},{0,4},{16,8},{4,12},{24,16},{12,20},{28,24},{20,28},{9,1},{1... | collective-permute-start | bytes 393224 | tf_op jit(solution)/shard_map/ppermute | solution.py:361
  21.3 6.4 %collective-permute-start.10 = (bf16[32,16,128]{2,1,0:T(8,128)(2,1)S(1)}, bf16[32,16,128]{2,1,0:T(8,128)(2,1)S(1)}, u32[]{:S(2)}, u32[]{:S(2)}) collective-permute-start(bf16[32,16,128]{2,1,0:T(8,128)(2,1)S(1)} %get-tuple-element.34), channel_id=1, source_target_pairs={{0,2},{1,3},{2,0},{3,1},{4,6},{5,7},{6,4},{7,5},{8,10},{9,11},{10,... | collective-permute-start | bytes 393224 | tf_op jit(solution)/shard_map/ppermute | solution.py:365
  22.6 5.5 %collective-permute-start.11 = (bf16[2,2,128,128]{3,2,1,0:T(8,128)(2,1)S(1)}, bf16[2,2,128,128]{3,2,1,0:T(8,128)(2,1)S(1)}, u32[]{:S(2)}, u32[]{:S(2)}) collective-permute-start(bf16[2,2,128,128]{3,2,1,0:T(8,128)(2,1)S(1)} %get-tuple-element.35), channel_id=1, source_target_pairs={{0,4},{4,0},{8,12},{12,8},{16,20},{20,16},{24,28},{28,24},{1,5},{5... | collective-permute-start | bytes 393224 | tf_op jit(solution)/shard_map/ppermute | solution.py:352
  24.3 5.2 %collective-permute-start.8 = (bf16[2,2,128,128]{3,2,1,0:T(8,128)(2,1)S(1)}, bf16[2,2,128,128]{3,2,1,0:T(8,128)(2,1)S(1)}, u32[]{:S(2)}, u32[]{:S(2)}) collective-permute-start(bf16[2,2,128,128]{3,2,1,0:T(8,128)(2,1)S(1)} %add.1), channel_id=1, source_target_pairs={{0,8},{4,0},{8,16},{12,4},{16,24},{20,12},{24,28},{28,20},{1,9},{5... | collective-permute-start | bytes 393224 | tf_op jit(solution)/shard_map/ppermute | solution.py:361

commit v12 on v11

--- a/solution.py
+++ b/solution.py
@@ -13,15 +13,17 @@
 VMEM_BYTES = 40 * 1024 * 1024
 NEG = -1e30
 TILE = 8
+RECEIVED = ("rest", "far", "even", "odd", "core")
 
 _VMEM = pl.BlockSpec(memory_space=pltpu.VMEM)
 _SMEM = pl.BlockSpec(memory_space=pltpu.SMEM)
 _HBM = pl.BlockSpec(memory_space=pltpu.HBM)
 
 
-def stages(parts):
+def stages(parts, kv_heads):
     rest = list(range(parts - 1, 1, -1))
-    return [[0, 1, *rest[:-1]], rest[-1:]]
+    every = list(range(kv_heads))
+    return [(every, [0, 1, *rest[:-1]]), (every, rest[-1:])]
 
 
 def regroup(buf):
@@ -30,7 +32,9 @@
 
 
 def prep_kernel(parts, lengths_ref, prefixes_ref, cot_ref, key_ref, value_ref, *rest):
-    kv_outs, cot_outs, rest = rest[:3], rest[3 : parts + 3], rest[parts + 3 :]
+    kv_heads = key_ref.shape[1]
+    kv_outs, rest = rest[: kv_heads + 2], rest[kv_heads + 2 :]
+    cot_outs, rest = rest[:parts], rest[parts:]
     range_out, key_buf, value_buf, lengths, prefixes, sems, scalar_sems = rest
     heads = cot_ref.shape[1] // parts
     me = lax.axis_index("kvh")
@@ -56,8 +60,9 @@
     for number, buf in enumerate((key_buf, value_buf)):
         loads[number].wait()
         for group, block in enumerate(regroup(buf)):
-            for kv_out in kv_outs:
+            for kv_out in kv_outs[:2]:
                 kv_out[number, group] = block
+            kv_outs[2 + group][number] = block
     for copy in scalars:
         copy.wait()
     rows = key_buf.shape[0]
@@ -81,15 +86,19 @@
     lanes = kv_rows // parts * (heads // parts // kv_heads)
     piece = pltpu.VMEM((rows, heads // parts, size), jnp.bfloat16)
     block = pltpu.VMEM((2, kv_heads, kv_rows, size), jnp.bfloat16)
+    head_block = pltpu.VMEM((2, kv_rows, size), jnp.bfloat16)
     operands = [
         pltpu.with_memory_space_constraint(array, pltpu.HBM)
         for array in (lengths, prefixes, cotangent, keys, values)
     ]
     outs = pl.pallas_call(
         functools.partial(prep_kernel, parts),
-        out_shape=(block,) * 3 + (piece,) * parts + (pltpu.VMEM((parts, 2, lanes), jnp.int32),),
+        out_shape=(block,) * 2
+        + (head_block,) * kv_heads
+        + (piece,) * parts
+        + (pltpu.VMEM((parts, 2, lanes), jnp.int32),),
         in_specs=[_HBM] * 5,
-        out_specs=(_VMEM,) * (parts + 4),
+        out_specs=(_VMEM,) * (parts + kv_heads + 3),
         scratch_shapes=[
             pltpu.VMEM(keys.shape, jnp.bfloat16),
             pltpu.VMEM(values.shape, jnp.bfloat16),
@@ -101,7 +110,7 @@
         compiler_params=pltpu.CompilerParams(vmem_limit_bytes=VMEM_BYTES),
         name="prepare",
     )(*operands)
-    return outs[:3], outs[3:-1], outs[-1]
+    return outs[: kv_heads + 2], outs[kv_heads + 2 : -1], outs[-1]
 
 
 def bounds(position, lengths, prefixes):
@@ -130,17 +139,33 @@
     return jnp.where(odd == 1, behind, ahead), jnp.where(odd == 1, ahead, behind)
 
 
-def grad_kernel(masks, parts, is_first, is_last, range_ref, q_ref, *refs):
+def received_counts(kv_heads, heads_here, masks):
+    core = sum(mask < 2 for mask in masks)
+    return {
+        "far": 1, "even": kv_heads, "odd": len(heads_here), "core": core, "rest": len(masks) - core,
+    }
+
+
+def grad_kernel(heads_here, masks, parts, is_last, range_ref, q_ref, kv_own, *refs):
     refs = list(refs)
-    kv_own, kv_even, kv_far, kv_odd = [refs.pop(0) for _ in range(4)]
-    cots = [refs.pop(0) for _ in masks]
-    carried = None if is_first else refs.pop(0)
-    dqs = [refs.pop(0) for _ in masks]
-    outs, (window, acc, score_buf, dprob_buf, prob_buf, dscore_buf) = refs[:-6], refs[-6:]
+
+    def take(count):
+        taken = refs[:count]
+        del refs[:count]
+        return taken
+
     rows, heads, size = q_ref.shape
     tokens = rows // parts
     kv_heads = kv_own.shape[1]
+    counts = received_counts(kv_heads, heads_here, masks)
+    got = {name: take(counts[name]) for name in RECEIVED}
+    kv_far = got["far"][0]
+    kv_evens, kv_odds = [got["even"][head] for head in heads_here], got["odd"]
+    cots = got["core"] + got["rest"]
     group_size = heads // kv_heads
+    carried = take(kv_heads) if is_last else []
+    dqs = take(len(masks))
+    outs, (window, acc, score_buf, dprob_buf, prob_buf, dscore_buf) = refs[:-6], refs[-6:]
     span = (BACK + 1 + AHEAD) * rows
     reach = span - rows + tokens
     lanes = tokens * group_size
@@ -149,22 +174,31 @@
     me = lax.axis_index("kvh")
 
     even_slot, odd_slot = neighbour_slots(shard)
-    for slot, ref in ((BACK, kv_own), (0, kv_far), (even_slot, kv_even), (odd_slot, kv_odd)):
-        part = pl.ds(pl.multiple_of(slot * rows, rows), rows)
-        for number in range(2):
-            for group in range(kv_heads):
-                window[number, group, part] = ref[number, group]
-    acc[...] = jnp.zeros_like(acc) if is_first else carried[...]
+    for local_head, head in enumerate(heads_here):
+        for slot, ref in (
+            (BACK, kv_own.at[:, head]),
+            (0, kv_far.at[:, head]),
+            (even_slot, kv_evens[local_head]),
+            (odd_slot, kv_odds[local_head]),
+        ):
+            part = pl.ds(pl.multiple_of(slot * rows, rows), rows)
+            for number in range(2):
+                window[number, local_head, part] = ref[number]
+    if is_last:
+        for local_head, ref in enumerate(carried):
+            acc[:, local_head] = ref[...]
+    else:
+        acc[...] = jnp.zeros_like(acc)
 
     contract_last = (((1,), (1,)), ((), ()))
     contract_first = (((0,), (0,)), ((), ()))
     sublane = lax.broadcasted_iota(jnp.int32, (TILE, lanes), 0)
-    items = [(place, group) for place in range(len(masks)) for group in range(kv_heads)]
+    items = [(place, local) for place in range(len(masks)) for local in range(len(heads_here))]
 
     def operands(item):
         place, group = items[item]
         first = pl.multiple_of((me ^ masks[place]) * tokens, tokens)
-        of_group = pl.ds(group * group_size, group_size)
+        of_group = pl.ds(heads_here[group] * group_size, group_size)
         q = q_ref[pl.ds(first, tokens), of_group].astype(jnp.float32)
         cot = cots[place][:, of_group].astype(jnp.float32)
         return (
@@ -223,7 +257,8 @@
             window[0, group, here], dscores, contract_first, preferred_element_type=jnp.float32
         )
         dq = jnp.transpose(dq * scale).reshape(tokens, group_size, size)
-        dqs[place][:, pl.ds(group * group_size, group_size)] = dq.astype(jnp.bfloat16)
+        head = heads_here[group]
+        dqs[place][:, pl.ds(head * group_size, group_size)] = dq.astype(jnp.bfloat16)
 
     top = scores_of(0)
     for item in range(len(items)):
@@ -233,7 +268,8 @@
         top = later
 
     if not is_last:
-        outs[0][...] = acc[...]
+        for local_head, ref in enumerate(outs):
+            ref[...] = acc[:, local_head]
         return
     is_odd = (shard % 2).astype(jnp.float32)
     weights = (1.0, 1.0 - is_odd, is_odd, 1.0, 1.0)
@@ -244,26 +280,28 @@
             ref[1, group] = (acc[1, group, part] * weight).astype(ref.dtype)
 
 
-def gradients(masks, parts, ranges, queries, cots, blocks, carried):
+def gradients(heads_here, masks, parts, ranges, queries, cots, own, far, evens, odds, carried):
     rows, heads, size = queries.shape
-    is_last = masks == stages(parts)[-1]
-    kv_shape = blocks[0].shape
+    kv_shape = own.shape
     kv_heads = kv_shape[1]
+    is_last = len(carried) == kv_heads
+    group_size = heads // kv_heads
     span = (BACK + 1 + AHEAD) * rows
-    acc_shape = (2, kv_heads, span, size)
+    acc_shape = (2, len(heads_here), span, size)
     tokens = rows // parts
-    tile_shape = (2, span - rows + tokens, tokens * (heads // kv_heads))
-    work = heads * rows // parts * span * len(masks)
-    outs = [pltpu.VMEM(cots[0].shape, jnp.bfloat16)] * len(masks)
+    tile_shape = (2, span - rows + tokens, tokens * group_size)
+    work = group_size * len(heads_here) * tokens * span * len(masks)
+    outs = [pltpu.VMEM((tokens, heads, size), jnp.bfloat16)] * len(masks)
+    core = received_counts(kv_heads, heads_here, masks)["core"]
+    got = {"far": [far], "even": evens, "odd": odds, "core": cots[:core], "rest": cots[core:]}
+    operands = [ranges, queries, own] + [array for name in RECEIVED for array in got[name]]
     if is_last:
         outs += [pltpu.VMEM(kv_shape, jnp.float32)] + [pltpu.VMEM(kv_shape, jnp.bfloat16)] * 4
+        operands += carried
     else:
-        outs += [pltpu.VMEM(acc_shape, jnp.float32)]
-    own, far, even, odd = blocks
-    operands = [ranges, queries, own, even, far, odd, *cots]
-    operands += [] if carried is None else [carried]
+        outs += [pltpu.VMEM((2, span, size), jnp.float32)] * len(heads_here)
     outs = pl.pallas_call(
-        functools.partial(grad_kernel, masks, parts, carried is None, is_last),
+        functools.partial(grad_kernel, heads_here, masks, parts, is_last),
         out_shape=tuple(outs),
         in_specs=[_VMEM] * len(operands),
         out_specs=(_VMEM,) * len(outs),
@@ -370,16 +408,21 @@
     kv, cots, ranges = prepare(
         doc_lengths, prefix_lengths, output_gradient, keys, values, parts
     )
-    even = paired(kv[2])
-    blocks = [kv[0], shifted(kv[1], BACK), even, ringed(even)]
+    own, far = kv[0], shifted(kv[1], BACK)
+    evens = [paired(block) for block in kv[2:]]
+    odds = [ringed(block) for block in evens]
     cots = [cots[0]] + [swapped(cots[mask], mask) for mask in range(1, parts)]
-    dqs, carried = {}, [None]
-    for masks in stages(parts):
-        found, carried = gradients(
-            masks, parts, ranges, queries, [cots[mask] for mask in masks], blocks, carried[0]
-        )
+    dqs, carried = {}, []
+    for heads_here, masks in stages(parts, len(evens)):
+        found, left = gradients(
+            heads_here, masks, parts, ranges, queries, [cots[mask] for mask in masks], own, far,
+            evens, [odds[head] for head in heads_here],
+            list(carried),
+        )
+        carried = left
         for mask, dq in zip(masks, found):
-            dqs[mask] = swapped(dq, mask) if mask else dq
+            dqs[mask] = dq
+    dqs = {mask: swapped(dq, mask) if mask else dq for mask, dq in dqs.items()}
     own, far_even, far_odd, even, odd = carried
     relayed = add(paired(odd), far_odd)
     partials = [own, ringed(far_even, -1), paired(even), ringed(relayed)]

time: 30.7 us -> 35.5 us (1.16)
  starting transfers between devices: 17 us -> 19.5 us
  waiting for transfers between devices: 6.54 us -> 8.84 us
    ppermute x3 -> x4, starting transfers between devices: 6.37 us -> 9.37 us  [paired(): lax.ppermute(block, 'seq', [(i, i ^ 1) for i in range(lax.axis_size('seq'...]
    ppermute x6, waiting for transfers between devices: 1.78 us -> 3.28 us  [swapped(): lax.ppermute(block, 'kvh', [(i, i ^ mask) for i in range(lax.axis_size('k...]
    ppermute x3 -> x4, starting transfers between devices: 3.84 us -> 3.3 us  [ringed(): return lax.ppermute(block, 'seq', route)]
    ppermute x3 -> x4, waiting for transfers between devices: 3.36 us -> 3.82 us  [ringed(): return lax.ppermute(block, 'seq', route)]
    ppermute x3 -> x4, waiting for transfers between devices: 1.4 us -> 1.74 us  [paired(): lax.ppermute(block, 'seq', [(i, i ^ 1) for i in range(lax.axis_size('seq'...]
  transfers between devices with their start and end apart: 13 -> 15, of which waited for: 8 -> 7; matrix products, arithmetic and copies ran while one was open for 0% -> 0% of each run, Pallas kernels for 9% -> 8%
where the time goes in v12:
time: 35.5 us; the launch traced here: 35.4 us
  starting transfers between devices  19.5 us (55%)
  waiting for transfers between devices  8.84 us (25%)
  Pallas kernels  6.29 us (18%)
  between operations  0.72 us (2%)
    ppermute x4, starting transfers between devices, paired(): lax.ppermute(block, 'seq', [(i, i ^ 1) for i in range(lax.axis_size('seq'...  9.37 us
    ppermute x6, starting transfers between devices, swapped(): lax.ppermute(block, 'kvh', [(i, i ^ mask) for i in range(lax.axis_size('k...  5.29 us
    pallas_call x2, Pallas kernels, gradients(): pl.pallas_call(functools.partial(grad_kernel, heads_here, masks, parts, i...  3.94 us
    ppermute x4, waiting for transfers between devices, ringed(): return lax.ppermute(block, 'seq', route)  3.82 us
    ppermute x4, starting transfers between devices, ringed(): return lax.ppermute(block, 'seq', route)  3.3 us
    ppermute x6, waiting for transfers between devices, swapped(): lax.ppermute(block, 'kvh', [(i, i ^ mask) for i in range(lax.axis_size('k...  3.28 us
    ppermute x4, waiting for transfers between devices, paired(): lax.ppermute(block, 'seq', [(i, i ^ 1) for i in range(lax.axis_size('seq'...  1.74 us
    ppermute x1, starting transfers between devices, shifted(): lax.ppermute(block, 'seq', [(i, (i + distance) % count) for i in range(co...  1.58 us
  transfers between devices with their start and end apart: 15, of which 7 were waited for; matrix products, arithmetic and copies ran while one was open for 0% of the time, Pallas kernels for 8%

profile of v12, /device:TPU:0, one launch (start us, length us, event | category | flops | bytes accessed | tf_op | source)
XLA Modules:
  0.0 35.4 jit_solution(1896096378180646569)
XLA Ops:
  0.6 0.0 copy-start
  0.6 1.3 %prepare.1 = (bf16[2,2,128,128]{3,2,1,0:T(8,128)(2,1)S(1)}, bf16[2,2,128,128]{3,2,1,0:T(8,128)(2,1)S(1)}, bf16[2,128,128]{2,1,0:T(8,128)(2,1)S(1)}, bf16[2,128,1...) custom-call(s32[8]{0:T(128)} %lengths_ref.1, ...), custom_call_target="tpu_custom_call" | custom-call | tf_op jit(solution)/shard_map/prepare/pallas_call | solution.py:94
  1.9 3.0 %collective-permute-start.2 = (bf16[2,128,128]{2,1,0:T(8,128)(2,1)S(1)}, bf16[2,128,128]{2,1,0:T(8,128)(2,1)S(1)}, u32[]{:S(2)}, u32[]{:S(2)}) collective-permute-start(bf16[2,128,128]{2,1,0:T(8,128)(2,1)S(1)} %get-tuple-element.27), channel_id=1, source_target_pairs={{0,4},{4,0},{8,12},{12,8},{16,20},{20,16},{24,28},{28,24},{1,5},{5... | collective-permute-start | bytes 196616 | tf_op jit(solution)/shard_map/ppermute | solution.py:390
  4.9 0.1 collective-permute-start.3
  5.0 0.9 %collective-permute-start = (bf16[32,16,128]{2,1,0:T(8,128)(2,1)S(1)}, bf16[32,16,128]{2,1,0:T(8,128)(2,1)S(1)}, u32[]{:S(2)}, u32[]{:S(2)}) collective-permute-start(bf16[32,16,128]{2,1,0:T(8,128)(2,1)S(1)} %get-tuple-element.25), channel_id=1, source_target_pairs={{0,3},{1,2},{2,1},{3,0},{4,7},{5,6},{6,5},{7,4},{8,11},{9,10},{10,... | collective-permute-start | bytes 393224 | tf_op jit(solution)/shard_map/ppermute | solution.py:403
  5.9 1.6 %collective-permute-start.1 = (bf16[2,2,128,128]{3,2,1,0:T(8,128)(2,1)S(1)}, bf16[2,2,128,128]{3,2,1,0:T(8,128)(2,1)S(1)}, u32[]{:S(2)}, u32[]{:S(2)}) collective-permute-start(bf16[2,2,128,128]{3,2,1,0:T(8,128)(2,1)S(1)} %get-tuple-element.26), channel_id=1, source_target_pairs={{0,8},{4,12},{8,16},{12,20},{16,24},{20,28},{24,0},{28,4},{1,9},{5... | collective-permute-start | bytes 393224 | tf_op jit(solution)/shard_map/ppermute | solution.py:386
  7.5 1.0 %collective-permute-start.6 = (bf16[32,16,128]{2,1,0:T(8,128)(2,1)S(1)}, bf16[32,16,128]{2,1,0:T(8,128)(2,1)S(1)}, u32[]{:S(2)}, u32[]{:S(2)}) collective-permute-start(bf16[32,16,128]{2,1,0:T(8,128)(2,1)S(1)} %get-tuple-element.30), channel_id=1, source_target_pairs={{0,1},{1,0},{2,3},{3,2},{4,5},{5,4},{6,7},{7,6},{8,9},{9,8},{10,11... | collective-permute-start | bytes 393224 | tf_op jit(solution)/shard_map/ppermute | solution.py:403
  8.4 0.0 collective-permute-done.2.refs_2_
  8.4 1.6 %collective-permute-start.4 = (bf16[2,128,128]{2,1,0:T(8,128)(2,1)S(1)}, bf16[2,128,128]{2,1,0:T(8,128)(2,1)S(1)}, u32[]{:S(2)}, u32[]{:S(2)}) collective-permute-start(bf16[2,128,128]{2,1,0:T(8,128)(2,1)S(1)} %collective-permute-done.2.refs_2_), channel_id=1, source_target_pairs={{0,8},{4,0},{8,16},{12,4},{16,24},{20,12},{24,28},{28,20},{1,9},{5... | collective-permute-start | bytes 196616 | tf_op jit(solution)/shard_map/ppermute | solution.py:399
  10.0 0.0 collective-permute-done.3.refs_3_
  10.0 1.6 %collective-permute-start.5 = (bf16[2,128,128]{2,1,0:T(8,128)(2,1)S(1)}, bf16[2,128,128]{2,1,0:T(8,128)(2,1)S(1)}, u32[]{:S(2)}, u32[]{:S(2)}) collective-permute-start(bf16[2,128,128]{2,1,0:T(8,128)(2,1)S(1)} %collective-permute-done.3.refs_3_), channel_id=1, source_target_pairs={{0,8},{4,0},{8,16},{12,4},{16,24},{20,12},{24,28},{28,20},{1,9},{5... | collective-permute-start | bytes 196616 | tf_op jit(solution)/shard_map/ppermute | solution.py:399
  11.6 1.5 %collective-permute-done.4.refs_4_ = bf16[2,128,128]{2,1,0:T(8,128)(2,1)S(1)} collective-permute-done((bf16[2,128,128]{2,1,0:T(8,128)(2,1)S(1)}, bf16[2,128,128]{2,1,0:T(8,128)(2,1)S(1)}, u32[]{:S(2)}, u32[]{:S(2)}) %collective-permute-start.4) | collective-permute-done | bytes 65568 | tf_op jit(solution)/shard_map/ppermute | solution.py:399
  13.1 1.3 %collective-permute-start.8 = (bf16[32,16,128]{2,1,0:T(8,128)(2,1)S(1)}, bf16[32,16,128]{2,1,0:T(8,128)(2,1)S(1)}, u32[]{:S(2)}, u32[]{:S(2)}) collective-permute-start(bf16[32,16,128]{2,1,0:T(8,128)(2,1)S(1)} %get-tuple-element.32), channel_id=1, source_target_pairs={{0,2},{1,3},{2,0},{3,1},{4,6},{5,7},{6,4},{7,5},{8,10},{9,11},{10,... | collective-permute-start | bytes 393224 | tf_op jit(solution)/shard_map/ppermute | solution.py:403
  14.4 0.0 collective-permute-done.5.refs_5_
  14.4 0.0 collective-permute-done.refs_0_
  14.4 0.0 collective-permute-done.1.refs_1_
  14.4 0.0 collective-permute-done.6.refs_7_
  14.4 0.0 copy-done
  14.4 2.8 %gradients.2 = (bf16[32,16,128]{2,1,0:T(8,128)(2,1)S(1)}, bf16[32,16,128]{2,1,0:T(8,128)(2,1)S(1)}, bf16[32,16,128]{2,1,0:T(8,128)(2,1)S(1)}, f32[2,512,128]{2,1,0:T(8,128)S(1)}, f32[2,512,128]{2,1,0:T(8,128)S(1)}) custom-call(s32[4,2,256]{2,1,0:T(2,128)S(1)} %get-tuple-element.23.range_ref, bf16[128,16,128]{2,1,0:T(8,128)(2,1)S(1)} %copy-done, ...), custom_call_target="tpu_custom_call" | custom-call | flops 1006632960 | bytes 2097152 | tf_op jit(solution)/shard_map/gradients/pallas_call | solution.py:303
  17.2 1.1 %collective-permute-done.8.refs_0_ = bf16[32,16,128]{2,1,0:T(8,128)(2,1)S(1)} collective-permute-done((bf16[32,16,128]{2,1,0:T(8,128)(2,1)S(1)}, bf16[32,16,128]{2,1,0:T(8,128)(2,1)S(1)}, u32[]{:S(2)}, u32[]{:S(2)}) %collective-permute-start.8) | collective-permute-done | bytes 131104 | tf_op jit(solution)/shard_map/ppermute | solution.py:403
  18.3 1.2 %gradients.3 = (bf16[32,16,128]{2,1,0:T(8,128)(2,1)S(1)}, f32[2,2,128,128]{3,2,1,0:T(8,128)S(1)}, bf16[2,2,128,128]{3,2,1,0:T(8,128)(2,1)S(1)}, bf16[2,2,128,128...) custom-call(s32[4,2,256]{2,1,0:T(2,128)S(1)} %get-tuple-element.23.range_ref, ...), custom_call_target="tpu_custom_call" | custom-call | flops 335544320 | bytes 2097152 | tf_op jit(solution)/shard_map/gradients/pallas_call | solution.py:303
  19.4 3.8 %collective-permute-start.9 = (bf16[2,2,128,128]{3,2,1,0:T(8,128)(2,1)S(1)}, bf16[2,2,128,128]{3,2,1,0:T(8,128)(2,1)S(1)}, u32[]{:S(2)}, u32[]{:S(2)}) collective-permute-start(bf16[2,2,128,128]{3,2,1,0:T(8,128)(2,1)S(1)} %get-tuple-element.35), channel_id=1, source_target_pairs={{0,4},{4,0},{8,12},{12,8},{16,20},{20,16},{24,28},{28,24},{1,5},{5... | collective-permute-start | bytes 393224 | tf_op jit(solution)/shard_map/ppermute | solution.py:390
  23.2 0.0 collective-permute-start.7
  23.3 1.0 %collective-permute-start.14 = (bf16[32,16,128]{2,1,0:T(8,128)(2,1)S(1)}, bf16[32,16,128]{2,1,0:T(8,128)(2,1)S(1)}, u32[]{:S(2)}, u32[]{:S(2)}) collective-permute-start(bf16[32,16,128]{2,1,0:T(8,128)(2,1)S(1)} %get-tuple-element.40), channel_id=1, source_target_pairs={{0,3},{1,2},{2,1},{3,0},{4,7},{5,6},{6,5},{7,4},{8,11},{9,10},{10,... | collective-permute-start | bytes 393224 | tf_op jit(solution)/shard_map/ppermute | solution.py:403
  24.2 0.1 collective-permute-start.11
  24.3 1.1 %collective-permute-start.12 = (bf16[32,16,128]{2,1,0:T(8,128)(2,1)S(1)}, bf16[32,16,128]{2,1,0:T(8,128)(2,1)S(1)}, u32[]{:S(2)}, u32[]{:S(2)}) collective-permute-start(bf16[32,16,128]{2,1,0:T(8,128)(2,1)S(1)} %get-tuple-element.38), channel_id=1, source_target_pairs={{0,2},{1,3},{2,0},{3,1},{4,6},{5,7},{6,4},{7,5},{8,10},{9,11},{10,... | collective-permute-start | bytes 393224 | tf_op jit(solution)/shard_map/ppermute | solution.py:403
  25.5 1.3 %collective-permute-done.9.left = bf16[2,2,128,128]{3,2,1,0:T(8,128)(2,1)S(1)} collective-permute-done((bf16[2,2,128,128]{3,2,1,0:T(8,128)(2,1)S(1)}, bf16[2,2,128,128]{3,2,1,0:T(8,128)(2,1)S(1)}, u32[]{:S(2)}, u32[]{:S(2)}) %collective-permute-start.9) | collective-permute-done | bytes 131104 | tf_op jit(solution)/shard_map/ppermute | solution.py:390
  26.8 2.5 %collective-permute-start.13 = (bf16[2,2,128,128]{3,2,1,0:T(8,128)(2,1)S(1)}, bf16[2,2,128,128]{3,2,1,0:T(8,128)(2,1)S(1)}, u32[]{:S(2)}, u32[]{:S(2)}) collective-permute-start(bf16[2,2,128,128]{3,2,1,0:T(8,128)(2,1)S(1)} %get-tuple-element.39), channel_id=1, source_target_pairs={{0,4},{4,0},{8,12},{12,8},{16,20},{20,16},{24,28},{28,24},{1,5},{5... | collective-permute-start | bytes 393224 | tf_op jit(solution)/shard_map/ppermute | solution.py:390
  29.3 0.0 collective-permute-done.7.refs_0_
  29.4 0.1 collective-permute-start.10
  29.4 0.0 collective-permute-done.14.refs_5_
  29.4 0.2 collective-permute-done.11.refs_2_
  29.7 2.2 %collective-permute-done.12.refs_3_ = bf16[32,16,128]{2,1,0:T(8,128)(2,1)S(1)} collective-permute-done((bf16[32,16,128]{2,1,0:T(8,128)(2,1)S(1)}, bf16[32,16,128]{2,1,0:T(8,128)(2,1)S(1)}, u32[]{:S(2)}, u32[]{:S(2)}) %collective-permute-start.12) | collective-permute-done | bytes 131104 | tf_op jit(solution)/shard_map/ppermute | solution.py:403
  31.9 0.4 %collective-permute-done.13.refs_4_ = bf16[2,2,128,128]{3,2,1,0:T(8,128)(2,1)S(1)} collective-permute-done((bf16[2,2,128,128]{3,2,1,0:T(8,128)(2,1)S(1)}, bf16[2,2,128,128]{3,2,1,0:T(8,128)(2,1)S(1)}, u32[]{:S(2)}, u32[]{:S(2)}) %collective-permute-start.13) | collective-permute-done | bytes 131104 | tf_op jit(solution)/shard_map/ppermute | solution.py:390
  32.3 2.1 %collective-permute-done.10.refs_1_ = bf16[2,2,128,128]{3,2,1,0:T(8,128)(2,1)S(1)} collective-permute-done((bf16[2,2,128,128]{3,2,1,0:T(8,128)(2,1)S(1)}, bf16[2,2,128,128]{3,2,1,0:T(8,128)(2,1)S(1)}, u32[]{:S(2)}, u32[]{:S(2)}) %collective-permute-start.10) | collective-permute-done | bytes 131104 | tf_op jit(solution)/shard_map/ppermute | solution.py:399
  34.4 1.0 %finish.1 = (bf16[32,64,128]{2,1,0:T(8,128)(2,1)}, bf16[128,2,128]{2,1,0:T(2,128)(2,1)}, bf16[128,2,128]{2,1,0:T(2,128)(2,1)}) custom-call(bf16[32,16,128]{2,1,0:T(8,128)(2,1)S(1)} %collective-permute-done.7.refs_0_, bf16[2,2,128,128]{3,2,1,0:T(8,128)(2,1)S(1)} %collective-permute-done.10.refs_1_, ...), custom_call_target="tpu_custom_call" | custom-call | tf_op jit(solution)/shard_map/finish/pallas_call | solution.py:370
  (1 shorter events, 0.0 us)
Async XLA Ops:
  0.6 13.8 %copy-start = (bf16[128,16,128]{2,1,0:T(8,128)(2,1)S(1)}, bf16[128,16,128]{2,1,0:T(8,128)(2,1)}, u32[]{:S(2)}) copy-start(bf16[128,16,128]{2,1,0:T(8,128)(2,1)} %q_ref.3) | copy-start | bytes 1572868
  1.9 6.5 %collective-permute-start.2 = (bf16[2,128,128]{2,1,0:T(8,128)(2,1)S(1)}, bf16[2,128,128]{2,1,0:T(8,128)(2,1)S(1)}, u32[]{:S(2)}, u32[]{:S(2)}) collective-permute-start(bf16[2,128,128]{2,1,0:T(8,128)(2,1)S(1)} %get-tuple-element.27), channel_id=1, source_target_pairs={{0,4},{4,0},{8,12},{12,8},{16,20},{20,16},{24,28},{28,24},{1,5},{5... | collective-permute-start | bytes 196616 | tf_op jit(solution)/shard_map/ppermute | solution.py:390
  4.9 5.1 %collective-permute-start.3 = (bf16[2,128,128]{2,1,0:T(8,128)(2,1)S(1)}, bf16[2,128,128]{2,1,0:T(8,128)(2,1)S(1)}, u32[]{:S(2)}, u32[]{:S(2)}) collective-permute-start(bf16[2,128,128]{2,1,0:T(8,128)(2,1)S(1)} %get-tuple-element.28), channel_id=1, source_target_pairs={{0,4},{4,0},{8,12},{12,8},{16,20},{20,16},{24,28},{28,24},{1,5},{5... | collective-permute-start | bytes 196616 | tf_op jit(solution)/shard_map/ppermute | solution.py:390
  5.0 9.4 %collective-permute-start = (bf16[32,16,128]{2,1,0:T(8,128)(2,1)S(1)}, bf16[32,16,128]{2,1,0:T(8,128)(2,1)S(1)}, u32[]{:S(2)}, u32[]{:S(2)}) collective-permute-start(bf16[32,16,128]{2,1,0:T(8,128)(2,1)S(1)} %get-tuple-element.25), channel_id=1, source_target_pairs={{0,3},{1,2},{2,1},{3,0},{4,7},{5,6},{6,5},{7,4},{8,11},{9,10},{10,... | collective-permute-start | bytes 393224 | tf_op jit(solution)/shard_map/ppermute | solution.py:403
  5.9 8.5 %collective-permute-start.1 = (bf16[2,2,128,128]{3,2,1,0:T(8,128)(2,1)S(1)}, bf16[2,2,128,128]{3,2,1,0:T(8,128)(2,1)S(1)}, u32[]{:S(2)}, u32[]{:S(2)}) collective-permute-start(bf16[2,2,128,128]{3,2,1,0:T(8,128)(2,1)S(1)} %get-tuple-element.26), channel_id=1, source_target_pairs={{0,8},{4,12},{8,16},{12,20},{16,24},{20,28},{24,0},{28,4},{1,9},{5... | collective-permute-start | bytes 393224 | tf_op jit(solution)/shard_map/ppermute | solution.py:386
  7.5 7.0 %collective-permute-start.6 = (bf16[32,16,128]{2,1,0:T(8,128)(2,1)S(1)}, bf16[32,16,128]{2,1,0:T(8,128)(2,1)S(1)}, u32[]{:S(2)}, u32[]{:S(2)}) collective-permute-start(bf16[32,16,128]{2,1,0:T(8,128)(2,1)S(1)} %get-tuple-element.30), channel_id=1, source_target_pairs={{0,1},{1,0},{2,3},{3,2},{4,5},{5,4},{6,7},{7,6},{8,9},{9,8},{10,11... | collective-permute-start | bytes 393224 | tf_op jit(solution)/shard_map/ppermute | solution.py:403
  8.4 4.6 %collective-permute-start.4 = (bf16[2,128,128]{2,1,0:T(8,128)(2,1)S(1)}, bf16[2,128,128]{2,1,0:T(8,128)(2,1)S(1)}, u32[]{:S(2)}, u32[]{:S(2)}) collective-permute-start(bf16[2,128,128]{2,1,0:T(8,128)(2,1)S(1)} %collective-permute-done.2.refs_2_), channel_id=1, source_target_pairs={{0,8},{4,0},{8,16},{12,4},{16,24},{20,12},{24,28},{28,20},{1,9},{5... | collective-permute-start | bytes 196616 | tf_op jit(solution)/shard_map/ppermute | solution.py:399
  10.0 4.4 %collective-permute-start.5 = (bf16[2,128,128]{2,1,0:T(8,128)(2,1)S(1)}, bf16[2,128,128]{2,1,0:T(8,128)(2,1)S(1)}, u32[]{:S(2)}, u32[]{:S(2)}) collective-permute-start(bf16[2,128,128]{2,1,0:T(8,128)(2,1)S(1)} %collective-permute-done.3.refs_3_), channel_id=1, source_target_pairs={{0,8},{4,0},{8,16},{12,4},{16,24},{20,12},{24,28},{28,20},{1,9},{5... | collective-permute-start | bytes 196616 | tf_op jit(solution)/shard_map/ppermute | solution.py:399
  13.1 5.2 %collective-permute-start.8 = (bf16[32,16,128]{2,1,0:T(8,128)(2,1)S(1)}, bf16[32,16,128]{2,1,0:T(8,128)(2,1)S(1)}, u32[]{:S(2)}, u32[]{:S(2)}) collective-permute-start(bf16[32,16,128]{2,1,0:T(8,128)(2,1)S(1)} %get-tuple-element.32), channel_id=1, source_target_pairs={{0,2},{1,3},{2,0},{3,1},{4,6},{5,7},{6,4},{7,5},{8,10},{9,11},{10,... | collective-permute-start | bytes 393224 | tf_op jit(solution)/shard_map/ppermute | solution.py:403
  19.4 7.4 %collective-permute-start.9 = (bf16[2,2,128,128]{3,2,1,0:T(8,128)(2,1)S(1)}, bf16[2,2,128,128]{3,2,1,0:T(8,128)(2,1)S(1)}, u32[]{:S(2)}, u32[]{:S(2)}) collective-permute-start(bf16[2,2,128,128]{3,2,1,0:T(8,128)(2,1)S(1)} %get-tuple-element.35), channel_id=1, source_target_pairs={{0,4},{4,0},{8,12},{12,8},{16,20},{20,16},{24,28},{28,24},{1,5},{5... | collective-permute-start | bytes 393224 | tf_op jit(solution)/shard_map/ppermute | solution.py:390
  23.2 6.1 %collective-permute-start.7 = (bf16[32,16,128]{2,1,0:T(8,128)(2,1)S(1)}, bf16[32,16,128]{2,1,0:T(8,128)(2,1)S(1)}, u32[]{:S(2)}, u32[]{:S(2)}) collective-permute-start(bf16[32,16,128]{2,1,0:T(8,128)(2,1)S(1)} %get-tuple-element.31), channel_id=1, source_target_pairs={{0,1},{1,0},{2,3},{3,2},{4,5},{5,4},{6,7},{7,6},{8,9},{9,8},{10,11... | collective-permute-start | bytes 393224 | tf_op jit(solution)/shard_map/ppermute | solution.py:403
  23.3 6.2 %collective-permute-start.14 = (bf16[32,16,128]{2,1,0:T(8,128)(2,1)S(1)}, bf16[32,16,128]{2,1,0:T(8,128)(2,1)S(1)}, u32[]{:S(2)}, u32[]{:S(2)}) collective-permute-start(bf16[32,16,128]{2,1,0:T(8,128)(2,1)S(1)} %get-tuple-element.40), channel_id=1, source_target_pairs={{0,3},{1,2},{2,1},{3,0},{4,7},{5,6},{6,5},{7,4},{8,11},{9,10},{10,... | collective-permute-start | bytes 393224 | tf_op jit(solution)/shard_map/ppermute | solution.py:403
  24.2 5.4 %collective-permute-start.11 = (bf16[2,2,128,128]{3,2,1,0:T(8,128)(2,1)S(1)}, bf16[2,2,128,128]{3,2,1,0:T(8,128)(2,1)S(1)}, u32[]{:S(2)}, u32[]{:S(2)}) collective-permute-start(bf16[2,2,128,128]{3,2,1,0:T(8,128)(2,1)S(1)} %get-tuple-element.37), channel_id=1, source_target_pairs={{8,0},{0,4},{16,8},{4,12},{24,16},{12,20},{28,24},{20,28},{9,1},{1... | collective-permute-start | bytes 393224 | tf_op jit(solution)/shard_map/ppermute | solution.py:399
  24.3 7.5 %collective-permute-start.12 = (bf16[32,16,128]{2,1,0:T(8,128)(2,1)S(1)}, bf16[32,16,128]{2,1,0:T(8,128)(2,1)S(1)}, u32[]{:S(2)}, u32[]{:S(2)}) collective-permute-start(bf16[32,16,128]{2,1,0:T(8,128)(2,1)S(1)} %get-tuple-element.38), channel_id=1, source_target_pairs={{0,2},{1,3},{2,0},{3,1},{4,6},{5,7},{6,4},{7,5},{8,10},{9,11},{10,... | collective-permute-start | bytes 393224 | tf_op jit(solution)/shard_map/ppermute | solution.py:403
  26.8 5.4 %collective-permute-start.13 = (bf16[2,2,128,128]{3,2,1,0:T(8,128)(2,1)S(1)}, bf16[2,2,128,128]{3,2,1,0:T(8,128)(2,1)S(1)}, u32[]{:S(2)}, u32[]{:S(2)}) collective-permute-start(bf16[2,2,128,128]{3,2,1,0:T(8,128)(2,1)S(1)} %get-tuple-element.39), channel_id=1, source_target_pairs={{0,4},{4,0},{8,12},{12,8},{16,20},{20,16},{24,28},{28,24},{1,5},{5... | collective-permute-start | bytes 393224 | tf_op jit(solution)/shard_map/ppermute | solution.py:390
  29.4 5.0 %collective-permute-start.10 = (bf16[2,2,128,128]{3,2,1,0:T(8,128)(2,1)S(1)}, bf16[2,2,128,128]{3,2,1,0:T(8,128)(2,1)S(1)}, u32[]{:S(2)}, u32[]{:S(2)}) collective-permute-start(bf16[2,2,128,128]{3,2,1,0:T(8,128)(2,1)S(1)} %add.1), channel_id=1, source_target_pairs={{0,8},{4,0},{8,16},{12,4},{16,24},{20,12},{24,28},{28,20},{1,9},{5... | collective-permute-start | bytes 393224 | tf_op jit(solution)/shard_map/ppermute | solution.py:399

commit v13 on v11

--- a/solution.py
+++ b/solution.py
@@ -29,9 +29,39 @@
     return [wide[:, group, :].astype(jnp.bfloat16) for group in range(buf.shape[1])]
 
 
-def prep_kernel(parts, lengths_ref, prefixes_ref, cot_ref, key_ref, value_ref, *rest):
-    kv_outs, cot_outs, rest = rest[:3], rest[3 : parts + 3], rest[parts + 3 :]
-    range_out, key_buf, value_buf, lengths, prefixes, sems, scalar_sems = rest
+def pack_kernel(key_ref, value_ref, *rest):
+    kv_outs, (key_buf, value_buf, sems) = rest[:-3], rest[-3:]
+    loads = []
+    for number, (ref, buf) in enumerate(((key_ref, key_buf), (value_ref, value_buf))):
+        loads.append(pltpu.make_async_copy(ref, buf, sems.at[number]))
+        loads[-1].start()
+    for number, buf in enumerate((key_buf, value_buf)):
+        loads[number].wait()
+        for group, block in enumerate(regroup(buf)):
+            for kv_out in kv_outs:
+                kv_out[number, group] = block
+
+
+def pack(keys, values):
+    kv_rows, kv_heads, size = keys.shape
+    block = pltpu.VMEM((2, kv_heads, kv_rows, size), jnp.bfloat16)
+    return pl.pallas_call(
+        pack_kernel,
+        out_shape=(block,) * 3,
+        in_specs=[_HBM] * 2,
+        out_specs=(_VMEM,) * 3,
+        scratch_shapes=[
+            pltpu.VMEM(keys.shape, jnp.bfloat16),
+            pltpu.VMEM(values.shape, jnp.bfloat16),
+            pltpu.SemaphoreType.DMA((2,)),
+        ],
+        compiler_params=pltpu.CompilerParams(vmem_limit_bytes=VMEM_BYTES),
+        name="pack",
+    )(*[pltpu.with_memory_space_constraint(array, pltpu.HBM) for array in (keys, values)])
+
+
+def prep_kernel(parts, kv_rows, lengths_ref, prefixes_ref, cot_ref, kv_ref, *rest):
+    cot_outs, (range_out, lengths, prefixes, sems, scalar_sems) = rest[:parts], rest[parts:]
     heads = cot_ref.shape[1] // parts
     me = lax.axis_index("kvh")
     scalars = [
@@ -40,68 +70,55 @@
     ]
     for copy in scalars:
         copy.start()
-    loads = []
-    for number, (ref, buf) in enumerate(((key_ref, key_buf), (value_ref, value_buf))):
-        loads.append(pltpu.make_async_copy(ref, buf, sems.at[number]))
-        loads[-1].start()
     copies = []
     for mask in range(parts):
         first = pl.multiple_of((me ^ mask) * heads, heads)
         copies.append(
             pltpu.make_async_copy(
-                cot_ref.at[:, pl.ds(first, heads), :], cot_outs[mask], sems.at[mask + 2]
+                cot_ref.at[:, pl.ds(first, heads), :], cot_outs[mask], sems.at[mask]
             )
         )
         copies[-1].start()
-    for number, buf in enumerate((key_buf, value_buf)):
-        loads[number].wait()
-        for group, block in enumerate(regroup(buf)):
-            for kv_out in kv_outs:
-                kv_out[number, group] = block
     for copy in scalars:
         copy.wait()
-    rows = key_buf.shape[0]
-    tokens = rows // parts
+    tokens = kv_rows // parts
     lanes = range_out.shape[2]
     lane_token = lax.broadcasted_iota(jnp.int32, (1, lanes), 1) // (lanes // tokens)
     shard = lax.axis_index("seq")
     for mask in range(parts):
         first = (me ^ mask) * tokens
-        low, high = bounds(shard * rows + first + lane_token, lengths, prefixes)
-        origin = (shard - BACK) * rows + first
+        low, high = bounds(shard * kv_rows + first + lane_token, lengths, prefixes)
+        origin = (shard - BACK) * kv_rows + first
         range_out[mask, 0:1, :] = low - origin
         range_out[mask, 1:2, :] = high - origin
     for copy in copies:
         copy.wait()
 
 
-def prepare(lengths, prefixes, cotangent, keys, values, parts):
+def prepare(lengths, prefixes, cotangent, kv, parts):
     rows, heads, size = cotangent.shape
-    kv_rows, kv_heads, _ = keys.shape
+    _, kv_heads, kv_rows, _ = kv.shape
     lanes = kv_rows // parts * (heads // parts // kv_heads)
     piece = pltpu.VMEM((rows, heads // parts, size), jnp.bfloat16)
-    block = pltpu.VMEM((2, kv_heads, kv_rows, size), jnp.bfloat16)
     operands = [
         pltpu.with_memory_space_constraint(array, pltpu.HBM)
-        for array in (lengths, prefixes, cotangent, keys, values)
+        for array in (lengths, prefixes, cotangent)
     ]
     outs = pl.pallas_call(
-        functools.partial(prep_kernel, parts),
-        out_shape=(block,) * 3 + (piece,) * parts + (pltpu.VMEM((parts, 2, lanes), jnp.int32),),
-        in_specs=[_HBM] * 5,
-        out_specs=(_VMEM,) * (parts + 4),
+        functools.partial(prep_kernel, parts, kv_rows),
+        out_shape=(piece,) * parts + (pltpu.VMEM((parts, 2, lanes), jnp.int32),),
+        in_specs=[_HBM] * 3 + [pl.BlockSpec(memory_space=pl.ANY)],
+        out_specs=(_VMEM,) * (parts + 1),
         scratch_shapes=[
-            pltpu.VMEM(keys.shape, jnp.bfloat16),
-            pltpu.VMEM(values.shape, jnp.bfloat16),
             pltpu.SMEM(lengths.shape, jnp.int32),
             pltpu.SMEM(prefixes.shape, jnp.int32),
-            pltpu.SemaphoreType.DMA((parts + 2,)),
+            pltpu.SemaphoreType.DMA((parts,)),
             pltpu.SemaphoreType.DMA((2,)),
         ],
         compiler_params=pltpu.CompilerParams(vmem_limit_bytes=VMEM_BYTES),
         name="prepare",
-    )(*operands)
-    return outs[:3], outs[3:-1], outs[-1]
+    )(*operands, kv)
+    return outs[:-1], outs[-1]
 
 
 def bounds(position, lengths, prefixes):
@@ -304,30 +321,37 @@
 
 
 def finish_kernel(parts, *refs):
-    *refs, dq_out, dk_out, dv_out = refs
+    *refs, dq_out, dk_out, dv_out, dk_buf, dv_buf, sems = refs
     refs = dict(zip(finish_order(parts), refs))
-    dqs = [refs[mask] for mask in range(parts)]
-    own, far, even, odd = [refs[name] for name in ("own", "far", "even", "odd")]
-    heads = dqs[0].shape[1]
+    heads = refs[0].shape[1]
     me = lax.axis_index("kvh")
+    copies = []
     for mask in range(parts):
         first = pl.multiple_of((me ^ mask) * heads, heads)
-        dq_out[:, pl.ds(first, heads), :] = dqs[mask][...]
-    for number, ref in enumerate((dk_out, dv_out)):
+        copies.append(
+            pltpu.make_async_copy(refs[mask], dq_out.at[:, pl.ds(first, heads), :], sems.at[mask])
+        )
+        copies[-1].start()
+    for number, (buf, ref) in enumerate(((dk_buf, dk_out), (dv_buf, dv_out))):
         sums = []
-        for group in range(ref.shape[1]):
-            total = own[number, group]
-            for other in (far, even, odd):
-                total = total + other[number, group].astype(jnp.float32)
+        for group in range(buf.shape[1]):
+            total = refs["own"][number, group]
+            for name in ("far", "even", "odd"):
+                total = total + refs[name][number, group].astype(jnp.float32)
             sums.append(total)
-        ref[...] = jnp.stack(sums, axis=1).astype(jnp.bfloat16)
+        buf[...] = jnp.stack(sums, axis=1).astype(jnp.bfloat16)
+        copies.append(pltpu.make_async_copy(buf, ref, sems.at[parts + number]))
+        copies[-1].start()
+    for copy in copies:
+        copy.wait()
 
 
 def finish(dqs, partials):
     parts = len(dqs)
     rows, heads, size = dqs[0].shape
     _, kv_heads, kv_rows, _ = partials[0].shape
-    kv_out = jax.ShapeDtypeStruct((kv_rows, kv_heads, size), jnp.bfloat16)
+    kv_shape = (kv_rows, kv_heads, size)
+    kv_out = jax.ShapeDtypeStruct(kv_shape, jnp.bfloat16)
     operands = dict(enumerate(dqs)) | dict(zip(("own", "far", "even", "odd"), partials))
     return pl.pallas_call(
         functools.partial(finish_kernel, parts),
@@ -337,7 +361,12 @@
             kv_out,
         ),
         in_specs=[_VMEM] * (parts + 4),
-        out_specs=(_VMEM,) * 3,
+        out_specs=(_HBM,) * 3,
+        scratch_shapes=[
+            pltpu.VMEM(kv_shape, jnp.bfloat16),
+            pltpu.VMEM(kv_shape, jnp.bfloat16),
+            pltpu.SemaphoreType.DMA((parts + 2,)),
+        ],
         compiler_params=pltpu.CompilerParams(vmem_limit_bytes=VMEM_BYTES),
         name="finish",
     )(*[operands[name] for name in finish_order(parts)])
@@ -367,9 +396,8 @@
 
 def local(queries, keys, values, output_gradient, doc_lengths, prefix_lengths):
     parts = lax.axis_size("kvh")
-    kv, cots, ranges = prepare(
-        doc_lengths, prefix_lengths, output_gradient, keys, values, parts
-    )
+    kv = pack(keys, values)
+    cots, ranges = prepare(doc_lengths, prefix_lengths, output_gradient, kv[0], parts)
     even = paired(kv[2])
     blocks = [kv[0], shifted(kv[1], BACK), even, ringed(even)]
     cots = [cots[0]] + [swapped(cots[mask], mask) for mask in range(1, parts)]

time: 30.7 us -> 31.6 us (1.029)
  waiting for transfers between devices: 6.54 us -> 8.28 us
  starting transfers between devices: 17 us -> 15.3 us
  Pallas kernels: 6.28 us -> 7.17 us
    ppermute x3, starting transfers between devices: 6.37 us -> 4.39 us  [paired(): lax.ppermute(block, 'seq', [(i, i ^ 1) for i in range(lax.axis_size('seq'...]
    ppermute x6, waiting for transfers between devices: 1.78 us -> 3.16 us  [swapped(): lax.ppermute(block, 'kvh', [(i, i ^ mask) for i in range(lax.axis_size('k...]
    pallas_call x1 -> x2, Pallas kernels: 1.3 us -> 2.27 us  [the longest x1 1.15 us: prepare(): pl.pallas_call(functools.partial(prep_kernel, parts, kv_rows), out_shape=...]
    ppermute x3, waiting for transfers between devices: 1.4 us -> 2.08 us  [paired(): lax.ppermute(block, 'seq', [(i, i ^ 1) for i in range(lax.axis_size('seq'...]
  transfers between devices with their start and end apart: 13 -> 13, of which waited for: 8 -> 6; matrix products, arithmetic and copies ran while one was open for 0% -> 0% of each run, Pallas kernels for 9% -> 13%
where the time goes in v13:
time: 31.6 us; the launch traced here: 31.5 us
  starting transfers between devices  15.3 us (48%)
  waiting for transfers between devices  8.28 us (26%)
  Pallas kernels  7.17 us (23%)
  between operations  0.7 us (2%)
    ppermute x6, starting transfers between devices, swapped(): lax.ppermute(block, 'kvh', [(i, i ^ mask) for i in range(lax.axis_size('k...  5.43 us
    ppermute x3, starting transfers between devices, paired(): lax.ppermute(block, 'seq', [(i, i ^ 1) for i in range(lax.axis_size('seq'...  4.39 us
    ppermute x3, starting transfers between devices, ringed(): return lax.ppermute(block, 'seq', route)  3.92 us
    pallas_call x2, Pallas kernels, gradients(): pl.pallas_call(functools.partial(grad_kernel, masks, parts, carried is No...  3.91 us
    ppermute x6, waiting for transfers between devices, swapped(): lax.ppermute(block, 'kvh', [(i, i ^ mask) for i in range(lax.axis_size('k...  3.16 us
    ppermute x3, waiting for transfers between devices, ringed(): return lax.ppermute(block, 'seq', route)  3.05 us
    ppermute x3, waiting for transfers between devices, paired(): lax.ppermute(block, 'seq', [(i, i ^ 1) for i in range(lax.axis_size('seq'...  2.08 us
    ppermute x1, starting transfers between devices, shifted(): lax.ppermute(block, 'seq', [(i, (i + distance) % count) for i in range(co...  1.58 us
  transfers between devices with their start and end apart: 13, of which 6 were waited for; matrix products, arithmetic and copies ran while one was open for 0% of the time, Pallas kernels for 13%

profile of v13, /device:TPU:0, one launch (start us, length us, event | category | flops | bytes accessed | tf_op | source)
XLA Modules:
  0.0 31.5 jit_solution(16213076425834601302)
XLA Ops:
  0.6 0.0 copy-start
  0.6 1.1 %pack.1 = (bf16[2,2,128,128]{3,2,1,0:T(8,128)(2,1)S(1)}, bf16[2,2,128,128]{3,2,1,0:T(8,128)(2,1)S(1)}, bf16[2,2,128,128]{3,2,1,0:T(8,128)(2,1)S(1)}) custom-call(bf16[128,2,128]{2,1,0:T(2,128)(2,1)} %key_ref.1, bf16[128,2,128]{2,1,0:T(2,128)(2,1)} %value_ref.1), custom_call_target="tpu_custom_call" | custom-call | tf_op jit(solution)/shard_map/pack/pallas_call | solution.py:48
  1.8 3.0 %collective-permute-start = (bf16[2,2,128,128]{3,2,1,0:T(8,128)(2,1)S(1)}, bf16[2,2,128,128]{3,2,1,0:T(8,128)(2,1)S(1)}, u32[]{:S(2)}, u32[]{:S(2)}) collective-permute-start(bf16[2,2,128,128]{3,2,1,0:T(8,128)(2,1)S(1)} %get-tuple-element.23), channel_id=1, source_target_pairs={{0,4},{4,0},{8,12},{12,8},{16,20},{20,16},{24,28},{28,24},{1,5},{5... | collective-permute-start | bytes 393224 | tf_op jit(solution)/shard_map/ppermute | solution.py:381
  4.8 1.6 %collective-permute-start.1 = (bf16[2,2,128,128]{3,2,1,0:T(8,128)(2,1)S(1)}, bf16[2,2,128,128]{3,2,1,0:T(8,128)(2,1)S(1)}, u32[]{:S(2)}, u32[]{:S(2)}) collective-permute-start(bf16[2,2,128,128]{3,2,1,0:T(8,128)(2,1)S(1)} %get-tuple-element.24), channel_id=1, source_target_pairs={{0,8},{4,12},{8,16},{12,20},{16,24},{20,28},{24,0},{28,4},{1,9},{5... | collective-permute-start | bytes 393224 | tf_op jit(solution)/shard_map/ppermute | solution.py:377
  6.3 1.2 %prepare.1 = (bf16[32,16,128]{2,1,0:T(8,128)(2,1)S(1)}, bf16[32,16,128]{2,1,0:T(8,128)(2,1)S(1)}, bf16[32,16,128]{2,1,0:T(8,128)(2,1)S(1)}, bf16[32,16,128]{2,1,0:T(8,128)(2,1)S(1)}, s32[4,2,256]{2,1,0:T(2,128)S(1)}) custom-call(s32[8]{0:T(128)} %lengths_ref.1, s32[8]{0:T(128)} %prefixes_ref.1, bf16[32,64,128]{2,1,0:T(8,128)(2,1)} %cot_ref.1, ...), custom_call_target="tpu_custom_call" | custom-call | tf_op jit(solution)/shard_map/prepare/pallas_call | solution.py:107
  7.5 0.1 collective-permute-start.3
  7.6 1.6 %collective-permute-start.4 = (bf16[32,16,128]{2,1,0:T(8,128)(2,1)S(1)}, bf16[32,16,128]{2,1,0:T(8,128)(2,1)S(1)}, u32[]{:S(2)}, u32[]{:S(2)}) collective-permute-start(bf16[32,16,128]{2,1,0:T(8,128)(2,1)S(1)} %get-tuple-element.27), channel_id=1, source_target_pairs={{0,3},{1,2},{2,1},{3,0},{4,7},{5,6},{6,5},{7,4},{8,11},{9,10},{10,... | collective-permute-start | bytes 393224 | tf_op jit(solution)/shard_map/ppermute | solution.py:394
  9.2 0.0 collective-permute-done.refs_1_
  9.2 1.6 %collective-permute-start.2 = (bf16[2,2,128,128]{3,2,1,0:T(8,128)(2,1)S(1)}, bf16[2,2,128,128]{3,2,1,0:T(8,128)(2,1)S(1)}, u32[]{:S(2)}, u32[]{:S(2)}) collective-permute-start(bf16[2,2,128,128]{3,2,1,0:T(8,128)(2,1)S(1)} %collective-permute-done.refs_1_), channel_id=1, source_target_pairs={{0,8},{4,0},{8,16},{12,4},{16,24},{20,12},{24,28},{28,20},{1,9},{5... | collective-permute-start | bytes 393224 | tf_op jit(solution)/shard_map/ppermute | solution.py:390
  10.8 0.8 %collective-permute-start.6 = (bf16[32,16,128]{2,1,0:T(8,128)(2,1)S(1)}, bf16[32,16,128]{2,1,0:T(8,128)(2,1)S(1)}, u32[]{:S(2)}, u32[]{:S(2)}) collective-permute-start(bf16[32,16,128]{2,1,0:T(8,128)(2,1)S(1)} %get-tuple-element.29), channel_id=1, source_target_pairs={{0,2},{1,3},{2,0},{3,1},{4,6},{5,7},{6,4},{7,5},{8,10},{9,11},{10,... | collective-permute-start | bytes 393224 | tf_op jit(solution)/shard_map/ppermute | solution.py:394
  11.6 0.0 collective-permute-done.1.refs_2_
  11.6 0.0 collective-permute-done.3.refs_5_
  11.6 1.4 %collective-permute-done.4.refs_6_ = bf16[32,16,128]{2,1,0:T(8,128)(2,1)S(1)} collective-permute-done((bf16[32,16,128]{2,1,0:T(8,128)(2,1)S(1)}, bf16[32,16,128]{2,1,0:T(8,128)(2,1)S(1)}, u32[]{:S(2)}, u32[]{:S(2)}) %collective-permute-start.4) | collective-permute-done | bytes 131104 | tf_op jit(solution)/shard_map/ppermute | solution.py:394
  13.1 1.6 %collective-permute-done.2.refs_3_ = bf16[2,2,128,128]{3,2,1,0:T(8,128)(2,1)S(1)} collective-permute-done((bf16[2,2,128,128]{3,2,1,0:T(8,128)(2,1)S(1)}, bf16[2,2,128,128]{3,2,1,0:T(8,128)(2,1)S(1)}, u32[]{:S(2)}, u32[]{:S(2)}) %collective-permute-start.2) | collective-permute-done | bytes 131104 | tf_op jit(solution)/shard_map/ppermute | solution.py:390
  14.7 0.0 copy-done
  14.7 2.8 %gradients.2 = (bf16[32,16,128]{2,1,0:T(8,128)(2,1)S(1)}, bf16[32,16,128]{2,1,0:T(8,128)(2,1)S(1)}, bf16[32,16,128]{2,1,0:T(8,128)(2,1)S(1)}, f32[2,2,512,128]{3,2,1,0:T(8,128)S(1)}) custom-call(s32[4,2,256]{2,1,0:T(2,128)S(1)} %get-tuple-element.22.range_ref, bf16[128,16,128]{2,1,0:T(8,128)(2,1)S(1)} %copy-done, ...), custom_call_target="tpu_custom_call" | custom-call | flops 1006632960 | bytes 2097152 | tf_op jit(solution)/shard_map/gradients/pallas_call | solution.py:282
  17.5 0.0 collective-permute-done.6.refs_4_
  17.5 1.2 %gradients.3 = (bf16[32,16,128]{2,1,0:T(8,128)(2,1)S(1)}, f32[2,2,128,128]{3,2,1,0:T(8,128)S(1)}, bf16[2,2,128,128]{3,2,1,0:T(8,128)(2,1)S(1)}, bf16[2,2,128,128...) custom-call(s32[4,2,256]{2,1,0:T(2,128)S(1)} %get-tuple-element.22.range_ref, ...), custom_call_target="tpu_custom_call" | custom-call | flops 335544320 | bytes 2097152 | tf_op jit(solution)/shard_map/gradients/pallas_call | solution.py:282
  18.6 0.6 %collective-permute-start.7 = (bf16[2,2,128,128]{3,2,1,0:T(8,128)(2,1)S(1)}, bf16[2,2,128,128]{3,2,1,0:T(8,128)(2,1)S(1)}, u32[]{:S(2)}, u32[]{:S(2)}) collective-permute-start(bf16[2,2,128,128]{3,2,1,0:T(8,128)(2,1)S(1)} %get-tuple-element.31), channel_id=1, source_target_pairs={{0,4},{4,0},{8,12},{12,8},{16,20},{20,16},{24,28},{28,24},{1,5},{5... | collective-permute-start | bytes 393224 | tf_op jit(solution)/shard_map/ppermute | solution.py:381
  19.2 0.0 collective-permute-start.5
  19.2 1.4 %collective-permute-start.12 = (bf16[32,16,128]{2,1,0:T(8,128)(2,1)S(1)}, bf16[32,16,128]{2,1,0:T(8,128)(2,1)S(1)}, u32[]{:S(2)}, u32[]{:S(2)}) collective-permute-start(bf16[32,16,128]{2,1,0:T(8,128)(2,1)S(1)} %get-tuple-element.36), channel_id=1, source_target_pairs={{0,3},{1,2},{2,1},{3,0},{4,7},{5,6},{6,5},{7,4},{8,11},{9,10},{10,... | collective-permute-start | bytes 393224 | tf_op jit(solution)/shard_map/ppermute | solution.py:394
  20.6 0.7 %collective-permute-start.9 = (bf16[2,2,128,128]{3,2,1,0:T(8,128)(2,1)S(1)}, bf16[2,2,128,128]{3,2,1,0:T(8,128)(2,1)S(1)}, u32[]{:S(2)}, u32[]{:S(2)}) collective-permute-start(bf16[2,2,128,128]{3,2,1,0:T(8,128)(2,1)S(1)} %get-tuple-element.33), channel_id=1, source_target_pairs={{8,0},{0,4},{16,8},{4,12},{24,16},{12,20},{28,24},{20,28},{9,1},{1... | collective-permute-start | bytes 393224 | tf_op jit(solution)/shard_map/ppermute | solution.py:390
  21.3 1.5 %collective-permute-start.10 = (bf16[32,16,128]{2,1,0:T(8,128)(2,1)S(1)}, bf16[32,16,128]{2,1,0:T(8,128)(2,1)S(1)}, u32[]{:S(2)}, u32[]{:S(2)}) collective-permute-start(bf16[32,16,128]{2,1,0:T(8,128)(2,1)S(1)} %get-tuple-element.34), channel_id=1, source_target_pairs={{0,2},{1,3},{2,0},{3,1},{4,6},{5,7},{6,4},{7,5},{8,10},{9,11},{10,... | collective-permute-start | bytes 393224 | tf_op jit(solution)/shard_map/ppermute | solution.py:394
  22.9 0.8 %collective-permute-done.7.left = bf16[2,2,128,128]{3,2,1,0:T(8,128)(2,1)S(1)} collective-permute-done((bf16[2,2,128,128]{3,2,1,0:T(8,128)(2,1)S(1)}, bf16[2,2,128,128]{3,2,1,0:T(8,128)(2,1)S(1)}, u32[]{:S(2)}, u32[]{:S(2)}) %collective-permute-start.7) | collective-permute-done | bytes 131104 | tf_op jit(solution)/shard_map/ppermute | solution.py:381
  23.7 0.8 %collective-permute-start.11 = (bf16[2,2,128,128]{3,2,1,0:T(8,128)(2,1)S(1)}, bf16[2,2,128,128]{3,2,1,0:T(8,128)(2,1)S(1)}, u32[]{:S(2)}, u32[]{:S(2)}) collective-permute-start(bf16[2,2,128,128]{3,2,1,0:T(8,128)(2,1)S(1)} %get-tuple-element.35), channel_id=1, source_target_pairs={{0,4},{4,0},{8,12},{12,8},{16,20},{20,16},{24,28},{28,24},{1,5},{5... | collective-permute-start | bytes 393224 | tf_op jit(solution)/shard_map/ppermute | solution.py:381
  24.5 0.0 collective-permute-done.5.refs_0_
  24.5 1.6 %collective-permute-start.8 = (bf16[2,2,128,128]{3,2,1,0:T(8,128)(2,1)S(1)}, bf16[2,2,128,128]{3,2,1,0:T(8,128)(2,1)S(1)}, u32[]{:S(2)}, u32[]{:S(2)}) collective-permute-start(bf16[2,2,128,128]{3,2,1,0:T(8,128)(2,1)S(1)} %add.1), channel_id=1, source_target_pairs={{0,8},{4,0},{8,16},{12,4},{16,24},{20,12},{24,28},{28,20},{1,9},{5... | collective-permute-start | bytes 393224 | tf_op jit(solution)/shard_map/ppermute | solution.py:390
  26.1 0.0 collective-permute-done.12.refs_5_
  26.1 0.0 collective-permute-done.9.refs_2_
  26.1 1.7 %collective-permute-done.10.refs_3_ = bf16[32,16,128]{2,1,0:T(8,128)(2,1)S(1)} collective-permute-done((bf16[32,16,128]{2,1,0:T(8,128)(2,1)S(1)}, bf16[32,16,128]{2,1,0:T(8,128)(2,1)S(1)}, u32[]{:S(2)}, u32[]{:S(2)}) %collective-permute-start.10) | collective-permute-done | bytes 131104 | tf_op jit(solution)/shard_map/ppermute | solution.py:394
  27.8 1.3 %collective-permute-done.11.refs_4_ = bf16[2,2,128,128]{3,2,1,0:T(8,128)(2,1)S(1)} collective-permute-done((bf16[2,2,128,128]{3,2,1,0:T(8,128)(2,1)S(1)}, bf16[2,2,128,128]{3,2,1,0:T(8,128)(2,1)S(1)}, u32[]{:S(2)}, u32[]{:S(2)}) %collective-permute-start.11) | collective-permute-done | bytes 131104 | tf_op jit(solution)/shard_map/ppermute | solution.py:381
  29.1 1.4 %collective-permute-done.8.refs_1_ = bf16[2,2,128,128]{3,2,1,0:T(8,128)(2,1)S(1)} collective-permute-done((bf16[2,2,128,128]{3,2,1,0:T(8,128)(2,1)S(1)}, bf16[2,2,128,128]{3,2,1,0:T(8,128)(2,1)S(1)}, u32[]{:S(2)}, u32[]{:S(2)}) %collective-permute-start.8) | collective-permute-done | bytes 131104 | tf_op jit(solution)/shard_map/ppermute | solution.py:390
  30.5 1.0 %finish.1 = (bf16[32,64,128]{2,1,0:T(8,128)(2,1)}, bf16[128,2,128]{2,1,0:T(2,128)(2,1)}, bf16[128,2,128]{2,1,0:T(2,128)(2,1)}) custom-call(bf16[32,16,128]{2,1,0:T(8,128)(2,1)S(1)} %collective-permute-done.5.refs_0_, bf16[2,2,128,128]{3,2,1,0:T(8,128)(2,1)S(1)} %collective-permute-done.8.refs_1_, ...), custom_call_target="tpu_custom_call" | custom-call | tf_op jit(solution)/shard_map/finish/pallas_call | solution.py:356
  (1 shorter events, 0.0 us)
Async XLA Ops:
  0.6 14.1 %copy-start = (bf16[128,16,128]{2,1,0:T(8,128)(2,1)S(1)}, bf16[128,16,128]{2,1,0:T(8,128)(2,1)}, u32[]{:S(2)}) copy-start(bf16[128,16,128]{2,1,0:T(8,128)(2,1)} %q_ref.3) | copy-start | bytes 1572868
  1.8 7.5 %collective-permute-start = (bf16[2,2,128,128]{3,2,1,0:T(8,128)(2,1)S(1)}, bf16[2,2,128,128]{3,2,1,0:T(8,128)(2,1)S(1)}, u32[]{:S(2)}, u32[]{:S(2)}) collective-permute-start(bf16[2,2,128,128]{3,2,1,0:T(8,128)(2,1)S(1)} %get-tuple-element.23), channel_id=1, source_target_pairs={{0,4},{4,0},{8,12},{12,8},{16,20},{20,16},{24,28},{28,24},{1,5},{5... | collective-permute-start | bytes 393224 | tf_op jit(solution)/shard_map/ppermute | solution.py:381
  4.8 6.8 %collective-permute-start.1 = (bf16[2,2,128,128]{3,2,1,0:T(8,128)(2,1)S(1)}, bf16[2,2,128,128]{3,2,1,0:T(8,128)(2,1)S(1)}, u32[]{:S(2)}, u32[]{:S(2)}) collective-permute-start(bf16[2,2,128,128]{3,2,1,0:T(8,128)(2,1)S(1)} %get-tuple-element.24), channel_id=1, source_target_pairs={{0,8},{4,12},{8,16},{12,20},{16,24},{20,28},{24,0},{28,4},{1,9},{5... | collective-permute-start | bytes 393224 | tf_op jit(solution)/shard_map/ppermute | solution.py:377
  7.5 4.1 %collective-permute-start.3 = (bf16[32,16,128]{2,1,0:T(8,128)(2,1)S(1)}, bf16[32,16,128]{2,1,0:T(8,128)(2,1)S(1)}, u32[]{:S(2)}, u32[]{:S(2)}) collective-permute-start(bf16[32,16,128]{2,1,0:T(8,128)(2,1)S(1)} %get-tuple-element.26), channel_id=1, source_target_pairs={{0,1},{1,0},{2,3},{3,2},{4,5},{5,4},{6,7},{7,6},{8,9},{9,8},{10,11... | collective-permute-start | bytes 393224 | tf_op jit(solution)/shard_map/ppermute | solution.py:394
  7.6 5.5 %collective-permute-start.4 = (bf16[32,16,128]{2,1,0:T(8,128)(2,1)S(1)}, bf16[32,16,128]{2,1,0:T(8,128)(2,1)S(1)}, u32[]{:S(2)}, u32[]{:S(2)}) collective-permute-start(bf16[32,16,128]{2,1,0:T(8,128)(2,1)S(1)} %get-tuple-element.27), channel_id=1, source_target_pairs={{0,3},{1,2},{2,1},{3,0},{4,7},{5,6},{6,5},{7,4},{8,11},{9,10},{10,... | collective-permute-start | bytes 393224 | tf_op jit(solution)/shard_map/ppermute | solution.py:394
  9.2 5.5 %collective-permute-start.2 = (bf16[2,2,128,128]{3,2,1,0:T(8,128)(2,1)S(1)}, bf16[2,2,128,128]{3,2,1,0:T(8,128)(2,1)S(1)}, u32[]{:S(2)}, u32[]{:S(2)}) collective-permute-start(bf16[2,2,128,128]{3,2,1,0:T(8,128)(2,1)S(1)} %collective-permute-done.refs_1_), channel_id=1, source_target_pairs={{0,8},{4,0},{8,16},{12,4},{16,24},{20,12},{24,28},{28,20},{1,9},{5... | collective-permute-start | bytes 393224 | tf_op jit(solution)/shard_map/ppermute | solution.py:390
  10.8 6.7 %collective-permute-start.6 = (bf16[32,16,128]{2,1,0:T(8,128)(2,1)S(1)}, bf16[32,16,128]{2,1,0:T(8,128)(2,1)S(1)}, u32[]{:S(2)}, u32[]{:S(2)}) collective-permute-start(bf16[32,16,128]{2,1,0:T(8,128)(2,1)S(1)} %get-tuple-element.29), channel_id=1, source_target_pairs={{0,2},{1,3},{2,0},{3,1},{4,6},{5,7},{6,4},{7,5},{8,10},{9,11},{10,... | collective-permute-start | bytes 393224 | tf_op jit(solution)/shard_map/ppermute | solution.py:394
  18.6 5.0 %collective-permute-start.7 = (bf16[2,2,128,128]{3,2,1,0:T(8,128)(2,1)S(1)}, bf16[2,2,128,128]{3,2,1,0:T(8,128)(2,1)S(1)}, u32[]{:S(2)}, u32[]{:S(2)}) collective-permute-start(bf16[2,2,128,128]{3,2,1,0:T(8,128)(2,1)S(1)} %get-tuple-element.31), channel_id=1, source_target_pairs={{0,4},{4,0},{8,12},{12,8},{16,20},{20,16},{24,28},{28,24},{1,5},{5... | collective-permute-start | bytes 393224 | tf_op jit(solution)/shard_map/ppermute | solution.py:381
  19.2 5.3 %collective-permute-start.5 = (bf16[32,16,128]{2,1,0:T(8,128)(2,1)S(1)}, bf16[32,16,128]{2,1,0:T(8,128)(2,1)S(1)}, u32[]{:S(2)}, u32[]{:S(2)}) collective-permute-start(bf16[32,16,128]{2,1,0:T(8,128)(2,1)S(1)} %get-tuple-element.28), channel_id=1, source_target_pairs={{0,1},{1,0},{2,3},{3,2},{4,5},{5,4},{6,7},{7,6},{8,9},{9,8},{10,11... | collective-permute-start | bytes 393224 | tf_op jit(solution)/shard_map/ppermute | solution.py:394
  19.2 6.9 %collective-permute-start.12 = (bf16[32,16,128]{2,1,0:T(8,128)(2,1)S(1)}, bf16[32,16,128]{2,1,0:T(8,128)(2,1)S(1)}, u32[]{:S(2)}, u32[]{:S(2)}) collective-permute-start(bf16[32,16,128]{2,1,0:T(8,128)(2,1)S(1)} %get-tuple-element.36), channel_id=1, source_target_pairs={{0,3},{1,2},{2,1},{3,0},{4,7},{5,6},{6,5},{7,4},{8,11},{9,10},{10,... | collective-permute-start | bytes 393224 | tf_op jit(solution)/shard_map/ppermute | solution.py:394
  20.6 5.5 %collective-permute-start.9 = (bf16[2,2,128,128]{3,2,1,0:T(8,128)(2,1)S(1)}, bf16[2,2,128,128]{3,2,1,0:T(8,128)(2,1)S(1)}, u32[]{:S(2)}, u32[]{:S(2)}) collective-permute-start(bf16[2,2,128,128]{3,2,1,0:T(8,128)(2,1)S(1)} %get-tuple-element.33), channel_id=1, source_target_pairs={{8,0},{0,4},{16,8},{4,12},{24,16},{12,20},{28,24},{20,28},{9,1},{1... | collective-permute-start | bytes 393224 | tf_op jit(solution)/shard_map/ppermute | solution.py:390
  21.3 6.5 %collective-permute-start.10 = (bf16[32,16,128]{2,1,0:T(8,128)(2,1)S(1)}, bf16[32,16,128]{2,1,0:T(8,128)(2,1)S(1)}, u32[]{:S(2)}, u32[]{:S(2)}) collective-permute-start(bf16[32,16,128]{2,1,0:T(8,128)(2,1)S(1)} %get-tuple-element.34), channel_id=1, source_target_pairs={{0,2},{1,3},{2,0},{3,1},{4,6},{5,7},{6,4},{7,5},{8,10},{9,11},{10,... | collective-permute-start | bytes 393224 | tf_op jit(solution)/shard_map/ppermute | solution.py:394
  23.7 5.5 %collective-permute-start.11 = (bf16[2,2,128,128]{3,2,1,0:T(8,128)(2,1)S(1)}, bf16[2,2,128,128]{3,2,1,0:T(8,128)(2,1)S(1)}, u32[]{:S(2)}, u32[]{:S(2)}) collective-permute-start(bf16[2,2,128,128]{3,2,1,0:T(8,128)(2,1)S(1)} %get-tuple-element.35), channel_id=1, source_target_pairs={{0,4},{4,0},{8,12},{12,8},{16,20},{20,16},{24,28},{28,24},{1,5},{5... | collective-permute-start | bytes 393224 | tf_op jit(solution)/shard_map/ppermute | solution.py:381
  24.5 6.0 %collective-permute-start.8 = (bf16[2,2,128,128]{3,2,1,0:T(8,128)(2,1)S(1)}, bf16[2,2,128,128]{3,2,1,0:T(8,128)(2,1)S(1)}, u32[]{:S(2)}, u32[]{:S(2)}) collective-permute-start(bf16[2,2,128,128]{3,2,1,0:T(8,128)(2,1)S(1)} %add.1), channel_id=1, source_target_pairs={{0,8},{4,0},{8,16},{12,4},{16,24},{20,12},{24,28},{28,20},{1,9},{5... | collective-permute-start | bytes 393224 | tf_op jit(solution)/shard_map/ppermute | solution.py:390

commit v14 on v11

--- a/solution.py
+++ b/solution.py
@@ -13,6 +13,8 @@
 VMEM_BYTES = 40 * 1024 * 1024
 NEG = -1e30
 TILE = 8
+ALIGN = 16
+WIDTHS = (160, 288)
 
 _VMEM = pl.BlockSpec(memory_space=pltpu.VMEM)
 _SMEM = pl.BlockSpec(memory_space=pltpu.SMEM)
@@ -161,43 +163,43 @@
     sublane = lax.broadcasted_iota(jnp.int32, (TILE, lanes), 0)
     items = [(place, group) for place in range(len(masks)) for group in range(kv_heads)]
 
-    def operands(item):
+    def operands(item, starts, width):
         place, group = items[item]
         first = pl.multiple_of((me ^ masks[place]) * tokens, tokens)
         of_group = pl.ds(group * group_size, group_size)
         q = q_ref[pl.ds(first, tokens), of_group].astype(jnp.float32)
         cot = cots[place][:, of_group].astype(jnp.float32)
         return (
-            pl.ds(first, reach),
+            pl.ds(pl.multiple_of(first + starts[place], ALIGN), width),
             q.reshape(lanes, size).astype(jnp.bfloat16),
             cot.reshape(lanes, size).astype(jnp.bfloat16),
         )
 
-    def scores_of(item):
+    def scores_of(item, starts, width):
         place, group = items[item]
         slot = item % 2
-        here, q, cot = operands(item)
+        here, q, cot = operands(item, starts, width)
         scores = lax.dot_general(
             window[0, group, here], q, contract_last, preferred_element_type=jnp.float32
         )
-        low = range_ref[masks[place], 0:1, :] - sublane
-        high = range_ref[masks[place], 1:2, :] - sublane
+        low = range_ref[masks[place], 0:1, :] - starts[place] - sublane
+        high = range_ref[masks[place], 1:2, :] - starts[place] - sublane
         top = jnp.full((TILE, lanes), NEG, jnp.float32)
-        for row in range(0, reach, TILE):
+        for row in range(0, width, TILE):
             visible = (low <= row) & (high > row)
             tile = jnp.where(visible, scores[row : row + TILE] * (scale * LOG2E), NEG)
             top = jnp.maximum(top, tile)
             score_buf[slot, row : row + TILE] = tile
-        dprob_buf[slot] = lax.dot_general(
+        dprob_buf[slot, :width] = lax.dot_general(
             window[1, group, here], cot, contract_last, preferred_element_type=jnp.float32
         )
         return jnp.max(top, axis=0, keepdims=True)
 
-    def softmax_of(item, top):
+    def softmax_of(item, top, width):
         slot = item % 2
         total = jnp.zeros((TILE, lanes), jnp.float32)
         delta = jnp.zeros((TILE, lanes), jnp.float32)
-        for row in range(0, reach, TILE):
+        for row in range(0, width, TILE):
             tile = slice(row, row + TILE)
             expo = jnp.exp2(score_buf[slot, tile] - top)
             total = total + expo
@@ -205,19 +207,19 @@
             score_buf[slot, tile] = expo
         inverse = 1.0 / jnp.sum(total, axis=0, keepdims=True)
         delta = jnp.sum(delta, axis=0, keepdims=True) * inverse
-        for row in range(0, reach, 2 * TILE):
+        for row in range(0, width, 2 * TILE):
             tile = slice(row, row + 2 * TILE)
             probs = score_buf[slot, tile] * inverse
             dscores = probs * (dprob_buf[slot, tile] - delta)
             prob_buf[slot, tile] = probs.astype(jnp.bfloat16)
             dscore_buf[slot, tile] = dscores.astype(jnp.bfloat16)
 
-    def gradients_of(item):
+    def gradients_of(item, starts, width):
         place, group = items[item]
         slot = item % 2
-        here, q, cot = operands(item)
-        dscores = dscore_buf[slot]
-        acc[1, group, here] += jnp.dot(prob_buf[slot], cot, preferred_element_type=jnp.float32)
+        here, q, cot = operands(item, starts, width)
+        probs, dscores = prob_buf[slot, :width], dscore_buf[slot, :width]
+        acc[1, group, here] += jnp.dot(probs, cot, preferred_element_type=jnp.float32)
         acc[0, group, here] += jnp.dot(dscores, q, preferred_element_type=jnp.float32)
         dq = lax.dot_general(
             window[0, group, here], dscores, contract_first, preferred_element_type=jnp.float32
@@ -225,12 +227,25 @@
         dq = jnp.transpose(dq * scale).reshape(tokens, group_size, size)
         dqs[place][:, pl.ds(group * group_size, group_size)] = dq.astype(jnp.bfloat16)
 
-    top = scores_of(0)
-    for item in range(len(items)):
-        later = scores_of(item + 1) if item + 1 < len(items) else None
-        softmax_of(item, top)
-        gradients_of(item)
-        top = later
+    lowest = [jnp.min(range_ref[mask, 0:1, :]) & -ALIGN for mask in masks]
+    needed = [jnp.max(range_ref[mask, 1:2, :]) - low for mask, low in zip(masks, lowest)]
+    needed = functools.reduce(jnp.maximum, needed)
+
+    def all_items(width):
+        starts = [jnp.clip(low, 0, reach - width) for low in lowest]
+        top = scores_of(0, starts, width)
+        for item in range(len(items)):
+            later = scores_of(item + 1, starts, width) if item + 1 < len(items) else None
+            softmax_of(item, top, width)
+            gradients_of(item, starts, width)
+            top = later
+
+    widths = [width for width in WIDTHS if width < reach] + [reach]
+    for floor, width in zip([-1] + widths, widths):
+        fits = needed > floor
+        if width < reach:
+            fits = fits & (needed <= width)
+        pl.when(fits)(functools.partial(all_items, width))
 
     if not is_last:
         outs[0][...] = acc[...]
@@ -344,8 +359,9 @@
 
 
 def shifted(block, distance):
-    count = lax.axis_size("seq")
-    return lax.ppermute(block, "seq", [(i, (i + distance) % count) for i in range(count)])
+    devices = range(lax.axis_size("seq"))
+    route = [(i, i + distance) for i in devices if i + distance in devices]
+    return lax.ppermute(block, "seq", route)
 
 
 def paired(block):

time: 30.7 us -> 32 us (1.042)
  starting transfers between devices: 17 us -> 18.5 us
  Pallas kernels: 6.28 us -> 4.9 us
  waiting for transfers between devices: 6.54 us -> 7.74 us
    ppermute x1, starting transfers between devices: 1.58 us -> 3.48 us  [shifted(): return lax.ppermute(block, 'seq', route)]
    ppermute x3, starting transfers between devices: 3.84 us -> 5.54 us  [ringed(): return lax.ppermute(block, 'seq', route)]
    ppermute x6, starting transfers between devices: 5.21 us -> 3.64 us  [swapped(): lax.ppermute(block, 'kvh', [(i, i ^ mask) for i in range(lax.axis_size('k...]
    pallas_call x2, Pallas kernels: 3.93 us -> 2.55 us  [gradients(): pl.pallas_call(functools.partial(grad_kernel, masks, parts, carried is No...]
    ppermute x6, waiting for transfers between devices: 1.78 us -> 2.61 us  [swapped(): lax.ppermute(block, 'kvh', [(i, i ^ mask) for i in range(lax.axis_size('k...]
    ppermute x3, waiting for transfers between devices: 1.4 us -> 2.08 us  [paired(): lax.ppermute(block, 'seq', [(i, i ^ 1) for i in range(lax.axis_size('seq'...]
    ppermute x3, starting transfers between devices: 6.37 us -> 5.81 us  [paired(): lax.ppermute(block, 'seq', [(i, i ^ 1) for i in range(lax.axis_size('seq'...]
  transfers between devices with their start and end apart: 13 -> 13, of which waited for: 8 -> 6; matrix products, arithmetic and copies ran while one was open for 0% -> 0% of each run, Pallas kernels for 9% -> 5%
where the time goes in v14:
time: 32 us; the launch traced here: 31.8 us
  starting transfers between devices  18.5 us (58%)
  waiting for transfers between devices  7.74 us (24%)
  Pallas kernels  4.9 us (15%)
  between operations  0.71 us (2%)
    ppermute x3, starting transfers between devices, paired(): lax.ppermute(block, 'seq', [(i, i ^ 1) for i in range(lax.axis_size('seq'...  5.81 us
    ppermute x3, starting transfers between devices, ringed(): return lax.ppermute(block, 'seq', route)  5.54 us
    ppermute x6, starting transfers between devices, swapped(): lax.ppermute(block, 'kvh', [(i, i ^ mask) for i in range(lax.axis_size('k...  3.64 us
    ppermute x1, starting transfers between devices, shifted(): return lax.ppermute(block, 'seq', route)  3.48 us
    ppermute x3, waiting for transfers between devices, ringed(): return lax.ppermute(block, 'seq', route)  3.05 us
    ppermute x6, waiting for transfers between devices, swapped(): lax.ppermute(block, 'kvh', [(i, i ^ mask) for i in range(lax.axis_size('k...  2.61 us
    pallas_call x2, Pallas kernels, gradients(): pl.pallas_call(functools.partial(grad_kernel, masks, parts, carried is No...  2.55 us
    ppermute x3, waiting for transfers between devices, paired(): lax.ppermute(block, 'seq', [(i, i ^ 1) for i in range(lax.axis_size('seq'...  2.08 us
  transfers between devices with their start and end apart: 13, of which 6 were waited for; matrix products, arithmetic and copies ran while one was open for 0% of the time, Pallas kernels for 5%

profile of v14, /device:TPU:0, one launch (start us, length us, event | category | flops | bytes accessed | tf_op | source)
XLA Modules:
  0.0 31.8 jit_solution(14583944249358780042)
XLA Ops:
  0.6 0.0 copy-start
  0.6 1.3 %prepare.1 = (bf16[2,2,128,128]{3,2,1,0:T(8,128)(2,1)S(1)}, bf16[2,2,128,128]{3,2,1,0:T(8,128)(2,1)S(1)}, bf16[2,2,128,128]{3,2,1,0:T(8,128)(2,1)S(1)}, bf16[32,...) custom-call(s32[8]{0:T(128)} %lengths_ref.1, ...), custom_call_target="tpu_custom_call" | custom-call | tf_op jit(solution)/shard_map/prepare/pallas_call | solution.py:90
  1.9 3.0 %collective-permute-start = (bf16[2,2,128,128]{3,2,1,0:T(8,128)(2,1)S(1)}, bf16[2,2,128,128]{3,2,1,0:T(8,128)(2,1)S(1)}, u32[]{:S(2)}, u32[]{:S(2)}) collective-permute-start(bf16[2,2,128,128]{3,2,1,0:T(8,128)(2,1)S(1)} %get-tuple-element.23), channel_id=1, source_target_pairs={{0,4},{4,0},{8,12},{12,8},{16,20},{20,16},{24,28},{28,24},{1,5},{5... | collective-permute-start | bytes 393224 | tf_op jit(solution)/shard_map/ppermute | solution.py:368
  4.9 3.5 %collective-permute-start.1 = (bf16[2,2,128,128]{3,2,1,0:T(8,128)(2,1)S(1)}, bf16[2,2,128,128]{3,2,1,0:T(8,128)(2,1)S(1)}, u32[]{:S(2)}, u32[]{:S(2)}) collective-permute-start(bf16[2,2,128,128]{3,2,1,0:T(8,128)(2,1)S(1)} %get-tuple-element.24), channel_id=1, source_target_pairs={{0,8},{4,12},{8,16},{12,20},{16,24},{20,28},{1,9},{5,13},{9,17},{1... | collective-permute-start | bytes 393224 | tf_op jit(solution)/shard_map/ppermute | solution.py:364
  8.4 0.1 collective-permute-start.3
  8.5 1.6 %collective-permute-start.4 = (bf16[32,16,128]{2,1,0:T(8,128)(2,1)S(1)}, bf16[32,16,128]{2,1,0:T(8,128)(2,1)S(1)}, u32[]{:S(2)}, u32[]{:S(2)}) collective-permute-start(bf16[32,16,128]{2,1,0:T(8,128)(2,1)S(1)} %get-tuple-element.27), channel_id=1, source_target_pairs={{0,3},{1,2},{2,1},{3,0},{4,7},{5,6},{6,5},{7,4},{8,11},{9,10},{10,... | collective-permute-start | bytes 393224 | tf_op jit(solution)/shard_map/ppermute | solution.py:381
  10.1 0.0 collective-permute-done.refs_1_
  10.2 1.6 %collective-permute-start.2 = (bf16[2,2,128,128]{3,2,1,0:T(8,128)(2,1)S(1)}, bf16[2,2,128,128]{3,2,1,0:T(8,128)(2,1)S(1)}, u32[]{:S(2)}, u32[]{:S(2)}) collective-permute-start(bf16[2,2,128,128]{3,2,1,0:T(8,128)(2,1)S(1)} %collective-permute-done.refs_1_), channel_id=1, source_target_pairs={{0,8},{4,0},{8,16},{12,4},{16,24},{20,12},{24,28},{28,20},{1,9},{5... | collective-permute-start | bytes 393224 | tf_op jit(solution)/shard_map/ppermute | solution.py:377
  11.7 0.5 %collective-permute-start.6 = (bf16[32,16,128]{2,1,0:T(8,128)(2,1)S(1)}, bf16[32,16,128]{2,1,0:T(8,128)(2,1)S(1)}, u32[]{:S(2)}, u32[]{:S(2)}) collective-permute-start(bf16[32,16,128]{2,1,0:T(8,128)(2,1)S(1)} %get-tuple-element.29), channel_id=1, source_target_pairs={{0,2},{1,3},{2,0},{3,1},{4,6},{5,7},{6,4},{7,5},{8,10},{9,11},{10,... | collective-permute-start | bytes 393224 | tf_op jit(solution)/shard_map/ppermute | solution.py:381
  12.2 0.0 collective-permute-done.1.refs_2_
  12.2 0.0 collective-permute-done.3.refs_5_
  12.2 1.7 %collective-permute-done.4.refs_6_ = bf16[32,16,128]{2,1,0:T(8,128)(2,1)S(1)} collective-permute-done((bf16[32,16,128]{2,1,0:T(8,128)(2,1)S(1)}, bf16[32,16,128]{2,1,0:T(8,128)(2,1)S(1)}, u32[]{:S(2)}, u32[]{:S(2)}) %collective-permute-start.4) | collective-permute-done | bytes 131104 | tf_op jit(solution)/shard_map/ppermute | solution.py:381
  14.0 1.6 %collective-permute-done.2.refs_3_ = bf16[2,2,128,128]{3,2,1,0:T(8,128)(2,1)S(1)} collective-permute-done((bf16[2,2,128,128]{3,2,1,0:T(8,128)(2,1)S(1)}, bf16[2,2,128,128]{3,2,1,0:T(8,128)(2,1)S(1)}, u32[]{:S(2)}, u32[]{:S(2)}) %collective-permute-start.2) | collective-permute-done | bytes 131104 | tf_op jit(solution)/shard_map/ppermute | solution.py:377
  15.6 0.0 copy-done
  15.6 1.6 %gradients.2 = (bf16[32,16,128]{2,1,0:T(8,128)(2,1)S(1)}, bf16[32,16,128]{2,1,0:T(8,128)(2,1)S(1)}, bf16[32,16,128]{2,1,0:T(8,128)(2,1)S(1)}, f32[2,2,512,128]{3,2,1,0:T(8,128)S(1)}) custom-call(s32[4,2,256]{2,1,0:T(2,128)S(1)} %get-tuple-element.21.range_ref, bf16[128,16,128]{2,1,0:T(8,128)(2,1)S(1)} %copy-done, ...), custom_call_target="tpu_custom_call" | custom-call | flops 1006632960 | bytes 2097152 | tf_op jit(solution)/shard_map/gradients/pallas_call | solution.py:280
  17.3 0.0 collective-permute-done.6.refs_4_
  17.3 0.9 %gradients.3 = (bf16[32,16,128]{2,1,0:T(8,128)(2,1)S(1)}, f32[2,2,128,128]{3,2,1,0:T(8,128)S(1)}, bf16[2,2,128,128]{3,2,1,0:T(8,128)(2,1)S(1)}, bf16[2,2,128,128...) custom-call(s32[4,2,256]{2,1,0:T(2,128)S(1)} %get-tuple-element.21.range_ref, ...), custom_call_target="tpu_custom_call" | custom-call | flops 335544320 | bytes 2097152 | tf_op jit(solution)/shard_map/gradients/pallas_call | solution.py:280
  18.2 1.3 %collective-permute-start.7 = (bf16[2,2,128,128]{3,2,1,0:T(8,128)(2,1)S(1)}, bf16[2,2,128,128]{3,2,1,0:T(8,128)(2,1)S(1)}, u32[]{:S(2)}, u32[]{:S(2)}) collective-permute-start(bf16[2,2,128,128]{3,2,1,0:T(8,128)(2,1)S(1)} %get-tuple-element.31), channel_id=1, source_target_pairs={{0,4},{4,0},{8,12},{12,8},{16,20},{20,16},{24,28},{28,24},{1,5},{5... | collective-permute-start | bytes 393224 | tf_op jit(solution)/shard_map/ppermute | solution.py:368
  19.5 0.0 collective-permute-start.5
  19.5 0.8 %collective-permute-start.12 = (bf16[32,16,128]{2,1,0:T(8,128)(2,1)S(1)}, bf16[32,16,128]{2,1,0:T(8,128)(2,1)S(1)}, u32[]{:S(2)}, u32[]{:S(2)}) collective-permute-start(bf16[32,16,128]{2,1,0:T(8,128)(2,1)S(1)} %get-tuple-element.36), channel_id=1, source_target_pairs={{0,3},{1,2},{2,1},{3,0},{4,7},{5,6},{6,5},{7,4},{8,11},{9,10},{10,... | collective-permute-start | bytes 393224 | tf_op jit(solution)/shard_map/ppermute | solution.py:381
  20.3 1.5 %collective-permute-start.9 = (bf16[2,2,128,128]{3,2,1,0:T(8,128)(2,1)S(1)}, bf16[2,2,128,128]{3,2,1,0:T(8,128)(2,1)S(1)}, u32[]{:S(2)}, u32[]{:S(2)}) collective-permute-start(bf16[2,2,128,128]{3,2,1,0:T(8,128)(2,1)S(1)} %get-tuple-element.33), channel_id=1, source_target_pairs={{8,0},{0,4},{16,8},{4,12},{24,16},{12,20},{28,24},{20,28},{9,1},{1... | collective-permute-start | bytes 393224 | tf_op jit(solution)/shard_map/ppermute | solution.py:377
  21.8 0.6 %collective-permute-start.10 = (bf16[32,16,128]{2,1,0:T(8,128)(2,1)S(1)}, bf16[32,16,128]{2,1,0:T(8,128)(2,1)S(1)}, u32[]{:S(2)}, u32[]{:S(2)}) collective-permute-start(bf16[32,16,128]{2,1,0:T(8,128)(2,1)S(1)} %get-tuple-element.34), channel_id=1, source_target_pairs={{0,2},{1,3},{2,0},{3,1},{4,6},{5,7},{6,4},{7,5},{8,10},{9,11},{10,... | collective-permute-start | bytes 393224 | tf_op jit(solution)/shard_map/ppermute | solution.py:381
  22.4 0.8 %collective-permute-done.7.left = bf16[2,2,128,128]{3,2,1,0:T(8,128)(2,1)S(1)} collective-permute-done((bf16[2,2,128,128]{3,2,1,0:T(8,128)(2,1)S(1)}, bf16[2,2,128,128]{3,2,1,0:T(8,128)(2,1)S(1)}, u32[]{:S(2)}, u32[]{:S(2)}) %collective-permute-start.7) | collective-permute-done | bytes 131104 | tf_op jit(solution)/shard_map/ppermute | solution.py:368
  23.2 1.5 %collective-permute-start.11 = (bf16[2,2,128,128]{3,2,1,0:T(8,128)(2,1)S(1)}, bf16[2,2,128,128]{3,2,1,0:T(8,128)(2,1)S(1)}, u32[]{:S(2)}, u32[]{:S(2)}) collective-permute-start(bf16[2,2,128,128]{3,2,1,0:T(8,128)(2,1)S(1)} %get-tuple-element.35), channel_id=1, source_target_pairs={{0,4},{4,0},{8,12},{12,8},{16,20},{20,16},{24,28},{28,24},{1,5},{5... | collective-permute-start | bytes 393224 | tf_op jit(solution)/shard_map/ppermute | solution.py:368
  24.8 0.0 collective-permute-done.5.refs_0_
  24.8 2.5 %collective-permute-start.8 = (bf16[2,2,128,128]{3,2,1,0:T(8,128)(2,1)S(1)}, bf16[2,2,128,128]{3,2,1,0:T(8,128)(2,1)S(1)}, u32[]{:S(2)}, u32[]{:S(2)}) collective-permute-start(bf16[2,2,128,128]{3,2,1,0:T(8,128)(2,1)S(1)} %add.1), channel_id=1, source_target_pairs={{0,8},{4,0},{8,16},{12,4},{16,24},{20,12},{24,28},{28,20},{1,9},{5... | collective-permute-start | bytes 393224 | tf_op jit(solution)/shard_map/ppermute | solution.py:377
  27.2 0.0 collective-permute-done.12.refs_5_
  27.3 0.0 collective-permute-done.9.refs_2_
  27.3 0.9 %collective-permute-done.10.refs_3_ = bf16[32,16,128]{2,1,0:T(8,128)(2,1)S(1)} collective-permute-done((bf16[32,16,128]{2,1,0:T(8,128)(2,1)S(1)}, bf16[32,16,128]{2,1,0:T(8,128)(2,1)S(1)}, u32[]{:S(2)}, u32[]{:S(2)}) %collective-permute-start.10) | collective-permute-done | bytes 131104 | tf_op jit(solution)/shard_map/ppermute | solution.py:381
  28.1 1.3 %collective-permute-done.11.refs_4_ = bf16[2,2,128,128]{3,2,1,0:T(8,128)(2,1)S(1)} collective-permute-done((bf16[2,2,128,128]{3,2,1,0:T(8,128)(2,1)S(1)}, bf16[2,2,128,128]{3,2,1,0:T(8,128)(2,1)S(1)}, u32[]{:S(2)}, u32[]{:S(2)}) %collective-permute-start.11) | collective-permute-done | bytes 131104 | tf_op jit(solution)/shard_map/ppermute | solution.py:368
  29.4 1.4 %collective-permute-done.8.refs_1_ = bf16[2,2,128,128]{3,2,1,0:T(8,128)(2,1)S(1)} collective-permute-done((bf16[2,2,128,128]{3,2,1,0:T(8,128)(2,1)S(1)}, bf16[2,2,128,128]{3,2,1,0:T(8,128)(2,1)S(1)}, u32[]{:S(2)}, u32[]{:S(2)}) %collective-permute-start.8) | collective-permute-done | bytes 131104 | tf_op jit(solution)/shard_map/ppermute | solution.py:377
  30.8 1.0 %finish.1 = (bf16[32,64,128]{2,1,0:T(8,128)(2,1)}, bf16[128,2,128]{2,1,0:T(2,128)(2,1)}, bf16[128,2,128]{2,1,0:T(2,128)(2,1)}) custom-call(bf16[32,16,128]{2,1,0:T(8,128)(2,1)S(1)} %collective-permute-done.5.refs_0_, bf16[2,2,128,128]{3,2,1,0:T(8,128)(2,1)S(1)} %collective-permute-done.8.refs_1_, ...), custom_call_target="tpu_custom_call" | custom-call | tf_op jit(solution)/shard_map/finish/pallas_call | solution.py:347
  (1 shorter events, 0.0 us)
Async XLA Ops:
  0.6 15.0 %copy-start = (bf16[128,16,128]{2,1,0:T(8,128)(2,1)S(1)}, bf16[128,16,128]{2,1,0:T(8,128)(2,1)}, u32[]{:S(2)}) copy-start(bf16[128,16,128]{2,1,0:T(8,128)(2,1)} %q_ref.3) | copy-start | bytes 1572868
  1.9 8.2 %collective-permute-start = (bf16[2,2,128,128]{3,2,1,0:T(8,128)(2,1)S(1)}, bf16[2,2,128,128]{3,2,1,0:T(8,128)(2,1)S(1)}, u32[]{:S(2)}, u32[]{:S(2)}) collective-permute-start(bf16[2,2,128,128]{3,2,1,0:T(8,128)(2,1)S(1)} %get-tuple-element.23), channel_id=1, source_target_pairs={{0,4},{4,0},{8,12},{12,8},{16,20},{20,16},{24,28},{28,24},{1,5},{5... | collective-permute-start | bytes 393224 | tf_op jit(solution)/shard_map/ppermute | solution.py:368
  4.9 7.3 %collective-permute-start.1 = (bf16[2,2,128,128]{3,2,1,0:T(8,128)(2,1)S(1)}, bf16[2,2,128,128]{3,2,1,0:T(8,128)(2,1)S(1)}, u32[]{:S(2)}, u32[]{:S(2)}) collective-permute-start(bf16[2,2,128,128]{3,2,1,0:T(8,128)(2,1)S(1)} %get-tuple-element.24), channel_id=1, source_target_pairs={{0,8},{4,12},{8,16},{12,20},{16,24},{20,28},{1,9},{5,13},{9,17},{1... | collective-permute-start | bytes 393224 | tf_op jit(solution)/shard_map/ppermute | solution.py:364
  8.4 3.8 %collective-permute-start.3 = (bf16[32,16,128]{2,1,0:T(8,128)(2,1)S(1)}, bf16[32,16,128]{2,1,0:T(8,128)(2,1)S(1)}, u32[]{:S(2)}, u32[]{:S(2)}) collective-permute-start(bf16[32,16,128]{2,1,0:T(8,128)(2,1)S(1)} %get-tuple-element.26), channel_id=1, source_target_pairs={{0,1},{1,0},{2,3},{3,2},{4,5},{5,4},{6,7},{7,6},{8,9},{9,8},{10,11... | collective-permute-start | bytes 393224 | tf_op jit(solution)/shard_map/ppermute | solution.py:381
  8.5 5.5 %collective-permute-start.4 = (bf16[32,16,128]{2,1,0:T(8,128)(2,1)S(1)}, bf16[32,16,128]{2,1,0:T(8,128)(2,1)S(1)}, u32[]{:S(2)}, u32[]{:S(2)}) collective-permute-start(bf16[32,16,128]{2,1,0:T(8,128)(2,1)S(1)} %get-tuple-element.27), channel_id=1, source_target_pairs={{0,3},{1,2},{2,1},{3,0},{4,7},{5,6},{6,5},{7,4},{8,11},{9,10},{10,... | collective-permute-start | bytes 393224 | tf_op jit(solution)/shard_map/ppermute | solution.py:381
  10.2 5.5 %collective-permute-start.2 = (bf16[2,2,128,128]{3,2,1,0:T(8,128)(2,1)S(1)}, bf16[2,2,128,128]{3,2,1,0:T(8,128)(2,1)S(1)}, u32[]{:S(2)}, u32[]{:S(2)}) collective-permute-start(bf16[2,2,128,128]{3,2,1,0:T(8,128)(2,1)S(1)} %collective-permute-done.refs_1_), channel_id=1, source_target_pairs={{0,8},{4,0},{8,16},{12,4},{16,24},{20,12},{24,28},{28,20},{1,9},{5... | collective-permute-start | bytes 393224 | tf_op jit(solution)/shard_map/ppermute | solution.py:377
  11.7 5.5 %collective-permute-start.6 = (bf16[32,16,128]{2,1,0:T(8,128)(2,1)S(1)}, bf16[32,16,128]{2,1,0:T(8,128)(2,1)S(1)}, u32[]{:S(2)}, u32[]{:S(2)}) collective-permute-start(bf16[32,16,128]{2,1,0:T(8,128)(2,1)S(1)} %get-tuple-element.29), channel_id=1, source_target_pairs={{0,2},{1,3},{2,0},{3,1},{4,6},{5,7},{6,4},{7,5},{8,10},{9,11},{10,... | collective-permute-start | bytes 393224 | tf_op jit(solution)/shard_map/ppermute | solution.py:381
  18.2 5.0 %collective-permute-start.7 = (bf16[2,2,128,128]{3,2,1,0:T(8,128)(2,1)S(1)}, bf16[2,2,128,128]{3,2,1,0:T(8,128)(2,1)S(1)}, u32[]{:S(2)}, u32[]{:S(2)}) collective-permute-start(bf16[2,2,128,128]{3,2,1,0:T(8,128)(2,1)S(1)} %get-tuple-element.31), channel_id=1, source_target_pairs={{0,4},{4,0},{8,12},{12,8},{16,20},{20,16},{24,28},{28,24},{1,5},{5... | collective-permute-start | bytes 393224 | tf_op jit(solution)/shard_map/ppermute | solution.py:368
  19.5 5.3 %collective-permute-start.5 = (bf16[32,16,128]{2,1,0:T(8,128)(2,1)S(1)}, bf16[32,16,128]{2,1,0:T(8,128)(2,1)S(1)}, u32[]{:S(2)}, u32[]{:S(2)}) collective-permute-start(bf16[32,16,128]{2,1,0:T(8,128)(2,1)S(1)} %get-tuple-element.28), channel_id=1, source_target_pairs={{0,1},{1,0},{2,3},{3,2},{4,5},{5,4},{6,7},{7,6},{8,9},{9,8},{10,11... | collective-permute-start | bytes 393224 | tf_op jit(solution)/shard_map/ppermute | solution.py:381
  19.5 7.7 %collective-permute-start.12 = (bf16[32,16,128]{2,1,0:T(8,128)(2,1)S(1)}, bf16[32,16,128]{2,1,0:T(8,128)(2,1)S(1)}, u32[]{:S(2)}, u32[]{:S(2)}) collective-permute-start(bf16[32,16,128]{2,1,0:T(8,128)(2,1)S(1)} %get-tuple-element.36), channel_id=1, source_target_pairs={{0,3},{1,2},{2,1},{3,0},{4,7},{5,6},{6,5},{7,4},{8,11},{9,10},{10,... | collective-permute-start | bytes 393224 | tf_op jit(solution)/shard_map/ppermute | solution.py:381
  20.3 6.9 %collective-permute-start.9 = (bf16[2,2,128,128]{3,2,1,0:T(8,128)(2,1)S(1)}, bf16[2,2,128,128]{3,2,1,0:T(8,128)(2,1)S(1)}, u32[]{:S(2)}, u32[]{:S(2)}) collective-permute-start(bf16[2,2,128,128]{3,2,1,0:T(8,128)(2,1)S(1)} %get-tuple-element.33), channel_id=1, source_target_pairs={{8,0},{0,4},{16,8},{4,12},{24,16},{12,20},{28,24},{20,28},{9,1},{1... | collective-permute-start | bytes 393224 | tf_op jit(solution)/shard_map/ppermute | solution.py:377
  21.8 6.3 %collective-permute-start.10 = (bf16[32,16,128]{2,1,0:T(8,128)(2,1)S(1)}, bf16[32,16,128]{2,1,0:T(8,128)(2,1)S(1)}, u32[]{:S(2)}, u32[]{:S(2)}) collective-permute-start(bf16[32,16,128]{2,1,0:T(8,128)(2,1)S(1)} %get-tuple-element.34), channel_id=1, source_target_pairs={{0,2},{1,3},{2,0},{3,1},{4,6},{5,7},{6,4},{7,5},{8,10},{9,11},{10,... | collective-permute-start | bytes 393224 | tf_op jit(solution)/shard_map/ppermute | solution.py:381
  23.2 6.2 %collective-permute-start.11 = (bf16[2,2,128,128]{3,2,1,0:T(8,128)(2,1)S(1)}, bf16[2,2,128,128]{3,2,1,0:T(8,128)(2,1)S(1)}, u32[]{:S(2)}, u32[]{:S(2)}) collective-permute-start(bf16[2,2,128,128]{3,2,1,0:T(8,128)(2,1)S(1)} %get-tuple-element.35), channel_id=1, source_target_pairs={{0,4},{4,0},{8,12},{12,8},{16,20},{20,16},{24,28},{28,24},{1,5},{5... | collective-permute-start | bytes 393224 | tf_op jit(solution)/shard_map/ppermute | solution.py:368
  24.8 6.0 %collective-permute-start.8 = (bf16[2,2,128,128]{3,2,1,0:T(8,128)(2,1)S(1)}, bf16[2,2,128,128]{3,2,1,0:T(8,128)(2,1)S(1)}, u32[]{:S(2)}, u32[]{:S(2)}) collective-permute-start(bf16[2,2,128,128]{3,2,1,0:T(8,128)(2,1)S(1)} %add.1), channel_id=1, source_target_pairs={{0,8},{4,0},{8,16},{12,4},{16,24},{20,12},{24,28},{28,20},{1,9},{5... | collective-permute-start | bytes 393224 | tf_op jit(solution)/shard_map/ppermute | solution.py:377

commit v15 on v14

--- a/solution.py
+++ b/solution.py
@@ -14,7 +14,7 @@
 NEG = -1e30
 TILE = 8
 ALIGN = 16
-WIDTHS = (160, 288)
+WIDTHS = (176, 304)
 
 _VMEM = pl.BlockSpec(memory_space=pltpu.VMEM)
 _SMEM = pl.BlockSpec(memory_space=pltpu.SMEM)
@@ -32,7 +32,7 @@
 
 
 def prep_kernel(parts, lengths_ref, prefixes_ref, cot_ref, key_ref, value_ref, *rest):
-    kv_outs, cot_outs, rest = rest[:3], rest[3 : parts + 3], rest[parts + 3 :]
+    kv_outs, cot_outs, rest = rest[:2], rest[2 : parts + 2], rest[parts + 2 :]
     range_out, key_buf, value_buf, lengths, prefixes, sems, scalar_sems = rest
     heads = cot_ref.shape[1] // parts
     me = lax.axis_index("kvh")
@@ -89,9 +89,9 @@
     ]
     outs = pl.pallas_call(
         functools.partial(prep_kernel, parts),
-        out_shape=(block,) * 3 + (piece,) * parts + (pltpu.VMEM((parts, 2, lanes), jnp.int32),),
+        out_shape=(block,) * 2 + (piece,) * parts + (pltpu.VMEM((parts, 2, lanes), jnp.int32),),
         in_specs=[_HBM] * 5,
-        out_specs=(_VMEM,) * (parts + 4),
+        out_specs=(_VMEM,) * (parts + 3),
         scratch_shapes=[
             pltpu.VMEM(keys.shape, jnp.bfloat16),
             pltpu.VMEM(values.shape, jnp.bfloat16),
@@ -103,7 +103,25 @@
         compiler_params=pltpu.CompilerParams(vmem_limit_bytes=VMEM_BYTES),
         name="prepare",
     )(*operands)
-    return outs[:3], outs[3:-1], outs[-1]
+    return outs[:2], outs[2:-1], outs[-1]
+
+
+def pack_kernel(key_ref, value_ref, out):
+    for number, ref in enumerate((key_ref, value_ref)):
+        for group, block in enumerate(regroup(ref)):
+            out[number, group] = block
+
+
+def pack(keys, values):
+    kv_rows, kv_heads, size = keys.shape
+    return pl.pallas_call(
+        pack_kernel,
+        out_shape=pltpu.VMEM((2, kv_heads, kv_rows, size), jnp.bfloat16),
+        in_specs=[_VMEM] * 2,
+        out_specs=_VMEM,
+        compiler_params=pltpu.CompilerParams(vmem_limit_bytes=VMEM_BYTES),
+        name="pack",
+    )(keys, values)
 
 
 def bounds(position, lengths, prefixes):
@@ -359,9 +377,8 @@
 
 
 def shifted(block, distance):
-    devices = range(lax.axis_size("seq"))
-    route = [(i, i + distance) for i in devices if i + distance in devices]
-    return lax.ppermute(block, "seq", route)
+    count = lax.axis_size("seq")
+    return lax.ppermute(block, "seq", [(i, (i + distance) % count) for i in range(count)])
 
 
 def paired(block):
@@ -386,7 +403,7 @@
     kv, cots, ranges = prepare(
         doc_lengths, prefix_lengths, output_gradient, keys, values, parts
     )
-    even = paired(kv[2])
+    even = pack(paired(keys), paired(values))
     blocks = [kv[0], shifted(kv[1], BACK), even, ringed(even)]
     cots = [cots[0]] + [swapped(cots[mask], mask) for mask in range(1, parts)]
     dqs, carried = {}, [None]

time: 32 us -> 33.1 us (1.034); the launches traced: 31.8 us -> 33.5 us
  waiting for transfers between devices: 7.74 us -> 10.9 us
  starting transfers between devices: 18.5 us -> 16.7 us
    ppermute x3, starting transfers between devices: 5.54 us -> 1.78 us  [ringed(): return lax.ppermute(block, 'seq', route)]
    ppermute x3, waiting for transfers between devices: 3.05 us -> 5.12 us  [ringed(): return lax.ppermute(block, 'seq', route)]
    ppermute x3 -> x4, starting transfers between devices: 5.81 us -> 7.86 us  [paired(): lax.ppermute(block, 'seq', [(i, i ^ 1) for i in range(lax.axis_size('seq'...]
    ppermute x1, starting transfers between devices: 3.48 us -> 2.09 us  [shifted(): lax.ppermute(block, 'seq', [(i, (i + distance) % count) for i in range(co...]
    ppermute x6, starting transfers between devices: 3.64 us -> 5 us  [swapped(): lax.ppermute(block, 'kvh', [(i, i ^ mask) for i in range(lax.axis_size('k...]
    ppermute x3 -> x4, waiting for transfers between devices: 2.08 us -> 3.24 us  [paired(): lax.ppermute(block, 'seq', [(i, i ^ 1) for i in range(lax.axis_size('seq'...]
    ppermute x6, waiting for transfers between devices: 2.61 us -> 1.97 us  [swapped(): lax.ppermute(block, 'kvh', [(i, i ^ mask) for i in range(lax.axis_size('k...]
    ppermute x1, waiting for transfers between devices: 0.01 us -> 0.54 us  [shifted(): lax.ppermute(block, 'seq', [(i, (i + distance) % count) for i in range(co...]
  transfers between devices with their start and end apart: 13 -> 14, of which waited for: 6 -> 8; matrix products, arithmetic and copies ran while one was open for 0% -> 0% of each run, Pallas kernels for 5% -> 10%
where the time goes in v15:
time: 33.1 us; the launch traced here: 33.5 us
  starting transfers between devices  16.7 us (50%)
  waiting for transfers between devices  10.9 us (33%)
  Pallas kernels  5.19 us (16%)
  between operations  0.72 us (2%)
    ppermute x4, starting transfers between devices, paired(): lax.ppermute(block, 'seq', [(i, i ^ 1) for i in range(lax.axis_size('seq'...  7.86 us
    ppermute x3, waiting for transfers between devices, ringed(): return lax.ppermute(block, 'seq', route)  5.12 us
    ppermute x6, starting transfers between devices, swapped(): lax.ppermute(block, 'kvh', [(i, i ^ mask) for i in range(lax.axis_size('k...  5 us
    ppermute x4, waiting for transfers between devices, paired(): lax.ppermute(block, 'seq', [(i, i ^ 1) for i in range(lax.axis_size('seq'...  3.24 us
    pallas_call x2, Pallas kernels, gradients(): pl.pallas_call(functools.partial(grad_kernel, masks, parts, carried is No...  2.67 us
    ppermute x1, starting transfers between devices, shifted(): lax.ppermute(block, 'seq', [(i, (i + distance) % count) for i in range(co...  2.09 us
    ppermute x6, waiting for transfers between devices, swapped(): lax.ppermute(block, 'kvh', [(i, i ^ mask) for i in range(lax.axis_size('k...  1.97 us
    ppermute x3, starting transfers between devices, ringed(): return lax.ppermute(block, 'seq', route)  1.78 us
  transfers between devices with their start and end apart: 14, of which 8 were waited for; matrix products, arithmetic and copies ran while one was open for 0% of the time, Pallas kernels for 10%

profile of v15, /device:TPU:0, one launch (start us, length us, event | category | flops | bytes accessed | tf_op | source)
XLA Modules:
  0.0 33.5 jit_solution(18107156927905728348)
XLA Ops:
  0.6 0.0 copy-start
  0.6 3.0 %collective-permute-start = (bf16[128,2,128]{2,1,0:T(2,128)(2,1)}, bf16[128,2,128]{2,1,0:T(2,128)(2,1)S(1)}, u32[]{:S(2)}, u32[]{:S(2)}) collective-permute-start(bf16[128,2,128]{2,1,0:T(2,128)(2,1)} %key_ref.1), channel_id=1, source_target_pairs={{0,4},{4,0},{8,12},{12,8},{16,20},{20,16},{24,28},{28,24},{1,5},{5... | collective-permute-start | bytes 196616 | tf_op jit(solution)/shard_map/ppermute | solution.py:385
  3.6 0.1 collective-permute-start.1
  3.7 1.2 %prepare.1 = (bf16[2,2,128,128]{3,2,1,0:T(8,128)(2,1)S(1)}, bf16[2,2,128,128]{3,2,1,0:T(8,128)(2,1)S(1)}, bf16[32,16,128]{2,1,0:T(8,128)(2,1)S(1)}, bf16[32,16,1...) custom-call(s32[8]{0:T(128)} %lengths_ref.1, ...), custom_call_target="tpu_custom_call" | custom-call | tf_op jit(solution)/shard_map/prepare/pallas_call | solution.py:90
  5.0 2.1 %collective-permute-start.2 = (bf16[2,2,128,128]{3,2,1,0:T(8,128)(2,1)S(1)}, bf16[2,2,128,128]{3,2,1,0:T(8,128)(2,1)S(1)}, u32[]{:S(2)}, u32[]{:S(2)}) collective-permute-start(bf16[2,2,128,128]{3,2,1,0:T(8,128)(2,1)S(1)} %get-tuple-element.22), channel_id=1, source_target_pairs={{0,8},{4,12},{8,16},{12,20},{16,24},{20,28},{24,0},{28,4},{1,9},{5... | collective-permute-start | bytes 393224 | tf_op jit(solution)/shard_map/ppermute | solution.py:381
  7.1 0.0 collective-permute-start.4
  7.1 1.6 %collective-permute-start.5 = (bf16[32,16,128]{2,1,0:T(8,128)(2,1)S(1)}, bf16[32,16,128]{2,1,0:T(8,128)(2,1)S(1)}, u32[]{:S(2)}, u32[]{:S(2)}) collective-permute-start(bf16[32,16,128]{2,1,0:T(8,128)(2,1)S(1)} %get-tuple-element.25), channel_id=1, source_target_pairs={{0,3},{1,2},{2,1},{3,0},{4,7},{5,6},{6,5},{7,4},{8,11},{9,10},{10,... | collective-permute-start | bytes 393224 | tf_op jit(solution)/shard_map/ppermute | solution.py:398
  8.7 0.0 collective-permute-done.key_ref
  8.7 0.0 collective-permute-done.1.value_ref
  8.7 0.2 pack.1.refs_1_
  8.9 1.6 %collective-permute-start.3 = (bf16[2,2,128,128]{3,2,1,0:T(8,128)(2,1)S(1)}, bf16[2,2,128,128]{3,2,1,0:T(8,128)(2,1)S(1)}, u32[]{:S(2)}, u32[]{:S(2)}) collective-permute-start(bf16[2,2,128,128]{3,2,1,0:T(8,128)(2,1)S(1)} %pack.1.refs_1_), channel_id=1, source_target_pairs={{0,8},{4,0},{8,16},{12,4},{16,24},{20,12},{24,28},{28,20},{1,9},{5... | collective-permute-start | bytes 393224 | tf_op jit(solution)/shard_map/ppermute | solution.py:394
  10.6 0.9 %collective-permute-start.7 = (bf16[32,16,128]{2,1,0:T(8,128)(2,1)S(1)}, bf16[32,16,128]{2,1,0:T(8,128)(2,1)S(1)}, u32[]{:S(2)}, u32[]{:S(2)}) collective-permute-start(bf16[32,16,128]{2,1,0:T(8,128)(2,1)S(1)} %get-tuple-element.27), channel_id=1, source_target_pairs={{0,2},{1,3},{2,0},{3,1},{4,6},{5,7},{6,4},{7,5},{8,10},{9,11},{10,... | collective-permute-start | bytes 393224 | tf_op jit(solution)/shard_map/ppermute | solution.py:398
  11.5 0.5 %collective-permute-done.2.refs_2_ = bf16[2,2,128,128]{3,2,1,0:T(8,128)(2,1)S(1)} collective-permute-done((bf16[2,2,128,128]{3,2,1,0:T(8,128)(2,1)S(1)}, bf16[2,2,128,128]{3,2,1,0:T(8,128)(2,1)S(1)}, u32[]{:S(2)}, u32[]{:S(2)}) %collective-permute-start.2) | collective-permute-done | bytes 131104 | tf_op jit(solution)/shard_map/ppermute | solution.py:381
  12.0 0.0 collective-permute-done.4.refs_5_
  12.0 0.5 %collective-permute-done.5.refs_6_ = bf16[32,16,128]{2,1,0:T(8,128)(2,1)S(1)} collective-permute-done((bf16[32,16,128]{2,1,0:T(8,128)(2,1)S(1)}, bf16[32,16,128]{2,1,0:T(8,128)(2,1)S(1)}, u32[]{:S(2)}, u32[]{:S(2)}) %collective-permute-start.5) | collective-permute-done | bytes 131104 | tf_op jit(solution)/shard_map/ppermute | solution.py:398
  12.5 1.8 %collective-permute-done.3.refs_3_ = bf16[2,2,128,128]{3,2,1,0:T(8,128)(2,1)S(1)} collective-permute-done((bf16[2,2,128,128]{3,2,1,0:T(8,128)(2,1)S(1)}, bf16[2,2,128,128]{3,2,1,0:T(8,128)(2,1)S(1)}, u32[]{:S(2)}, u32[]{:S(2)}) %collective-permute-start.3) | collective-permute-done | bytes 131104 | tf_op jit(solution)/shard_map/ppermute | solution.py:394
  14.4 0.0 copy-done
  14.4 1.7 %gradients.2 = (bf16[32,16,128]{2,1,0:T(8,128)(2,1)S(1)}, bf16[32,16,128]{2,1,0:T(8,128)(2,1)S(1)}, bf16[32,16,128]{2,1,0:T(8,128)(2,1)S(1)}, f32[2,2,512,128]{3,2,1,0:T(8,128)S(1)}) custom-call(s32[4,2,256]{2,1,0:T(2,128)S(1)} %get-tuple-element.20.range_ref, bf16[128,16,128]{2,1,0:T(8,128)(2,1)S(1)} %copy-done, ...), custom_call_target="tpu_custom_call" | custom-call | flops 1006632960 | bytes 2097152 | tf_op jit(solution)/shard_map/gradients/pallas_call | solution.py:298
  16.1 0.0 collective-permute-done.7.refs_4_
  16.1 1.0 %gradients.3 = (bf16[32,16,128]{2,1,0:T(8,128)(2,1)S(1)}, f32[2,2,128,128]{3,2,1,0:T(8,128)S(1)}, bf16[2,2,128,128]{3,2,1,0:T(8,128)(2,1)S(1)}, bf16[2,2,128,128...) custom-call(s32[4,2,256]{2,1,0:T(2,128)S(1)} %get-tuple-element.20.range_ref, ...), custom_call_target="tpu_custom_call" | custom-call | flops 335544320 | bytes 2097152 | tf_op jit(solution)/shard_map/gradients/pallas_call | solution.py:298
  17.1 2.7 %collective-permute-start.8 = (bf16[2,2,128,128]{3,2,1,0:T(8,128)(2,1)S(1)}, bf16[2,2,128,128]{3,2,1,0:T(8,128)(2,1)S(1)}, u32[]{:S(2)}, u32[]{:S(2)}) collective-permute-start(bf16[2,2,128,128]{3,2,1,0:T(8,128)(2,1)S(1)} %get-tuple-element.29), channel_id=1, source_target_pairs={{0,4},{4,0},{8,12},{12,8},{16,20},{20,16},{24,28},{28,24},{1,5},{5... | collective-permute-start | bytes 393224 | tf_op jit(solution)/shard_map/ppermute | solution.py:385
  19.8 0.5 %collective-permute-start.6 = (bf16[32,16,128]{2,1,0:T(8,128)(2,1)S(1)}, bf16[32,16,128]{2,1,0:T(8,128)(2,1)S(1)}, u32[]{:S(2)}, u32[]{:S(2)}) collective-permute-start(bf16[32,16,128]{2,1,0:T(8,128)(2,1)S(1)} %get-tuple-element.26), channel_id=1, source_target_pairs={{0,1},{1,0},{2,3},{3,2},{4,5},{5,4},{6,7},{7,6},{8,9},{9,8},{10,11... | collective-permute-start | bytes 393224 | tf_op jit(solution)/shard_map/ppermute | solution.py:398
  20.3 1.9 %collective-permute-start.13 = (bf16[32,16,128]{2,1,0:T(8,128)(2,1)S(1)}, bf16[32,16,128]{2,1,0:T(8,128)(2,1)S(1)}, u32[]{:S(2)}, u32[]{:S(2)}) collective-permute-start(bf16[32,16,128]{2,1,0:T(8,128)(2,1)S(1)} %get-tuple-element.34), channel_id=1, source_target_pairs={{0,3},{1,2},{2,1},{3,0},{4,7},{5,6},{6,5},{7,4},{8,11},{9,10},{10,... | collective-permute-start | bytes 393224 | tf_op jit(solution)/shard_map/ppermute | solution.py:398
  22.2 0.1 collective-permute-start.10
  22.3 0.1 collective-permute-start.11
  22.3 1.8 %collective-permute-done.8.left = bf16[2,2,128,128]{3,2,1,0:T(8,128)(2,1)S(1)} collective-permute-done((bf16[2,2,128,128]{3,2,1,0:T(8,128)(2,1)S(1)}, bf16[2,2,128,128]{3,2,1,0:T(8,128)(2,1)S(1)}, u32[]{:S(2)}, u32[]{:S(2)}) %collective-permute-start.8) | collective-permute-done | bytes 131104 | tf_op jit(solution)/shard_map/ppermute | solution.py:385
  24.1 2.1 %collective-permute-start.12 = (bf16[2,2,128,128]{3,2,1,0:T(8,128)(2,1)S(1)}, bf16[2,2,128,128]{3,2,1,0:T(8,128)(2,1)S(1)}, u32[]{:S(2)}, u32[]{:S(2)}) collective-permute-start(bf16[2,2,128,128]{3,2,1,0:T(8,128)(2,1)S(1)} %get-tuple-element.33), channel_id=1, source_target_pairs={{0,4},{4,0},{8,12},{12,8},{16,20},{20,16},{24,28},{28,24},{1,5},{5... | collective-permute-start | bytes 393224 | tf_op jit(solution)/shard_map/ppermute | solution.py:385
  26.2 0.0 collective-permute-done.6.refs_0_
  26.2 0.1 collective-permute-start.9
  26.3 0.0 collective-permute-done.13.refs_5_
  26.3 1.3 %collective-permute-done.10.refs_2_ = bf16[2,2,128,128]{3,2,1,0:T(8,128)(2,1)S(1)} collective-permute-done((bf16[2,2,128,128]{3,2,1,0:T(8,128)(2,1)S(1)}, bf16[2,2,128,128]{3,2,1,0:T(8,128)(2,1)S(1)}, u32[]{:S(2)}, u32[]{:S(2)}) %collective-permute-start.10) | collective-permute-done | bytes 131104 | tf_op jit(solution)/shard_map/ppermute | solution.py:394
  27.6 1.5 %collective-permute-done.11.refs_3_ = bf16[32,16,128]{2,1,0:T(8,128)(2,1)S(1)} collective-permute-done((bf16[32,16,128]{2,1,0:T(8,128)(2,1)S(1)}, bf16[32,16,128]{2,1,0:T(8,128)(2,1)S(1)}, u32[]{:S(2)}, u32[]{:S(2)}) %collective-permute-start.11) | collective-permute-done | bytes 131104 | tf_op jit(solution)/shard_map/ppermute | solution.py:398
  29.0 1.5 %collective-permute-done.12.refs_4_ = bf16[2,2,128,128]{3,2,1,0:T(8,128)(2,1)S(1)} collective-permute-done((bf16[2,2,128,128]{3,2,1,0:T(8,128)(2,1)S(1)}, bf16[2,2,128,128]{3,2,1,0:T(8,128)(2,1)S(1)}, u32[]{:S(2)}, u32[]{:S(2)}) %collective-permute-start.12) | collective-permute-done | bytes 131104 | tf_op jit(solution)/shard_map/ppermute | solution.py:385
  30.5 2.0 %collective-permute-done.9.refs_1_ = bf16[2,2,128,128]{3,2,1,0:T(8,128)(2,1)S(1)} collective-permute-done((bf16[2,2,128,128]{3,2,1,0:T(8,128)(2,1)S(1)}, bf16[2,2,128,128]{3,2,1,0:T(8,128)(2,1)S(1)}, u32[]{:S(2)}, u32[]{:S(2)}) %collective-permute-start.9) | collective-permute-done | bytes 131104 | tf_op jit(solution)/shard_map/ppermute | solution.py:394
  32.5 1.0 %finish.1 = (bf16[32,64,128]{2,1,0:T(8,128)(2,1)}, bf16[128,2,128]{2,1,0:T(2,128)(2,1)}, bf16[128,2,128]{2,1,0:T(2,128)(2,1)}) custom-call(bf16[32,16,128]{2,1,0:T(8,128)(2,1)S(1)} %collective-permute-done.6.refs_0_, bf16[2,2,128,128]{3,2,1,0:T(8,128)(2,1)S(1)} %collective-permute-done.9.refs_1_, ...), custom_call_target="tpu_custom_call" | custom-call | tf_op jit(solution)/shard_map/finish/pallas_call | solution.py:365
  (1 shorter events, 0.0 us)
Async XLA Ops:
  0.6 13.8 %copy-start = (bf16[128,16,128]{2,1,0:T(8,128)(2,1)S(1)}, bf16[128,16,128]{2,1,0:T(8,128)(2,1)}, u32[]{:S(2)}) copy-start(bf16[128,16,128]{2,1,0:T(8,128)(2,1)} %q_ref.3) | copy-start | bytes 1572868
  0.6 8.1 %collective-permute-start = (bf16[128,2,128]{2,1,0:T(2,128)(2,1)}, bf16[128,2,128]{2,1,0:T(2,128)(2,1)S(1)}, u32[]{:S(2)}, u32[]{:S(2)}) collective-permute-start(bf16[128,2,128]{2,1,0:T(2,128)(2,1)} %key_ref.1), channel_id=1, source_target_pairs={{0,4},{4,0},{8,12},{12,8},{16,20},{20,16},{24,28},{28,24},{1,5},{5... | collective-permute-start | bytes 196616 | tf_op jit(solution)/shard_map/ppermute | solution.py:385
  3.6 5.1 %collective-permute-start.1 = (bf16[128,2,128]{2,1,0:T(2,128)(2,1)}, bf16[128,2,128]{2,1,0:T(2,128)(2,1)S(1)}, u32[]{:S(2)}, u32[]{:S(2)}) collective-permute-start(bf16[128,2,128]{2,1,0:T(2,128)(2,1)} %value_ref.1), channel_id=1, source_target_pairs={{0,4},{4,0},{8,12},{12,8},{16,20},{20,16},{24,28},{28,24},{1,5},{5... | collective-permute-start | bytes 196616 | tf_op jit(solution)/shard_map/ppermute | solution.py:385
  5.0 7.1 %collective-permute-start.2 = (bf16[2,2,128,128]{3,2,1,0:T(8,128)(2,1)S(1)}, bf16[2,2,128,128]{3,2,1,0:T(8,128)(2,1)S(1)}, u32[]{:S(2)}, u32[]{:S(2)}) collective-permute-start(bf16[2,2,128,128]{3,2,1,0:T(8,128)(2,1)S(1)} %get-tuple-element.22), channel_id=1, source_target_pairs={{0,8},{4,12},{8,16},{12,20},{16,24},{20,28},{24,0},{28,4},{1,9},{5... | collective-permute-start | bytes 393224 | tf_op jit(solution)/shard_map/ppermute | solution.py:381
  7.1 5.0 %collective-permute-start.4 = (bf16[32,16,128]{2,1,0:T(8,128)(2,1)S(1)}, bf16[32,16,128]{2,1,0:T(8,128)(2,1)S(1)}, u32[]{:S(2)}, u32[]{:S(2)}) collective-permute-start(bf16[32,16,128]{2,1,0:T(8,128)(2,1)S(1)} %get-tuple-element.24), channel_id=1, source_target_pairs={{0,1},{1,0},{2,3},{3,2},{4,5},{5,4},{6,7},{7,6},{8,9},{9,8},{10,11... | collective-permute-start | bytes 393224 | tf_op jit(solution)/shard_map/ppermute | solution.py:398
  7.1 5.5 %collective-permute-start.5 = (bf16[32,16,128]{2,1,0:T(8,128)(2,1)S(1)}, bf16[32,16,128]{2,1,0:T(8,128)(2,1)S(1)}, u32[]{:S(2)}, u32[]{:S(2)}) collective-permute-start(bf16[32,16,128]{2,1,0:T(8,128)(2,1)S(1)} %get-tuple-element.25), channel_id=1, source_target_pairs={{0,3},{1,2},{2,1},{3,0},{4,7},{5,6},{6,5},{7,4},{8,11},{9,10},{10,... | collective-permute-start | bytes 393224 | tf_op jit(solution)/shard_map/ppermute | solution.py:398
  8.9 5.5 %collective-permute-start.3 = (bf16[2,2,128,128]{3,2,1,0:T(8,128)(2,1)S(1)}, bf16[2,2,128,128]{3,2,1,0:T(8,128)(2,1)S(1)}, u32[]{:S(2)}, u32[]{:S(2)}) collective-permute-start(bf16[2,2,128,128]{3,2,1,0:T(8,128)(2,1)S(1)} %pack.1.refs_1_), channel_id=1, source_target_pairs={{0,8},{4,0},{8,16},{12,4},{16,24},{20,12},{24,28},{28,20},{1,9},{5... | collective-permute-start | bytes 393224 | tf_op jit(solution)/shard_map/ppermute | solution.py:394
  10.6 5.6 %collective-permute-start.7 = (bf16[32,16,128]{2,1,0:T(8,128)(2,1)S(1)}, bf16[32,16,128]{2,1,0:T(8,128)(2,1)S(1)}, u32[]{:S(2)}, u32[]{:S(2)}) collective-permute-start(bf16[32,16,128]{2,1,0:T(8,128)(2,1)S(1)} %get-tuple-element.27), channel_id=1, source_target_pairs={{0,2},{1,3},{2,0},{3,1},{4,6},{5,7},{6,4},{7,5},{8,10},{9,11},{10,... | collective-permute-start | bytes 393224 | tf_op jit(solution)/shard_map/ppermute | solution.py:398
  17.1 7.0 %collective-permute-start.8 = (bf16[2,2,128,128]{3,2,1,0:T(8,128)(2,1)S(1)}, bf16[2,2,128,128]{3,2,1,0:T(8,128)(2,1)S(1)}, u32[]{:S(2)}, u32[]{:S(2)}) collective-permute-start(bf16[2,2,128,128]{3,2,1,0:T(8,128)(2,1)S(1)} %get-tuple-element.29), channel_id=1, source_target_pairs={{0,4},{4,0},{8,12},{12,8},{16,20},{20,16},{24,28},{28,24},{1,5},{5... | collective-permute-start | bytes 393224 | tf_op jit(solution)/shard_map/ppermute | solution.py:385
  19.8 6.4 %collective-permute-start.6 = (bf16[32,16,128]{2,1,0:T(8,128)(2,1)S(1)}, bf16[32,16,128]{2,1,0:T(8,128)(2,1)S(1)}, u32[]{:S(2)}, u32[]{:S(2)}) collective-permute-start(bf16[32,16,128]{2,1,0:T(8,128)(2,1)S(1)} %get-tuple-element.26), channel_id=1, source_target_pairs={{0,1},{1,0},{2,3},{3,2},{4,5},{5,4},{6,7},{7,6},{8,9},{9,8},{10,11... | collective-permute-start | bytes 393224 | tf_op jit(solution)/shard_map/ppermute | solution.py:398
  20.3 6.0 %collective-permute-start.13 = (bf16[32,16,128]{2,1,0:T(8,128)(2,1)S(1)}, bf16[32,16,128]{2,1,0:T(8,128)(2,1)S(1)}, u32[]{:S(2)}, u32[]{:S(2)}) collective-permute-start(bf16[32,16,128]{2,1,0:T(8,128)(2,1)S(1)} %get-tuple-element.34), channel_id=1, source_target_pairs={{0,3},{1,2},{2,1},{3,0},{4,7},{5,6},{6,5},{7,4},{8,11},{9,10},{10,... | collective-permute-start | bytes 393224 | tf_op jit(solution)/shard_map/ppermute | solution.py:398
  22.2 5.4 %collective-permute-start.10 = (bf16[2,2,128,128]{3,2,1,0:T(8,128)(2,1)S(1)}, bf16[2,2,128,128]{3,2,1,0:T(8,128)(2,1)S(1)}, u32[]{:S(2)}, u32[]{:S(2)}) collective-permute-start(bf16[2,2,128,128]{3,2,1,0:T(8,128)(2,1)S(1)} %get-tuple-element.31), channel_id=1, source_target_pairs={{8,0},{0,4},{16,8},{4,12},{24,16},{12,20},{28,24},{20,28},{9,1},{1... | collective-permute-start | bytes 393224 | tf_op jit(solution)/shard_map/ppermute | solution.py:394
  22.3 6.8 %collective-permute-start.11 = (bf16[32,16,128]{2,1,0:T(8,128)(2,1)S(1)}, bf16[32,16,128]{2,1,0:T(8,128)(2,1)S(1)}, u32[]{:S(2)}, u32[]{:S(2)}) collective-permute-start(bf16[32,16,128]{2,1,0:T(8,128)(2,1)S(1)} %get-tuple-element.32), channel_id=1, source_target_pairs={{0,2},{1,3},{2,0},{3,1},{4,6},{5,7},{6,4},{7,5},{8,10},{9,11},{10,... | collective-permute-start | bytes 393224 | tf_op jit(solution)/shard_map/ppermute | solution.py:398
  24.1 6.4 %collective-permute-start.12 = (bf16[2,2,128,128]{3,2,1,0:T(8,128)(2,1)S(1)}, bf16[2,2,128,128]{3,2,1,0:T(8,128)(2,1)S(1)}, u32[]{:S(2)}, u32[]{:S(2)}) collective-permute-start(bf16[2,2,128,128]{3,2,1,0:T(8,128)(2,1)S(1)} %get-tuple-element.33), channel_id=1, source_target_pairs={{0,4},{4,0},{8,12},{12,8},{16,20},{20,16},{24,28},{28,24},{1,5},{5... | collective-permute-start | bytes 393224 | tf_op jit(solution)/shard_map/ppermute | solution.py:385
  26.2 6.3 %collective-permute-start.9 = (bf16[2,2,128,128]{3,2,1,0:T(8,128)(2,1)S(1)}, bf16[2,2,128,128]{3,2,1,0:T(8,128)(2,1)S(1)}, u32[]{:S(2)}, u32[]{:S(2)}) collective-permute-start(bf16[2,2,128,128]{3,2,1,0:T(8,128)(2,1)S(1)} %add.1), channel_id=1, source_target_pairs={{0,8},{4,0},{8,16},{12,4},{16,24},{20,12},{24,28},{28,20},{1,9},{5... | collective-permute-start | bytes 393224 | tf_op jit(solution)/shard_map/ppermute | solution.py:394

commit v16 on v14

--- a/solution.py
+++ b/solution.py
@@ -14,7 +14,7 @@
 NEG = -1e30
 TILE = 8
 ALIGN = 16
-WIDTHS = (160, 288)
+WIDTHS = (176, 304)
 
 _VMEM = pl.BlockSpec(memory_space=pltpu.VMEM)
 _SMEM = pl.BlockSpec(memory_space=pltpu.SMEM)
@@ -227,25 +227,25 @@
         dq = jnp.transpose(dq * scale).reshape(tokens, group_size, size)
         dqs[place][:, pl.ds(group * group_size, group_size)] = dq.astype(jnp.bfloat16)
 
-    lowest = [jnp.min(range_ref[mask, 0:1, :]) & -ALIGN for mask in masks]
-    needed = [jnp.max(range_ref[mask, 1:2, :]) - low for mask, low in zip(masks, lowest)]
-    needed = functools.reduce(jnp.maximum, needed)
-
-    def all_items(width):
-        starts = [jnp.clip(low, 0, reach - width) for low in lowest]
-        top = scores_of(0, starts, width)
-        for item in range(len(items)):
-            later = scores_of(item + 1, starts, width) if item + 1 < len(items) else None
+    def chunk(place, width):
+        starts = {place: jnp.clip(lowest[place], 0, reach - width)}
+        here = [item for item, (of_place, _) in enumerate(items) if of_place == place]
+        top = scores_of(here[0], starts, width)
+        for item in here:
+            later = scores_of(item + 1, starts, width) if item + 1 in here else None
             softmax_of(item, top, width)
             gradients_of(item, starts, width)
             top = later
 
+    lowest = [jnp.min(range_ref[mask, 0:1, :]) & -ALIGN for mask in masks]
+    needed = [jnp.max(range_ref[mask, 1:2, :]) - low for mask, low in zip(masks, lowest)]
     widths = [width for width in WIDTHS if width < reach] + [reach]
-    for floor, width in zip([-1] + widths, widths):
-        fits = needed > floor
-        if width < reach:
-            fits = fits & (needed <= width)
-        pl.when(fits)(functools.partial(all_items, width))
+    for place in range(len(masks)):
+        for floor, width in zip([-1] + widths, widths):
+            fits = needed[place] > floor
+            if width < reach:
+                fits = fits & (needed[place] <= width)
+            pl.when(fits)(functools.partial(chunk, place, width))
 
     if not is_last:
         outs[0][...] = acc[...]
@@ -359,9 +359,8 @@
 
 
 def shifted(block, distance):
-    devices = range(lax.axis_size("seq"))
-    route = [(i, i + distance) for i in devices if i + distance in devices]
-    return lax.ppermute(block, "seq", route)
+    count = lax.axis_size("seq")
+    return lax.ppermute(block, "seq", [(i, (i + distance) % count) for i in range(count)])
 
 
 def paired(block):

time: 32 us -> 30.5 us (0.953)
  waiting for transfers between devices: 7.74 us -> 6.43 us
  starting transfers between devices: 18.5 us -> 17.6 us
  Pallas kernels: 4.9 us -> 5.59 us
    ppermute x3, starting transfers between devices: 5.54 us -> 3.52 us  [ringed(): return lax.ppermute(block, 'seq', route)]
    ppermute x1, starting transfers between devices: 3.48 us -> 1.58 us  [shifted(): lax.ppermute(block, 'seq', [(i, (i + distance) % count) for i in range(co...]
    ppermute x6, starting transfers between devices: 3.64 us -> 5.2 us  [swapped(): lax.ppermute(block, 'kvh', [(i, i ^ mask) for i in range(lax.axis_size('k...]
    ppermute x3, starting transfers between devices: 5.81 us -> 7.28 us  [paired(): lax.ppermute(block, 'seq', [(i, i ^ 1) for i in range(lax.axis_size('seq'...]
    ppermute x6, waiting for transfers between devices: 2.61 us -> 1.67 us  [swapped(): lax.ppermute(block, 'kvh', [(i, i ^ mask) for i in range(lax.axis_size('k...]
    ppermute x3, waiting for transfers between devices: 2.08 us -> 1.3 us  [paired(): lax.ppermute(block, 'seq', [(i, i ^ 1) for i in range(lax.axis_size('seq'...]
    pallas_call x2, Pallas kernels: 2.55 us -> 3.24 us  [gradients(): pl.pallas_call(functools.partial(grad_kernel, masks, parts, carried is No...]
    ppermute x3, waiting for transfers between devices: 3.05 us -> 3.46 us  [ringed(): return lax.ppermute(block, 'seq', route)]
  transfers between devices with their start and end apart: 13 -> 13, of which waited for: 6 -> 8; matrix products, arithmetic and copies ran while one was open for 0% -> 0% of each run, Pallas kernels for 5% -> 8%
where the time goes in v16:
time: 30.5 us; the launch traced here: 30.3 us
  starting transfers between devices  17.6 us (58%)
  waiting for transfers between devices  6.43 us (21%)
  Pallas kernels  5.59 us (18%)
  between operations  0.69 us (2%)
    ppermute x3, starting transfers between devices, paired(): lax.ppermute(block, 'seq', [(i, i ^ 1) for i in range(lax.axis_size('seq'...  7.28 us
    ppermute x6, starting transfers between devices, swapped(): lax.ppermute(block, 'kvh', [(i, i ^ mask) for i in range(lax.axis_size('k...  5.2 us
    ppermute x3, starting transfers between devices, ringed(): return lax.ppermute(block, 'seq', route)  3.52 us
    ppermute x3, waiting for transfers between devices, ringed(): return lax.ppermute(block, 'seq', route)  3.46 us
    pallas_call x2, Pallas kernels, gradients(): pl.pallas_call(functools.partial(grad_kernel, masks, parts, carried is No...  3.24 us
    ppermute x6, waiting for transfers between devices, swapped(): lax.ppermute(block, 'kvh', [(i, i ^ mask) for i in range(lax.axis_size('k...  1.67 us
    ppermute x1, starting transfers between devices, shifted(): lax.ppermute(block, 'seq', [(i, (i + distance) % count) for i in range(co...  1.58 us
    pallas_call x1, Pallas kernels, prepare(): pl.pallas_call(functools.partial(prep_kernel, parts), out_shape=(block,)...  1.3 us
  transfers between devices with their start and end apart: 13, of which 8 were waited for; matrix products, arithmetic and copies ran while one was open for 0% of the time, Pallas kernels for 8%

profile of v16, /device:TPU:0, one launch (start us, length us, event | category | flops | bytes accessed | tf_op | source)
XLA Modules:
  0.0 30.3 jit_solution(1808639960386645402)
XLA Ops:
  0.6 0.0 copy-start
  0.6 1.3 %prepare.1 = (bf16[2,2,128,128]{3,2,1,0:T(8,128)(2,1)S(1)}, bf16[2,2,128,128]{3,2,1,0:T(8,128)(2,1)S(1)}, bf16[2,2,128,128]{3,2,1,0:T(8,128)(2,1)S(1)}, bf16[32,...) custom-call(s32[8]{0:T(128)} %lengths_ref.1, ...), custom_call_target="tpu_custom_call" | custom-call | tf_op jit(solution)/shard_map/prepare/pallas_call | solution.py:90
  1.9 3.0 %collective-permute-start = (bf16[2,2,128,128]{3,2,1,0:T(8,128)(2,1)S(1)}, bf16[2,2,128,128]{3,2,1,0:T(8,128)(2,1)S(1)}, u32[]{:S(2)}, u32[]{:S(2)}) collective-permute-start(bf16[2,2,128,128]{3,2,1,0:T(8,128)(2,1)S(1)} %get-tuple-element.23), channel_id=1, source_target_pairs={{0,4},{4,0},{8,12},{12,8},{16,20},{20,16},{24,28},{28,24},{1,5},{5... | collective-permute-start | bytes 393224 | tf_op jit(solution)/shard_map/ppermute | solution.py:367
  4.9 1.6 %collective-permute-start.1 = (bf16[2,2,128,128]{3,2,1,0:T(8,128)(2,1)S(1)}, bf16[2,2,128,128]{3,2,1,0:T(8,128)(2,1)S(1)}, u32[]{:S(2)}, u32[]{:S(2)}) collective-permute-start(bf16[2,2,128,128]{3,2,1,0:T(8,128)(2,1)S(1)} %get-tuple-element.24), channel_id=1, source_target_pairs={{0,8},{4,12},{8,16},{12,20},{16,24},{20,28},{24,0},{28,4},{1,9},{5... | collective-permute-start | bytes 393224 | tf_op jit(solution)/shard_map/ppermute | solution.py:363
  6.5 0.0 collective-permute-start.3
  6.5 1.6 %collective-permute-start.4 = (bf16[32,16,128]{2,1,0:T(8,128)(2,1)S(1)}, bf16[32,16,128]{2,1,0:T(8,128)(2,1)S(1)}, u32[]{:S(2)}, u32[]{:S(2)}) collective-permute-start(bf16[32,16,128]{2,1,0:T(8,128)(2,1)S(1)} %get-tuple-element.27), channel_id=1, source_target_pairs={{0,3},{1,2},{2,1},{3,0},{4,7},{5,6},{6,5},{7,4},{8,11},{9,10},{10,... | collective-permute-start | bytes 393224 | tf_op jit(solution)/shard_map/ppermute | solution.py:380
  8.2 0.3 collective-permute-done.refs_1_
  8.4 1.8 %collective-permute-start.2 = (bf16[2,2,128,128]{3,2,1,0:T(8,128)(2,1)S(1)}, bf16[2,2,128,128]{3,2,1,0:T(8,128)(2,1)S(1)}, u32[]{:S(2)}, u32[]{:S(2)}) collective-permute-start(bf16[2,2,128,128]{3,2,1,0:T(8,128)(2,1)S(1)} %collective-permute-done.refs_1_), channel_id=1, source_target_pairs={{0,8},{4,0},{8,16},{12,4},{16,24},{20,12},{24,28},{28,20},{1,9},{5... | collective-permute-start | bytes 393224 | tf_op jit(solution)/shard_map/ppermute | solution.py:376
  10.3 1.5 %collective-permute-start.6 = (bf16[32,16,128]{2,1,0:T(8,128)(2,1)S(1)}, bf16[32,16,128]{2,1,0:T(8,128)(2,1)S(1)}, u32[]{:S(2)}, u32[]{:S(2)}) collective-permute-start(bf16[32,16,128]{2,1,0:T(8,128)(2,1)S(1)} %get-tuple-element.29), channel_id=1, source_target_pairs={{0,2},{1,3},{2,0},{3,1},{4,6},{5,7},{6,4},{7,5},{8,10},{9,11},{10,... | collective-permute-start | bytes 393224 | tf_op jit(solution)/shard_map/ppermute | solution.py:380
  11.8 0.0 collective-permute-done.1.refs_2_
  11.8 0.0 collective-permute-done.3.refs_5_
  11.8 0.2 collective-permute-done.4.refs_6_
  12.0 1.6 %collective-permute-done.2.refs_3_ = bf16[2,2,128,128]{3,2,1,0:T(8,128)(2,1)S(1)} collective-permute-done((bf16[2,2,128,128]{3,2,1,0:T(8,128)(2,1)S(1)}, bf16[2,2,128,128]{3,2,1,0:T(8,128)(2,1)S(1)}, u32[]{:S(2)}, u32[]{:S(2)}) %collective-permute-start.2) | collective-permute-done | bytes 131104 | tf_op jit(solution)/shard_map/ppermute | solution.py:376
  13.6 0.0 copy-done
  13.6 2.3 %gradients.2 = (bf16[32,16,128]{2,1,0:T(8,128)(2,1)S(1)}, bf16[32,16,128]{2,1,0:T(8,128)(2,1)S(1)}, bf16[32,16,128]{2,1,0:T(8,128)(2,1)S(1)}, f32[2,2,512,128]{3,2,1,0:T(8,128)S(1)}) custom-call(s32[4,2,256]{2,1,0:T(2,128)S(1)} %get-tuple-element.21.range_ref, bf16[128,16,128]{2,1,0:T(8,128)(2,1)S(1)} %copy-done, ...), custom_call_target="tpu_custom_call" | custom-call | flops 1006632960 | bytes 2097152 | tf_op jit(solution)/shard_map/gradients/pallas_call | solution.py:280
  15.9 0.0 collective-permute-done.6.refs_4_
  15.9 1.0 %gradients.3 = (bf16[32,16,128]{2,1,0:T(8,128)(2,1)S(1)}, f32[2,2,128,128]{3,2,1,0:T(8,128)S(1)}, bf16[2,2,128,128]{3,2,1,0:T(8,128)(2,1)S(1)}, bf16[2,2,128,128...) custom-call(s32[4,2,256]{2,1,0:T(2,128)S(1)} %get-tuple-element.21.range_ref, ...), custom_call_target="tpu_custom_call" | custom-call | flops 335544320 | bytes 2097152 | tf_op jit(solution)/shard_map/gradients/pallas_call | solution.py:280
  16.8 1.9 %collective-permute-start.7 = (bf16[2,2,128,128]{3,2,1,0:T(8,128)(2,1)S(1)}, bf16[2,2,128,128]{3,2,1,0:T(8,128)(2,1)S(1)}, u32[]{:S(2)}, u32[]{:S(2)}) collective-permute-start(bf16[2,2,128,128]{3,2,1,0:T(8,128)(2,1)S(1)} %get-tuple-element.31), channel_id=1, source_target_pairs={{0,4},{4,0},{8,12},{12,8},{16,20},{20,16},{24,28},{28,24},{1,5},{5... | collective-permute-start | bytes 393224 | tf_op jit(solution)/shard_map/ppermute | solution.py:367
  18.8 0.0 collective-permute-start.5
  18.8 1.6 %collective-permute-start.12 = (bf16[32,16,128]{2,1,0:T(8,128)(2,1)S(1)}, bf16[32,16,128]{2,1,0:T(8,128)(2,1)S(1)}, u32[]{:S(2)}, u32[]{:S(2)}) collective-permute-start(bf16[32,16,128]{2,1,0:T(8,128)(2,1)S(1)} %get-tuple-element.36), channel_id=1, source_target_pairs={{0,3},{1,2},{2,1},{3,0},{4,7},{5,6},{6,5},{7,4},{8,11},{9,10},{10,... | collective-permute-start | bytes 393224 | tf_op jit(solution)/shard_map/ppermute | solution.py:380
  20.4 0.2 collective-permute-start.9
  20.7 0.4 %collective-permute-start.10 = (bf16[32,16,128]{2,1,0:T(8,128)(2,1)S(1)}, bf16[32,16,128]{2,1,0:T(8,128)(2,1)S(1)}, u32[]{:S(2)}, u32[]{:S(2)}) collective-permute-start(bf16[32,16,128]{2,1,0:T(8,128)(2,1)S(1)} %get-tuple-element.34), channel_id=1, source_target_pairs={{0,2},{1,3},{2,0},{3,1},{4,6},{5,7},{6,4},{7,5},{8,10},{9,11},{10,... | collective-permute-start | bytes 393224 | tf_op jit(solution)/shard_map/ppermute | solution.py:380
  21.1 0.8 %collective-permute-done.7.left = bf16[2,2,128,128]{3,2,1,0:T(8,128)(2,1)S(1)} collective-permute-done((bf16[2,2,128,128]{3,2,1,0:T(8,128)(2,1)S(1)}, bf16[2,2,128,128]{3,2,1,0:T(8,128)(2,1)S(1)}, u32[]{:S(2)}, u32[]{:S(2)}) %collective-permute-start.7) | collective-permute-done | bytes 131104 | tf_op jit(solution)/shard_map/ppermute | solution.py:367
  21.9 2.3 %collective-permute-start.11 = (bf16[2,2,128,128]{3,2,1,0:T(8,128)(2,1)S(1)}, bf16[2,2,128,128]{3,2,1,0:T(8,128)(2,1)S(1)}, u32[]{:S(2)}, u32[]{:S(2)}) collective-permute-start(bf16[2,2,128,128]{3,2,1,0:T(8,128)(2,1)S(1)} %get-tuple-element.35), channel_id=1, source_target_pairs={{0,4},{4,0},{8,12},{12,8},{16,20},{20,16},{24,28},{28,24},{1,5},{5... | collective-permute-start | bytes 393224 | tf_op jit(solution)/shard_map/ppermute | solution.py:367
  24.2 0.0 collective-permute-done.5.refs_0_
  24.3 1.4 %collective-permute-start.8 = (bf16[2,2,128,128]{3,2,1,0:T(8,128)(2,1)S(1)}, bf16[2,2,128,128]{3,2,1,0:T(8,128)(2,1)S(1)}, u32[]{:S(2)}, u32[]{:S(2)}) collective-permute-start(bf16[2,2,128,128]{3,2,1,0:T(8,128)(2,1)S(1)} %add.1), channel_id=1, source_target_pairs={{0,8},{4,0},{8,16},{12,4},{16,24},{20,12},{24,28},{28,20},{1,9},{5... | collective-permute-start | bytes 393224 | tf_op jit(solution)/shard_map/ppermute | solution.py:376
  25.7 0.0 collective-permute-done.12.refs_5_
  25.7 0.2 collective-permute-done.9.refs_2_
  25.9 1.5 %collective-permute-done.10.refs_3_ = bf16[32,16,128]{2,1,0:T(8,128)(2,1)S(1)} collective-permute-done((bf16[32,16,128]{2,1,0:T(8,128)(2,1)S(1)}, bf16[32,16,128]{2,1,0:T(8,128)(2,1)S(1)}, u32[]{:S(2)}, u32[]{:S(2)}) %collective-permute-start.10) | collective-permute-done | bytes 131104 | tf_op jit(solution)/shard_map/ppermute | solution.py:380
  27.4 0.2 collective-permute-done.11.refs_4_
  27.6 1.7 %collective-permute-done.8.refs_1_ = bf16[2,2,128,128]{3,2,1,0:T(8,128)(2,1)S(1)} collective-permute-done((bf16[2,2,128,128]{3,2,1,0:T(8,128)(2,1)S(1)}, bf16[2,2,128,128]{3,2,1,0:T(8,128)(2,1)S(1)}, u32[]{:S(2)}, u32[]{:S(2)}) %collective-permute-start.8) | collective-permute-done | bytes 131104 | tf_op jit(solution)/shard_map/ppermute | solution.py:376
  29.3 1.0 %finish.1 = (bf16[32,64,128]{2,1,0:T(8,128)(2,1)}, bf16[128,2,128]{2,1,0:T(2,128)(2,1)}, bf16[128,2,128]{2,1,0:T(2,128)(2,1)}) custom-call(bf16[32,16,128]{2,1,0:T(8,128)(2,1)S(1)} %collective-permute-done.5.refs_0_, bf16[2,2,128,128]{3,2,1,0:T(8,128)(2,1)S(1)} %collective-permute-done.8.refs_1_, ...), custom_call_target="tpu_custom_call" | custom-call | tf_op jit(solution)/shard_map/finish/pallas_call | solution.py:347
  (1 shorter events, 0.0 us)
Async XLA Ops:
  0.6 12.9 %copy-start = (bf16[128,16,128]{2,1,0:T(8,128)(2,1)S(1)}, bf16[128,16,128]{2,1,0:T(8,128)(2,1)}, u32[]{:S(2)}) copy-start(bf16[128,16,128]{2,1,0:T(8,128)(2,1)} %q_ref.3) | copy-start | bytes 1572868
  1.9 6.5 %collective-permute-start = (bf16[2,2,128,128]{3,2,1,0:T(8,128)(2,1)S(1)}, bf16[2,2,128,128]{3,2,1,0:T(8,128)(2,1)S(1)}, u32[]{:S(2)}, u32[]{:S(2)}) collective-permute-start(bf16[2,2,128,128]{3,2,1,0:T(8,128)(2,1)S(1)} %get-tuple-element.23), channel_id=1, source_target_pairs={{0,4},{4,0},{8,12},{12,8},{16,20},{20,16},{24,28},{28,24},{1,5},{5... | collective-permute-start | bytes 393224 | tf_op jit(solution)/shard_map/ppermute | solution.py:367
  4.9 6.8 %collective-permute-start.1 = (bf16[2,2,128,128]{3,2,1,0:T(8,128)(2,1)S(1)}, bf16[2,2,128,128]{3,2,1,0:T(8,128)(2,1)S(1)}, u32[]{:S(2)}, u32[]{:S(2)}) collective-permute-start(bf16[2,2,128,128]{3,2,1,0:T(8,128)(2,1)S(1)} %get-tuple-element.24), channel_id=1, source_target_pairs={{0,8},{4,12},{8,16},{12,20},{16,24},{20,28},{24,0},{28,4},{1,9},{5... | collective-permute-start | bytes 393224 | tf_op jit(solution)/shard_map/ppermute | solution.py:363
  6.5 5.3 %collective-permute-start.3 = (bf16[32,16,128]{2,1,0:T(8,128)(2,1)S(1)}, bf16[32,16,128]{2,1,0:T(8,128)(2,1)S(1)}, u32[]{:S(2)}, u32[]{:S(2)}) collective-permute-start(bf16[32,16,128]{2,1,0:T(8,128)(2,1)S(1)} %get-tuple-element.26), channel_id=1, source_target_pairs={{0,1},{1,0},{2,3},{3,2},{4,5},{5,4},{6,7},{7,6},{8,9},{9,8},{10,11... | collective-permute-start | bytes 393224 | tf_op jit(solution)/shard_map/ppermute | solution.py:380
  6.5 5.5 %collective-permute-start.4 = (bf16[32,16,128]{2,1,0:T(8,128)(2,1)S(1)}, bf16[32,16,128]{2,1,0:T(8,128)(2,1)S(1)}, u32[]{:S(2)}, u32[]{:S(2)}) collective-permute-start(bf16[32,16,128]{2,1,0:T(8,128)(2,1)S(1)} %get-tuple-element.27), channel_id=1, source_target_pairs={{0,3},{1,2},{2,1},{3,0},{4,7},{5,6},{6,5},{7,4},{8,11},{9,10},{10,... | collective-permute-start | bytes 393224 | tf_op jit(solution)/shard_map/ppermute | solution.py:380
  8.4 5.1 %collective-permute-start.2 = (bf16[2,2,128,128]{3,2,1,0:T(8,128)(2,1)S(1)}, bf16[2,2,128,128]{3,2,1,0:T(8,128)(2,1)S(1)}, u32[]{:S(2)}, u32[]{:S(2)}) collective-permute-start(bf16[2,2,128,128]{3,2,1,0:T(8,128)(2,1)S(1)} %collective-permute-done.refs_1_), channel_id=1, source_target_pairs={{0,8},{4,0},{8,16},{12,4},{16,24},{20,12},{24,28},{28,20},{1,9},{5... | collective-permute-start | bytes 393224 | tf_op jit(solution)/shard_map/ppermute | solution.py:376
  10.3 5.6 %collective-permute-start.6 = (bf16[32,16,128]{2,1,0:T(8,128)(2,1)S(1)}, bf16[32,16,128]{2,1,0:T(8,128)(2,1)S(1)}, u32[]{:S(2)}, u32[]{:S(2)}) collective-permute-start(bf16[32,16,128]{2,1,0:T(8,128)(2,1)S(1)} %get-tuple-element.29), channel_id=1, source_target_pairs={{0,2},{1,3},{2,0},{3,1},{4,6},{5,7},{6,4},{7,5},{8,10},{9,11},{10,... | collective-permute-start | bytes 393224 | tf_op jit(solution)/shard_map/ppermute | solution.py:380
  16.8 5.0 %collective-permute-start.7 = (bf16[2,2,128,128]{3,2,1,0:T(8,128)(2,1)S(1)}, bf16[2,2,128,128]{3,2,1,0:T(8,128)(2,1)S(1)}, u32[]{:S(2)}, u32[]{:S(2)}) collective-permute-start(bf16[2,2,128,128]{3,2,1,0:T(8,128)(2,1)S(1)} %get-tuple-element.31), channel_id=1, source_target_pairs={{0,4},{4,0},{8,12},{12,8},{16,20},{20,16},{24,28},{28,24},{1,5},{5... | collective-permute-start | bytes 393224 | tf_op jit(solution)/shard_map/ppermute | solution.py:367
  18.8 5.5 %collective-permute-start.5 = (bf16[32,16,128]{2,1,0:T(8,128)(2,1)S(1)}, bf16[32,16,128]{2,1,0:T(8,128)(2,1)S(1)}, u32[]{:S(2)}, u32[]{:S(2)}) collective-permute-start(bf16[32,16,128]{2,1,0:T(8,128)(2,1)S(1)} %get-tuple-element.28), channel_id=1, source_target_pairs={{0,1},{1,0},{2,3},{3,2},{4,5},{5,4},{6,7},{7,6},{8,9},{9,8},{10,11... | collective-permute-start | bytes 393224 | tf_op jit(solution)/shard_map/ppermute | solution.py:380
  18.8 6.9 %collective-permute-start.12 = (bf16[32,16,128]{2,1,0:T(8,128)(2,1)S(1)}, bf16[32,16,128]{2,1,0:T(8,128)(2,1)S(1)}, u32[]{:S(2)}, u32[]{:S(2)}) collective-permute-start(bf16[32,16,128]{2,1,0:T(8,128)(2,1)S(1)} %get-tuple-element.36), channel_id=1, source_target_pairs={{0,3},{1,2},{2,1},{3,0},{4,7},{5,6},{6,5},{7,4},{8,11},{9,10},{10,... | collective-permute-start | bytes 393224 | tf_op jit(solution)/shard_map/ppermute | solution.py:380
  20.4 5.5 %collective-permute-start.9 = (bf16[2,2,128,128]{3,2,1,0:T(8,128)(2,1)S(1)}, bf16[2,2,128,128]{3,2,1,0:T(8,128)(2,1)S(1)}, u32[]{:S(2)}, u32[]{:S(2)}) collective-permute-start(bf16[2,2,128,128]{3,2,1,0:T(8,128)(2,1)S(1)} %get-tuple-element.33), channel_id=1, source_target_pairs={{8,0},{0,4},{16,8},{4,12},{24,16},{12,20},{28,24},{20,28},{9,1},{1... | collective-permute-start | bytes 393224 | tf_op jit(solution)/shard_map/ppermute | solution.py:376
  20.7 6.7 %collective-permute-start.10 = (bf16[32,16,128]{2,1,0:T(8,128)(2,1)S(1)}, bf16[32,16,128]{2,1,0:T(8,128)(2,1)S(1)}, u32[]{:S(2)}, u32[]{:S(2)}) collective-permute-start(bf16[32,16,128]{2,1,0:T(8,128)(2,1)S(1)} %get-tuple-element.34), channel_id=1, source_target_pairs={{0,2},{1,3},{2,0},{3,1},{4,6},{5,7},{6,4},{7,5},{8,10},{9,11},{10,... | collective-permute-start | bytes 393224 | tf_op jit(solution)/shard_map/ppermute | solution.py:380
  21.9 5.7 %collective-permute-start.11 = (bf16[2,2,128,128]{3,2,1,0:T(8,128)(2,1)S(1)}, bf16[2,2,128,128]{3,2,1,0:T(8,128)(2,1)S(1)}, u32[]{:S(2)}, u32[]{:S(2)}) collective-permute-start(bf16[2,2,128,128]{3,2,1,0:T(8,128)(2,1)S(1)} %get-tuple-element.35), channel_id=1, source_target_pairs={{0,4},{4,0},{8,12},{12,8},{16,20},{20,16},{24,28},{28,24},{1,5},{5... | collective-permute-start | bytes 393224 | tf_op jit(solution)/shard_map/ppermute | solution.py:367
  24.3 5.0 %collective-permute-start.8 = (bf16[2,2,128,128]{3,2,1,0:T(8,128)(2,1)S(1)}, bf16[2,2,128,128]{3,2,1,0:T(8,128)(2,1)S(1)}, u32[]{:S(2)}, u32[]{:S(2)}) collective-permute-start(bf16[2,2,128,128]{3,2,1,0:T(8,128)(2,1)S(1)} %add.1), channel_id=1, source_target_pairs={{0,8},{4,0},{8,16},{12,4},{16,24},{20,12},{24,28},{28,20},{1,9},{5... | collective-permute-start | bytes 393224 | tf_op jit(solution)/shard_map/ppermute | solution.py:376

commit v17 on v16

--- a/solution.py
+++ b/solution.py
@@ -134,14 +134,19 @@
 
 def grad_kernel(masks, parts, is_first, is_last, range_ref, q_ref, *refs):
     refs = list(refs)
-    kv_own, kv_even, kv_far, kv_odd = [refs.pop(0) for _ in range(4)]
+    received = [refs.pop(0) for _ in range(4)] if is_first else []
     cots = [refs.pop(0) for _ in masks]
-    carried = None if is_first else refs.pop(0)
+    window, carried = (None, None) if is_first else (refs.pop(0), refs.pop(0))
     dqs = [refs.pop(0) for _ in masks]
-    outs, (window, acc, score_buf, dprob_buf, prob_buf, dscore_buf) = refs[:-6], refs[-6:]
+    score_buf, dprob_buf, prob_buf, dscore_buf, q_rows, cot_rows = refs[-6:]
+    outs = refs[:-6]
+    if is_first:
+        window, acc = outs
+    else:
+        acc = outs.pop()
     rows, heads, size = q_ref.shape
     tokens = rows // parts
-    kv_heads = kv_own.shape[1]
+    kv_heads = window.shape[1]
     group_size = heads // kv_heads
     span = (BACK + 1 + AHEAD) * rows
     reach = span - rows + tokens
@@ -151,17 +156,24 @@
     me = lax.axis_index("kvh")
 
     even_slot, odd_slot = neighbour_slots(shard)
-    for slot, ref in ((BACK, kv_own), (0, kv_far), (even_slot, kv_even), (odd_slot, kv_odd)):
-        part = pl.ds(pl.multiple_of(slot * rows, rows), rows)
-        for number in range(2):
-            for group in range(kv_heads):
-                window[number, group, part] = ref[number, group]
-    acc[...] = jnp.zeros_like(acc) if is_first else carried[...]
+    if is_first:
+        for slot, ref in zip((BACK, even_slot, 0, odd_slot), received):
+            part = pl.ds(pl.multiple_of(slot * rows, rows), rows)
+            for number in range(2):
+                for group in range(kv_heads):
+                    window[number, group, part] = ref[number, group]
+        acc[...] = jnp.zeros_like(acc)
+    else:
+        acc[...] = carried[...]
 
     contract_last = (((1,), (1,)), ((), ()))
     contract_first = (((0,), (0,)), ((), ()))
     sublane = lax.broadcasted_iota(jnp.int32, (TILE, lanes), 0)
     items = [(place, group) for place in range(len(masks)) for group in range(kv_heads)]
+
+    def key_rows(place, starts, width):
+        first = pl.multiple_of((me ^ masks[place]) * tokens, tokens)
+        return pl.ds(pl.multiple_of(first + starts[place], ALIGN), width)
 
     def operands(item, starts, width):
         place, group = items[item]
@@ -170,7 +182,7 @@
         q = q_ref[pl.ds(first, tokens), of_group].astype(jnp.float32)
         cot = cots[place][:, of_group].astype(jnp.float32)
         return (
-            pl.ds(pl.multiple_of(first + starts[place], ALIGN), width),
+            key_rows(place, starts, width),
             q.reshape(lanes, size).astype(jnp.bfloat16),
             cot.reshape(lanes, size).astype(jnp.bfloat16),
         )
@@ -179,6 +191,7 @@
         place, group = items[item]
         slot = item % 2
         here, q, cot = operands(item, starts, width)
+        q_rows[slot], cot_rows[slot] = q, cot
         scores = lax.dot_general(
             window[0, group, here], q, contract_last, preferred_element_type=jnp.float32
         )
@@ -217,7 +230,7 @@
     def gradients_of(item, starts, width):
         place, group = items[item]
         slot = item % 2
-        here, q, cot = operands(item, starts, width)
+        here, q, cot = key_rows(place, starts, width), q_rows[slot], cot_rows[slot]
         probs, dscores = prob_buf[slot, :width], dscore_buf[slot, :width]
         acc[1, group, here] += jnp.dot(probs, cot, preferred_element_type=jnp.float32)
         acc[0, group, here] += jnp.dot(dscores, q, preferred_element_type=jnp.float32)
@@ -248,7 +261,6 @@
             pl.when(fits)(functools.partial(chunk, place, width))
 
     if not is_last:
-        outs[0][...] = acc[...]
         return
     is_odd = (shard % 2).astype(jnp.float32)
     weights = (1.0, 1.0 - is_odd, is_odd, 1.0, 1.0)
@@ -273,22 +285,23 @@
     if is_last:
         outs += [pltpu.VMEM(kv_shape, jnp.float32)] + [pltpu.VMEM(kv_shape, jnp.bfloat16)] * 4
     else:
-        outs += [pltpu.VMEM(acc_shape, jnp.float32)]
+        outs += [pltpu.VMEM(acc_shape, jnp.bfloat16), pltpu.VMEM(acc_shape, jnp.float32)]
     own, far, even, odd = blocks
-    operands = [ranges, queries, own, even, far, odd, *cots]
-    operands += [] if carried is None else [carried]
+    operands = [ranges, queries] + ([own, even, far, odd] if carried is None else [])
+    operands += [*cots] + ([] if carried is None else list(carried))
     outs = pl.pallas_call(
         functools.partial(grad_kernel, masks, parts, carried is None, is_last),
         out_shape=tuple(outs),
         in_specs=[_VMEM] * len(operands),
         out_specs=(_VMEM,) * len(outs),
-        scratch_shapes=[
-            pltpu.VMEM(acc_shape, jnp.bfloat16),
-            pltpu.VMEM(acc_shape, jnp.float32),
+        scratch_shapes=([pltpu.VMEM(acc_shape, jnp.float32)] if is_last else [])
+        + [
             pltpu.VMEM(tile_shape, jnp.float32),
             pltpu.VMEM(tile_shape, jnp.float32),
             pltpu.VMEM(tile_shape, jnp.bfloat16),
             pltpu.VMEM(tile_shape, jnp.bfloat16),
+            pltpu.VMEM((2, tile_shape[2], size), jnp.bfloat16),
+            pltpu.VMEM((2, tile_shape[2], size), jnp.bfloat16),
         ],
         compiler_params=pltpu.CompilerParams(vmem_limit_bytes=VMEM_BYTES),
         cost_estimate=pl.CostEstimate(
@@ -319,30 +332,37 @@
 
 
 def finish_kernel(parts, *refs):
-    *refs, dq_out, dk_out, dv_out = refs
+    *refs, dq_out, dk_out, dv_out, dk_buf, dv_buf, sems = refs
     refs = dict(zip(finish_order(parts), refs))
-    dqs = [refs[mask] for mask in range(parts)]
-    own, far, even, odd = [refs[name] for name in ("own", "far", "even", "odd")]
-    heads = dqs[0].shape[1]
+    heads = refs[0].shape[1]
     me = lax.axis_index("kvh")
+    copies = []
     for mask in range(parts):
         first = pl.multiple_of((me ^ mask) * heads, heads)
-        dq_out[:, pl.ds(first, heads), :] = dqs[mask][...]
-    for number, ref in enumerate((dk_out, dv_out)):
+        copies.append(
+            pltpu.make_async_copy(refs[mask], dq_out.at[:, pl.ds(first, heads), :], sems.at[mask])
+        )
+        copies[-1].start()
+    for number, (buf, ref) in enumerate(((dk_buf, dk_out), (dv_buf, dv_out))):
         sums = []
-        for group in range(ref.shape[1]):
-            total = own[number, group]
-            for other in (far, even, odd):
-                total = total + other[number, group].astype(jnp.float32)
+        for group in range(buf.shape[1]):
+            total = refs["own"][number, group]
+            for name in ("far", "even", "odd"):
+                total = total + refs[name][number, group].astype(jnp.float32)
             sums.append(total)
-        ref[...] = jnp.stack(sums, axis=1).astype(jnp.bfloat16)
+        buf[...] = jnp.stack(sums, axis=1).astype(jnp.bfloat16)
+        copies.append(pltpu.make_async_copy(buf, ref, sems.at[parts + number]))
+        copies[-1].start()
+    for copy in copies:
+        copy.wait()
 
 
 def finish(dqs, partials):
     parts = len(dqs)
     rows, heads, size = dqs[0].shape
     _, kv_heads, kv_rows, _ = partials[0].shape
-    kv_out = jax.ShapeDtypeStruct((kv_rows, kv_heads, size), jnp.bfloat16)
+    kv_shape = (kv_rows, kv_heads, size)
+    kv_out = jax.ShapeDtypeStruct(kv_shape, jnp.bfloat16)
     operands = dict(enumerate(dqs)) | dict(zip(("own", "far", "even", "odd"), partials))
     return pl.pallas_call(
         functools.partial(finish_kernel, parts),
@@ -352,7 +372,12 @@
             kv_out,
         ),
         in_specs=[_VMEM] * (parts + 4),
-        out_specs=(_VMEM,) * 3,
+        out_specs=(_HBM,) * 3,
+        scratch_shapes=[
+            pltpu.VMEM(kv_shape, jnp.bfloat16),
+            pltpu.VMEM(kv_shape, jnp.bfloat16),
+            pltpu.SemaphoreType.DMA((parts + 2,)),
+        ],
         compiler_params=pltpu.CompilerParams(vmem_limit_bytes=VMEM_BYTES),
         name="finish",
     )(*[operands[name] for name in finish_order(parts)])
@@ -388,10 +413,10 @@
     even = paired(kv[2])
     blocks = [kv[0], shifted(kv[1], BACK), even, ringed(even)]
     cots = [cots[0]] + [swapped(cots[mask], mask) for mask in range(1, parts)]
-    dqs, carried = {}, [None]
+    dqs, carried = {}, None
     for masks in stages(parts):
         found, carried = gradients(
-            masks, parts, ranges, queries, [cots[mask] for mask in masks], blocks, carried[0]
+            masks, parts, ranges, queries, [cots[mask] for mask in masks], blocks, carried
         )
         for mask, dq in zip(masks, found):
             dqs[mask] = swapped(dq, mask) if mask else dq

time: 30.5 us -> 30.3 us (level)
  starting transfers between devices: 17.6 us -> 17 us
  waiting for transfers between devices: 6.43 us -> 6.77 us
    ppermute x3, starting transfers between devices: 7.28 us -> 5.69 us  [paired(): lax.ppermute(block, 'seq', [(i, i ^ 1) for i in range(lax.axis_size('seq'...]
    ppermute x3, starting transfers between devices: 3.52 us -> 4.53 us  [ringed(): return lax.ppermute(block, 'seq', route)]
    ppermute x3, waiting for transfers between devices: 1.3 us -> 1.89 us  [paired(): lax.ppermute(block, 'seq', [(i, i ^ 1) for i in range(lax.axis_size('seq'...]
where the time goes in v17:
time: 30.3 us; the launch traced here: 30.2 us
  starting transfers between devices  17 us (56%)
  waiting for transfers between devices  6.77 us (22%)
  Pallas kernels  5.74 us (19%)
  between operations  0.69 us (2%)
    ppermute x3, starting transfers between devices, paired(): lax.ppermute(block, 'seq', [(i, i ^ 1) for i in range(lax.axis_size('seq'...  5.69 us
    ppermute x6, starting transfers between devices, swapped(): lax.ppermute(block, 'kvh', [(i, i ^ mask) for i in range(lax.axis_size('k...  5.21 us
    ppermute x3, starting transfers between devices, ringed(): return lax.ppermute(block, 'seq', route)  4.53 us
    pallas_call x2, Pallas kernels, gradients(): pl.pallas_call(functools.partial(grad_kernel, masks, parts, carried is No...  3.46 us
    ppermute x3, waiting for transfers between devices, ringed(): return lax.ppermute(block, 'seq', route)  3.19 us
    ppermute x3, waiting for transfers between devices, paired(): lax.ppermute(block, 'seq', [(i, i ^ 1) for i in range(lax.axis_size('seq'...  1.89 us
    ppermute x6, waiting for transfers between devices, swapped(): lax.ppermute(block, 'kvh', [(i, i ^ mask) for i in range(lax.axis_size('k...  1.69 us
    ppermute x1, starting transfers between devices, shifted(): lax.ppermute(block, 'seq', [(i, (i + distance) % count) for i in range(co...  1.58 us
  transfers between devices with their start and end apart: 13, of which 8 were waited for; matrix products, arithmetic and copies ran while one was open for 0% of the time, Pallas kernels for 8%

profile of v17, /device:TPU:0, one launch (start us, length us, event | category | flops | bytes accessed | tf_op | source)
XLA Modules:
  0.0 30.2 jit_solution(11542815812599973663)
XLA Ops:
  0.6 0.0 copy-start
  0.6 1.3 %prepare.1 = (bf16[2,2,128,128]{3,2,1,0:T(8,128)(2,1)S(1)}, bf16[2,2,128,128]{3,2,1,0:T(8,128)(2,1)S(1)}, bf16[2,2,128,128]{3,2,1,0:T(8,128)(2,1)S(1)}, bf16[32,...) custom-call(s32[8]{0:T(128)} %lengths_ref.1, ...), custom_call_target="tpu_custom_call" | custom-call | tf_op jit(solution)/shard_map/prepare/pallas_call | solution.py:90
  1.9 3.0 %collective-permute-start = (bf16[2,2,128,128]{3,2,1,0:T(8,128)(2,1)S(1)}, bf16[2,2,128,128]{3,2,1,0:T(8,128)(2,1)S(1)}, u32[]{:S(2)}, u32[]{:S(2)}) collective-permute-start(bf16[2,2,128,128]{3,2,1,0:T(8,128)(2,1)S(1)} %get-tuple-element.24), channel_id=1, source_target_pairs={{0,4},{4,0},{8,12},{12,8},{16,20},{20,16},{24,28},{28,24},{1,5},{5... | collective-permute-start | bytes 393224 | tf_op jit(solution)/shard_map/ppermute | solution.py:392
  4.9 1.6 %collective-permute-start.1 = (bf16[2,2,128,128]{3,2,1,0:T(8,128)(2,1)S(1)}, bf16[2,2,128,128]{3,2,1,0:T(8,128)(2,1)S(1)}, u32[]{:S(2)}, u32[]{:S(2)}) collective-permute-start(bf16[2,2,128,128]{3,2,1,0:T(8,128)(2,1)S(1)} %get-tuple-element.25), channel_id=1, source_target_pairs={{0,8},{4,12},{8,16},{12,20},{16,24},{20,28},{24,0},{28,4},{1,9},{5... | collective-permute-start | bytes 393224 | tf_op jit(solution)/shard_map/ppermute | solution.py:388
  6.5 0.0 collective-permute-start.3
  6.5 1.6 %collective-permute-start.4 = (bf16[32,16,128]{2,1,0:T(8,128)(2,1)S(1)}, bf16[32,16,128]{2,1,0:T(8,128)(2,1)S(1)}, u32[]{:S(2)}, u32[]{:S(2)}) collective-permute-start(bf16[32,16,128]{2,1,0:T(8,128)(2,1)S(1)} %get-tuple-element.28), channel_id=1, source_target_pairs={{0,3},{1,2},{2,1},{3,0},{4,7},{5,6},{6,5},{7,4},{8,11},{9,10},{10,... | collective-permute-start | bytes 393224 | tf_op jit(solution)/shard_map/ppermute | solution.py:405
  8.2 0.3 collective-permute-done.refs_1_
  8.4 1.8 %collective-permute-start.2 = (bf16[2,2,128,128]{3,2,1,0:T(8,128)(2,1)S(1)}, bf16[2,2,128,128]{3,2,1,0:T(8,128)(2,1)S(1)}, u32[]{:S(2)}, u32[]{:S(2)}) collective-permute-start(bf16[2,2,128,128]{3,2,1,0:T(8,128)(2,1)S(1)} %collective-permute-done.refs_1_), channel_id=1, source_target_pairs={{0,8},{4,0},{8,16},{12,4},{16,24},{20,12},{24,28},{28,20},{1,9},{5... | collective-permute-start | bytes 393224 | tf_op jit(solution)/shard_map/ppermute | solution.py:401
  10.3 1.5 %collective-permute-start.6 = (bf16[32,16,128]{2,1,0:T(8,128)(2,1)S(1)}, bf16[32,16,128]{2,1,0:T(8,128)(2,1)S(1)}, u32[]{:S(2)}, u32[]{:S(2)}) collective-permute-start(bf16[32,16,128]{2,1,0:T(8,128)(2,1)S(1)} %get-tuple-element.30), channel_id=1, source_target_pairs={{0,2},{1,3},{2,0},{3,1},{4,6},{5,7},{6,4},{7,5},{8,10},{9,11},{10,... | collective-permute-start | bytes 393224 | tf_op jit(solution)/shard_map/ppermute | solution.py:405
  11.8 0.0 collective-permute-done.1.refs_2_
  11.8 0.0 collective-permute-done.3.refs_5_
  11.8 0.2 collective-permute-done.4.refs_6_
  12.0 1.6 %collective-permute-done.2.refs_3_ = bf16[2,2,128,128]{3,2,1,0:T(8,128)(2,1)S(1)} collective-permute-done((bf16[2,2,128,128]{3,2,1,0:T(8,128)(2,1)S(1)}, bf16[2,2,128,128]{3,2,1,0:T(8,128)(2,1)S(1)}, u32[]{:S(2)}, u32[]{:S(2)}) %collective-permute-start.2) | collective-permute-done | bytes 131104 | tf_op jit(solution)/shard_map/ppermute | solution.py:401
  13.6 0.0 copy-done
  13.6 2.5 %gradients.2 = (bf16[32,16,128]{2,1,0:T(8,128)(2,1)S(1)}, bf16[32,16,128]{2,1,0:T(8,128)(2,1)S(1)}, bf16[32,16,128]{2,1,0:T(8,128)(2,1)S(1)}, bf16[2,2,512,128]{3,2,1,0:T(8,128)(2,1)S(1)}, f32[2,2,512,128]{3,2,1,0:T(8,128)S(1)}) custom-call(s32[4,2,256]{2,1,0:T(2,128)S(1)} %get-tuple-element.22.range_ref, bf16[128,16,128]{2,1,0:T(8,128)(2,1)S(1)} %copy-done, ...), custom_call_target="tpu_custom_call" | custom-call | flops 1006632960 | bytes 2097152 | tf_op jit(solution)/shard_map/gradients/pallas_call | solution.py:292
  16.1 0.0 collective-permute-done.6.refs_0_
  16.1 1.0 %gradients.3 = (bf16[32,16,128]{2,1,0:T(8,128)(2,1)S(1)}, f32[2,2,128,128]{3,2,1,0:T(8,128)S(1)}, bf16[2,2,128,128]{3,2,1,0:T(8,128)(2,1)S(1)}, bf16[2,2,128,128...) custom-call(s32[4,2,256]{2,1,0:T(2,128)S(1)} %get-tuple-element.22.range_ref, ...), custom_call_target="tpu_custom_call" | custom-call | flops 335544320 | bytes 2097152 | tf_op jit(solution)/shard_map/gradients/pallas_call | solution.py:292
  17.1 1.4 %collective-permute-start.7 = (bf16[2,2,128,128]{3,2,1,0:T(8,128)(2,1)S(1)}, bf16[2,2,128,128]{3,2,1,0:T(8,128)(2,1)S(1)}, u32[]{:S(2)}, u32[]{:S(2)}) collective-permute-start(bf16[2,2,128,128]{3,2,1,0:T(8,128)(2,1)S(1)} %get-tuple-element.33), channel_id=1, source_target_pairs={{0,4},{4,0},{8,12},{12,8},{16,20},{20,16},{24,28},{28,24},{1,5},{5... | collective-permute-start | bytes 393224 | tf_op jit(solution)/shard_map/ppermute | solution.py:392
  18.4 0.0 collective-permute-start.5
  18.4 1.6 %collective-permute-start.12 = (bf16[32,16,128]{2,1,0:T(8,128)(2,1)S(1)}, bf16[32,16,128]{2,1,0:T(8,128)(2,1)S(1)}, u32[]{:S(2)}, u32[]{:S(2)}) collective-permute-start(bf16[32,16,128]{2,1,0:T(8,128)(2,1)S(1)} %get-tuple-element.38), channel_id=1, source_target_pairs={{0,3},{1,2},{2,1},{3,0},{4,7},{5,6},{6,5},{7,4},{8,11},{9,10},{10,... | collective-permute-start | bytes 393224 | tf_op jit(solution)/shard_map/ppermute | solution.py:405
  20.1 0.8 %collective-permute-start.9 = (bf16[2,2,128,128]{3,2,1,0:T(8,128)(2,1)S(1)}, bf16[2,2,128,128]{3,2,1,0:T(8,128)(2,1)S(1)}, u32[]{:S(2)}, u32[]{:S(2)}) collective-permute-start(bf16[2,2,128,128]{3,2,1,0:T(8,128)(2,1)S(1)} %get-tuple-element.35), channel_id=1, source_target_pairs={{8,0},{0,4},{16,8},{4,12},{24,16},{12,20},{28,24},{20,28},{9,1},{1... | collective-permute-start | bytes 393224 | tf_op jit(solution)/shard_map/ppermute | solution.py:401
  20.9 0.4 %collective-permute-start.10 = (bf16[32,16,128]{2,1,0:T(8,128)(2,1)S(1)}, bf16[32,16,128]{2,1,0:T(8,128)(2,1)S(1)}, u32[]{:S(2)}, u32[]{:S(2)}) collective-permute-start(bf16[32,16,128]{2,1,0:T(8,128)(2,1)S(1)} %get-tuple-element.36), channel_id=1, source_target_pairs={{0,2},{1,3},{2,0},{3,1},{4,6},{5,7},{6,4},{7,5},{8,10},{9,11},{10,... | collective-permute-start | bytes 393224 | tf_op jit(solution)/shard_map/ppermute | solution.py:405
  21.3 0.8 %collective-permute-done.7.left = bf16[2,2,128,128]{3,2,1,0:T(8,128)(2,1)S(1)} collective-permute-done((bf16[2,2,128,128]{3,2,1,0:T(8,128)(2,1)S(1)}, bf16[2,2,128,128]{3,2,1,0:T(8,128)(2,1)S(1)}, u32[]{:S(2)}, u32[]{:S(2)}) %collective-permute-start.7) | collective-permute-done | bytes 131104 | tf_op jit(solution)/shard_map/ppermute | solution.py:392
  22.1 1.3 %collective-permute-start.11 = (bf16[2,2,128,128]{3,2,1,0:T(8,128)(2,1)S(1)}, bf16[2,2,128,128]{3,2,1,0:T(8,128)(2,1)S(1)}, u32[]{:S(2)}, u32[]{:S(2)}) collective-permute-start(bf16[2,2,128,128]{3,2,1,0:T(8,128)(2,1)S(1)} %get-tuple-element.37), channel_id=1, source_target_pairs={{0,4},{4,0},{8,12},{12,8},{16,20},{20,16},{24,28},{28,24},{1,5},{5... | collective-permute-start | bytes 393224 | tf_op jit(solution)/shard_map/ppermute | solution.py:392
  23.4 0.0 collective-permute-done.5.refs_0_
  23.4 1.9 %collective-permute-start.8 = (bf16[2,2,128,128]{3,2,1,0:T(8,128)(2,1)S(1)}, bf16[2,2,128,128]{3,2,1,0:T(8,128)(2,1)S(1)}, u32[]{:S(2)}, u32[]{:S(2)}) collective-permute-start(bf16[2,2,128,128]{3,2,1,0:T(8,128)(2,1)S(1)} %add.1), channel_id=1, source_target_pairs={{0,8},{4,0},{8,16},{12,4},{16,24},{20,12},{24,28},{28,20},{1,9},{5... | collective-permute-start | bytes 393224 | tf_op jit(solution)/shard_map/ppermute | solution.py:401
  25.3 0.0 collective-permute-done.12.refs_5_
  25.3 0.2 collective-permute-done.9.refs_2_
  25.6 1.5 %collective-permute-done.10.refs_3_ = bf16[32,16,128]{2,1,0:T(8,128)(2,1)S(1)} collective-permute-done((bf16[32,16,128]{2,1,0:T(8,128)(2,1)S(1)}, bf16[32,16,128]{2,1,0:T(8,128)(2,1)S(1)}, u32[]{:S(2)}, u32[]{:S(2)}) %collective-permute-start.10) | collective-permute-done | bytes 131104 | tf_op jit(solution)/shard_map/ppermute | solution.py:405
  27.0 0.8 %collective-permute-done.11.refs_4_ = bf16[2,2,128,128]{3,2,1,0:T(8,128)(2,1)S(1)} collective-permute-done((bf16[2,2,128,128]{3,2,1,0:T(8,128)(2,1)S(1)}, bf16[2,2,128,128]{3,2,1,0:T(8,128)(2,1)S(1)}, u32[]{:S(2)}, u32[]{:S(2)}) %collective-permute-start.11) | collective-permute-done | bytes 131104 | tf_op jit(solution)/shard_map/ppermute | solution.py:392
  27.8 1.4 %collective-permute-done.8.refs_1_ = bf16[2,2,128,128]{3,2,1,0:T(8,128)(2,1)S(1)} collective-permute-done((bf16[2,2,128,128]{3,2,1,0:T(8,128)(2,1)S(1)}, bf16[2,2,128,128]{3,2,1,0:T(8,128)(2,1)S(1)}, u32[]{:S(2)}, u32[]{:S(2)}) %collective-permute-start.8) | collective-permute-done | bytes 131104 | tf_op jit(solution)/shard_map/ppermute | solution.py:401
  29.2 1.0 %finish.1 = (bf16[32,64,128]{2,1,0:T(8,128)(2,1)}, bf16[128,2,128]{2,1,0:T(2,128)(2,1)}, bf16[128,2,128]{2,1,0:T(2,128)(2,1)}) custom-call(bf16[32,16,128]{2,1,0:T(8,128)(2,1)S(1)} %collective-permute-done.5.refs_0_, bf16[2,2,128,128]{3,2,1,0:T(8,128)(2,1)S(1)} %collective-permute-done.8.refs_1_, ...), custom_call_target="tpu_custom_call" | custom-call | tf_op jit(solution)/shard_map/finish/pallas_call | solution.py:367
  (1 shorter events, 0.0 us)
Async XLA Ops:
  0.6 12.9 %copy-start = (bf16[128,16,128]{2,1,0:T(8,128)(2,1)S(1)}, bf16[128,16,128]{2,1,0:T(8,128)(2,1)}, u32[]{:S(2)}) copy-start(bf16[128,16,128]{2,1,0:T(8,128)(2,1)} %q_ref.3) | copy-start | bytes 1572868
  1.9 6.5 %collective-permute-start = (bf16[2,2,128,128]{3,2,1,0:T(8,128)(2,1)S(1)}, bf16[2,2,128,128]{3,2,1,0:T(8,128)(2,1)S(1)}, u32[]{:S(2)}, u32[]{:S(2)}) collective-permute-start(bf16[2,2,128,128]{3,2,1,0:T(8,128)(2,1)S(1)} %get-tuple-element.24), channel_id=1, source_target_pairs={{0,4},{4,0},{8,12},{12,8},{16,20},{20,16},{24,28},{28,24},{1,5},{5... | collective-permute-start | bytes 393224 | tf_op jit(solution)/shard_map/ppermute | solution.py:392
  4.9 6.8 %collective-permute-start.1 = (bf16[2,2,128,128]{3,2,1,0:T(8,128)(2,1)S(1)}, bf16[2,2,128,128]{3,2,1,0:T(8,128)(2,1)S(1)}, u32[]{:S(2)}, u32[]{:S(2)}) collective-permute-start(bf16[2,2,128,128]{3,2,1,0:T(8,128)(2,1)S(1)} %get-tuple-element.25), channel_id=1, source_target_pairs={{0,8},{4,12},{8,16},{12,20},{16,24},{20,28},{24,0},{28,4},{1,9},{5... | collective-permute-start | bytes 393224 | tf_op jit(solution)/shard_map/ppermute | solution.py:388
  6.5 5.3 %collective-permute-start.3 = (bf16[32,16,128]{2,1,0:T(8,128)(2,1)S(1)}, bf16[32,16,128]{2,1,0:T(8,128)(2,1)S(1)}, u32[]{:S(2)}, u32[]{:S(2)}) collective-permute-start(bf16[32,16,128]{2,1,0:T(8,128)(2,1)S(1)} %get-tuple-element.27), channel_id=1, source_target_pairs={{0,1},{1,0},{2,3},{3,2},{4,5},{5,4},{6,7},{7,6},{8,9},{9,8},{10,11... | collective-permute-start | bytes 393224 | tf_op jit(solution)/shard_map/ppermute | solution.py:405
  6.5 5.5 %collective-permute-start.4 = (bf16[32,16,128]{2,1,0:T(8,128)(2,1)S(1)}, bf16[32,16,128]{2,1,0:T(8,128)(2,1)S(1)}, u32[]{:S(2)}, u32[]{:S(2)}) collective-permute-start(bf16[32,16,128]{2,1,0:T(8,128)(2,1)S(1)} %get-tuple-element.28), channel_id=1, source_target_pairs={{0,3},{1,2},{2,1},{3,0},{4,7},{5,6},{6,5},{7,4},{8,11},{9,10},{10,... | collective-permute-start | bytes 393224 | tf_op jit(solution)/shard_map/ppermute | solution.py:405
  8.4 5.1 %collective-permute-start.2 = (bf16[2,2,128,128]{3,2,1,0:T(8,128)(2,1)S(1)}, bf16[2,2,128,128]{3,2,1,0:T(8,128)(2,1)S(1)}, u32[]{:S(2)}, u32[]{:S(2)}) collective-permute-start(bf16[2,2,128,128]{3,2,1,0:T(8,128)(2,1)S(1)} %collective-permute-done.refs_1_), channel_id=1, source_target_pairs={{0,8},{4,0},{8,16},{12,4},{16,24},{20,12},{24,28},{28,20},{1,9},{5... | collective-permute-start | bytes 393224 | tf_op jit(solution)/shard_map/ppermute | solution.py:401
  10.3 5.8 %collective-permute-start.6 = (bf16[32,16,128]{2,1,0:T(8,128)(2,1)S(1)}, bf16[32,16,128]{2,1,0:T(8,128)(2,1)S(1)}, u32[]{:S(2)}, u32[]{:S(2)}) collective-permute-start(bf16[32,16,128]{2,1,0:T(8,128)(2,1)S(1)} %get-tuple-element.30), channel_id=1, source_target_pairs={{0,2},{1,3},{2,0},{3,1},{4,6},{5,7},{6,4},{7,5},{8,10},{9,11},{10,... | collective-permute-start | bytes 393224 | tf_op jit(solution)/shard_map/ppermute | solution.py:405
  17.1 5.0 %collective-permute-start.7 = (bf16[2,2,128,128]{3,2,1,0:T(8,128)(2,1)S(1)}, bf16[2,2,128,128]{3,2,1,0:T(8,128)(2,1)S(1)}, u32[]{:S(2)}, u32[]{:S(2)}) collective-permute-start(bf16[2,2,128,128]{3,2,1,0:T(8,128)(2,1)S(1)} %get-tuple-element.33), channel_id=1, source_target_pairs={{0,4},{4,0},{8,12},{12,8},{16,20},{20,16},{24,28},{28,24},{1,5},{5... | collective-permute-start | bytes 393224 | tf_op jit(solution)/shard_map/ppermute | solution.py:392
  18.4 5.0 %collective-permute-start.5 = (bf16[32,16,128]{2,1,0:T(8,128)(2,1)S(1)}, bf16[32,16,128]{2,1,0:T(8,128)(2,1)S(1)}, u32[]{:S(2)}, u32[]{:S(2)}) collective-permute-start(bf16[32,16,128]{2,1,0:T(8,128)(2,1)S(1)} %get-tuple-element.29), channel_id=1, source_target_pairs={{0,1},{1,0},{2,3},{3,2},{4,5},{5,4},{6,7},{7,6},{8,9},{9,8},{10,11... | collective-permute-start | bytes 393224 | tf_op jit(solution)/shard_map/ppermute | solution.py:405
  18.4 6.9 %collective-permute-start.12 = (bf16[32,16,128]{2,1,0:T(8,128)(2,1)S(1)}, bf16[32,16,128]{2,1,0:T(8,128)(2,1)S(1)}, u32[]{:S(2)}, u32[]{:S(2)}) collective-permute-start(bf16[32,16,128]{2,1,0:T(8,128)(2,1)S(1)} %get-tuple-element.38), channel_id=1, source_target_pairs={{0,3},{1,2},{2,1},{3,0},{4,7},{5,6},{6,5},{7,4},{8,11},{9,10},{10,... | collective-permute-start | bytes 393224 | tf_op jit(solution)/shard_map/ppermute | solution.py:405
  20.1 5.5 %collective-permute-start.9 = (bf16[2,2,128,128]{3,2,1,0:T(8,128)(2,1)S(1)}, bf16[2,2,128,128]{3,2,1,0:T(8,128)(2,1)S(1)}, u32[]{:S(2)}, u32[]{:S(2)}) collective-permute-start(bf16[2,2,128,128]{3,2,1,0:T(8,128)(2,1)S(1)} %get-tuple-element.35), channel_id=1, source_target_pairs={{8,0},{0,4},{16,8},{4,12},{24,16},{12,20},{28,24},{20,28},{9,1},{1... | collective-permute-start | bytes 393224 | tf_op jit(solution)/shard_map/ppermute | solution.py:401
  20.9 6.2 %collective-permute-start.10 = (bf16[32,16,128]{2,1,0:T(8,128)(2,1)S(1)}, bf16[32,16,128]{2,1,0:T(8,128)(2,1)S(1)}, u32[]{:S(2)}, u32[]{:S(2)}) collective-permute-start(bf16[32,16,128]{2,1,0:T(8,128)(2,1)S(1)} %get-tuple-element.36), channel_id=1, source_target_pairs={{0,2},{1,3},{2,0},{3,1},{4,6},{5,7},{6,4},{7,5},{8,10},{9,11},{10,... | collective-permute-start | bytes 393224 | tf_op jit(solution)/shard_map/ppermute | solution.py:405
  22.1 5.8 %collective-permute-start.11 = (bf16[2,2,128,128]{3,2,1,0:T(8,128)(2,1)S(1)}, bf16[2,2,128,128]{3,2,1,0:T(8,128)(2,1)S(1)}, u32[]{:S(2)}, u32[]{:S(2)}) collective-permute-start(bf16[2,2,128,128]{3,2,1,0:T(8,128)(2,1)S(1)} %get-tuple-element.37), channel_id=1, source_target_pairs={{0,4},{4,0},{8,12},{12,8},{16,20},{20,16},{24,28},{28,24},{1,5},{5... | collective-permute-start | bytes 393224 | tf_op jit(solution)/shard_map/ppermute | solution.py:392
  23.4 5.8 %collective-permute-start.8 = (bf16[2,2,128,128]{3,2,1,0:T(8,128)(2,1)S(1)}, bf16[2,2,128,128]{3,2,1,0:T(8,128)(2,1)S(1)}, u32[]{:S(2)}, u32[]{:S(2)}) collective-permute-start(bf16[2,2,128,128]{3,2,1,0:T(8,128)(2,1)S(1)} %add.1), channel_id=1, source_target_pairs={{0,8},{4,0},{8,16},{12,4},{16,24},{20,12},{24,28},{28,20},{1,9},{5... | collective-permute-start | bytes 393224 | tf_op jit(solution)/shard_map/ppermute | solution.py:401

commit v18 on v17

--- a/solution.py
+++ b/solution.py
@@ -328,7 +328,7 @@
 
 
 def finish_order(parts):
-    return [1, "odd", "far", *range(2, parts - 1), "even", parts - 1, 0, "own"]
+    return [1, *range(3, parts), "far", "odd", "even", 2, 0, "own"]
 
 
 def finish_kernel(parts, *refs):

time: 30.3 us -> 30.3 us (level)
  starting transfers between devices: 17 us -> 18.1 us
  waiting for transfers between devices: 6.77 us -> 5.92 us
    ppermute x6, waiting for transfers between devices: 1.69 us -> 0.73 us  [swapped(): lax.ppermute(block, 'kvh', [(i, i ^ mask) for i in range(lax.axis_size('k...]
    ppermute x6, starting transfers between devices: 5.21 us -> 6.05 us  [swapped(): lax.ppermute(block, 'kvh', [(i, i ^ mask) for i in range(lax.axis_size('k...]
    ppermute x3, starting transfers between devices: 5.69 us -> 6.47 us  [paired(): lax.ppermute(block, 'seq', [(i, i ^ 1) for i in range(lax.axis_size('seq'...]
    ppermute x3, starting transfers between devices: 4.53 us -> 4 us  [ringed(): return lax.ppermute(block, 'seq', route)]
  transfers between devices with their start and end apart: 13 -> 13, of which waited for: 8 -> 7; matrix products, arithmetic and copies ran while one was open for 0% -> 0% of each run, Pallas kernels for 8% -> 8%
where the time goes in v18:
time: 30.3 us; the launch traced here: 30.2 us
  starting transfers between devices  18.1 us (60%)
  waiting for transfers between devices  5.92 us (20%)
  Pallas kernels  5.47 us (18%)
  between operations  0.69 us (2%)
    ppermute x3, starting transfers between devices, paired(): lax.ppermute(block, 'seq', [(i, i ^ 1) for i in range(lax.axis_size('seq'...  6.47 us
    ppermute x6, starting transfers between devices, swapped(): lax.ppermute(block, 'kvh', [(i, i ^ mask) for i in range(lax.axis_size('k...  6.05 us
    ppermute x3, starting transfers between devices, ringed(): return lax.ppermute(block, 'seq', route)  4 us
    ppermute x3, waiting for transfers between devices, ringed(): return lax.ppermute(block, 'seq', route)  3.46 us
    pallas_call x2, Pallas kernels, gradients(): pl.pallas_call(functools.partial(grad_kernel, masks, parts, carried is No...  3.19 us
    ppermute x3, waiting for transfers between devices, paired(): lax.ppermute(block, 'seq', [(i, i ^ 1) for i in range(lax.axis_size('seq'...  1.72 us
    ppermute x1, starting transfers between devices, shifted(): lax.ppermute(block, 'seq', [(i, (i + distance) % count) for i in range(co...  1.58 us
    pallas_call x1, Pallas kernels, prepare(): pl.pallas_call(functools.partial(prep_kernel, parts), out_shape=(block,)...  1.3 us
  transfers between devices with their start and end apart: 13, of which 7 were waited for; matrix products, arithmetic and copies ran while one was open for 0% of the time, Pallas kernels for 8%

profile of v18, /device:TPU:0, one launch (start us, length us, event | category | flops | bytes accessed | tf_op | source)
XLA Modules:
  0.0 30.2 jit_solution(3792895121676582617)
XLA Ops:
  0.6 0.0 copy-start
  0.6 1.3 %prepare.1 = (bf16[2,2,128,128]{3,2,1,0:T(8,128)(2,1)S(1)}, bf16[2,2,128,128]{3,2,1,0:T(8,128)(2,1)S(1)}, bf16[2,2,128,128]{3,2,1,0:T(8,128)(2,1)S(1)}, bf16[32,...) custom-call(s32[8]{0:T(128)} %lengths_ref.1, ...), custom_call_target="tpu_custom_call" | custom-call | tf_op jit(solution)/shard_map/prepare/pallas_call | solution.py:90
  1.9 3.0 %collective-permute-start = (bf16[2,2,128,128]{3,2,1,0:T(8,128)(2,1)S(1)}, bf16[2,2,128,128]{3,2,1,0:T(8,128)(2,1)S(1)}, u32[]{:S(2)}, u32[]{:S(2)}) collective-permute-start(bf16[2,2,128,128]{3,2,1,0:T(8,128)(2,1)S(1)} %get-tuple-element.24), channel_id=1, source_target_pairs={{0,4},{4,0},{8,12},{12,8},{16,20},{20,16},{24,28},{28,24},{1,5},{5... | collective-permute-start | bytes 393224 | tf_op jit(solution)/shard_map/ppermute | solution.py:392
  4.9 1.6 %collective-permute-start.1 = (bf16[2,2,128,128]{3,2,1,0:T(8,128)(2,1)S(1)}, bf16[2,2,128,128]{3,2,1,0:T(8,128)(2,1)S(1)}, u32[]{:S(2)}, u32[]{:S(2)}) collective-permute-start(bf16[2,2,128,128]{3,2,1,0:T(8,128)(2,1)S(1)} %get-tuple-element.25), channel_id=1, source_target_pairs={{0,8},{4,12},{8,16},{12,20},{16,24},{20,28},{24,0},{28,4},{1,9},{5... | collective-permute-start | bytes 393224 | tf_op jit(solution)/shard_map/ppermute | solution.py:388
  6.5 0.0 collective-permute-start.3
  6.5 1.6 %collective-permute-start.4 = (bf16[32,16,128]{2,1,0:T(8,128)(2,1)S(1)}, bf16[32,16,128]{2,1,0:T(8,128)(2,1)S(1)}, u32[]{:S(2)}, u32[]{:S(2)}) collective-permute-start(bf16[32,16,128]{2,1,0:T(8,128)(2,1)S(1)} %get-tuple-element.28), channel_id=1, source_target_pairs={{0,3},{1,2},{2,1},{3,0},{4,7},{5,6},{6,5},{7,4},{8,11},{9,10},{10,... | collective-permute-start | bytes 393224 | tf_op jit(solution)/shard_map/ppermute | solution.py:405
  8.2 0.3 collective-permute-done.refs_1_
  8.4 1.8 %collective-permute-start.2 = (bf16[2,2,128,128]{3,2,1,0:T(8,128)(2,1)S(1)}, bf16[2,2,128,128]{3,2,1,0:T(8,128)(2,1)S(1)}, u32[]{:S(2)}, u32[]{:S(2)}) collective-permute-start(bf16[2,2,128,128]{3,2,1,0:T(8,128)(2,1)S(1)} %collective-permute-done.refs_1_), channel_id=1, source_target_pairs={{0,8},{4,0},{8,16},{12,4},{16,24},{20,12},{24,28},{28,20},{1,9},{5... | collective-permute-start | bytes 393224 | tf_op jit(solution)/shard_map/ppermute | solution.py:401
  10.3 1.5 %collective-permute-start.7 = (bf16[32,16,128]{2,1,0:T(8,128)(2,1)S(1)}, bf16[32,16,128]{2,1,0:T(8,128)(2,1)S(1)}, u32[]{:S(2)}, u32[]{:S(2)}) collective-permute-start(bf16[32,16,128]{2,1,0:T(8,128)(2,1)S(1)} %get-tuple-element.31), channel_id=1, source_target_pairs={{0,2},{1,3},{2,0},{3,1},{4,6},{5,7},{6,4},{7,5},{8,10},{9,11},{10,... | collective-permute-start | bytes 393224 | tf_op jit(solution)/shard_map/ppermute | solution.py:405
  11.8 0.0 collective-permute-done.1.refs_2_
  11.8 0.0 collective-permute-done.3.refs_5_
  11.8 0.2 collective-permute-done.4.refs_6_
  12.0 1.6 %collective-permute-done.2.refs_3_ = bf16[2,2,128,128]{3,2,1,0:T(8,128)(2,1)S(1)} collective-permute-done((bf16[2,2,128,128]{3,2,1,0:T(8,128)(2,1)S(1)}, bf16[2,2,128,128]{3,2,1,0:T(8,128)(2,1)S(1)}, u32[]{:S(2)}, u32[]{:S(2)}) %collective-permute-start.2) | collective-permute-done | bytes 131104 | tf_op jit(solution)/shard_map/ppermute | solution.py:401
  13.6 0.0 copy-done
  13.6 2.2 %gradients.2 = (bf16[32,16,128]{2,1,0:T(8,128)(2,1)S(1)}, bf16[32,16,128]{2,1,0:T(8,128)(2,1)S(1)}, bf16[32,16,128]{2,1,0:T(8,128)(2,1)S(1)}, bf16[2,2,512,128]{3,2,1,0:T(8,128)(2,1)S(1)}, f32[2,2,512,128]{3,2,1,0:T(8,128)S(1)}) custom-call(s32[4,2,256]{2,1,0:T(2,128)S(1)} %get-tuple-element.22.range_ref, bf16[128,16,128]{2,1,0:T(8,128)(2,1)S(1)} %copy-done, ...), custom_call_target="tpu_custom_call" | custom-call | flops 1006632960 | bytes 2097152 | tf_op jit(solution)/shard_map/gradients/pallas_call | solution.py:292
  15.8 0.0 collective-permute-done.7.refs_0_
  15.8 1.0 %gradients.3 = (bf16[32,16,128]{2,1,0:T(8,128)(2,1)S(1)}, f32[2,2,128,128]{3,2,1,0:T(8,128)S(1)}, bf16[2,2,128,128]{3,2,1,0:T(8,128)(2,1)S(1)}, bf16[2,2,128,128...) custom-call(s32[4,2,256]{2,1,0:T(2,128)S(1)} %get-tuple-element.22.range_ref, ...), custom_call_target="tpu_custom_call" | custom-call | flops 335544320 | bytes 2097152 | tf_op jit(solution)/shard_map/gradients/pallas_call | solution.py:292
  16.8 1.6 %collective-permute-start.9 = (bf16[2,2,128,128]{3,2,1,0:T(8,128)(2,1)S(1)}, bf16[2,2,128,128]{3,2,1,0:T(8,128)(2,1)S(1)}, u32[]{:S(2)}, u32[]{:S(2)}) collective-permute-start(bf16[2,2,128,128]{3,2,1,0:T(8,128)(2,1)S(1)} %get-tuple-element.35), channel_id=1, source_target_pairs={{0,4},{4,0},{8,12},{12,8},{16,20},{20,16},{24,28},{28,24},{1,5},{5... | collective-permute-start | bytes 393224 | tf_op jit(solution)/shard_map/ppermute | solution.py:392
  18.4 0.0 collective-permute-start.5
  18.4 1.6 %collective-permute-start.6 = (bf16[32,16,128]{2,1,0:T(8,128)(2,1)S(1)}, bf16[32,16,128]{2,1,0:T(8,128)(2,1)S(1)}, u32[]{:S(2)}, u32[]{:S(2)}) collective-permute-start(bf16[32,16,128]{2,1,0:T(8,128)(2,1)S(1)} %get-tuple-element.30), channel_id=1, source_target_pairs={{0,3},{1,2},{2,1},{3,0},{4,7},{5,6},{6,5},{7,4},{8,11},{9,10},{10,... | collective-permute-start | bytes 393224 | tf_op jit(solution)/shard_map/ppermute | solution.py:405
  20.1 0.5 %collective-permute-start.8 = (bf16[2,2,128,128]{3,2,1,0:T(8,128)(2,1)S(1)}, bf16[2,2,128,128]{3,2,1,0:T(8,128)(2,1)S(1)}, u32[]{:S(2)}, u32[]{:S(2)}) collective-permute-start(bf16[2,2,128,128]{3,2,1,0:T(8,128)(2,1)S(1)} %get-tuple-element.34), channel_id=1, source_target_pairs={{8,0},{0,4},{16,8},{4,12},{24,16},{12,20},{28,24},{20,28},{9,1},{1... | collective-permute-start | bytes 393224 | tf_op jit(solution)/shard_map/ppermute | solution.py:401
  20.6 1.8 %collective-permute-start.11 = (bf16[2,2,128,128]{3,2,1,0:T(8,128)(2,1)S(1)}, bf16[2,2,128,128]{3,2,1,0:T(8,128)(2,1)S(1)}, u32[]{:S(2)}, u32[]{:S(2)}) collective-permute-start(bf16[2,2,128,128]{3,2,1,0:T(8,128)(2,1)S(1)} %get-tuple-element.37), channel_id=1, source_target_pairs={{0,4},{4,0},{8,12},{12,8},{16,20},{20,16},{24,28},{28,24},{1,5},{5... | collective-permute-start | bytes 393224 | tf_op jit(solution)/shard_map/ppermute | solution.py:392
  22.4 0.0 collective-permute-done.9.left
  22.4 1.3 %collective-permute-start.12 = (bf16[32,16,128]{2,1,0:T(8,128)(2,1)S(1)}, bf16[32,16,128]{2,1,0:T(8,128)(2,1)S(1)}, u32[]{:S(2)}, u32[]{:S(2)}) collective-permute-start(bf16[32,16,128]{2,1,0:T(8,128)(2,1)S(1)} %get-tuple-element.38), channel_id=1, source_target_pairs={{0,2},{1,3},{2,0},{3,1},{4,6},{5,7},{6,4},{7,5},{8,10},{9,11},{10,... | collective-permute-start | bytes 393224 | tf_op jit(solution)/shard_map/ppermute | solution.py:405
  23.7 0.0 collective-permute-done.5.refs_0_
  23.8 1.6 %collective-permute-start.10 = (bf16[2,2,128,128]{3,2,1,0:T(8,128)(2,1)S(1)}, bf16[2,2,128,128]{3,2,1,0:T(8,128)(2,1)S(1)}, u32[]{:S(2)}, u32[]{:S(2)}) collective-permute-start(bf16[2,2,128,128]{3,2,1,0:T(8,128)(2,1)S(1)} %add.1), channel_id=1, source_target_pairs={{0,8},{4,0},{8,16},{12,4},{16,24},{20,12},{24,28},{28,20},{1,9},{5... | collective-permute-start | bytes 393224 | tf_op jit(solution)/shard_map/ppermute | solution.py:401
  25.4 0.0 collective-permute-done.6.refs_1_
  25.4 0.1 collective-permute-done.8.refs_2_
  25.5 1.4 %collective-permute-done.11.refs_4_ = bf16[2,2,128,128]{3,2,1,0:T(8,128)(2,1)S(1)} collective-permute-done((bf16[2,2,128,128]{3,2,1,0:T(8,128)(2,1)S(1)}, bf16[2,2,128,128]{3,2,1,0:T(8,128)(2,1)S(1)}, u32[]{:S(2)}, u32[]{:S(2)}) %collective-permute-start.11) | collective-permute-done | bytes 131104 | tf_op jit(solution)/shard_map/ppermute | solution.py:392
  26.9 0.5 %collective-permute-done.12.refs_5_ = bf16[32,16,128]{2,1,0:T(8,128)(2,1)S(1)} collective-permute-done((bf16[32,16,128]{2,1,0:T(8,128)(2,1)S(1)}, bf16[32,16,128]{2,1,0:T(8,128)(2,1)S(1)}, u32[]{:S(2)}, u32[]{:S(2)}) %collective-permute-start.12) | collective-permute-done | bytes 131104 | tf_op jit(solution)/shard_map/ppermute | solution.py:405
  27.4 1.8 %collective-permute-done.10.refs_3_ = bf16[2,2,128,128]{3,2,1,0:T(8,128)(2,1)S(1)} collective-permute-done((bf16[2,2,128,128]{3,2,1,0:T(8,128)(2,1)S(1)}, bf16[2,2,128,128]{3,2,1,0:T(8,128)(2,1)S(1)}, u32[]{:S(2)}, u32[]{:S(2)}) %collective-permute-start.10) | collective-permute-done | bytes 131104 | tf_op jit(solution)/shard_map/ppermute | solution.py:401
  29.2 1.0 %finish.1 = (bf16[32,64,128]{2,1,0:T(8,128)(2,1)}, bf16[128,2,128]{2,1,0:T(2,128)(2,1)}, bf16[128,2,128]{2,1,0:T(2,128)(2,1)}) custom-call(bf16[32,16,128]{2,1,0:T(8,128)(2,1)S(1)} %collective-permute-done.5.refs_0_, bf16[32,16,128]{2,1,0:T(8,128)(2,1)S(1)} %collective-permute-done.6.refs_1_, bf16[2,2,128,128]{3,2,1,0:T(8,128)(2,1)S(1)} %collective-permute-done.8.refs_2_, ...), custom_call_target="tpu_custom_call" | custom-call | tf_op jit(solution)/shard_map/finish/pallas_call | solution.py:367
  (1 shorter events, 0.0 us)
Async XLA Ops:
  0.6 12.9 %copy-start = (bf16[128,16,128]{2,1,0:T(8,128)(2,1)S(1)}, bf16[128,16,128]{2,1,0:T(8,128)(2,1)}, u32[]{:S(2)}) copy-start(bf16[128,16,128]{2,1,0:T(8,128)(2,1)} %q_ref.3) | copy-start | bytes 1572868
  1.9 6.5 %collective-permute-start = (bf16[2,2,128,128]{3,2,1,0:T(8,128)(2,1)S(1)}, bf16[2,2,128,128]{3,2,1,0:T(8,128)(2,1)S(1)}, u32[]{:S(2)}, u32[]{:S(2)}) collective-permute-start(bf16[2,2,128,128]{3,2,1,0:T(8,128)(2,1)S(1)} %get-tuple-element.24), channel_id=1, source_target_pairs={{0,4},{4,0},{8,12},{12,8},{16,20},{20,16},{24,28},{28,24},{1,5},{5... | collective-permute-start | bytes 393224 | tf_op jit(solution)/shard_map/ppermute | solution.py:392
  4.9 6.8 %collective-permute-start.1 = (bf16[2,2,128,128]{3,2,1,0:T(8,128)(2,1)S(1)}, bf16[2,2,128,128]{3,2,1,0:T(8,128)(2,1)S(1)}, u32[]{:S(2)}, u32[]{:S(2)}) collective-permute-start(bf16[2,2,128,128]{3,2,1,0:T(8,128)(2,1)S(1)} %get-tuple-element.25), channel_id=1, source_target_pairs={{0,8},{4,12},{8,16},{12,20},{16,24},{20,28},{24,0},{28,4},{1,9},{5... | collective-permute-start | bytes 393224 | tf_op jit(solution)/shard_map/ppermute | solution.py:388
  6.5 5.3 %collective-permute-start.3 = (bf16[32,16,128]{2,1,0:T(8,128)(2,1)S(1)}, bf16[32,16,128]{2,1,0:T(8,128)(2,1)S(1)}, u32[]{:S(2)}, u32[]{:S(2)}) collective-permute-start(bf16[32,16,128]{2,1,0:T(8,128)(2,1)S(1)} %get-tuple-element.27), channel_id=1, source_target_pairs={{0,1},{1,0},{2,3},{3,2},{4,5},{5,4},{6,7},{7,6},{8,9},{9,8},{10,11... | collective-permute-start | bytes 393224 | tf_op jit(solution)/shard_map/ppermute | solution.py:405
  6.5 5.5 %collective-permute-start.4 = (bf16[32,16,128]{2,1,0:T(8,128)(2,1)S(1)}, bf16[32,16,128]{2,1,0:T(8,128)(2,1)S(1)}, u32[]{:S(2)}, u32[]{:S(2)}) collective-permute-start(bf16[32,16,128]{2,1,0:T(8,128)(2,1)S(1)} %get-tuple-element.28), channel_id=1, source_target_pairs={{0,3},{1,2},{2,1},{3,0},{4,7},{5,6},{6,5},{7,4},{8,11},{9,10},{10,... | collective-permute-start | bytes 393224 | tf_op jit(solution)/shard_map/ppermute | solution.py:405
  8.4 5.1 %collective-permute-start.2 = (bf16[2,2,128,128]{3,2,1,0:T(8,128)(2,1)S(1)}, bf16[2,2,128,128]{3,2,1,0:T(8,128)(2,1)S(1)}, u32[]{:S(2)}, u32[]{:S(2)}) collective-permute-start(bf16[2,2,128,128]{3,2,1,0:T(8,128)(2,1)S(1)} %collective-permute-done.refs_1_), channel_id=1, source_target_pairs={{0,8},{4,0},{8,16},{12,4},{16,24},{20,12},{24,28},{28,20},{1,9},{5... | collective-permute-start | bytes 393224 | tf_op jit(solution)/shard_map/ppermute | solution.py:401
  10.3 5.5 %collective-permute-start.7 = (bf16[32,16,128]{2,1,0:T(8,128)(2,1)S(1)}, bf16[32,16,128]{2,1,0:T(8,128)(2,1)S(1)}, u32[]{:S(2)}, u32[]{:S(2)}) collective-permute-start(bf16[32,16,128]{2,1,0:T(8,128)(2,1)S(1)} %get-tuple-element.31), channel_id=1, source_target_pairs={{0,2},{1,3},{2,0},{3,1},{4,6},{5,7},{6,4},{7,5},{8,10},{9,11},{10,... | collective-permute-start | bytes 393224 | tf_op jit(solution)/shard_map/ppermute | solution.py:405
  16.8 5.7 %collective-permute-start.9 = (bf16[2,2,128,128]{3,2,1,0:T(8,128)(2,1)S(1)}, bf16[2,2,128,128]{3,2,1,0:T(8,128)(2,1)S(1)}, u32[]{:S(2)}, u32[]{:S(2)}) collective-permute-start(bf16[2,2,128,128]{3,2,1,0:T(8,128)(2,1)S(1)} %get-tuple-element.35), channel_id=1, source_target_pairs={{0,4},{4,0},{8,12},{12,8},{16,20},{20,16},{24,28},{28,24},{1,5},{5... | collective-permute-start | bytes 393224 | tf_op jit(solution)/shard_map/ppermute | solution.py:392
  18.4 5.3 %collective-permute-start.5 = (bf16[32,16,128]{2,1,0:T(8,128)(2,1)S(1)}, bf16[32,16,128]{2,1,0:T(8,128)(2,1)S(1)}, u32[]{:S(2)}, u32[]{:S(2)}) collective-permute-start(bf16[32,16,128]{2,1,0:T(8,128)(2,1)S(1)} %get-tuple-element.29), channel_id=1, source_target_pairs={{0,1},{1,0},{2,3},{3,2},{4,5},{5,4},{6,7},{7,6},{8,9},{9,8},{10,11... | collective-permute-start | bytes 393224 | tf_op jit(solution)/shard_map/ppermute | solution.py:405
  18.4 7.0 %collective-permute-start.6 = (bf16[32,16,128]{2,1,0:T(8,128)(2,1)S(1)}, bf16[32,16,128]{2,1,0:T(8,128)(2,1)S(1)}, u32[]{:S(2)}, u32[]{:S(2)}) collective-permute-start(bf16[32,16,128]{2,1,0:T(8,128)(2,1)S(1)} %get-tuple-element.30), channel_id=1, source_target_pairs={{0,3},{1,2},{2,1},{3,0},{4,7},{5,6},{6,5},{7,4},{8,11},{9,10},{10,... | collective-permute-start | bytes 393224 | tf_op jit(solution)/shard_map/ppermute | solution.py:405
  20.1 5.4 %collective-permute-start.8 = (bf16[2,2,128,128]{3,2,1,0:T(8,128)(2,1)S(1)}, bf16[2,2,128,128]{3,2,1,0:T(8,128)(2,1)S(1)}, u32[]{:S(2)}, u32[]{:S(2)}) collective-permute-start(bf16[2,2,128,128]{3,2,1,0:T(8,128)(2,1)S(1)} %get-tuple-element.34), channel_id=1, source_target_pairs={{8,0},{0,4},{16,8},{4,12},{24,16},{12,20},{28,24},{20,28},{9,1},{1... | collective-permute-start | bytes 393224 | tf_op jit(solution)/shard_map/ppermute | solution.py:401
  20.6 6.3 %collective-permute-start.11 = (bf16[2,2,128,128]{3,2,1,0:T(8,128)(2,1)S(1)}, bf16[2,2,128,128]{3,2,1,0:T(8,128)(2,1)S(1)}, u32[]{:S(2)}, u32[]{:S(2)}) collective-permute-start(bf16[2,2,128,128]{3,2,1,0:T(8,128)(2,1)S(1)} %get-tuple-element.37), channel_id=1, source_target_pairs={{0,4},{4,0},{8,12},{12,8},{16,20},{20,16},{24,28},{28,24},{1,5},{5... | collective-permute-start | bytes 393224 | tf_op jit(solution)/shard_map/ppermute | solution.py:392
  22.4 5.0 %collective-permute-start.12 = (bf16[32,16,128]{2,1,0:T(8,128)(2,1)S(1)}, bf16[32,16,128]{2,1,0:T(8,128)(2,1)S(1)}, u32[]{:S(2)}, u32[]{:S(2)}) collective-permute-start(bf16[32,16,128]{2,1,0:T(8,128)(2,1)S(1)} %get-tuple-element.38), channel_id=1, source_target_pairs={{0,2},{1,3},{2,0},{3,1},{4,6},{5,7},{6,4},{7,5},{8,10},{9,11},{10,... | collective-permute-start | bytes 393224 | tf_op jit(solution)/shard_map/ppermute | solution.py:405
  23.8 5.5 %collective-permute-start.10 = (bf16[2,2,128,128]{3,2,1,0:T(8,128)(2,1)S(1)}, bf16[2,2,128,128]{3,2,1,0:T(8,128)(2,1)S(1)}, u32[]{:S(2)}, u32[]{:S(2)}) collective-permute-start(bf16[2,2,128,128]{3,2,1,0:T(8,128)(2,1)S(1)} %add.1), channel_id=1, source_target_pairs={{0,8},{4,0},{8,16},{12,4},{16,24},{20,12},{24,28},{28,20},{1,9},{5... | collective-permute-start | bytes 393224 | tf_op jit(solution)/shard_map/ppermute | solution.py:401

commit v19 on v18

--- a/solution.py
+++ b/solution.py
@@ -240,9 +240,9 @@
         dq = jnp.transpose(dq * scale).reshape(tokens, group_size, size)
         dqs[place][:, pl.ds(group * group_size, group_size)] = dq.astype(jnp.bfloat16)
 
-    def chunk(place, width):
-        starts = {place: jnp.clip(lowest[place], 0, reach - width)}
-        here = [item for item, (of_place, _) in enumerate(items) if of_place == place]
+    def run(places, width):
+        starts = {place: jnp.clip(lowest[place], 0, reach - width) for place in places}
+        here = [item for item, (place, _) in enumerate(items) if place in places]
         top = scores_of(here[0], starts, width)
         for item in here:
             later = scores_of(item + 1, starts, width) if item + 1 in here else None
@@ -253,12 +253,19 @@
     lowest = [jnp.min(range_ref[mask, 0:1, :]) & -ALIGN for mask in masks]
     needed = [jnp.max(range_ref[mask, 1:2, :]) - low for mask, low in zip(masks, lowest)]
     widths = [width for width in WIDTHS if width < reach] + [reach]
-    for place in range(len(masks)):
-        for floor, width in zip([-1] + widths, widths):
-            fits = needed[place] > floor
-            if width < reach:
-                fits = fits & (needed[place] <= width)
-            pl.when(fits)(functools.partial(chunk, place, width))
+    every = range(len(masks))
+    together = functools.reduce(jnp.maximum, needed) <= widths[0]
+    pl.when(together)(functools.partial(run, every, widths[0]))
+
+    def apart():
+        for place in every:
+            for floor, width in zip([-1] + widths, widths):
+                fits = needed[place] > floor
+                if width < reach:
+                    fits = fits & (needed[place] <= width)
+                pl.when(fits)(functools.partial(run, [place], width))
+
+    pl.when(jnp.logical_not(together))(apart)
 
     if not is_last:
         return

time: 30.3 us -> 30.8 us (1.017)
  starting transfers between devices: 18.1 us -> 20.6 us
  waiting for transfers between devices: 5.92 us -> 4.62 us
  Pallas kernels: 5.47 us -> 4.85 us
    ppermute x3, starting transfers between devices: 6.47 us -> 8.13 us  [paired(): lax.ppermute(block, 'seq', [(i, i ^ 1) for i in range(lax.axis_size('seq'...]
    ppermute x3, starting transfers between devices: 4 us -> 5.58 us  [ringed(): return lax.ppermute(block, 'seq', route)]
    ppermute x3, waiting for transfers between devices: 1.72 us -> 0.84 us  [paired(): lax.ppermute(block, 'seq', [(i, i ^ 1) for i in range(lax.axis_size('seq'...]
    ppermute x6, starting transfers between devices: 6.05 us -> 5.3 us  [swapped(): lax.ppermute(block, 'kvh', [(i, i ^ mask) for i in range(lax.axis_size('k...]
    pallas_call x2, Pallas kernels: 3.19 us -> 2.57 us  [gradients(): pl.pallas_call(functools.partial(grad_kernel, masks, parts, carried is No...]
    ppermute x3, waiting for transfers between devices: 3.46 us -> 2.9 us  [ringed(): return lax.ppermute(block, 'seq', route)]
  transfers between devices with their start and end apart: 13 -> 13, of which waited for: 7 -> 6; matrix products, arithmetic and copies ran while one was open for 0% -> 0% of each run, Pallas kernels for 8% -> 5%
where the time goes in v19:
time: 30.8 us; the launch traced here: 30.7 us
  starting transfers between devices  20.6 us (67%)
  Pallas kernels  4.85 us (16%)
  waiting for transfers between devices  4.62 us (15%)
  between operations  0.69 us (2%)
    ppermute x3, starting transfers between devices, paired(): lax.ppermute(block, 'seq', [(i, i ^ 1) for i in range(lax.axis_size('seq'...  8.13 us
    ppermute x3, starting transfers between devices, ringed(): return lax.ppermute(block, 'seq', route)  5.58 us
    ppermute x6, starting transfers between devices, swapped(): lax.ppermute(block, 'kvh', [(i, i ^ mask) for i in range(lax.axis_size('k...  5.3 us
    ppermute x3, waiting for transfers between devices, ringed(): return lax.ppermute(block, 'seq', route)  2.9 us
    pallas_call x2, Pallas kernels, gradients(): pl.pallas_call(functools.partial(grad_kernel, masks, parts, carried is No...  2.57 us
    ppermute x1, starting transfers between devices, shifted(): lax.ppermute(block, 'seq', [(i, (i + distance) % count) for i in range(co...  1.58 us
    pallas_call x1, Pallas kernels, prepare(): pl.pallas_call(functools.partial(prep_kernel, parts), out_shape=(block,)...  1.3 us
    pallas_call x1, Pallas kernels, finish(): pl.pallas_call(functools.partial(finish_kernel, parts), out_shape=(jax.Sh...  0.95 us
  transfers between devices with their start and end apart: 13, of which 6 were waited for; matrix products, arithmetic and copies ran while one was open for 0% of the time, Pallas kernels for 5%

profile of v19, /device:TPU:0, one launch (start us, length us, event | category | flops | bytes accessed | tf_op | source)
XLA Modules:
  0.0 30.7 jit_solution(1338469032958358447)
XLA Ops:
  0.6 0.0 copy-start
  0.6 1.3 %prepare.1 = (bf16[2,2,128,128]{3,2,1,0:T(8,128)(2,1)S(1)}, bf16[2,2,128,128]{3,2,1,0:T(8,128)(2,1)S(1)}, bf16[2,2,128,128]{3,2,1,0:T(8,128)(2,1)S(1)}, bf16[32,...) custom-call(s32[8]{0:T(128)} %lengths_ref.1, ...), custom_call_target="tpu_custom_call" | custom-call | tf_op jit(solution)/shard_map/prepare/pallas_call | solution.py:90
  1.9 3.0 %collective-permute-start = (bf16[2,2,128,128]{3,2,1,0:T(8,128)(2,1)S(1)}, bf16[2,2,128,128]{3,2,1,0:T(8,128)(2,1)S(1)}, u32[]{:S(2)}, u32[]{:S(2)}) collective-permute-start(bf16[2,2,128,128]{3,2,1,0:T(8,128)(2,1)S(1)} %get-tuple-element.24), channel_id=1, source_target_pairs={{0,4},{4,0},{8,12},{12,8},{16,20},{20,16},{24,28},{28,24},{1,5},{5... | collective-permute-start | bytes 393224 | tf_op jit(solution)/shard_map/ppermute | solution.py:399
  4.9 1.6 %collective-permute-start.1 = (bf16[2,2,128,128]{3,2,1,0:T(8,128)(2,1)S(1)}, bf16[2,2,128,128]{3,2,1,0:T(8,128)(2,1)S(1)}, u32[]{:S(2)}, u32[]{:S(2)}) collective-permute-start(bf16[2,2,128,128]{3,2,1,0:T(8,128)(2,1)S(1)} %get-tuple-element.25), channel_id=1, source_target_pairs={{0,8},{4,12},{8,16},{12,20},{16,24},{20,28},{24,0},{28,4},{1,9},{5... | collective-permute-start | bytes 393224 | tf_op jit(solution)/shard_map/ppermute | solution.py:395
  6.5 0.0 collective-permute-start.3
  6.5 1.6 %collective-permute-start.4 = (bf16[32,16,128]{2,1,0:T(8,128)(2,1)S(1)}, bf16[32,16,128]{2,1,0:T(8,128)(2,1)S(1)}, u32[]{:S(2)}, u32[]{:S(2)}) collective-permute-start(bf16[32,16,128]{2,1,0:T(8,128)(2,1)S(1)} %get-tuple-element.28), channel_id=1, source_target_pairs={{0,3},{1,2},{2,1},{3,0},{4,7},{5,6},{6,5},{7,4},{8,11},{9,10},{10,... | collective-permute-start | bytes 393224 | tf_op jit(solution)/shard_map/ppermute | solution.py:412
  8.2 0.3 collective-permute-done.refs_1_
  8.4 1.8 %collective-permute-start.2 = (bf16[2,2,128,128]{3,2,1,0:T(8,128)(2,1)S(1)}, bf16[2,2,128,128]{3,2,1,0:T(8,128)(2,1)S(1)}, u32[]{:S(2)}, u32[]{:S(2)}) collective-permute-start(bf16[2,2,128,128]{3,2,1,0:T(8,128)(2,1)S(1)} %collective-permute-done.refs_1_), channel_id=1, source_target_pairs={{0,8},{4,0},{8,16},{12,4},{16,24},{20,12},{24,28},{28,20},{1,9},{5... | collective-permute-start | bytes 393224 | tf_op jit(solution)/shard_map/ppermute | solution.py:408
  10.3 1.5 %collective-permute-start.7 = (bf16[32,16,128]{2,1,0:T(8,128)(2,1)S(1)}, bf16[32,16,128]{2,1,0:T(8,128)(2,1)S(1)}, u32[]{:S(2)}, u32[]{:S(2)}) collective-permute-start(bf16[32,16,128]{2,1,0:T(8,128)(2,1)S(1)} %get-tuple-element.31), channel_id=1, source_target_pairs={{0,2},{1,3},{2,0},{3,1},{4,6},{5,7},{6,4},{7,5},{8,10},{9,11},{10,... | collective-permute-start | bytes 393224 | tf_op jit(solution)/shard_map/ppermute | solution.py:412
  11.8 0.0 collective-permute-done.1.refs_2_
  11.8 0.0 collective-permute-done.3.refs_5_
  11.8 0.2 collective-permute-done.4.refs_6_
  12.0 1.6 %collective-permute-done.2.refs_3_ = bf16[2,2,128,128]{3,2,1,0:T(8,128)(2,1)S(1)} collective-permute-done((bf16[2,2,128,128]{3,2,1,0:T(8,128)(2,1)S(1)}, bf16[2,2,128,128]{3,2,1,0:T(8,128)(2,1)S(1)}, u32[]{:S(2)}, u32[]{:S(2)}) %collective-permute-start.2) | collective-permute-done | bytes 131104 | tf_op jit(solution)/shard_map/ppermute | solution.py:408
  13.6 0.0 copy-done
  13.6 1.6 %gradients.2 = (bf16[32,16,128]{2,1,0:T(8,128)(2,1)S(1)}, bf16[32,16,128]{2,1,0:T(8,128)(2,1)S(1)}, bf16[32,16,128]{2,1,0:T(8,128)(2,1)S(1)}, bf16[2,2,512,128]{3,2,1,0:T(8,128)(2,1)S(1)}, f32[2,2,512,128]{3,2,1,0:T(8,128)S(1)}) custom-call(s32[4,2,256]{2,1,0:T(2,128)S(1)} %get-tuple-element.22.range_ref, bf16[128,16,128]{2,1,0:T(8,128)(2,1)S(1)} %copy-done, ...), custom_call_target="tpu_custom_call" | custom-call | flops 1006632960 | bytes 2097152 | tf_op jit(solution)/shard_map/gradients/pallas_call | solution.py:299
  15.2 0.0 collective-permute-done.7.refs_0_
  15.2 0.9 %gradients.3 = (bf16[32,16,128]{2,1,0:T(8,128)(2,1)S(1)}, f32[2,2,128,128]{3,2,1,0:T(8,128)S(1)}, bf16[2,2,128,128]{3,2,1,0:T(8,128)(2,1)S(1)}, bf16[2,2,128,128...) custom-call(s32[4,2,256]{2,1,0:T(2,128)S(1)} %get-tuple-element.22.range_ref, ...), custom_call_target="tpu_custom_call" | custom-call | flops 335544320 | bytes 2097152 | tf_op jit(solution)/shard_map/gradients/pallas_call | solution.py:299
  16.2 1.6 %collective-permute-start.9 = (bf16[2,2,128,128]{3,2,1,0:T(8,128)(2,1)S(1)}, bf16[2,2,128,128]{3,2,1,0:T(8,128)(2,1)S(1)}, u32[]{:S(2)}, u32[]{:S(2)}) collective-permute-start(bf16[2,2,128,128]{3,2,1,0:T(8,128)(2,1)S(1)} %get-tuple-element.35), channel_id=1, source_target_pairs={{0,4},{4,0},{8,12},{12,8},{16,20},{20,16},{24,28},{28,24},{1,5},{5... | collective-permute-start | bytes 393224 | tf_op jit(solution)/shard_map/ppermute | solution.py:399
  17.8 0.0 collective-permute-start.5
  17.8 1.6 %collective-permute-start.6 = (bf16[32,16,128]{2,1,0:T(8,128)(2,1)S(1)}, bf16[32,16,128]{2,1,0:T(8,128)(2,1)S(1)}, u32[]{:S(2)}, u32[]{:S(2)}) collective-permute-start(bf16[32,16,128]{2,1,0:T(8,128)(2,1)S(1)} %get-tuple-element.30), channel_id=1, source_target_pairs={{0,3},{1,2},{2,1},{3,0},{4,7},{5,6},{6,5},{7,4},{8,11},{9,10},{10,... | collective-permute-start | bytes 393224 | tf_op jit(solution)/shard_map/ppermute | solution.py:412
  19.5 0.5 %collective-permute-start.8 = (bf16[2,2,128,128]{3,2,1,0:T(8,128)(2,1)S(1)}, bf16[2,2,128,128]{3,2,1,0:T(8,128)(2,1)S(1)}, u32[]{:S(2)}, u32[]{:S(2)}) collective-permute-start(bf16[2,2,128,128]{3,2,1,0:T(8,128)(2,1)S(1)} %get-tuple-element.34), channel_id=1, source_target_pairs={{8,0},{0,4},{16,8},{4,12},{24,16},{12,20},{28,24},{20,28},{9,1},{1... | collective-permute-start | bytes 393224 | tf_op jit(solution)/shard_map/ppermute | solution.py:408
  20.0 3.5 %collective-permute-start.11 = (bf16[2,2,128,128]{3,2,1,0:T(8,128)(2,1)S(1)}, bf16[2,2,128,128]{3,2,1,0:T(8,128)(2,1)S(1)}, u32[]{:S(2)}, u32[]{:S(2)}) collective-permute-start(bf16[2,2,128,128]{3,2,1,0:T(8,128)(2,1)S(1)} %get-tuple-element.37), channel_id=1, source_target_pairs={{0,4},{4,0},{8,12},{12,8},{16,20},{20,16},{24,28},{28,24},{1,5},{5... | collective-permute-start | bytes 393224 | tf_op jit(solution)/shard_map/ppermute | solution.py:399
  23.5 0.0 collective-permute-done.9.left
  23.5 0.5 %collective-permute-start.12 = (bf16[32,16,128]{2,1,0:T(8,128)(2,1)S(1)}, bf16[32,16,128]{2,1,0:T(8,128)(2,1)S(1)}, u32[]{:S(2)}, u32[]{:S(2)}) collective-permute-start(bf16[32,16,128]{2,1,0:T(8,128)(2,1)S(1)} %get-tuple-element.38), channel_id=1, source_target_pairs={{0,2},{1,3},{2,0},{3,1},{4,6},{5,7},{6,4},{7,5},{8,10},{9,11},{10,... | collective-permute-start | bytes 393224 | tf_op jit(solution)/shard_map/ppermute | solution.py:412
  24.0 0.0 collective-permute-done.5.refs_0_
  24.0 3.2 %collective-permute-start.10 = (bf16[2,2,128,128]{3,2,1,0:T(8,128)(2,1)S(1)}, bf16[2,2,128,128]{3,2,1,0:T(8,128)(2,1)S(1)}, u32[]{:S(2)}, u32[]{:S(2)}) collective-permute-start(bf16[2,2,128,128]{3,2,1,0:T(8,128)(2,1)S(1)} %add.1), channel_id=1, source_target_pairs={{0,8},{4,0},{8,16},{12,4},{16,24},{20,12},{24,28},{28,20},{1,9},{5... | collective-permute-start | bytes 393224 | tf_op jit(solution)/shard_map/ppermute | solution.py:408
  27.3 0.0 collective-permute-done.6.refs_1_
  27.3 0.0 collective-permute-done.8.refs_2_
  27.3 0.6 %collective-permute-done.11.refs_4_ = bf16[2,2,128,128]{3,2,1,0:T(8,128)(2,1)S(1)} collective-permute-done((bf16[2,2,128,128]{3,2,1,0:T(8,128)(2,1)S(1)}, bf16[2,2,128,128]{3,2,1,0:T(8,128)(2,1)S(1)}, u32[]{:S(2)}, u32[]{:S(2)}) %collective-permute-start.11) | collective-permute-done | bytes 131104 | tf_op jit(solution)/shard_map/ppermute | solution.py:399
  27.8 0.6 %collective-permute-done.12.refs_5_ = bf16[32,16,128]{2,1,0:T(8,128)(2,1)S(1)} collective-permute-done((bf16[32,16,128]{2,1,0:T(8,128)(2,1)S(1)}, bf16[32,16,128]{2,1,0:T(8,128)(2,1)S(1)}, u32[]{:S(2)}, u32[]{:S(2)}) %collective-permute-start.12) | collective-permute-done | bytes 131104 | tf_op jit(solution)/shard_map/ppermute | solution.py:412
  28.5 1.3 %collective-permute-done.10.refs_3_ = bf16[2,2,128,128]{3,2,1,0:T(8,128)(2,1)S(1)} collective-permute-done((bf16[2,2,128,128]{3,2,1,0:T(8,128)(2,1)S(1)}, bf16[2,2,128,128]{3,2,1,0:T(8,128)(2,1)S(1)}, u32[]{:S(2)}, u32[]{:S(2)}) %collective-permute-start.10) | collective-permute-done | bytes 131104 | tf_op jit(solution)/shard_map/ppermute | solution.py:408
  29.8 1.0 %finish.1 = (bf16[32,64,128]{2,1,0:T(8,128)(2,1)}, bf16[128,2,128]{2,1,0:T(2,128)(2,1)}, bf16[128,2,128]{2,1,0:T(2,128)(2,1)}) custom-call(bf16[32,16,128]{2,1,0:T(8,128)(2,1)S(1)} %collective-permute-done.5.refs_0_, bf16[32,16,128]{2,1,0:T(8,128)(2,1)S(1)} %collective-permute-done.6.refs_1_, bf16[2,2,128,128]{3,2,1,0:T(8,128)(2,1)S(1)} %collective-permute-done.8.refs_2_, ...), custom_call_target="tpu_custom_call" | custom-call | tf_op jit(solution)/shard_map/finish/pallas_call | solution.py:374
  (1 shorter events, 0.0 us)
Async XLA Ops:
  0.6 12.9 %copy-start = (bf16[128,16,128]{2,1,0:T(8,128)(2,1)S(1)}, bf16[128,16,128]{2,1,0:T(8,128)(2,1)}, u32[]{:S(2)}) copy-start(bf16[128,16,128]{2,1,0:T(8,128)(2,1)} %q_ref.3) | copy-start | bytes 1572868
  1.9 6.5 %collective-permute-start = (bf16[2,2,128,128]{3,2,1,0:T(8,128)(2,1)S(1)}, bf16[2,2,128,128]{3,2,1,0:T(8,128)(2,1)S(1)}, u32[]{:S(2)}, u32[]{:S(2)}) collective-permute-start(bf16[2,2,128,128]{3,2,1,0:T(8,128)(2,1)S(1)} %get-tuple-element.24), channel_id=1, source_target_pairs={{0,4},{4,0},{8,12},{12,8},{16,20},{20,16},{24,28},{28,24},{1,5},{5... | collective-permute-start | bytes 393224 | tf_op jit(solution)/shard_map/ppermute | solution.py:399
  4.9 6.8 %collective-permute-start.1 = (bf16[2,2,128,128]{3,2,1,0:T(8,128)(2,1)S(1)}, bf16[2,2,128,128]{3,2,1,0:T(8,128)(2,1)S(1)}, u32[]{:S(2)}, u32[]{:S(2)}) collective-permute-start(bf16[2,2,128,128]{3,2,1,0:T(8,128)(2,1)S(1)} %get-tuple-element.25), channel_id=1, source_target_pairs={{0,8},{4,12},{8,16},{12,20},{16,24},{20,28},{24,0},{28,4},{1,9},{5... | collective-permute-start | bytes 393224 | tf_op jit(solution)/shard_map/ppermute | solution.py:395
  6.5 5.3 %collective-permute-start.3 = (bf16[32,16,128]{2,1,0:T(8,128)(2,1)S(1)}, bf16[32,16,128]{2,1,0:T(8,128)(2,1)S(1)}, u32[]{:S(2)}, u32[]{:S(2)}) collective-permute-start(bf16[32,16,128]{2,1,0:T(8,128)(2,1)S(1)} %get-tuple-element.27), channel_id=1, source_target_pairs={{0,1},{1,0},{2,3},{3,2},{4,5},{5,4},{6,7},{7,6},{8,9},{9,8},{10,11... | collective-permute-start | bytes 393224 | tf_op jit(solution)/shard_map/ppermute | solution.py:412
  6.5 5.5 %collective-permute-start.4 = (bf16[32,16,128]{2,1,0:T(8,128)(2,1)S(1)}, bf16[32,16,128]{2,1,0:T(8,128)(2,1)S(1)}, u32[]{:S(2)}, u32[]{:S(2)}) collective-permute-start(bf16[32,16,128]{2,1,0:T(8,128)(2,1)S(1)} %get-tuple-element.28), channel_id=1, source_target_pairs={{0,3},{1,2},{2,1},{3,0},{4,7},{5,6},{6,5},{7,4},{8,11},{9,10},{10,... | collective-permute-start | bytes 393224 | tf_op jit(solution)/shard_map/ppermute | solution.py:412
  8.4 5.1 %collective-permute-start.2 = (bf16[2,2,128,128]{3,2,1,0:T(8,128)(2,1)S(1)}, bf16[2,2,128,128]{3,2,1,0:T(8,128)(2,1)S(1)}, u32[]{:S(2)}, u32[]{:S(2)}) collective-permute-start(bf16[2,2,128,128]{3,2,1,0:T(8,128)(2,1)S(1)} %collective-permute-done.refs_1_), channel_id=1, source_target_pairs={{0,8},{4,0},{8,16},{12,4},{16,24},{20,12},{24,28},{28,20},{1,9},{5... | collective-permute-start | bytes 393224 | tf_op jit(solution)/shard_map/ppermute | solution.py:408
  10.3 5.0 %collective-permute-start.7 = (bf16[32,16,128]{2,1,0:T(8,128)(2,1)S(1)}, bf16[32,16,128]{2,1,0:T(8,128)(2,1)S(1)}, u32[]{:S(2)}, u32[]{:S(2)}) collective-permute-start(bf16[32,16,128]{2,1,0:T(8,128)(2,1)S(1)} %get-tuple-element.31), channel_id=1, source_target_pairs={{0,2},{1,3},{2,0},{3,1},{4,6},{5,7},{6,4},{7,5},{8,10},{9,11},{10,... | collective-permute-start | bytes 393224 | tf_op jit(solution)/shard_map/ppermute | solution.py:412
  16.2 7.3 %collective-permute-start.9 = (bf16[2,2,128,128]{3,2,1,0:T(8,128)(2,1)S(1)}, bf16[2,2,128,128]{3,2,1,0:T(8,128)(2,1)S(1)}, u32[]{:S(2)}, u32[]{:S(2)}) collective-permute-start(bf16[2,2,128,128]{3,2,1,0:T(8,128)(2,1)S(1)} %get-tuple-element.35), channel_id=1, source_target_pairs={{0,4},{4,0},{8,12},{12,8},{16,20},{20,16},{24,28},{28,24},{1,5},{5... | collective-permute-start | bytes 393224 | tf_op jit(solution)/shard_map/ppermute | solution.py:399
  17.8 6.2 %collective-permute-start.5 = (bf16[32,16,128]{2,1,0:T(8,128)(2,1)S(1)}, bf16[32,16,128]{2,1,0:T(8,128)(2,1)S(1)}, u32[]{:S(2)}, u32[]{:S(2)}) collective-permute-start(bf16[32,16,128]{2,1,0:T(8,128)(2,1)S(1)} %get-tuple-element.29), channel_id=1, source_target_pairs={{0,1},{1,0},{2,3},{3,2},{4,5},{5,4},{6,7},{7,6},{8,9},{9,8},{10,11... | collective-permute-start | bytes 393224 | tf_op jit(solution)/shard_map/ppermute | solution.py:412
  17.8 9.5 %collective-permute-start.6 = (bf16[32,16,128]{2,1,0:T(8,128)(2,1)S(1)}, bf16[32,16,128]{2,1,0:T(8,128)(2,1)S(1)}, u32[]{:S(2)}, u32[]{:S(2)}) collective-permute-start(bf16[32,16,128]{2,1,0:T(8,128)(2,1)S(1)} %get-tuple-element.30), channel_id=1, source_target_pairs={{0,3},{1,2},{2,1},{3,0},{4,7},{5,6},{6,5},{7,4},{8,11},{9,10},{10,... | collective-permute-start | bytes 393224 | tf_op jit(solution)/shard_map/ppermute | solution.py:412
  19.5 7.8 %collective-permute-start.8 = (bf16[2,2,128,128]{3,2,1,0:T(8,128)(2,1)S(1)}, bf16[2,2,128,128]{3,2,1,0:T(8,128)(2,1)S(1)}, u32[]{:S(2)}, u32[]{:S(2)}) collective-permute-start(bf16[2,2,128,128]{3,2,1,0:T(8,128)(2,1)S(1)} %get-tuple-element.34), channel_id=1, source_target_pairs={{8,0},{0,4},{16,8},{4,12},{24,16},{12,20},{28,24},{20,28},{9,1},{1... | collective-permute-start | bytes 393224 | tf_op jit(solution)/shard_map/ppermute | solution.py:408
  20.0 7.8 %collective-permute-start.11 = (bf16[2,2,128,128]{3,2,1,0:T(8,128)(2,1)S(1)}, bf16[2,2,128,128]{3,2,1,0:T(8,128)(2,1)S(1)}, u32[]{:S(2)}, u32[]{:S(2)}) collective-permute-start(bf16[2,2,128,128]{3,2,1,0:T(8,128)(2,1)S(1)} %get-tuple-element.37), channel_id=1, source_target_pairs={{0,4},{4,0},{8,12},{12,8},{16,20},{20,16},{24,28},{28,24},{1,5},{5... | collective-permute-start | bytes 393224 | tf_op jit(solution)/shard_map/ppermute | solution.py:399
  23.5 5.0 %collective-permute-start.12 = (bf16[32,16,128]{2,1,0:T(8,128)(2,1)S(1)}, bf16[32,16,128]{2,1,0:T(8,128)(2,1)S(1)}, u32[]{:S(2)}, u32[]{:S(2)}) collective-permute-start(bf16[32,16,128]{2,1,0:T(8,128)(2,1)S(1)} %get-tuple-element.38), channel_id=1, source_target_pairs={{0,2},{1,3},{2,0},{3,1},{4,6},{5,7},{6,4},{7,5},{8,10},{9,11},{10,... | collective-permute-start | bytes 393224 | tf_op jit(solution)/shard_map/ppermute | solution.py:412
  24.0 5.7 %collective-permute-start.10 = (bf16[2,2,128,128]{3,2,1,0:T(8,128)(2,1)S(1)}, bf16[2,2,128,128]{3,2,1,0:T(8,128)(2,1)S(1)}, u32[]{:S(2)}, u32[]{:S(2)}) collective-permute-start(bf16[2,2,128,128]{3,2,1,0:T(8,128)(2,1)S(1)} %add.1), channel_id=1, source_target_pairs={{0,8},{4,0},{8,16},{12,4},{16,24},{20,12},{24,28},{28,20},{1,9},{5... | collective-permute-start | bytes 393224 | tf_op jit(solution)/shard_map/ppermute | solution.py:408

commit v20 on v19

--- a/solution.py
+++ b/solution.py
@@ -254,8 +254,10 @@
     needed = [jnp.max(range_ref[mask, 1:2, :]) - low for mask, low in zip(masks, lowest)]
     widths = [width for width in WIDTHS if width < reach] + [reach]
     every = range(len(masks))
-    together = functools.reduce(jnp.maximum, needed) <= widths[0]
-    pl.when(together)(functools.partial(run, every, widths[0]))
+    most = functools.reduce(jnp.maximum, needed)
+    together = most <= widths[-2]
+    for floor, width in zip([-1] + widths, widths[:-1]):
+        pl.when((most > floor) & (most <= width))(functools.partial(run, every, width))
 
     def apart():
         for place in every:

time: 30.8 us -> 30.5 us (level); the launches traced: 30.7 us -> 30 us
  starting transfers between devices: 20.6 us -> 18 us
  waiting for transfers between devices: 4.62 us -> 6.04 us
    ppermute x3, starting transfers between devices: 5.58 us -> 3.89 us  [ringed(): return lax.ppermute(block, 'seq', route)]
    ppermute x3, starting transfers between devices: 8.13 us -> 6.51 us  [paired(): lax.ppermute(block, 'seq', [(i, i ^ 1) for i in range(lax.axis_size('seq'...]
    ppermute x3, waiting for transfers between devices: 2.9 us -> 4.1 us  [ringed(): return lax.ppermute(block, 'seq', route)]
    ppermute x6, starting transfers between devices: 5.3 us -> 6.05 us  [swapped(): lax.ppermute(block, 'kvh', [(i, i ^ mask) for i in range(lax.axis_size('k...]
  transfers between devices with their start and end apart: 13 -> 13, of which waited for: 6 -> 7; matrix products, arithmetic and copies ran while one was open for 0% -> 0% of each run, Pallas kernels for 5% -> 6%
where the time goes in v20:
time: 30.5 us; the launch traced here: 30 us
  starting transfers between devices  18 us (59%)
  waiting for transfers between devices  6.04 us (20%)
  Pallas kernels  5.04 us (17%)
  between operations  0.85 us (3%)
    ppermute x3, starting transfers between devices, paired(): lax.ppermute(block, 'seq', [(i, i ^ 1) for i in range(lax.axis_size('seq'...  6.51 us
    ppermute x6, starting transfers between devices, swapped(): lax.ppermute(block, 'kvh', [(i, i ^ mask) for i in range(lax.axis_size('k...  6.05 us
    ppermute x3, waiting for transfers between devices, ringed(): return lax.ppermute(block, 'seq', route)  4.1 us
    ppermute x3, starting transfers between devices, ringed(): return lax.ppermute(block, 'seq', route)  3.89 us
    pallas_call x2, Pallas kernels, gradients(): pl.pallas_call(functools.partial(grad_kernel, masks, parts, carried is No...  2.76 us
    ppermute x1, starting transfers between devices, shifted(): lax.ppermute(block, 'seq', [(i, (i + distance) % count) for i in range(co...  1.58 us
    pallas_call x1, Pallas kernels, prepare(): pl.pallas_call(functools.partial(prep_kernel, parts), out_shape=(block,)...  1.3 us
    ppermute x6, waiting for transfers between devices, swapped(): lax.ppermute(block, 'kvh', [(i, i ^ mask) for i in range(lax.axis_size('k...  1.03 us
  transfers between devices with their start and end apart: 13, of which 7 were waited for; matrix products, arithmetic and copies ran while one was open for 0% of the time, Pallas kernels for 6%

profile of v20, /device:TPU:0, one launch (start us, length us, event | category | flops | bytes accessed | tf_op | source)
XLA Modules:
  0.0 30.0 jit_solution(14061746569302768020)
XLA Ops:
  0.6 0.0 copy-start
  0.6 1.3 %prepare.1 = (bf16[2,2,128,128]{3,2,1,0:T(8,128)(2,1)S(1)}, bf16[2,2,128,128]{3,2,1,0:T(8,128)(2,1)S(1)}, bf16[2,2,128,128]{3,2,1,0:T(8,128)(2,1)S(1)}, bf16[32,...) custom-call(s32[8]{0:T(128)} %lengths_ref.1, ...), custom_call_target="tpu_custom_call" | custom-call | tf_op jit(solution)/shard_map/prepare/pallas_call | solution.py:90
  1.9 3.0 %collective-permute-start = (bf16[2,2,128,128]{3,2,1,0:T(8,128)(2,1)S(1)}, bf16[2,2,128,128]{3,2,1,0:T(8,128)(2,1)S(1)}, u32[]{:S(2)}, u32[]{:S(2)}) collective-permute-start(bf16[2,2,128,128]{3,2,1,0:T(8,128)(2,1)S(1)} %get-tuple-element.24), channel_id=1, source_target_pairs={{0,4},{4,0},{8,12},{12,8},{16,20},{20,16},{24,28},{28,24},{1,5},{5... | collective-permute-start | bytes 393224 | tf_op jit(solution)/shard_map/ppermute | solution.py:401
  4.9 1.6 %collective-permute-start.1 = (bf16[2,2,128,128]{3,2,1,0:T(8,128)(2,1)S(1)}, bf16[2,2,128,128]{3,2,1,0:T(8,128)(2,1)S(1)}, u32[]{:S(2)}, u32[]{:S(2)}) collective-permute-start(bf16[2,2,128,128]{3,2,1,0:T(8,128)(2,1)S(1)} %get-tuple-element.25), channel_id=1, source_target_pairs={{0,8},{4,12},{8,16},{12,20},{16,24},{20,28},{24,0},{28,4},{1,9},{5... | collective-permute-start | bytes 393224 | tf_op jit(solution)/shard_map/ppermute | solution.py:397
  6.5 0.0 collective-permute-start.3
  6.5 1.6 %collective-permute-start.4 = (bf16[32,16,128]{2,1,0:T(8,128)(2,1)S(1)}, bf16[32,16,128]{2,1,0:T(8,128)(2,1)S(1)}, u32[]{:S(2)}, u32[]{:S(2)}) collective-permute-start(bf16[32,16,128]{2,1,0:T(8,128)(2,1)S(1)} %get-tuple-element.28), channel_id=1, source_target_pairs={{0,3},{1,2},{2,1},{3,0},{4,7},{5,6},{6,5},{7,4},{8,11},{9,10},{10,... | collective-permute-start | bytes 393224 | tf_op jit(solution)/shard_map/ppermute | solution.py:414
  8.2 0.3 collective-permute-done.refs_1_
  8.4 1.8 %collective-permute-start.2 = (bf16[2,2,128,128]{3,2,1,0:T(8,128)(2,1)S(1)}, bf16[2,2,128,128]{3,2,1,0:T(8,128)(2,1)S(1)}, u32[]{:S(2)}, u32[]{:S(2)}) collective-permute-start(bf16[2,2,128,128]{3,2,1,0:T(8,128)(2,1)S(1)} %collective-permute-done.refs_1_), channel_id=1, source_target_pairs={{0,8},{4,0},{8,16},{12,4},{16,24},{20,12},{24,28},{28,20},{1,9},{5... | collective-permute-start | bytes 393224 | tf_op jit(solution)/shard_map/ppermute | solution.py:410
  10.3 1.5 %collective-permute-start.7 = (bf16[32,16,128]{2,1,0:T(8,128)(2,1)S(1)}, bf16[32,16,128]{2,1,0:T(8,128)(2,1)S(1)}, u32[]{:S(2)}, u32[]{:S(2)}) collective-permute-start(bf16[32,16,128]{2,1,0:T(8,128)(2,1)S(1)} %get-tuple-element.31), channel_id=1, source_target_pairs={{0,2},{1,3},{2,0},{3,1},{4,6},{5,7},{6,4},{7,5},{8,10},{9,11},{10,... | collective-permute-start | bytes 393224 | tf_op jit(solution)/shard_map/ppermute | solution.py:414
  11.8 0.0 collective-permute-done.1.refs_2_
  11.8 0.0 collective-permute-done.3.refs_5_
  11.8 0.2 collective-permute-done.4.refs_6_
  12.0 1.6 %collective-permute-done.2.refs_3_ = bf16[2,2,128,128]{3,2,1,0:T(8,128)(2,1)S(1)} collective-permute-done((bf16[2,2,128,128]{3,2,1,0:T(8,128)(2,1)S(1)}, bf16[2,2,128,128]{3,2,1,0:T(8,128)(2,1)S(1)}, u32[]{:S(2)}, u32[]{:S(2)}) %collective-permute-start.2) | collective-permute-done | bytes 131104 | tf_op jit(solution)/shard_map/ppermute | solution.py:410
  13.6 0.0 copy-done
  13.6 1.6 %gradients.2 = (bf16[32,16,128]{2,1,0:T(8,128)(2,1)S(1)}, bf16[32,16,128]{2,1,0:T(8,128)(2,1)S(1)}, bf16[32,16,128]{2,1,0:T(8,128)(2,1)S(1)}, bf16[2,2,512,128]{3,2,1,0:T(8,128)(2,1)S(1)}, f32[2,2,512,128]{3,2,1,0:T(8,128)S(1)}) custom-call(s32[4,2,256]{2,1,0:T(2,128)S(1)} %get-tuple-element.22.range_ref, bf16[128,16,128]{2,1,0:T(8,128)(2,1)S(1)} %copy-done, ...), custom_call_target="tpu_custom_call" | custom-call | flops 1006632960 | bytes 2097152 | tf_op jit(solution)/shard_map/gradients/pallas_call | solution.py:301
  15.2 0.0 collective-permute-done.7.refs_0_
  15.2 1.1 %gradients.3 = (bf16[32,16,128]{2,1,0:T(8,128)(2,1)S(1)}, f32[2,2,128,128]{3,2,1,0:T(8,128)S(1)}, bf16[2,2,128,128]{3,2,1,0:T(8,128)(2,1)S(1)}, bf16[2,2,128,128...) custom-call(s32[4,2,256]{2,1,0:T(2,128)S(1)} %get-tuple-element.22.range_ref, ...), custom_call_target="tpu_custom_call" | custom-call | flops 335544320 | bytes 2097152 | tf_op jit(solution)/shard_map/gradients/pallas_call | solution.py:301
  16.4 1.6 %collective-permute-start.9 = (bf16[2,2,128,128]{3,2,1,0:T(8,128)(2,1)S(1)}, bf16[2,2,128,128]{3,2,1,0:T(8,128)(2,1)S(1)}, u32[]{:S(2)}, u32[]{:S(2)}) collective-permute-start(bf16[2,2,128,128]{3,2,1,0:T(8,128)(2,1)S(1)} %get-tuple-element.35), channel_id=1, source_target_pairs={{0,4},{4,0},{8,12},{12,8},{16,20},{20,16},{24,28},{28,24},{1,5},{5... | collective-permute-start | bytes 393224 | tf_op jit(solution)/shard_map/ppermute | solution.py:401
  18.0 0.0 collective-permute-start.5
  18.0 1.6 %collective-permute-start.6 = (bf16[32,16,128]{2,1,0:T(8,128)(2,1)S(1)}, bf16[32,16,128]{2,1,0:T(8,128)(2,1)S(1)}, u32[]{:S(2)}, u32[]{:S(2)}) collective-permute-start(bf16[32,16,128]{2,1,0:T(8,128)(2,1)S(1)} %get-tuple-element.30), channel_id=1, source_target_pairs={{0,3},{1,2},{2,1},{3,0},{4,7},{5,6},{6,5},{7,4},{8,11},{9,10},{10,... | collective-permute-start | bytes 393224 | tf_op jit(solution)/shard_map/ppermute | solution.py:414
  19.7 0.5 %collective-permute-start.8 = (bf16[2,2,128,128]{3,2,1,0:T(8,128)(2,1)S(1)}, bf16[2,2,128,128]{3,2,1,0:T(8,128)(2,1)S(1)}, u32[]{:S(2)}, u32[]{:S(2)}) collective-permute-start(bf16[2,2,128,128]{3,2,1,0:T(8,128)(2,1)S(1)} %get-tuple-element.34), channel_id=1, source_target_pairs={{8,0},{0,4},{16,8},{4,12},{24,16},{12,20},{28,24},{20,28},{9,1},{1... | collective-permute-start | bytes 393224 | tf_op jit(solution)/shard_map/ppermute | solution.py:410
  20.2 1.9 %collective-permute-start.11 = (bf16[2,2,128,128]{3,2,1,0:T(8,128)(2,1)S(1)}, bf16[2,2,128,128]{3,2,1,0:T(8,128)(2,1)S(1)}, u32[]{:S(2)}, u32[]{:S(2)}) collective-permute-start(bf16[2,2,128,128]{3,2,1,0:T(8,128)(2,1)S(1)} %get-tuple-element.37), channel_id=1, source_target_pairs={{0,4},{4,0},{8,12},{12,8},{16,20},{20,16},{24,28},{28,24},{1,5},{5... | collective-permute-start | bytes 393224 | tf_op jit(solution)/shard_map/ppermute | solution.py:401
  22.1 0.0 collective-permute-done.9.left
  22.1 1.3 %collective-permute-start.12 = (bf16[32,16,128]{2,1,0:T(8,128)(2,1)S(1)}, bf16[32,16,128]{2,1,0:T(8,128)(2,1)S(1)}, u32[]{:S(2)}, u32[]{:S(2)}) collective-permute-start(bf16[32,16,128]{2,1,0:T(8,128)(2,1)S(1)} %get-tuple-element.38), channel_id=1, source_target_pairs={{0,2},{1,3},{2,0},{3,1},{4,6},{5,7},{6,4},{7,5},{8,10},{9,11},{10,... | collective-permute-start | bytes 393224 | tf_op jit(solution)/shard_map/ppermute | solution.py:414
  23.4 0.0 collective-permute-done.5.refs_0_
  23.4 1.5 %collective-permute-start.10 = (bf16[2,2,128,128]{3,2,1,0:T(8,128)(2,1)S(1)}, bf16[2,2,128,128]{3,2,1,0:T(8,128)(2,1)S(1)}, u32[]{:S(2)}, u32[]{:S(2)}) collective-permute-start(bf16[2,2,128,128]{3,2,1,0:T(8,128)(2,1)S(1)} %add.1), channel_id=1, source_target_pairs={{0,8},{4,0},{8,16},{12,4},{16,24},{20,12},{24,28},{28,20},{1,9},{5... | collective-permute-start | bytes 393224 | tf_op jit(solution)/shard_map/ppermute | solution.py:410
  24.9 0.0 collective-permute-done.6.refs_1_
  24.9 0.7 %collective-permute-done.8.refs_2_ = bf16[2,2,128,128]{3,2,1,0:T(8,128)(2,1)S(1)} collective-permute-done((bf16[2,2,128,128]{3,2,1,0:T(8,128)(2,1)S(1)}, bf16[2,2,128,128]{3,2,1,0:T(8,128)(2,1)S(1)}, u32[]{:S(2)}, u32[]{:S(2)}) %collective-permute-start.8) | collective-permute-done | bytes 131104 | tf_op jit(solution)/shard_map/ppermute | solution.py:410
  25.6 0.6 %collective-permute-done.11.refs_4_ = bf16[2,2,128,128]{3,2,1,0:T(8,128)(2,1)S(1)} collective-permute-done((bf16[2,2,128,128]{3,2,1,0:T(8,128)(2,1)S(1)}, bf16[2,2,128,128]{3,2,1,0:T(8,128)(2,1)S(1)}, u32[]{:S(2)}, u32[]{:S(2)}) %collective-permute-start.11) | collective-permute-done | bytes 131104 | tf_op jit(solution)/shard_map/ppermute | solution.py:401
  26.2 0.8 %collective-permute-done.12.refs_5_ = bf16[32,16,128]{2,1,0:T(8,128)(2,1)S(1)} collective-permute-done((bf16[32,16,128]{2,1,0:T(8,128)(2,1)S(1)}, bf16[32,16,128]{2,1,0:T(8,128)(2,1)S(1)}, u32[]{:S(2)}, u32[]{:S(2)}) %collective-permute-start.12) | collective-permute-done | bytes 131104 | tf_op jit(solution)/shard_map/ppermute | solution.py:414
  27.0 1.8 %collective-permute-done.10.refs_3_ = bf16[2,2,128,128]{3,2,1,0:T(8,128)(2,1)S(1)} collective-permute-done((bf16[2,2,128,128]{3,2,1,0:T(8,128)(2,1)S(1)}, bf16[2,2,128,128]{3,2,1,0:T(8,128)(2,1)S(1)}, u32[]{:S(2)}, u32[]{:S(2)}) %collective-permute-start.10) | collective-permute-done | bytes 131104 | tf_op jit(solution)/shard_map/ppermute | solution.py:410
  28.8 1.0 %finish.1 = (bf16[32,64,128]{2,1,0:T(8,128)(2,1)}, bf16[128,2,128]{2,1,0:T(2,128)(2,1)}, bf16[128,2,128]{2,1,0:T(2,128)(2,1)}) custom-call(bf16[32,16,128]{2,1,0:T(8,128)(2,1)S(1)} %collective-permute-done.5.refs_0_, bf16[32,16,128]{2,1,0:T(8,128)(2,1)S(1)} %collective-permute-done.6.refs_1_, bf16[2,2,128,128]{3,2,1,0:T(8,128)(2,1)S(1)} %collective-permute-done.8.refs_2_, ...), custom_call_target="tpu_custom_call" | custom-call | tf_op jit(solution)/shard_map/finish/pallas_call | solution.py:376
  (1 shorter events, 0.0 us)
Async XLA Ops:
  0.6 12.9 %copy-start = (bf16[128,16,128]{2,1,0:T(8,128)(2,1)S(1)}, bf16[128,16,128]{2,1,0:T(8,128)(2,1)}, u32[]{:S(2)}) copy-start(bf16[128,16,128]{2,1,0:T(8,128)(2,1)} %q_ref.3) | copy-start | bytes 1572868
  1.9 6.5 %collective-permute-start = (bf16[2,2,128,128]{3,2,1,0:T(8,128)(2,1)S(1)}, bf16[2,2,128,128]{3,2,1,0:T(8,128)(2,1)S(1)}, u32[]{:S(2)}, u32[]{:S(2)}) collective-permute-start(bf16[2,2,128,128]{3,2,1,0:T(8,128)(2,1)S(1)} %get-tuple-element.24), channel_id=1, source_target_pairs={{0,4},{4,0},{8,12},{12,8},{16,20},{20,16},{24,28},{28,24},{1,5},{5... | collective-permute-start | bytes 393224 | tf_op jit(solution)/shard_map/ppermute | solution.py:401
  4.9 6.8 %collective-permute-start.1 = (bf16[2,2,128,128]{3,2,1,0:T(8,128)(2,1)S(1)}, bf16[2,2,128,128]{3,2,1,0:T(8,128)(2,1)S(1)}, u32[]{:S(2)}, u32[]{:S(2)}) collective-permute-start(bf16[2,2,128,128]{3,2,1,0:T(8,128)(2,1)S(1)} %get-tuple-element.25), channel_id=1, source_target_pairs={{0,8},{4,12},{8,16},{12,20},{16,24},{20,28},{24,0},{28,4},{1,9},{5... | collective-permute-start | bytes 393224 | tf_op jit(solution)/shard_map/ppermute | solution.py:397
  6.5 5.3 %collective-permute-start.3 = (bf16[32,16,128]{2,1,0:T(8,128)(2,1)S(1)}, bf16[32,16,128]{2,1,0:T(8,128)(2,1)S(1)}, u32[]{:S(2)}, u32[]{:S(2)}) collective-permute-start(bf16[32,16,128]{2,1,0:T(8,128)(2,1)S(1)} %get-tuple-element.27), channel_id=1, source_target_pairs={{0,1},{1,0},{2,3},{3,2},{4,5},{5,4},{6,7},{7,6},{8,9},{9,8},{10,11... | collective-permute-start | bytes 393224 | tf_op jit(solution)/shard_map/ppermute | solution.py:414
  6.5 5.5 %collective-permute-start.4 = (bf16[32,16,128]{2,1,0:T(8,128)(2,1)S(1)}, bf16[32,16,128]{2,1,0:T(8,128)(2,1)S(1)}, u32[]{:S(2)}, u32[]{:S(2)}) collective-permute-start(bf16[32,16,128]{2,1,0:T(8,128)(2,1)S(1)} %get-tuple-element.28), channel_id=1, source_target_pairs={{0,3},{1,2},{2,1},{3,0},{4,7},{5,6},{6,5},{7,4},{8,11},{9,10},{10,... | collective-permute-start | bytes 393224 | tf_op jit(solution)/shard_map/ppermute | solution.py:414
  8.4 5.1 %collective-permute-start.2 = (bf16[2,2,128,128]{3,2,1,0:T(8,128)(2,1)S(1)}, bf16[2,2,128,128]{3,2,1,0:T(8,128)(2,1)S(1)}, u32[]{:S(2)}, u32[]{:S(2)}) collective-permute-start(bf16[2,2,128,128]{3,2,1,0:T(8,128)(2,1)S(1)} %collective-permute-done.refs_1_), channel_id=1, source_target_pairs={{0,8},{4,0},{8,16},{12,4},{16,24},{20,12},{24,28},{28,20},{1,9},{5... | collective-permute-start | bytes 393224 | tf_op jit(solution)/shard_map/ppermute | solution.py:410
  10.3 5.0 %collective-permute-start.7 = (bf16[32,16,128]{2,1,0:T(8,128)(2,1)S(1)}, bf16[32,16,128]{2,1,0:T(8,128)(2,1)S(1)}, u32[]{:S(2)}, u32[]{:S(2)}) collective-permute-start(bf16[32,16,128]{2,1,0:T(8,128)(2,1)S(1)} %get-tuple-element.31), channel_id=1, source_target_pairs={{0,2},{1,3},{2,0},{3,1},{4,6},{5,7},{6,4},{7,5},{8,10},{9,11},{10,... | collective-permute-start | bytes 393224 | tf_op jit(solution)/shard_map/ppermute | solution.py:414
  16.4 5.7 %collective-permute-start.9 = (bf16[2,2,128,128]{3,2,1,0:T(8,128)(2,1)S(1)}, bf16[2,2,128,128]{3,2,1,0:T(8,128)(2,1)S(1)}, u32[]{:S(2)}, u32[]{:S(2)}) collective-permute-start(bf16[2,2,128,128]{3,2,1,0:T(8,128)(2,1)S(1)} %get-tuple-element.35), channel_id=1, source_target_pairs={{0,4},{4,0},{8,12},{12,8},{16,20},{20,16},{24,28},{28,24},{1,5},{5... | collective-permute-start | bytes 393224 | tf_op jit(solution)/shard_map/ppermute | solution.py:401
  18.0 5.4 %collective-permute-start.5 = (bf16[32,16,128]{2,1,0:T(8,128)(2,1)S(1)}, bf16[32,16,128]{2,1,0:T(8,128)(2,1)S(1)}, u32[]{:S(2)}, u32[]{:S(2)}) collective-permute-start(bf16[32,16,128]{2,1,0:T(8,128)(2,1)S(1)} %get-tuple-element.29), channel_id=1, source_target_pairs={{0,1},{1,0},{2,3},{3,2},{4,5},{5,4},{6,7},{7,6},{8,9},{9,8},{10,11... | collective-permute-start | bytes 393224 | tf_op jit(solution)/shard_map/ppermute | solution.py:414
  18.0 6.9 %collective-permute-start.6 = (bf16[32,16,128]{2,1,0:T(8,128)(2,1)S(1)}, bf16[32,16,128]{2,1,0:T(8,128)(2,1)S(1)}, u32[]{:S(2)}, u32[]{:S(2)}) collective-permute-start(bf16[32,16,128]{2,1,0:T(8,128)(2,1)S(1)} %get-tuple-element.30), channel_id=1, source_target_pairs={{0,3},{1,2},{2,1},{3,0},{4,7},{5,6},{6,5},{7,4},{8,11},{9,10},{10,... | collective-permute-start | bytes 393224 | tf_op jit(solution)/shard_map/ppermute | solution.py:414
  19.7 6.0 %collective-permute-start.8 = (bf16[2,2,128,128]{3,2,1,0:T(8,128)(2,1)S(1)}, bf16[2,2,128,128]{3,2,1,0:T(8,128)(2,1)S(1)}, u32[]{:S(2)}, u32[]{:S(2)}) collective-permute-start(bf16[2,2,128,128]{3,2,1,0:T(8,128)(2,1)S(1)} %get-tuple-element.34), channel_id=1, source_target_pairs={{8,0},{0,4},{16,8},{4,12},{24,16},{12,20},{28,24},{20,28},{9,1},{1... | collective-permute-start | bytes 393224 | tf_op jit(solution)/shard_map/ppermute | solution.py:410
  20.2 6.1 %collective-permute-start.11 = (bf16[2,2,128,128]{3,2,1,0:T(8,128)(2,1)S(1)}, bf16[2,2,128,128]{3,2,1,0:T(8,128)(2,1)S(1)}, u32[]{:S(2)}, u32[]{:S(2)}) collective-permute-start(bf16[2,2,128,128]{3,2,1,0:T(8,128)(2,1)S(1)} %get-tuple-element.37), channel_id=1, source_target_pairs={{0,4},{4,0},{8,12},{12,8},{16,20},{20,16},{24,28},{28,24},{1,5},{5... | collective-permute-start | bytes 393224 | tf_op jit(solution)/shard_map/ppermute | solution.py:401
  22.1 5.0 %collective-permute-start.12 = (bf16[32,16,128]{2,1,0:T(8,128)(2,1)S(1)}, bf16[32,16,128]{2,1,0:T(8,128)(2,1)S(1)}, u32[]{:S(2)}, u32[]{:S(2)}) collective-permute-start(bf16[32,16,128]{2,1,0:T(8,128)(2,1)S(1)} %get-tuple-element.38), channel_id=1, source_target_pairs={{0,2},{1,3},{2,0},{3,1},{4,6},{5,7},{6,4},{7,5},{8,10},{9,11},{10,... | collective-permute-start | bytes 393224 | tf_op jit(solution)/shard_map/ppermute | solution.py:414
  23.4 5.5 %collective-permute-start.10 = (bf16[2,2,128,128]{3,2,1,0:T(8,128)(2,1)S(1)}, bf16[2,2,128,128]{3,2,1,0:T(8,128)(2,1)S(1)}, u32[]{:S(2)}, u32[]{:S(2)}) collective-permute-start(bf16[2,2,128,128]{3,2,1,0:T(8,128)(2,1)S(1)} %add.1), channel_id=1, source_target_pairs={{0,8},{4,0},{8,16},{12,4},{16,24},{20,12},{24,28},{28,20},{1,9},{5... | collective-permute-start | bytes 393224 | tf_op jit(solution)/shard_map/ppermute | solution.py:410
